TPU v7x, 256 devices: a whole 4x4x8 slice. The times are simulated.
256 devices in a mesh: dom: 128 (over z, x, y_lo, core), band: 2 (over y_hi).
Axes of the slice: x: 4, y: 4 (y_hi: 2, y_lo: 2; y = y_hi * 2 + y_lo), z: 8, core: 2. Of those that a mesh axis runs over, the one named last changes fastest.
Arguments:
- orbitals: float32 [16, 1024, 32, 128], P('band', 'dom'), may hold values from -10 to 10
- potential: float32 [1024, 32, 128], P('dom'), may hold values from -1 to 1
- coefficients: float32 [16, 16], replicated, may hold values from -1.5 to 1.5
Outputs:
- intersection: float32 [16, 16], replicated
- rotated: float32 [16, 4096, 1024], P('band', 'dom')
All inputs are finite; a program needn't handle non-finite values.
Results may differ from a plain program's by a relative error of at most 0.000071.
Values sent between devices are 32-bit elements; how exact they have to be, the bound alone decides.
No kernel may reach another device: no remote copies, remote signals or barrier semaphores. Data moves between devices by JAX's collectives and lax.ppermute only.
A program may use at most 64 MiB of HBM per device.

v0:
```python
import jax
import jax.numpy as jnp
from jax import lax
from jax.sharding import PartitionSpec as P

STENCIL = (
    -5369.0 / 1800.0,
    12.0 / 7.0,
    -15.0 / 56.0,
    10.0 / 189.0,
    -1.0 / 112.0,
    2.0 / 1925.0,
    -1.0 / 16632.0,
)
filter_center = 8.5
filter_half = 6.5


def padded(x, sides, width):
    for axis, dim in sides:
        size, length = (lax.axis_size(axis), x.shape[dim])
        up = [(i, (i + 1) % size) for i in range(size - 1)]
        down = [(j, i) for i, j in up]
        last = lax.slice_in_dim(x, length - width, length, axis=dim)
        initial = lax.slice_in_dim(x, 0, width, axis=dim)
        before = lax.ppermute(last, axis, up)
        after = lax.ppermute(initial, axis, down)
        x = jnp.concatenate([before, x, after], axis=dim)
    return x


def hamiltonian(field, potential):
    size_x = field.shape[1]
    size_y = field.shape[2]
    size_z = field.shape[3]
    pad_x = padded(field, (("dom", 1),), 6)
    pad_y = jnp.pad(field, ((0, 0), (0, 0), (6, 6), (0, 0)))
    pad_z = jnp.pad(field, ((0, 0), (0, 0), (0, 0), (6, 6)))
    total = 3.0 * STENCIL[0] * field
    for offset in range(1, 7):
        beside = (
            pad_x[:, 6 + offset : 6 + offset + size_x] + pad_x[:, 6 - offset : 6 - offset + size_x]
        )
        beside = (
            beside
            + pad_y[:, :, 6 + offset : 6 + offset + size_y]
            + pad_y[:, :, 6 - offset : 6 - offset + size_y]
        )
        beside = (
            beside
            + pad_z[:, :, :, 6 + offset : 6 + offset + size_z]
            + pad_z[:, :, :, 6 - offset : 6 - offset + size_z]
        )
        total = total + STENCIL[offset] * beside
    return -0.5 * total + potential[None] * field


def scaled_step(field, potential):
    return (hamiltonian(field, potential) - filter_center * field) / filter_half


def arrange(received):
    count = received.shape[0]
    return received.reshape(count, received.shape[1] * received.shape[2], received.shape[3])


def intersection_and_turn(whole, coefficients, count_all):
    flat = whole.reshape(whole.shape[0], -1)
    partial_intersection = jnp.dot(flat, flat.T, precision=lax.Precision.HIGHEST)
    intersection = lax.psum(partial_intersection, "dom") / count_all
    block = whole.shape[0] // lax.axis_size("band")
    start = lax.axis_index("band") * block
    mine = lax.dynamic_slice_in_dim(coefficients, start, block, 1)
    turned = jnp.dot(mine.T, flat, precision=lax.Precision.HIGHEST)
    return (intersection, turned.reshape((block,) + whole.shape[1:]))


def local(orbitals, potential, coefficients):
    block, size_x, size_y, depth = orbitals.shape
    count_all = size_x * size_y * depth * lax.axis_size("dom")
    first = scaled_step(orbitals, potential)
    second = 2.0 * scaled_step(first, potential) - orbitals
    filtered = 2.0 * scaled_step(second, potential) - first
    lines = jnp.transpose(filtered, (0, 3, 2, 1))
    whole_slab = lax.all_gather(lines, "band", axis=0, tiled=True)
    received = lax.all_to_all(whole_slab, "dom", split_axis=1, concat_axis=3, tiled=True)
    intersection, rotated = intersection_and_turn(received, coefficients, count_all)
    rotated = arrange(rotated)
    return (intersection, rotated)


def solution(mesh):
    placed = (P("band", "dom", None, None), P("dom", None, None), P())
    return jax.shard_map(
        local, mesh=mesh, in_specs=placed, out_specs=(P(), P("band", "dom", None)), check_vma=False
    )
```

profile of v0, /device:TPU:1, one launch (start us, length us, event | category | flops | bytes accessed | tf_op | source)
XLA Modules:
  0.0 550.0 jit_solution(17760421238810585274)
XLA Ops:
  8.9 4.6 collective-permute-start.1
  13.5 1.9 collective-permute-start
  15.4 15.4 %collective-permute-done.1 = f32[8,6,32,128]{3,2,1,0:T(8,128)S(1)} collective-permute-done((f32[8,6,32,128]{3,2,1,0:T(8,128)S(1)}, f32[8,6,32,128]{3,2,1,0:T(8,128)S(1)}, u32[]{:S(2)}, u32[]{:S(2)}) %collective-permute-start.1) | collective-permute-done | bytes 786464 | tf_op jit(solution)/shard_map/ppermute | solution.py:26
  31.8 3.5 broadcast_multiply_fusion
  35.5 4.4 collective-permute-start.3
  39.9 1.9 collective-permute-start.2
  41.8 15.4 %collective-permute-done.3 = f32[8,6,32,128]{3,2,1,0:T(8,128)S(1)} collective-permute-done((f32[8,6,32,128]{3,2,1,0:T(8,128)S(1)}, f32[8,6,32,128]{3,2,1,0:T(8,128)S(1)}, u32[]{:S(2)}, u32[]{:S(2)}) %collective-permute-start.3) | collective-permute-done | bytes 786464 | tf_op jit(solution)/shard_map/ppermute | solution.py:26
  57.2 3.7 fusion.72
  61.0 4.4 collective-permute-start.5
  65.4 1.9 collective-permute-start.4
  67.4 15.4 %collective-permute-done.5 = f32[8,6,32,128]{3,2,1,0:T(8,128)S(1)} collective-permute-done((f32[8,6,32,128]{3,2,1,0:T(8,128)S(1)}, f32[8,6,32,128]{3,2,1,0:T(8,128)S(1)}, u32[]{:S(2)}, u32[]{:S(2)}) %collective-permute-start.5) | collective-permute-done | bytes 786464 | tf_op jit(solution)/shard_map/ppermute | solution.py:26
  82.8 3.7 fusion.21
  88.1 43.3 %all-gather.2.cloned.1.call-done = f32[16,128,32,8]{1,3,2,0:T(8,128)} async-done(((f32[8,128,32,8]{1,3,2,0:T(8,128)}), f32[16,128,32,8]{1,3,2,0:T(8,128)}) %all-gather.2.cloned.1.call-update) | async-done | bytes 2097168 | tf_op jit(solution)/shard_map/all_gather | solution.py:85
  131.4 8.5 %copy.64 = f32[16,128,32,8]{2,3,0,1:T(8,128)} copy(f32[16,128,32,8]{1,3,2,0:T(8,128)} %all-gather.2.cloned.1.call-done) | data formatting | bytes 4194304 | tf_op jit(solution)/shard_map/all_gather | solution.py:85
  139.9 7.7 %reshape.18 = f32[128,1,4096]{2,1,0:T(1,128)} reshape(f32[128,16,8,32]{3,2,1,0:T(8,128)} %bitcast.28) | data formatting | bytes 4194304
  147.6 11.5 %all-to-all-start = ((f32[128,1,4096]{2,1,0:T(1,128)}), f32[128,1,4096]{2,1,0:T(1,128)S(1)}, u32[]{:S(2)}, u32[]{:S(2)}) async-start(f32[128,1,4096]{2,1,0:T(1,128)} %reshape.18), calls=%async_computation | async-start | bytes 4194304 | tf_op jit(solution)/shard_map/all_to_all | solution.py:86
  159.1 50.2 %all-to-all-done = f32[128,1,4096]{2,1,0:T(1,128)S(1)} async-done(((f32[128,1,4096]{2,1,0:T(1,128)}), f32[128,1,4096]{2,1,0:T(1,128)S(1)}, u32[]{:S(2)}, u32[]{:S(2)}) %all-to-all-start) | async-done | bytes 2097184 | tf_op jit(solution)/shard_map/all_to_all | solution.py:86
  211.1 7.4 %reduce = f32[128,4096]{1,0:T(8,128)S(1)} reduce(f32[128,1,4096]{2,1,0:T(1,128)} %copy-done.2, f32[]{:T(128)} %broadcast.101), dimensions={1}, to_apply=%all_to_all.11.reduce_sub_computation | reduce | bytes 4194308 | tf_op jit(solution)/shard_map/all_to_all | solution.py:86
  218.6 4.8 reshape.19
  223.4 7.1 %copy.65 = f32[16,128,32,8]{1,0,3,2:T(8,128)S(1)} copy(f32[16,128,32,8]{2,3,0,1:T(8,128)} %bitcast.29) | data formatting | bytes 4194304 | tf_op jit(solution)/shard_map/all_to_all | solution.py:86
  230.5 2.9 fusion.4
  233.4 281.0 %psum.7 = f32[16,16]{1,0:T(8,128)S(1)} all-reduce(f32[16,16]{1,0:T(8,128)S(1)} %fusion.4), channel_id=1, replica_groups=mesh['dom'=128,'band'=2] {'dom'}, use_global_device_ids=true, to_apply=%region_0.1 | all-reduce | flops 256 | bytes 2048 | tf_op jit(solution)/shard_map/psum | solution.py:70
  515.0 8.9 %copy.67 = f32[16,1,32,128,8]{0,4,3,2,1:T(8,128)} copy(f32[16,1,32,128,8]{3,0,4,2,1:T(8,128)S(1)} %bitcast.30) | data formatting | bytes 4194304 | tf_op jit(solution)/shard_map/all_to_all | solution.py:86
  523.9 17.6 %fusion = f32[8,32,1024]{2,0,1:T(8,128)S(1)} fusion(f32[16,1,32,128,8]{0,4,3,2,1:T(8,128)} %copy.67, f32[16,16]{1,0:T(8,128)S(1)} %copy-done, s32[]{:T(128)S(6)} %select_n.3), kind=kOutput, calls=%fused_computation | convolution fusion | flops 50331648 | bytes 3146756 | tf_op jit(solution)/shard_map/dot_general | solution.py:74
  (24 shorter events, 8.5 us)
Async XLA Ops:
  7.2 516.8 %copy-start = (f32[16,16]{1,0:T(8,128)S(1)}, f32[16,16]{1,0:T(8,128)}, u32[]{:S(2)}) copy-start(f32[16,16]{1,0:T(8,128)} %param.5) | copy-start | bytes 3076
  7.2 23.7 %copy-start.1 = (f32[8,8,32,128]{3,2,1,0:T(8,128)S(1)}, f32[8,8,32,128]{3,2,1,0:T(8,128)}, u32[]{:S(2)}) copy-start(f32[8,8,32,128]{3,2,1,0:T(8,128)} %param.3) | copy-start | bytes 3145732
  7.2 124.2 %all-gather.2.cloned.1.call-start = ((), (), s32[]{:S(2)}) async-start(), calls=%async_computation.1 | async-start | bytes 3145728 | tf_op jit(solution)/shard_map/all_gather | solution.py:85
  8.9 21.9 %collective-permute-start.1 = (f32[8,6,32,128]{3,2,1,0:T(8,128)S(1)}, f32[8,6,32,128]{3,2,1,0:T(8,128)S(1)}, u32[]{:S(2)}, u32[]{:S(2)}) collective-permute-start(f32[8,6,32,128]{3,2,1,0:T(8,128)S(1)} %get-tuple-element.17), channel_id=1, source_target_pairs={{0,2},{2,4},{4,6},{6,8},{8,10},{10,12},{12,14},{14,16},{16,18},{18... | collective-permute-start | bytes 2359304 | tf_op jit(solution)/shard_map/ppermute | solution.py:26
  13.5 17.7 %collective-permute-start = (f32[8,6,32,128]{3,2,1,0:T(8,128)S(1)}, f32[8,6,32,128]{3,2,1,0:T(8,128)S(1)}, u32[]{:S(2)}, u32[]{:S(2)}) collective-permute-start(f32[8,6,32,128]{3,2,1,0:T(8,128)S(1)} %get-tuple-element.16), channel_id=1, source_target_pairs={{2,0},{4,2},{6,4},{8,6},{10,8},{12,10},{14,12},{16,14},{18,16},{20... | collective-permute-start | bytes 2359304 | tf_op jit(solution)/shard_map/ppermute | solution.py:27
  30.9 0.9 copy-start.3
  35.5 21.7 %collective-permute-start.3 = (f32[8,6,32,128]{3,2,1,0:T(8,128)S(1)}, f32[8,6,32,128]{3,2,1,0:T(8,128)S(1)}, u32[]{:S(2)}, u32[]{:S(2)}) collective-permute-start(f32[8,6,32,128]{3,2,1,0:T(8,128)S(1)} %get-tuple-element.15), channel_id=1, source_target_pairs={{0,2},{2,4},{4,6},{6,8},{8,10},{10,12},{12,14},{14,16},{16,18},{18... | collective-permute-start | bytes 2359304 | tf_op jit(solution)/shard_map/ppermute | solution.py:26
  39.9 17.3 %collective-permute-start.2 = (f32[8,6,32,128]{3,2,1,0:T(8,128)S(1)}, f32[8,6,32,128]{3,2,1,0:T(8,128)S(1)}, u32[]{:S(2)}, u32[]{:S(2)}) collective-permute-start(f32[8,6,32,128]{3,2,1,0:T(8,128)S(1)} %get-tuple-element.14), channel_id=1, source_target_pairs={{2,0},{4,2},{6,4},{8,6},{10,8},{12,10},{14,12},{16,14},{18,16},{20... | collective-permute-start | bytes 2359304 | tf_op jit(solution)/shard_map/ppermute | solution.py:27
  61.0 21.7 %collective-permute-start.5 = (f32[8,6,32,128]{3,2,1,0:T(8,128)S(1)}, f32[8,6,32,128]{3,2,1,0:T(8,128)S(1)}, u32[]{:S(2)}, u32[]{:S(2)}) collective-permute-start(f32[8,6,32,128]{3,2,1,0:T(8,128)S(1)} %get-tuple-element.13), channel_id=1, source_target_pairs={{0,2},{2,4},{4,6},{6,8},{8,10},{10,12},{12,14},{14,16},{16,18},{18... | collective-permute-start | bytes 2359304 | tf_op jit(solution)/shard_map/ppermute | solution.py:26
  65.4 17.3 %collective-permute-start.4 = (f32[8,6,32,128]{3,2,1,0:T(8,128)S(1)}, f32[8,6,32,128]{3,2,1,0:T(8,128)S(1)}, u32[]{:S(2)}, u32[]{:S(2)}) collective-permute-start(f32[8,6,32,128]{3,2,1,0:T(8,128)S(1)} %get-tuple-element.12), channel_id=1, source_target_pairs={{2,0},{4,2},{6,4},{8,6},{10,8},{12,10},{14,12},{16,14},{18,16},{20... | collective-permute-start | bytes 2359304 | tf_op jit(solution)/shard_map/ppermute | solution.py:27
  147.6 61.7 %all-to-all-start = ((f32[128,1,4096]{2,1,0:T(1,128)}), f32[128,1,4096]{2,1,0:T(1,128)S(1)}, u32[]{:S(2)}, u32[]{:S(2)}) async-start(f32[128,1,4096]{2,1,0:T(1,128)} %reshape.18), calls=%async_computation | async-start | bytes 4194304 | tf_op jit(solution)/shard_map/all_to_all | solution.py:86
  209.3 1.3 copy-start.2
Sparse Core Ops, SparseCore 0:
  88.2 43.1 all-gather.1
where the time goes:
time: 551 us; the launch traced here: 550 us
  blocking collectives  281 us (51%)
  waiting for transfers between devices  140 us (25%)
  local copies, waits for them, and re-layouts  44.9 us (8%)
  starting transfers between devices  30.6 us (6%)
  matrix products  20.6 us (4%)
  other arithmetic  19 us (3%)
  between operations  14.2 us (3%)
    psum x1, blocking collectives, intersection_and_turn(): intersection = lax.psum(partial_intersection, 'dom') / count_all  281 us
    all_to_all x1, waiting for transfers between devices, local(): lax.all_to_all(whole_slab, 'dom', split_axis=1, concat_axis=3, tiled=True)  50.2 us
    ppermute x3, waiting for transfers between devices, padded(): before = lax.ppermute(last, axis, up)  46.2 us
    all_gather x1, waiting for transfers between devices, local(): whole_slab = lax.all_gather(lines, 'band', axis=0, tiled=True)  43.3 us
    dot_general x1, matrix products, intersection_and_turn(): turned = jnp.dot(mine.T, flat, precision=lax.Precision.HIGHEST)  17.6 us
    all_to_all x3, local copies, waits for them, and re-layouts, local(): lax.all_to_all(whole_slab, 'dom', split_axis=1, concat_axis=3, tiled=True)  16.6 us
    unnamed x13, local copies, waits for them, and re-layouts  16.3 us
    ppermute x3, starting transfers between devices, padded(): before = lax.ppermute(last, axis, up)  13.4 us
  transfers between devices with their start and end apart: 8, of which 5 were waited for; matrix products, arithmetic and copies ran while one was open for 0% of the time, Pallas kernels for 0%

commit v1 on v0

v1 whole, which is shorter than its diff:
```python
import functools

import jax
import jax.numpy as jnp
import ml_dtypes
import numpy as np
from jax import lax
from jax.experimental import pallas as pl
from jax.experimental.pallas import tpu as pltpu
from jax.sharding import Mesh
from jax.sharding import PartitionSpec as P

STENCIL = (
    -5369.0 / 1800.0,
    12.0 / 7.0,
    -15.0 / 56.0,
    10.0 / 189.0,
    -1.0 / 112.0,
    2.0 / 1925.0,
    -1.0 / 16632.0,
)
CENTER = 8.5
HALF = 6.5
WIDTH = 6
NORB, NX, NY, NZ = 16, 1024, 32, 128
CHUNK = 32
OWN = 2
YPAD = 8
F32 = jnp.float32
BF16 = jnp.bfloat16


def banded(scale):
    band = np.zeros((NZ, NZ), np.float64)
    for k in range(1, 7):
        band += np.eye(NZ, k=k) * STENCIL[k] + np.eye(NZ, k=-k) * STENCIL[k]
    band = (-0.5 * scale * band).astype(np.float32)
    high = band.astype(ml_dtypes.bfloat16)
    low = (band - high.astype(np.float32)).astype(ml_dtypes.bfloat16)
    zero = np.zeros_like(high)
    return np.block([[high, low], [high, zero]]).astype(ml_dtypes.bfloat16)


def split(x):
    high = x.astype(BF16)
    low = (x - high.astype(F32)).astype(BF16)
    return high, low


def dot3(a, b, dims):
    ah, al = split(a)
    bh, bl = split(b)
    dot = functools.partial(lax.dot_general, dimension_numbers=(dims, ((), ())), preferred_element_type=F32)
    return dot(ah, bh) + (dot(ah, bl) + dot(al, bh))


def stencil(scale, field, before, after, potential, band, pad, zpart, put):
    run = 4
    span = CHUNK + 2 * WIDTH
    zeros = jnp.zeros((YPAD, NZ), F32)

    def clear(p, _):
        pad[p, 0:YPAD, :] = zeros
        pad[p, YPAD + NY :, :] = zeros
        return 0

    lax.fori_loop(0, OWN * span, clear, 0)
    for o in range(OWN):
        pad[o * span : o * span + WIDTH, YPAD : YPAD + NY, :] = before[o]
        pad[o * span + WIDTH + CHUNK : (o + 1) * span, YPAD : YPAD + NY, :] = after[o]
        for s in range(CHUNK // 8):
            block = field(o, s)
            start = o * span + WIDTH + s * 8
            pad[start : start + 8, YPAD : YPAD + NY, :] = block
            high, low = split(block.reshape(8 * NY, NZ))
            both = jnp.dot(jnp.concatenate([high, low], axis=1), band[...], preferred_element_type=F32)
            zpart[o * CHUNK + s * 8 : o * CHUNK + (s + 1) * 8] = (both[:, :NZ] + both[:, NZ:]).reshape(8, NY, NZ)

    def step(i, _):
        o = i // (CHUNK // run)
        x = (i % (CHUNK // run)) * run
        base = o * span + WIDTH + x
        here = pad[pl.ds(base, run), YPAD : YPAD + NY, :]
        total = zpart[pl.ds(o * CHUNK + x, run)]
        total = total + (scale * (-1.5 * STENCIL[0] - CENTER) + scale * potential[pl.ds(x, run)]) * here
        for k in range(1, 7):
            beside = pad[pl.ds(base + k, run), YPAD : YPAD + NY, :] + pad[pl.ds(base - k, run), YPAD : YPAD + NY, :]
            beside = beside + pad[pl.ds(base, run), YPAD + k : YPAD + NY + k, :]
            beside = beside + pad[pl.ds(base, run), YPAD - k : YPAD + NY - k, :]
            total = total + (-0.5 * scale * STENCIL[k]) * beside
        put(o, x, run, total)
        return 0

    lax.fori_loop(0, OWN * CHUNK // run, step, 0)


def ends(out, first, last):
    for o in range(OWN):
        first[o] = out[o, 0:WIDTH]
        last[o] = out[o, CHUNK - WIDTH :]


def first_kernel(slabs, before, after, potential, band, out, first, last, pad, zpart):
    def put(o, x, run, total):
        out[o, pl.ds(x, run)] = total

    stencil(1.0 / HALF, lambda o, s: slabs[s, o], before, after, potential, band, pad, zpart, put)
    ends(out, first, last)


def second_kernel(field, before, after, potential, slabs, band, out, first, last, pad, zpart):
    def put(o, x, run, total):
        out[o, pl.ds(x, run)] = total - slabs[x // 8, o, pl.ds(x % 8, run)]

    stencil(2.0 / HALF, lambda o, s: field[o, s * 8 : s * 8 + 8], before, after, potential, band, pad, zpart, put)
    ends(out, first, last)


def third_kernel(field, before, after, potential, previous, band, out, pad, zpart, result, turned):
    def put(o, x, run, total):
        result[o, pl.ds(x, run)] = total - previous[o, pl.ds(x, run)]

    stencil(2.0 / HALF, lambda o, s: field[o, s * 8 : s * 8 + 8], before, after, potential, band, pad, zpart, put)

    def turn(x, _):
        for b in range(2):
            rows = [result[o, t * 8 + x, b * 16 : b * 16 + 16, :] for t in range(4) for o in range(OWN)]
            turned[pl.ds((b * 8 + x) * NZ, NZ), :] = jnp.concatenate(rows, axis=0).T
        return 0

    lax.fori_loop(0, 8, turn, 0)

    def pick(q, _):
        for c in range(4):
            for b in range(2):
                out[c, b, q] = turned[pl.ds(b * 8 * NZ + 4 * q + c, 8, stride=NZ), :]
        return 0

    lax.fori_loop(0, NZ // 4, pick, 0)


def rotate_kernel(ring, weights, out, gram):
    lane = lax.broadcasted_iota(jnp.int32, (256, 128), 1) // 32
    sums = jnp.zeros((256, 256), F32)
    for t in range(4):
        halves = []
        for b in range(2):
            value = None
            for c in range(4):
                piece = ring[c * 2 + b]
                if c != t:
                    piece = pltpu.roll(piece, ((c - t) % 4) * 32, 1)
                value = piece if value is None else jnp.where(lane == c, piece, value)
            halves.append(value)
        all_orbitals = jnp.concatenate(halves, axis=1)
        turned = dot3(all_orbitals, weights[...], ((1,), (0,)))
        for b in range(2):
            out[:, b, t] = turned[:, b * 128 : (b + 1) * 128].reshape(32, 8, 128)
        sums = sums + dot3(all_orbitals, all_orbitals, ((0,), (0,)))
    row = lax.broadcasted_iota(jnp.int32, (256, 256), 0) % 16
    column = lax.broadcasted_iota(jnp.int32, (256, 256), 1) % 16
    diagonal = jnp.where(row == column, sums, 0.0).reshape(16, 16, 256).sum(axis=1)
    place = lax.broadcasted_iota(jnp.int32, (256, 16), 0) // 16
    ones = (place == lax.broadcasted_iota(jnp.int32, (256, 16), 1)).astype(F32)
    gram[...] = jnp.dot(diagonal, ones, precision=lax.Precision.HIGHEST, preferred_element_type=F32)


def lines_kernel(received, out):
    for b in range(2):
        for s in range(8):
            block = received[s * 4 : s * 4 + 4, b].reshape(128, 128).T.reshape(8, 16, 128)
            out[:, b * 16 : b * 16 + 16, s * 128 : (s + 1) * 128] = block


def call(kernel, outs, scratch=()):
    many = isinstance(outs, list)
    vmem = pl.BlockSpec(memory_space=pltpu.VMEM)
    return lambda *args: pl.pallas_call(
        kernel,
        out_shape=[jax.ShapeDtypeStruct(s, F32) for s in outs] if many else jax.ShapeDtypeStruct(outs, F32),
        in_specs=[vmem] * len(args),
        out_specs=[vmem] * len(outs) if many else vmem,
        scratch_shapes=[pltpu.VMEM(s, F32) for s in scratch],
        compiler_params=pltpu.CompilerParams(vmem_limit_bytes=48 * 1024 * 1024),
    )(*args)


def local(orbitals, potential, coefficients):
    chunks = ("z", "x")
    count = lax.axis_size(chunks)
    up = [(i, i + 1) for i in range(count - 1)]
    down = [(j, i) for i, j in up]

    def beside(first, last):
        return lax.ppermute(last, chunks, up), lax.ppermute(first, chunks, down)

    slabs = lax.all_to_all(orbitals.reshape(4, OWN, 8, NY, NZ), ("u", "c"), 0, 0, tiled=True)
    potential = lax.all_gather(potential, ("u", "c"), axis=0, tiled=True)
    weights = (coefficients[:, None, :, None] * jnp.eye(16, dtype=F32)[None, :, None, :]).reshape(256, 256)

    own = (OWN, CHUNK, NY, NZ)
    end = (OWN, WIDTH, NY, NZ)
    scratch = [(OWN * (CHUNK + 2 * WIDTH), NY + 2 * YPAD, NZ), (OWN * CHUNK, NY, NZ)]
    one = jnp.asarray(banded(1.0 / HALF))
    two = jnp.asarray(banded(2.0 / HALF))
    before, after = beside(slabs[0, :, :WIDTH], slabs[3, :, 8 - WIDTH :])
    first, low, high = call(first_kernel, [own, end, end], scratch)(slabs, before, after, potential, one)
    before, after = beside(low, high)
    second, low, high = call(second_kernel, [own, end, end], scratch)(first, before, after, potential, slabs, two)
    before, after = beside(low, high)
    message = call(third_kernel, (4, 2, 32, 8, 128), scratch + [own, (2 * 8 * NZ, 128)])(
        second, before, after, potential, first, two
    )
    ring = lax.all_to_all(message.reshape(8, 256, 128), ("u", "c", "b"), 0, 0, tiled=True)
    rotated, gram = call(rotate_kernel, [(32, 2, 4, 8, 128), (16, 16)])(ring, weights)
    received = lax.all_to_all(rotated.reshape(64, 32, 128), ("z", "x", "b"), 0, 0, tiled=True)
    parts = lax.all_gather(gram.reshape(2, 128), ("z", "x", "u", "c", "b"))
    intersection = (parts.sum(axis=0) / (NX * NY * NZ)).reshape(NORB, NORB)
    lines = call(lines_kernel, (8, NY, NX))(received.reshape(32, 2, 32, 128))
    return intersection, lines


def solution(mesh):
    grid = Mesh(mesh.devices.reshape(8, 4, 2, 2, 2), ("z", "x", "u", "c", "b"))
    dom = ("z", "x", "u", "c")
    return jax.shard_map(
        local,
        mesh=grid,
        in_specs=(P("b", dom, None, None), P(dom, None, None), P()),
        out_specs=(P(), P("b", dom, None)),
        check_vma=False,
    )
```

time: 551 us -> 749 us (1.36)
  the two profiles are of different devices: /device:TPU:1 before, /device:TPU:128 now
where the time goes in v1:
time: 749 us; the launch traced here: 748 us
  blocking collectives  664 us (89%)
  starting transfers between devices  45 us (6%)
  waiting for transfers between devices  22.1 us (3%)
  Pallas kernels  14.1 us (2%)
    all_gather x1, blocking collectives, local(): parts = lax.all_gather(gram.reshape(2, 128), ('z', 'x', 'u', 'c', 'b'))  639 us
    ppermute x6, starting transfers between devices, beside(): return (lax.ppermute(last, chunks, up), lax.ppermute(first, chunks, down))  28.1 us
    all_to_all x1, blocking collectives, local(): lax.all_to_all(orbitals.reshape(4, OWN, 8, NY, NZ), ('u', 'c'), 0, 0, til...  18.1 us
  transfers between devices with their start and end apart: 8, of which 5 were waited for; matrix products, arithmetic and copies ran while one was open for 0% of the time, Pallas kernels for 0%

profile of v1, /device:TPU:128, one launch (start us, length us, event | category | flops | bytes accessed | tf_op | source)
XLA Modules:
  0.0 748.3 jit_solution(17604784295520419694)
XLA Ops:
  0.7 18.1 %all_to_all.15.slabs = f32[4,2,8,32,128]{4,3,2,1,0:T(8,128)S(1)} all-to-all(f32[4,2,8,32,128]{4,3,2,1,0:T(8,128)} %bitcast.11), channel_id=1, replica_groups=mesh['z'=8,'x'=4,'u'=2,'c'=2,'b'=2] {'u','c'}, dimensions={0} | all-to-all | bytes 2097152 | tf_op jit(solution)/shard_map/all_to_all | solution.py:197
  18.8 3.5 collective-permute-start
  22.3 5.8 collective-permute-start.1
  28.1 6.5 all_gather.6.potential
  34.6 2.6 shard_map.68
  37.2 1.9 collective-permute-start.2
  39.1 7.2 collective-permute-start.3
  46.4 3.2 collective-permute-done.2.before
  49.6 1.2 collective-permute-done.3.after
  50.7 2.6 shard_map.69
  53.4 1.9 collective-permute-start.4
  55.3 7.7 %collective-permute-start.5 = (f32[2,6,32,128]{3,2,1,0:T(8,128)S(1)}, f32[2,6,32,128]{3,2,1,0:T(8,128)S(1)}, u32[]{:S(2)}, u32[]{:S(2)}) collective-permute-start(f32[2,6,32,128]{3,2,1,0:T(8,128)S(1)} %get-tuple-element.15), channel_id=1, source_target_pairs={{8,0},{16,8},{24,16},{32,24},{40,32},{48,40},{56,48},{64,56},{72,6... | collective-permute-start | bytes 589832 | tf_op jit(solution)/shard_map/ppermute | solution.py:195
  63.0 2.3 collective-permute-done.4.before
  65.4 1.2 collective-permute-done.5.after
  66.6 5.2 shard_map.70
  71.7 4.6 all-to-all-start.1
  76.6 0.9 mul.20.weights
  77.5 14.2 %all-to-all-done.1.ring = f32[8,256,128]{2,1,0:T(8,128)S(1)} async-done(((f32[8,256,128]{2,1,0:T(8,128)}), f32[8,256,128]{2,1,0:T(8,128)S(1)}, u32[]{:S(2)}, u32[]{:S(2)}) %all-to-all-start.1) | async-done | bytes 1048608 | tf_op jit(solution)/shard_map/all_to_all | solution.py:214
  91.7 2.5 shard_map.71
  94.1 12.3 %all-to-all-start.2 = ((f32[64,32,128]{2,1,0:T(8,128)}), f32[64,32,128]{2,1,0:T(8,128)S(1)}, u32[]{:S(2)}, u32[]{:S(2)}) async-start(f32[64,32,128]{2,1,0:T(8,128)} %bitcast.4), calls=%async_computation.2 | async-start | bytes 2097152 | tf_op jit(solution)/shard_map/all_to_all | solution.py:216
  106.5 639.5 %all_gather.7 = f32[256,2,128]{2,1,0:T(2,128)S(1)} all-gather(f32[1,2,128]{2,1,0:T(2,128)S(1)} %all_gather_reshape.3), channel_id=1, replica_groups=mesh['z'=8,'x'=4,'u'=2,'c'=2,'b'=2] {'z','x','u','c','b'}, dimensions={0}, use_global_device_ids=true | all-gather | bytes 263168 | tf_op jit(solution)/shard_map/all_gather | solution.py:217
  746.0 0.3 reduce_sum.9
  746.3 0.7 div.10
  747.0 1.3 shard_map.72
  (16 shorter events, 0.3 us)
Async XLA Ops:
  0.6 34.0 %copy-start.1 = (bf16[256,256]{1,0:T(8,128)(2,1)S(1)}, bf16[256,256]{1,0:T(8,128)(2,1)}, u32[]{:S(2)}) copy-start(bf16[256,256]{1,0:T(8,128)(2,1)} %constant.9.clone.band) | copy-start | bytes 393220
  0.6 27.4 %copy-start.2 = (f32[8,32,128]{2,1,0:T(8,128)S(1)}, f32[8,32,128]{2,1,0:T(8,128)}, u32[]{:S(2)}) copy-start(f32[8,32,128]{2,1,0:T(8,128)} %param.6) | copy-start | bytes 393220
  18.7 32.0 %copy-start = (bf16[256,256]{1,0:T(8,128)(2,1)S(1)}, bf16[256,256]{1,0:T(8,128)(2,1)}, u32[]{:S(2)}) copy-start(bf16[256,256]{1,0:T(8,128)(2,1)} %constant.10.clone.band) | copy-start | bytes 393220
  18.8 15.8 %collective-permute-start = (f32[2,6,32,128]{3,2,1,0:T(8,128)S(1)}, f32[2,6,32,128]{3,2,1,0:T(8,128)S(1)}, u32[]{:S(2)}, u32[]{:S(2)}) collective-permute-start(f32[2,6,32,128]{3,2,1,0:T(8,128)S(1)} %get-tuple-element.19), channel_id=1, source_target_pairs={{0,8},{8,16},{16,24},{24,32},{32,40},{40,48},{48,56},{56,64},{64,7... | collective-permute-start | bytes 589832 | tf_op jit(solution)/shard_map/ppermute | solution.py:195
  22.3 12.3 %collective-permute-start.1 = (f32[2,6,32,128]{3,2,1,0:T(8,128)S(1)}, f32[2,6,32,128]{3,2,1,0:T(8,128)S(1)}, u32[]{:S(2)}, u32[]{:S(2)}) collective-permute-start(f32[2,6,32,128]{3,2,1,0:T(8,128)S(1)} %get-tuple-element.18), channel_id=1, source_target_pairs={{8,0},{16,8},{24,16},{32,24},{40,32},{48,40},{56,48},{64,56},{72,6... | collective-permute-start | bytes 589832 | tf_op jit(solution)/shard_map/ppermute | solution.py:195
  37.2 12.4 %collective-permute-start.2 = (f32[2,6,32,128]{3,2,1,0:T(8,128)S(1)}, f32[2,6,32,128]{3,2,1,0:T(8,128)S(1)}, u32[]{:S(2)}, u32[]{:S(2)}) collective-permute-start(f32[2,6,32,128]{3,2,1,0:T(8,128)S(1)} %get-tuple-element.11), channel_id=1, source_target_pairs={{0,8},{8,16},{16,24},{24,32},{32,40},{40,48},{48,56},{56,64},{64,7... | collective-permute-start | bytes 589832 | tf_op jit(solution)/shard_map/ppermute | solution.py:195
  39.1 11.6 %collective-permute-start.3 = (f32[2,6,32,128]{3,2,1,0:T(8,128)S(1)}, f32[2,6,32,128]{3,2,1,0:T(8,128)S(1)}, u32[]{:S(2)}, u32[]{:S(2)}) collective-permute-start(f32[2,6,32,128]{3,2,1,0:T(8,128)S(1)} %get-tuple-element.12), channel_id=1, source_target_pairs={{8,0},{16,8},{24,16},{32,24},{40,32},{48,40},{56,48},{64,56},{72,6... | collective-permute-start | bytes 589832 | tf_op jit(solution)/shard_map/ppermute | solution.py:195
  53.4 12.0 %collective-permute-start.4 = (f32[2,6,32,128]{3,2,1,0:T(8,128)S(1)}, f32[2,6,32,128]{3,2,1,0:T(8,128)S(1)}, u32[]{:S(2)}, u32[]{:S(2)}) collective-permute-start(f32[2,6,32,128]{3,2,1,0:T(8,128)S(1)} %get-tuple-element.14), channel_id=1, source_target_pairs={{0,8},{8,16},{16,24},{24,32},{32,40},{40,48},{48,56},{56,64},{64,7... | collective-permute-start | bytes 589832 | tf_op jit(solution)/shard_map/ppermute | solution.py:195
  55.3 11.2 %collective-permute-start.5 = (f32[2,6,32,128]{3,2,1,0:T(8,128)S(1)}, f32[2,6,32,128]{3,2,1,0:T(8,128)S(1)}, u32[]{:S(2)}, u32[]{:S(2)}) collective-permute-start(f32[2,6,32,128]{3,2,1,0:T(8,128)S(1)} %get-tuple-element.15), channel_id=1, source_target_pairs={{8,0},{16,8},{24,16},{32,24},{40,32},{48,40},{56,48},{64,56},{72,6... | collective-permute-start | bytes 589832 | tf_op jit(solution)/shard_map/ppermute | solution.py:195
  71.7 4.6 copy-start.3
  71.7 19.9 %all-to-all-start.1 = ((f32[8,256,128]{2,1,0:T(8,128)}), f32[8,256,128]{2,1,0:T(8,128)S(1)}, u32[]{:S(2)}, u32[]{:S(2)}) async-start(f32[8,256,128]{2,1,0:T(8,128)} %bitcast.3), calls=%async_computation.1 | async-start | bytes 2097152 | tf_op jit(solution)/shard_map/all_to_all | solution.py:214
  94.1 652.9 %all-to-all-start.2 = ((f32[64,32,128]{2,1,0:T(8,128)}), f32[64,32,128]{2,1,0:T(8,128)S(1)}, u32[]{:S(2)}, u32[]{:S(2)}) async-start(f32[64,32,128]{2,1,0:T(8,128)} %bitcast.4), calls=%async_computation.2 | async-start | bytes 2097152 | tf_op jit(solution)/shard_map/all_to_all | solution.py:216

commit v2 on v1

v2 whole, which is shorter than its diff:
```python
import functools

import jax
import jax.numpy as jnp
import ml_dtypes
import numpy as np
from jax import lax
from jax.experimental import pallas as pl
from jax.experimental.pallas import tpu as pltpu
from jax.sharding import Mesh
from jax.sharding import PartitionSpec as P

STENCIL = (
    -5369.0 / 1800.0,
    12.0 / 7.0,
    -15.0 / 56.0,
    10.0 / 189.0,
    -1.0 / 112.0,
    2.0 / 1925.0,
    -1.0 / 16632.0,
)
CENTER = 8.5
HALF = 6.5
WIDTH = 6
NORB, NX, NY, NZ = 16, 1024, 32, 128
CHUNK = 32
OWN = 2
YPAD = 8
F32 = jnp.float32
BF16 = jnp.bfloat16


def banded(scale):
    band = np.zeros((NZ, NZ), np.float64)
    for k in range(1, 7):
        band += np.eye(NZ, k=k) * STENCIL[k] + np.eye(NZ, k=-k) * STENCIL[k]
    band = (-0.5 * scale * band).astype(np.float32)
    high = band.astype(ml_dtypes.bfloat16)
    low = (band - high.astype(np.float32)).astype(ml_dtypes.bfloat16)
    zero = np.zeros_like(high)
    return np.block([[high, low], [high, zero]]).astype(ml_dtypes.bfloat16)


def split(x):
    high = x.astype(BF16)
    low = (x - high.astype(F32)).astype(BF16)
    return high, low


def dot3(a, b, dims):
    ah, al = split(a)
    bh, bl = split(b)
    dot = functools.partial(lax.dot_general, dimension_numbers=(dims, ((), ())), preferred_element_type=F32)
    return dot(ah, bh) + (dot(ah, bl) + dot(al, bh))


def filter_kernel(chunk, slabs, before, after, potential, bands, out, field, other, local, zpart, result, turned):
    far, near = 3 * WIDTH, 2 * WIDTH + 2
    rows = slice(YPAD, YPAD + NY)
    zeros = jnp.zeros((YPAD, NZ), F32)

    def clear(p, _):
        for o in range(OWN):
            for pad in (field, other):
                pad[o, jnp.minimum(p, pad.shape[1] - 1), 0:YPAD, :] = zeros
                pad[o, jnp.minimum(p, pad.shape[1] - 1), YPAD + NY :, :] = zeros
        return 0

    lax.fori_loop(0, field.shape[1], clear, 0)
    for o in range(OWN):
        field[o, 0:far, rows, :] = before[o]
        field[o, far + CHUNK :, rows, :] = after[o]
        for s in range(4):
            field[o, far + 8 * s : far + 8 * s + 8, rows, :] = slabs[s, o]
    order = [(0, 1), (1, 1), (0, 0), (1, 0), (2, 0), (3, 0), (2, 1), (3, 1)]
    for j, (s, h) in enumerate(order):
        local[8 * j : 8 * j + 8] = (potential[s, h] + (-1.5 * STENCIL[0] - CENTER)) * (1.0 / HALF)

    def along_z(source, o, index, band):
        high, low = split(source[o, pl.ds(index, 8), rows, :].reshape(8 * NY, NZ))
        both = jnp.dot(jnp.concatenate([high, low], axis=1), band, preferred_element_type=F32)
        return (both[:, :NZ] + both[:, NZ:]).reshape(8, NY, NZ)

    def step(source, shift, first, blocks, scale, band, put):
        def body(i, _):
            o = i // blocks
            j = i % blocks
            start = first + 8 * j
            base = start + shift
            for y in range(0, NY, 8):
                beside = source[o, pl.ds(base - WIDTH, 8 + 2 * WIDTH), YPAD + y : YPAD + y + 8, :]
                here = beside[WIDTH : WIDTH + 8]
                total = local[pl.ds(start + 16, 8), y : y + 8, :] * here
                if scale != 1.0:
                    total = total * scale
                total = total + zpart[i, :, y : y + 8, :]
                for k in range(1, 7):
                    around = beside[WIDTH + k : WIDTH + 8 + k] + beside[WIDTH - k : WIDTH + 8 - k]
                    around = around + (
                        source[o, pl.ds(base, 8), YPAD + y + k : YPAD + y + 8 + k, :]
                        + source[o, pl.ds(base, 8), YPAD + y - k : YPAD + y + 8 - k, :]
                    )
                    total = total + (-0.5 * scale / HALF * STENCIL[k]) * around
                put(o, start, y, total)
            later = jnp.minimum(i + 1, OWN * blocks - 1)
            zpart[i + 1] = along_z(source, later // blocks, first + 8 * (later % blocks) + shift, band)
            return 0

        zpart[0] = along_z(source, 0, first + shift, band)
        lax.fori_loop(0, OWN * blocks, body, 0)

    def put_first(o, start, y, total):
        other[o, pl.ds(start + near, 8), YPAD + y : YPAD + y + 8, :] = total

    def put_second(o, start, y, total):
        place = (o, pl.ds(start + far, 8), slice(YPAD + y, YPAD + y + 8), slice(None))
        field[place] = total - field[place]

    def put_third(o, start, y, total):
        place = (o, pl.ds(start + near, 8), slice(YPAD + y, YPAD + y + 8), slice(None))
        result[o, pl.ds(start, 8), y : y + 8, :] = total - other[place]

    def outside(target, shift, count):
        blank = jnp.zeros((count, NY, NZ), F32)

        @pl.when(chunk[0] == 0)
        def _():
            for o in range(OWN):
                target[o, shift - count : shift, rows, :] = blank

        @pl.when(chunk[0] == NX // CHUNK - 1)
        def _():
            for o in range(OWN):
                target[o, shift + CHUNK : shift + CHUNK + count, rows, :] = blank

    step(field, far, -12, 7, 1.0, bands[0], put_first)
    outside(other, near, 12)
    step(other, near, -8, 6, 2.0, bands[1], put_second)
    outside(field, far, 8)
    step(field, far, 0, 4, 2.0, bands[1], put_third)

    def turn(x, _):
        for b in range(2):
            pieces = [result[o, t * 8 + x, b * 16 : b * 16 + 16, :] for t in range(4) for o in range(OWN)]
            turned[pl.ds((b * 8 + x) * NZ, NZ), :] = jnp.concatenate(pieces, axis=0).T
        return 0

    lax.fori_loop(0, 8, turn, 0)

    def pick(q, _):
        for c in range(4):
            for b in range(2):
                out[c, b, q] = turned[pl.ds(b * 8 * NZ + 4 * q + c, 8, stride=NZ), :]
        return 0

    lax.fori_loop(0, NZ // 4, pick, 0)


def rotate_kernel(ring, weights, out):
    lane = lax.broadcasted_iota(jnp.int32, (256, 128), 1) // 32
    sums = jnp.zeros((256, 256), F32)
    for t in range(4):
        halves = []
        for b in range(2):
            value = None
            for c in range(4):
                piece = ring[c * 2 + b]
                if c != t:
                    piece = pltpu.roll(piece, ((c - t) % 4) * 32, 1)
                value = piece if value is None else jnp.where(lane == c, piece, value)
            halves.append(value)
        all_orbitals = jnp.concatenate(halves, axis=1)
        turned = dot3(all_orbitals, weights[...], ((1,), (0,)))
        for b in range(2):
            out[:, b, t] = turned[:, b * 128 : (b + 1) * 128].reshape(32, 8, 128)
        sums = sums + dot3(all_orbitals, all_orbitals, ((0,), (0,)))
    row = lax.broadcasted_iota(jnp.int32, (256, 256), 0) % 16
    column = lax.broadcasted_iota(jnp.int32, (256, 256), 1) % 16
    diagonal = jnp.where(row == column, sums, 0.0).reshape(16, 16, 256).sum(axis=1)
    place = lax.broadcasted_iota(jnp.int32, (256, 128), 0) // 16
    ones = (place == lax.broadcasted_iota(jnp.int32, (256, 128), 1)).astype(F32)
    gram = jnp.dot(diagonal, ones, precision=lax.Precision.HIGHEST, preferred_element_type=F32)
    tile = gram[0:8] + pltpu.roll(gram[8:16], 16, 1)
    out[:, :, 4] = jnp.broadcast_to(tile, (32, 2, 8, 128))


def lines_kernel(received, out):
    for b in range(2):
        for s in range(8):
            block = received[s * 4 : s * 4 + 4, b, 0:4].reshape(128, 128).T.reshape(8, 16, 128)
            out[:, b * 16 : b * 16 + 16, s * 128 : (s + 1) * 128] = block


def call(kernel, out, scratch=()):
    vmem = pl.BlockSpec(memory_space=pltpu.VMEM)
    smem = pl.BlockSpec(memory_space=pltpu.SMEM)
    return lambda *args: pl.pallas_call(
        kernel,
        out_shape=jax.ShapeDtypeStruct(out, F32),
        in_specs=[smem if a.dtype == jnp.int32 else vmem for a in args],
        out_specs=vmem,
        scratch_shapes=[pltpu.VMEM(s, F32) for s in scratch],
        compiler_params=pltpu.CompilerParams(vmem_limit_bytes=48 * 1024 * 1024),
    )(*args)


def local(orbitals, potential, coefficients):
    chunks = ("z", "x")
    dom = ("z", "x", "u", "c")
    count = lax.axis_size(chunks)
    up = [(i, i + 1) for i in range(count - 1)]
    down = [(j, i) for i, j in up]

    shift = [(d, d + 2 if d % 4 >= 2 else d - 2) for d in range(4 * count)]
    beyond = lax.ppermute(potential, dom, [(i, j) for i, j in shift if 0 <= j < 4 * count])
    slabs = lax.all_to_all(orbitals.reshape(4, OWN, 8, NY, NZ), ("u", "c"), 0, 0, tiled=True)
    far = 3 * WIDTH
    part = far - 16
    before = lax.ppermute(jnp.concatenate([slabs[1, :, 8 - part :], slabs[2], slabs[3]], axis=1), chunks, up)
    after = lax.ppermute(jnp.concatenate([slabs[0], slabs[1], slabs[2, :, :part]], axis=1), chunks, down)
    window = lax.all_gather(jnp.stack([potential, beyond]), ("u", "c"))

    weights = (coefficients[:, None, :, None] * jnp.eye(16, dtype=F32)[None, :, None, :]).reshape(256, 256)
    bands = jnp.asarray(np.stack([banded(1.0 / HALF), banded(2.0 / HALF)]))
    scratch = [
        (OWN, CHUNK + 2 * far, NY + 2 * YPAD, NZ),
        (OWN, CHUNK + 2 * (2 * WIDTH + 2), NY + 2 * YPAD, NZ),
        (64, NY, NZ),
        (OWN * 7 + 1, 8, NY, NZ),
        (OWN, CHUNK, NY, NZ),
        (2 * 8 * NZ, NZ),
    ]
    chunk = lax.axis_index(chunks).reshape(1)
    message = call(filter_kernel, (4, 2, 32, 8, 128), scratch)(chunk, slabs, before, after, window, bands)
    ring = lax.all_to_all(message.reshape(8, 256, 128), ("u", "c", "b"), 0, 0, tiled=True)
    rotated = call(rotate_kernel, (32, 2, 5, 8, 128))(ring, weights)
    received = lax.all_to_all(rotated.reshape(64, 40, 128), ("z", "x", "b"), 0, 0, tiled=True)
    received = received.reshape(32, 2, 5, 8, 128)
    gram = lax.all_gather(received[:, :, 4].sum(axis=(0, 1)), ("u", "c")).sum(axis=0) / (NX * NY * NZ)
    intersection = jnp.concatenate([gram[:, :NORB], gram[:, NORB : 2 * NORB]], axis=0)
    return intersection, call(lines_kernel, (8, NY, NX))(received)


def solution(mesh):
    grid = Mesh(mesh.devices.reshape(8, 4, 2, 2, 2), ("z", "x", "u", "c", "b"))
    dom = ("z", "x", "u", "c")
    return jax.shard_map(
        local,
        mesh=grid,
        in_specs=(P("b", dom, None, None), P(dom, None, None), P()),
        out_specs=(P(), P("b", dom, None)),
        check_vma=False,
    )
```

time: 749 us -> 154 us (0.21)
  the two profiles are of different devices: /device:TPU:128 before, /device:TPU:32 now
where the time goes in v2:
time: 154 us; the launch traced here: 151 us
  blocking collectives  52.2 us (34%)
  waiting for transfers between devices  41.9 us (27%)
  starting transfers between devices  20 us (13%)
  Pallas kernels  18.3 us (12%)
  between operations  14.1 us (9%)
  other arithmetic  2.51 us (2%)
  local copies, waits for them, and re-layouts  2.33 us (2%)
    all_to_all x1, blocking collectives, local(): lax.all_to_all(rotated.reshape(64, 40, 128), ('z', 'x', 'b'), 0, 0, tiled...  47 us
    pallas_call x3, Pallas kernels, call(): pl.pallas_call(kernel, out_shape=jax.ShapeDtypeStruct(out, F32), in_specs...  18.3 us
    all_to_all x1, waiting for transfers between devices, local(): lax.all_to_all(message.reshape(8, 256, 128), ('u', 'c', 'b'), 0, 0, tiled...  14.2 us
    ppermute x1, waiting for transfers between devices, local(): lax.ppermute(jnp.concatenate([slabs[0], slabs[1], slabs[2, :, :part]], ax...  9.77 us
    ppermute x1, waiting for transfers between devices, local(): lax.ppermute(jnp.concatenate([slabs[1, :, 8 - part:], slabs[2], slabs[3]]...  7.1 us
    all_to_all x1, waiting for transfers between devices, local(): lax.all_to_all(orbitals.reshape(4, OWN, 8, NY, NZ), ('u', 'c'), 0, 0, til...  5.58 us
    ppermute x1, starting transfers between devices, local(): lax.ppermute(potential, dom, [(i, j) for i, j in shift if 0 <= j < 4 * co...  5.57 us
    ppermute x1, waiting for transfers between devices, local(): lax.ppermute(potential, dom, [(i, j) for i, j in shift if 0 <= j < 4 * co...  5.26 us
  transfers between devices with their start and end apart: 6, of which 5 were waited for; matrix products, arithmetic and copies ran while one was open for 2% of the time, Pallas kernels for 0%

profile of v2, /device:TPU:32, one launch (start us, length us, event | category | flops | bytes accessed | tf_op | source)
XLA Modules:
  0.0 151.3 jit_solution(6911875501285579216)
XLA Ops:
  7.2 3.7 %all-to-all-start = ((f32[4,2,8,32,128]{4,3,2,1,0:T(8,128)}), f32[4,2,8,32,128]{4,3,2,1,0:T(8,128)S(1)}, u32[]{:S(2)}, u32[]{:S(2)}) async-start(f32[4,2,8,32,128]{4,3,2,1,0:T(8,128)} %bitcast.28), calls=%async_computation | async-start | bytes 2097152 | tf_op jit(solution)/shard_map/all_to_all | solution.py:216
  10.9 5.6 %collective-permute-start.2 = (f32[8,32,128]{2,1,0:T(8,128)S(1)}, f32[8,32,128]{2,1,0:T(8,128)S(1)}, u32[]{:S(2)}, u32[]{:S(2)}) collective-permute-start(f32[8,32,128]{2,1,0:T(8,128)S(1)} %copy-done.2), channel_id=1, source_target_pairs={{4,8},{6,10},{8,4},{10,6},{12,16},{14,18},{16,12},{18,14},{20,24},... | collective-permute-start | bytes 393224 | tf_op jit(solution)/shard_map/ppermute | solution.py:215
  16.5 5.3 %collective-permute-done.2 = f32[8,32,128]{2,1,0:T(8,128)S(1)} collective-permute-done((f32[8,32,128]{2,1,0:T(8,128)S(1)}, f32[8,32,128]{2,1,0:T(8,128)S(1)}, u32[]{:S(2)}, u32[]{:S(2)}) %collective-permute-start.2) | collective-permute-done | bytes 131104 | tf_op jit(solution)/shard_map/ppermute | solution.py:215
  21.7 0.7 pad_maximum_fusion.2
  22.5 5.6 %all-to-all-done.slabs = f32[4,2,8,32,128]{4,3,2,1,0:T(8,128)S(1)} async-done(((f32[4,2,8,32,128]{4,3,2,1,0:T(8,128)}), f32[4,2,8,32,128]{4,3,2,1,0:T(8,128)S(1)}, u32[]{:S(2)}, u32[]{:S(2)}) %all-to-all-start) | async-done | bytes 1048608 | tf_op jit(solution)/shard_map/all_to_all | solution.py:216
  28.1 0.1 slice_bitcast_fusion.1
  28.2 4.2 %collective-permute-start.1 = (f32[2,18,32,128]{3,2,1,0:T(8,128)S(1)}, f32[2,18,32,128]{3,2,1,0:T(8,128)S(1)}, u32[]{:S(2)}, u32[]{:S(2)}) collective-permute-start(f32[2,18,32,128]{3,2,1,0:T(8,128)S(1)} %pad_maximum_fusion.1), channel_id=1, source_target_pairs={{8,0},{16,8},{24,16},{32,24},{40,32},{48,40},{56,48},{64,56},{72,6... | collective-permute-start | bytes 1769480 | tf_op jit(solution)/shard_map/ppermute | solution.py:220
  32.5 0.9 pad_maximum_fusion
  33.3 1.9 %collective-permute-start = (f32[2,18,32,128]{3,2,1,0:T(8,128)}, f32[2,18,32,128]{3,2,1,0:T(8,128)S(1)}, u32[]{:S(2)}, u32[]{:S(2)}) collective-permute-start(f32[2,18,32,128]{3,2,1,0:T(8,128)} %pad_maximum_fusion), channel_id=1, source_target_pairs={{0,8},{8,16},{16,24},{24,32},{32,40},{40,48},{48,56},{56,64},{64,7... | collective-permute-start | bytes 1769480 | tf_op jit(solution)/shard_map/ppermute | solution.py:219
  35.2 9.8 %collective-permute-done.1.after = f32[2,18,32,128]{3,2,1,0:T(8,128)S(1)} collective-permute-done((f32[2,18,32,128]{3,2,1,0:T(8,128)S(1)}, f32[2,18,32,128]{3,2,1,0:T(8,128)S(1)}, u32[]{:S(2)}, u32[]{:S(2)}) %collective-permute-start.1) | collective-permute-done | bytes 589856 | tf_op jit(solution)/shard_map/ppermute | solution.py:220
  45.0 7.1 %collective-permute-done.before = f32[2,18,32,128]{3,2,1,0:T(8,128)S(1)} collective-permute-done((f32[2,18,32,128]{3,2,1,0:T(8,128)}, f32[2,18,32,128]{3,2,1,0:T(8,128)S(1)}, u32[]{:S(2)}, u32[]{:S(2)}) %collective-permute-start) | collective-permute-done | bytes 589856 | tf_op jit(solution)/shard_map/ppermute | solution.py:219
  52.1 1.2 copy-done
  53.3 15.2 %shard_map.59 = f32[4,2,32,8,128]{4,3,2,1,0:T(8,128)} custom-call(s32[1]{0:T(128)} %bitcast.chunk, f32[4,2,8,32,128]{4,3,2,1,0:T(8,128)S(1)} %all-to-all-done.slabs, f32[2,18,32,128]{3,2,1,0:T(8,128)S(1)} %collective-permute-done.before, f32[2,18,32,128]{3,2,1,0:T(8,128)S(1)} %collective-permute-done.1.after, f32[4,2,8,32,128]{4,3,2,1,0:T(8,128)S(1)} %bitcast.27, ...), custom_call_target="tpu_custom_call" | custom-call | tf_op jit(solution)/shard_map/pallas_call | solution.py:197
  68.5 4.6 %all-to-all-start.1 = ((f32[8,256,128]{2,1,0:T(8,128)}), f32[8,256,128]{2,1,0:T(8,128)S(1)}, u32[]{:S(2)}, u32[]{:S(2)}) async-start(f32[8,256,128]{2,1,0:T(8,128)} %bitcast.11), calls=%async_computation.1 | async-start | bytes 2097152 | tf_op jit(solution)/shard_map/all_to_all | solution.py:235
  73.1 0.2 broadcast_multiply_fusion
  73.3 0.9 mul.24.weights
  74.3 14.2 %all-to-all-done.1.ring = f32[8,256,128]{2,1,0:T(8,128)S(1)} async-done(((f32[8,256,128]{2,1,0:T(8,128)}), f32[8,256,128]{2,1,0:T(8,128)S(1)}, u32[]{:S(2)}, u32[]{:S(2)}) %all-to-all-start.1) | async-done | bytes 1048608 | tf_op jit(solution)/shard_map/all_to_all | solution.py:235
  88.4 1.8 %shard_map.60 = f32[32,2,5,8,128]{4,3,2,1,0:T(8,128)S(1)} custom-call(f32[8,256,128]{2,1,0:T(8,128)S(1)} %all-to-all-done.1.ring, f32[256,256]{1,0:T(8,128)S(1)} %mul.24.weights), custom_call_target="tpu_custom_call" | custom-call | tf_op jit(solution)/shard_map/pallas_call | solution.py:197
  90.2 47.0 %all_to_all.15 = f32[64,40,128]{2,1,0:T(8,128)S(1)} all-to-all(f32[64,40,128]{2,1,0:T(8,128)S(1)} %bitcast.26), channel_id=1, replica_groups=mesh['z'=8,'x'=4,'u'=2,'c'=2,'b'=2] {'z','x','b'}, dimensions={0} | all-to-all | bytes 2621440 | tf_op jit(solution)/shard_map/all_to_all | solution.py:237
  137.3 0.1 slice_reduce_fusion
  137.3 1.3 shard_map.61
  138.6 5.2 %all-gather.1 = f32[32,128]{1,0:T(8,128)S(1)} all-gather(f32[8,128]{1,0:T(8,128)S(1)} %slice_reduce_fusion), channel_id=3, replica_groups=mesh['z'=8,'x'=4,'u'=2,'c'=2,'b'=2] {'u','c'}, dimensions={0}, use_global_device_ids=true | all-gather | bytes 20480 | tf_op jit(solution)/shard_map/all_gather | solution.py:239
  143.8 0.1 fusion.1
  143.9 0.6 pad_maximum_fusion.3
  (15 shorter events, 0.1 us)
Async XLA Ops:
  7.2 3.7 %copy-start.2 = (f32[8,32,128]{2,1,0:T(8,128)S(1)}, f32[8,32,128]{2,1,0:T(8,128)}, u32[]{:S(2)}) copy-start(f32[8,32,128]{2,1,0:T(8,128)} %param.5) | copy-start | bytes 393220
  7.2 20.9 %all-to-all-start = ((f32[4,2,8,32,128]{4,3,2,1,0:T(8,128)}), f32[4,2,8,32,128]{4,3,2,1,0:T(8,128)S(1)}, u32[]{:S(2)}, u32[]{:S(2)}) async-start(f32[4,2,8,32,128]{4,3,2,1,0:T(8,128)} %bitcast.28), calls=%async_computation | async-start | bytes 2097152 | tf_op jit(solution)/shard_map/all_to_all | solution.py:216
  10.8 41.3 %all-gather.4.cloned.1.call-start = ((), (), s32[]{:S(2)}) async-start(), calls=%async_computation.3 | async-start | bytes 1310720 | tf_op jit(solution)/shard_map/all_gather | solution.py:221
  10.9 10.8 %collective-permute-start.2 = (f32[8,32,128]{2,1,0:T(8,128)S(1)}, f32[8,32,128]{2,1,0:T(8,128)S(1)}, u32[]{:S(2)}, u32[]{:S(2)}) collective-permute-start(f32[8,32,128]{2,1,0:T(8,128)S(1)} %copy-done.2), channel_id=1, source_target_pairs={{4,8},{6,10},{8,4},{10,6},{12,16},{14,18},{16,12},{18,14},{20,24},... | collective-permute-start | bytes 393224 | tf_op jit(solution)/shard_map/ppermute | solution.py:215
  28.1 24.0 %copy-start.1 = (bf16[2,256,256]{2,1,0:T(8,128)(2,1)S(1)}, bf16[2,256,256]{2,1,0:T(8,128)(2,1)}, u32[]{:S(2)}) copy-start(bf16[2,256,256]{2,1,0:T(8,128)(2,1)} %constant.19.clone.bands) | copy-start | bytes 786436
  28.2 16.8 %collective-permute-start.1 = (f32[2,18,32,128]{3,2,1,0:T(8,128)S(1)}, f32[2,18,32,128]{3,2,1,0:T(8,128)S(1)}, u32[]{:S(2)}, u32[]{:S(2)}) collective-permute-start(f32[2,18,32,128]{3,2,1,0:T(8,128)S(1)} %pad_maximum_fusion.1), channel_id=1, source_target_pairs={{8,0},{16,8},{24,16},{32,24},{40,32},{48,40},{56,48},{64,56},{72,6... | collective-permute-start | bytes 1769480 | tf_op jit(solution)/shard_map/ppermute | solution.py:220
  33.3 18.8 %collective-permute-start = (f32[2,18,32,128]{3,2,1,0:T(8,128)}, f32[2,18,32,128]{3,2,1,0:T(8,128)S(1)}, u32[]{:S(2)}, u32[]{:S(2)}) collective-permute-start(f32[2,18,32,128]{3,2,1,0:T(8,128)} %pad_maximum_fusion), channel_id=1, source_target_pairs={{0,8},{8,16},{16,24},{24,32},{32,40},{40,48},{48,56},{56,64},{64,7... | collective-permute-start | bytes 1769480 | tf_op jit(solution)/shard_map/ppermute | solution.py:219
  52.1 1.2 copy-start
  68.5 4.6 %copy-start.3 = (f32[16,16]{1,0:T(8,128)S(1)}, f32[16,16]{1,0:T(8,128)}, u32[]{:S(2)}) copy-start(f32[16,16]{1,0:T(8,128)} %param.6) | copy-start | bytes 3076
  68.5 19.9 %all-to-all-start.1 = ((f32[8,256,128]{2,1,0:T(8,128)}), f32[8,256,128]{2,1,0:T(8,128)S(1)}, u32[]{:S(2)}, u32[]{:S(2)}) async-start(f32[8,256,128]{2,1,0:T(8,128)} %bitcast.11), calls=%async_computation.1 | async-start | bytes 2097152 | tf_op jit(solution)/shard_map/all_to_all | solution.py:235
Sparse Core Ops, SparseCore 0:
  22.6 25.7 all-gather.3

commit v3 on v2

v3 whole, which is shorter than its diff:
```python
import functools

import jax
import jax.numpy as jnp
import ml_dtypes
import numpy as np
from jax import lax
from jax.experimental import pallas as pl
from jax.experimental.pallas import tpu as pltpu
from jax.sharding import Mesh
from jax.sharding import PartitionSpec as P

STENCIL = (
    -5369.0 / 1800.0,
    12.0 / 7.0,
    -15.0 / 56.0,
    10.0 / 189.0,
    -1.0 / 112.0,
    2.0 / 1925.0,
    -1.0 / 16632.0,
)
CENTER = 8.5
HALF = 6.5
WIDTH = 6
NORB, NX, NY, NZ = 16, 1024, 32, 128
CHUNK = 32
OWN = 2
F32 = jnp.float32
BF16 = jnp.bfloat16


def banded(size):
    band = np.zeros((size, size), np.float64)
    for k in range(1, 7):
        band += np.eye(size, k=k) * STENCIL[k] + np.eye(size, k=-k) * STENCIL[k]
    band = (-0.5 / HALF * band).astype(np.float32)
    high = band.astype(ml_dtypes.bfloat16)
    return high, (band - high.astype(np.float32)).astype(ml_dtypes.bfloat16)


def bands():
    high, low = banded(NZ)
    along_z = np.block([[high, low], [high, np.zeros_like(high)]])
    high, low = (np.kron(np.eye(8), part) for part in banded(NY))
    along_y = np.concatenate([high, high, low], axis=1)
    return jnp.asarray(along_z.astype(ml_dtypes.bfloat16)), jnp.asarray(along_y.astype(ml_dtypes.bfloat16))


def split(x):
    high = x.astype(BF16)
    low = (x - high.astype(F32)).astype(BF16)
    return high, low


def dot3(a, b, dims):
    ah, al = split(a)
    bh, bl = split(b)
    dot = functools.partial(lax.dot_general, dimension_numbers=(dims, ((), ())), preferred_element_type=F32)
    return dot(ah, bh) + (dot(ah, bl) + dot(al, bh))


def filter_kernel(
    chunk, slabs, before, after, own, beyond, band_z, band_y, out, field, other, local, zy, result, turned
):
    far, near = 3 * WIDTH, 2 * WIDTH + 2
    for o in range(OWN):
        field[o, 0:far] = before[o]
        field[o, far + CHUNK :] = after[o]
        for s in range(4):
            field[o, far + 8 * s : far + 8 * s + 8] = slabs[s, o]
    order = [beyond[0], beyond[1], own[0], own[1], own[2], own[3], beyond[2], beyond[3]]
    for j, slab in enumerate(order):
        local[8 * j : 8 * j + 8] = (slab + (-1.5 * STENCIL[0] - CENTER)) * (1.0 / HALF)

    def along_zy(source, o, index):
        high, low = split(source[o, pl.ds(index, 8)].reshape(8 * NY, NZ))
        z = jnp.dot(jnp.concatenate([high, low], axis=1), band_z[...], preferred_element_type=F32)
        y = jnp.dot(band_y[...], jnp.concatenate([high, low, high], axis=0), preferred_element_type=F32)
        return ((z[:, :NZ] + z[:, NZ:]) + y).reshape(8, NY, NZ)

    def step(source, shift, first, blocks, double, put):
        def body(i, _):
            o = i // blocks
            start = first + 8 * (i % blocks)
            for y in range(0, NY, 8):
                beside = source[o, pl.ds(start + shift - WIDTH, 8 + 2 * WIDTH), y : y + 8, :]
                total = local[pl.ds(start + 16, 8), y : y + 8, :] * beside[WIDTH : WIDTH + 8]
                total = total + zy[i, :, y : y + 8, :]
                for k in range(1, 7):
                    around = beside[WIDTH + k : WIDTH + 8 + k] + beside[WIDTH - k : WIDTH + 8 - k]
                    total = total + (-0.5 / HALF * STENCIL[k]) * around
                put(o, start, y, total + total if double else total)
            later = jnp.minimum(i + 1, OWN * blocks - 1)
            zy[i + 1] = along_zy(source, later // blocks, first + 8 * (later % blocks) + shift)
            return 0

        zy[0] = along_zy(source, 0, first + shift)
        lax.fori_loop(0, OWN * blocks, body, 0)

    def put_first(o, start, y, total):
        other[o, pl.ds(start + near, 8), y : y + 8, :] = total

    def put_second(o, start, y, total):
        place = (o, pl.ds(start + far, 8), slice(y, y + 8), slice(None))
        field[place] = total - field[place]

    def put_third(o, start, y, total):
        result[o, pl.ds(start, 8), y : y + 8, :] = total - other[o, pl.ds(start + near, 8), y : y + 8, :]

    def outside(target, shift, count):
        blank = jnp.zeros((count, NY, NZ), F32)

        @pl.when(chunk[0] == 0)
        def _():
            for o in range(OWN):
                target[o, shift - count : shift] = blank

        @pl.when(chunk[0] == NX // CHUNK - 1)
        def _():
            for o in range(OWN):
                target[o, shift + CHUNK : shift + CHUNK + count] = blank

    step(field, far, -12, 7, False, put_first)
    outside(other, near, 12)
    step(other, near, -8, 6, True, put_second)
    outside(field, far, 8)
    step(field, far, 0, 4, True, put_third)

    def turn(x, _):
        for b in range(2):
            pieces = [result[o, t * 8 + x, b * 16 : b * 16 + 16, :] for t in range(4) for o in range(OWN)]
            turned[pl.ds((b * 8 + x) * NZ, NZ), :] = jnp.concatenate(pieces, axis=0).T
        return 0

    lax.fori_loop(0, 8, turn, 0)

    def pick(z, _):
        for x in range(4):
            for c in range(4):
                for b in range(2):
                    out[x, c, b, z] = turned[pl.ds(b * 8 * NZ + 16 * z + 4 * x + c, 8, stride=NZ), :]
        return 0

    lax.fori_loop(0, 8, pick, 0)


def rotate_kernel(ring, weights, out, gram):
    lane = lax.broadcasted_iota(jnp.int32, (256, 128), 1) // 32
    sums = jnp.zeros((256, 256), F32)
    for t in range(4):
        halves = []
        for b in range(2):
            value = None
            for c in range(4):
                piece = ring[:, c * 2 + b].reshape(256, 128)
                if c != t:
                    piece = pltpu.roll(piece, ((c - t) % 4) * 32, 1)
                value = piece if value is None else jnp.where(lane == c, piece, value)
            halves.append(value)
        all_orbitals = jnp.concatenate(halves, axis=1)
        turned = dot3(all_orbitals, weights[...], ((1,), (0,)))
        for b in range(2):
            for x in range(4):
                out[:, b, x, t] = turned[x * 64 : (x + 1) * 64, b * 128 : (b + 1) * 128].reshape(8, 8, 128)
        sums = sums + dot3(all_orbitals, all_orbitals, ((0,), (0,)))
    row = lax.broadcasted_iota(jnp.int32, (256, 256), 0) % 16
    column = lax.broadcasted_iota(jnp.int32, (256, 256), 1) % 16
    diagonal = jnp.where(row == column, sums, 0.0).reshape(16, 16, 256).sum(axis=1)
    place = lax.broadcasted_iota(jnp.int32, (256, 128), 0) // 16
    ones = (place == lax.broadcasted_iota(jnp.int32, (256, 128), 1)).astype(F32)
    both = jnp.dot(diagonal, ones, precision=lax.Precision.HIGHEST, preferred_element_type=F32)
    gram[...] = both[0:8] + pltpu.roll(both[8:16], 16, 1)


def lines_kernel(received, out):
    for z in range(8):
        for b in range(2):
            out[:, b * 16 : b * 16 + 16, z * 128 : (z + 1) * 128] = received[z * 2 + b].T.reshape(8, 16, 128)


def call(kernel, out, scratch=()):
    vmem = pl.BlockSpec(memory_space=pltpu.VMEM)
    smem = pl.BlockSpec(memory_space=pltpu.SMEM)
    return lambda *args: pl.pallas_call(
        kernel,
        out_shape=[jax.ShapeDtypeStruct(s, F32) for s in out],
        in_specs=[smem if a.dtype == jnp.int32 else vmem for a in args],
        out_specs=[vmem] * len(out),
        scratch_shapes=[pltpu.VMEM(s, F32) for s in scratch],
        compiler_params=pltpu.CompilerParams(vmem_limit_bytes=48 * 1024 * 1024),
    )(*args)


def local(orbitals, potential, coefficients):
    chunks = ("z", "x")
    dom = ("z", "x", "u", "c")
    count = lax.axis_size(chunks)
    up = [(i, i + 1) for i in range(count - 1)]
    down = [(j, i) for i, j in up]

    shift = [(d, d + 2 if d % 4 >= 2 else d - 2) for d in range(4 * count)]
    beyond = lax.ppermute(potential, dom, [(i, j) for i, j in shift if 0 <= j < 4 * count])
    slabs = lax.all_to_all(orbitals.reshape(4, OWN, 8, NY, NZ), ("u", "c"), 0, 0, tiled=True)
    far = 3 * WIDTH
    part = far - 16
    before = lax.ppermute(jnp.concatenate([slabs[1, :, 8 - part :], slabs[2], slabs[3]], axis=1), chunks, up)
    after = lax.ppermute(jnp.concatenate([slabs[0], slabs[1], slabs[2, :, :part]], axis=1), chunks, down)
    own = lax.all_gather(potential, ("u", "c"))
    beyond = lax.all_gather(beyond, ("u", "c"))

    weights = (coefficients[:, None, :, None] * jnp.eye(16, dtype=F32)[None, :, None, :]).reshape(256, 256)
    scratch = [
        (OWN, CHUNK + 2 * far, NY, NZ),
        (OWN, CHUNK + 2 * (2 * WIDTH + 2), NY, NZ),
        (64, NY, NZ),
        (OWN * 7 + 1, 8, NY, NZ),
        (OWN, CHUNK, NY, NZ),
        (2 * 8 * NZ, NZ),
    ]
    chunk = lax.axis_index(chunks).reshape(1)
    (message,) = call(filter_kernel, [(4, 4, 2, 8, 8, 128)], scratch)(
        chunk, slabs, before, after, own, beyond, *bands()
    )
    ring = lax.all_to_all(message.reshape(32, 64, 128), ("x", "u", "c", "b"), 0, 0, tiled=True)
    rotated, gram = call(rotate_kernel, [(8, 2, 4, 4, 8, 128), (8, 128)])(ring.reshape(4, 8, 64, 128), weights)
    received = lax.all_to_all(rotated.reshape(16, 128, 128), ("z", "b"), 0, 0, tiled=True)
    for axes in (("u", "c"), ("x", "b"), ("z",)):
        gram = lax.all_gather(gram, axes).sum(axis=0)
    gram = gram / (NX * NY * NZ)
    intersection = jnp.concatenate([gram[:, :NORB], gram[:, NORB : 2 * NORB]], axis=0)
    (lines,) = call(lines_kernel, [(8, NY, NX)])(received)
    return intersection, lines


def solution(mesh):
    grid = Mesh(mesh.devices.reshape(8, 4, 2, 2, 2), ("z", "x", "u", "c", "b"))
    dom = ("z", "x", "u", "c")
    return jax.shard_map(
        local,
        mesh=grid,
        in_specs=(P("b", dom, None, None), P(dom, None, None), P()),
        out_specs=(P(), P("b", dom, None)),
        check_vma=False,
    )
```

time: 154 us -> 172 us (1.12); the launches traced: 151 us -> 171 us
  blocking collectives: 52.2 us -> 95.7 us
  waiting for transfers between devices: 41.9 us -> 24.4 us
  between operations: 14.1 us -> 0.76 us
  starting transfers between devices: 20 us -> 26.9 us
  Pallas kernels: 18.3 us -> 20.6 us
    all_gather x1 -> x5, blocking collectives: 5.17 us -> 77.7 us  [the longest x3 64 us: local(): gram = lax.all_gather(gram, axes).sum(axis=0)]
    all_to_all x1, blocking collectives: 47 us -> 18 us  [local(): lax.all_to_all(orbitals.reshape(4, OWN, 8, NY, NZ), ('u', 'c'), 0, 0, til...]
    ppermute x1, waiting for transfers between devices: 9.77 us -> 0.01 us  [local(): lax.ppermute(jnp.concatenate([slabs[0], slabs[1], slabs[2, :, :part]], ax...]
    ppermute x1, waiting for transfers between devices: 7.1 us -> 0.01 us  [local(): lax.ppermute(jnp.concatenate([slabs[1, :, 8 - part:], slabs[2], slabs[3]]...]
    all_to_all x2, starting transfers between devices: 8.26 us -> 14.8 us  [the longest x1 9.82 us: local(): lax.all_to_all(rotated.reshape(16, 128, 128), ('z', 'b'), 0, 0, tiled=True)]
    all_to_all x2, waiting for transfers between devices: 19.8 us -> 17.4 us  [the longest x1 17.4 us: local(): lax.all_to_all(message.reshape(32, 64, 128), ('x', 'u', 'c', 'b'), 0, 0,...]
    pallas_call x3, Pallas kernels: 18.3 us -> 20.6 us  [call(): pl.pallas_call(kernel, out_shape=[jax.ShapeDtypeStruct(s, F32) for s in o...]
    ppermute x1, waiting for transfers between devices: 5.26 us -> 7.01 us  [local(): lax.ppermute(potential, dom, [(i, j) for i, j in shift if 0 <= j < 4 * co...]
  transfers between devices with their start and end apart: 6 -> 5, of which waited for: 5 -> 2; matrix products, arithmetic and copies ran while one was open for 2% -> 2% of each run, Pallas kernels for 0% -> 0%
where the time goes in v3:
time: 172 us; the launch traced here: 171 us
  blocking collectives  95.7 us (56%)
  starting transfers between devices  26.9 us (16%)
  waiting for transfers between devices  24.4 us (14%)
  Pallas kernels  20.6 us (12%)
  other arithmetic  1.74 us (1%)
    all_gather x3, blocking collectives, local(): gram = lax.all_gather(gram, axes).sum(axis=0)  64 us
    pallas_call x3, Pallas kernels, call(): pl.pallas_call(kernel, out_shape=[jax.ShapeDtypeStruct(s, F32) for s in o...  20.6 us
    all_to_all x1, blocking collectives, local(): lax.all_to_all(orbitals.reshape(4, OWN, 8, NY, NZ), ('u', 'c'), 0, 0, til...  18 us
    all_to_all x1, waiting for transfers between devices, local(): lax.all_to_all(message.reshape(32, 64, 128), ('x', 'u', 'c', 'b'), 0, 0,...  17.4 us
    all_to_all x1, starting transfers between devices, local(): lax.all_to_all(rotated.reshape(16, 128, 128), ('z', 'b'), 0, 0, tiled=True)  9.82 us
    ppermute x1, waiting for transfers between devices, local(): lax.ppermute(potential, dom, [(i, j) for i, j in shift if 0 <= j < 4 * co...  7.01 us
    all_gather x1, blocking collectives, local(): own = lax.all_gather(potential, ('u', 'c'))  6.98 us
    all_gather x1, blocking collectives, local(): beyond = lax.all_gather(beyond, ('u', 'c'))  6.71 us
  transfers between devices with their start and end apart: 5, of which 2 were waited for; matrix products, arithmetic and copies ran while one was open for 2% of the time, Pallas kernels for 0%

profile of v3, /device:TPU:32, one launch (start us, length us, event | category | flops | bytes accessed | tf_op | source)
XLA Modules:
  0.0 171.2 jit_solution(8334711541436717164)
XLA Ops:
  0.6 18.0 %all_to_all.15.slabs = f32[4,2,8,32,128]{4,3,2,1,0:T(8,128)S(1)} all-to-all(f32[4,2,8,32,128]{4,3,2,1,0:T(8,128)} %bitcast.30), channel_id=1, replica_groups=mesh['z'=8,'x'=4,'u'=2,'c'=2,'b'=2] {'u','c'}, dimensions={0} | all-to-all | bytes 2097152 | tf_op jit(solution)/shard_map/all_to_all | solution.py:203
  18.6 0.1 slice_bitcast_fusion.1
  18.7 0.0 copy-start
  18.7 0.0 copy-start.1
  18.8 4.3 %collective-permute-start.1 = (f32[2,18,32,128]{3,2,1,0:T(8,128)S(1)}, f32[2,18,32,128]{3,2,1,0:T(8,128)S(1)}, u32[]{:S(2)}, u32[]{:S(2)}) collective-permute-start(f32[2,18,32,128]{3,2,1,0:T(8,128)S(1)} %pad_maximum_fusion.1), channel_id=1, source_target_pairs={{8,0},{16,8},{24,16},{32,24},{40,32},{48,40},{56,48},{64,56},{72,6... | collective-permute-start | bytes 1769480 | tf_op jit(solution)/shard_map/ppermute | solution.py:207
  23.1 0.9 pad_maximum_fusion
  24.0 1.9 %collective-permute-start = (f32[2,18,32,128]{3,2,1,0:T(8,128)}, f32[2,18,32,128]{3,2,1,0:T(8,128)S(1)}, u32[]{:S(2)}, u32[]{:S(2)}) collective-permute-start(f32[2,18,32,128]{3,2,1,0:T(8,128)} %pad_maximum_fusion), channel_id=1, source_target_pairs={{0,8},{8,16},{16,24},{24,32},{32,40},{40,48},{48,56},{56,64},{64,7... | collective-permute-start | bytes 1769480 | tf_op jit(solution)/shard_map/ppermute | solution.py:206
  25.9 5.8 %collective-permute-start.2 = (f32[8,32,128]{2,1,0:T(8,128)S(1)}, f32[8,32,128]{2,1,0:T(8,128)}, u32[]{:S(2)}, u32[]{:S(2)}) collective-permute-start(f32[8,32,128]{2,1,0:T(8,128)S(1)} %copy-done.2), channel_id=1, source_target_pairs={{4,8},{6,10},{8,4},{10,6},{12,16},{14,18},{16,12},{18,14},{20,24},... | collective-permute-start | bytes 393224 | tf_op jit(solution)/shard_map/ppermute | solution.py:202
  31.7 7.0 %all-gather = f32[32,32,128]{2,1,0:T(8,128)S(1)} all-gather(f32[8,32,128]{2,1,0:T(8,128)S(1)} %copy-done.2), channel_id=2, replica_groups=mesh['z'=8,'x'=4,'u'=2,'c'=2,'b'=2] {'u','c'}, dimensions={0}, use_global_device_ids=true | all-gather | bytes 655360 | tf_op jit(solution)/shard_map/all_gather | solution.py:208
  38.7 7.0 %collective-permute-done.2 = f32[8,32,128]{2,1,0:T(8,128)} collective-permute-done((f32[8,32,128]{2,1,0:T(8,128)S(1)}, f32[8,32,128]{2,1,0:T(8,128)}, u32[]{:S(2)}, u32[]{:S(2)}) %collective-permute-start.2) | collective-permute-done | bytes 131104 | tf_op jit(solution)/shard_map/ppermute | solution.py:202
  45.7 6.7 %all-gather.1 = f32[32,32,128]{2,1,0:T(8,128)S(1)} all-gather(f32[8,32,128]{2,1,0:T(8,128)} %collective-permute-done.2), channel_id=3, replica_groups=mesh['z'=8,'x'=4,'u'=2,'c'=2,'b'=2] {'u','c'}, dimensions={0}, use_global_device_ids=true | all-gather | bytes 655360 | tf_op jit(solution)/shard_map/all_gather | solution.py:209
  52.5 16.8 %shard_map.68 = f32[4,4,2,8,8,128]{5,4,3,2,1,0:T(8,128)} custom-call(s32[1]{0:T(128)} %bitcast.chunk, f32[4,2,8,32,128]{4,3,2,1,0:T(8,128)S(1)} %all_to_all.15.slabs, f32[2,18,32,128]{3,2,1,0:T(8,128)S(1)} %collective-permute-done.before, f32[2,18,32,128]{3,2,1,0:T(8,128)S(1)} %collective-permute-done.1.after, f32[4,8,32,128]{3,2,1,0:T(8,128)S(1)} %bitcast.28, ...), custom_call_target="tpu_custom_call" | custom-call | tf_op jit(solution)/shard_map/pallas_call | solution.py:184
  69.3 5.0 %all-to-all-start.1 = ((f32[32,64,128]{2,1,0:T(8,128)}), f32[32,64,128]{2,1,0:T(8,128)S(1)}, u32[]{:S(2)}, u32[]{:S(2)}) async-start(f32[32,64,128]{2,1,0:T(8,128)} %bitcast.10), calls=%async_computation.1 | async-start | bytes 2097152 | tf_op jit(solution)/shard_map/all_to_all | solution.py:224
  74.3 0.2 broadcast_multiply_fusion
  74.5 0.9 mul.24.weights
  75.4 17.4 %all-to-all-done.1 = f32[32,64,128]{2,1,0:T(8,128)S(1)} async-done(((f32[32,64,128]{2,1,0:T(8,128)}), f32[32,64,128]{2,1,0:T(8,128)S(1)}, u32[]{:S(2)}, u32[]{:S(2)}) %all-to-all-start.1) | async-done | bytes 1048608 | tf_op jit(solution)/shard_map/all_to_all | solution.py:224
  92.8 2.5 %shard_map.69 = (f32[8,2,4,4,8,128]{5,4,3,2,1,0:T(8,128)}, f32[8,128]{1,0:T(8,128)S(1)}) custom-call(f32[4,8,64,128]{3,2,1,0:T(8,128)S(1)} %bitcast.27, f32[256,256]{1,0:T(8,128)S(1)} %mul.24.weights), custom_call_target="tpu_custom_call" | custom-call | tf_op jit(solution)/shard_map/pallas_call | solution.py:184
  95.3 9.8 %all-to-all-start.2 = ((f32[16,128,128]{2,1,0:T(8,128)}), f32[16,128,128]{2,1,0:T(8,128)S(1)}, u32[]{:S(2)}, u32[]{:S(2)}) async-start(f32[16,128,128]{2,1,0:T(8,128)} %bitcast.15), calls=%async_computation.2 | async-start | bytes 2097152 | tf_op jit(solution)/shard_map/all_to_all | solution.py:226
  105.1 5.2 %all-gather.2 = f32[32,128]{1,0:T(8,128)S(1)} all-gather(f32[8,128]{1,0:T(8,128)S(1)} %get-tuple-element.4), channel_id=4, replica_groups=mesh['z'=8,'x'=4,'u'=2,'c'=2,'b'=2] {'u','c'}, dimensions={0}, use_global_device_ids=true | all-gather | bytes 20480 | tf_op jit(solution)/shard_map/all_gather | solution.py:228
  110.3 34.1 %all-gather.3 = f32[64,128]{1,0:T(8,128)S(1)} all-gather(f32[8,128]{1,0:T(8,128)S(1)} %bitcast_reduce_fusion.2), channel_id=5, replica_groups=mesh['z'=8,'x'=4,'u'=2,'c'=2,'b'=2] {'x','b'}, dimensions={0}, use_global_device_ids=true | all-gather | bytes 36864 | tf_op jit(solution)/shard_map/all_gather | solution.py:228
  144.4 24.8 %all-gather.4 = f32[64,128]{1,0:T(8,128)S(1)} all-gather(f32[8,128]{1,0:T(8,128)S(1)} %bitcast_reduce_fusion.1), channel_id=6, replica_groups=mesh['z'=8,'x'=4,'u'=2,'c'=2,'b'=2] {'z'}, dimensions={0}, use_global_device_ids=true | all-gather | bytes 36864 | tf_op jit(solution)/shard_map/all_gather | solution.py:228
  169.2 0.1 fusion.1
  169.2 0.6 pad_maximum_fusion.2
  169.8 1.3 shard_map.70
  (16 shorter events, 0.1 us)
Async XLA Ops:
  18.6 7.3 %copy-start.2 = (f32[8,32,128]{2,1,0:T(8,128)S(1)}, f32[8,32,128]{2,1,0:T(8,128)}, u32[]{:S(2)}) copy-start(f32[8,32,128]{2,1,0:T(8,128)} %param.6) | copy-start | bytes 393220
  18.7 33.8 %copy-start = (bf16[256,768]{1,0:T(8,128)(2,1)S(1)}, bf16[256,768]{1,0:T(8,128)(2,1)}, u32[]{:S(2)}) copy-start(bf16[256,768]{1,0:T(8,128)(2,1)} %constant.22.clone.band_y) | copy-start | bytes 1179652
  18.7 33.8 %copy-start.1 = (bf16[256,256]{1,0:T(8,128)(2,1)S(1)}, bf16[256,256]{1,0:T(8,128)(2,1)}, u32[]{:S(2)}) copy-start(bf16[256,256]{1,0:T(8,128)(2,1)} %constant.21.clone.band_z) | copy-start | bytes 393220
  18.8 33.7 %collective-permute-start.1 = (f32[2,18,32,128]{3,2,1,0:T(8,128)S(1)}, f32[2,18,32,128]{3,2,1,0:T(8,128)S(1)}, u32[]{:S(2)}, u32[]{:S(2)}) collective-permute-start(f32[2,18,32,128]{3,2,1,0:T(8,128)S(1)} %pad_maximum_fusion.1), channel_id=1, source_target_pairs={{8,0},{16,8},{24,16},{32,24},{40,32},{48,40},{56,48},{64,56},{72,6... | collective-permute-start | bytes 1769480 | tf_op jit(solution)/shard_map/ppermute | solution.py:207
  24.0 28.5 %collective-permute-start = (f32[2,18,32,128]{3,2,1,0:T(8,128)}, f32[2,18,32,128]{3,2,1,0:T(8,128)S(1)}, u32[]{:S(2)}, u32[]{:S(2)}) collective-permute-start(f32[2,18,32,128]{3,2,1,0:T(8,128)} %pad_maximum_fusion), channel_id=1, source_target_pairs={{0,8},{8,16},{16,24},{24,32},{32,40},{40,48},{48,56},{56,64},{64,7... | collective-permute-start | bytes 1769480 | tf_op jit(solution)/shard_map/ppermute | solution.py:206
  25.9 19.8 %collective-permute-start.2 = (f32[8,32,128]{2,1,0:T(8,128)S(1)}, f32[8,32,128]{2,1,0:T(8,128)}, u32[]{:S(2)}, u32[]{:S(2)}) collective-permute-start(f32[8,32,128]{2,1,0:T(8,128)S(1)} %copy-done.2), channel_id=1, source_target_pairs={{4,8},{6,10},{8,4},{10,6},{12,16},{14,18},{16,12},{18,14},{20,24},... | collective-permute-start | bytes 393224 | tf_op jit(solution)/shard_map/ppermute | solution.py:202
  69.3 5.0 %copy-start.3 = (f32[16,16]{1,0:T(8,128)S(1)}, f32[16,16]{1,0:T(8,128)}, u32[]{:S(2)}) copy-start(f32[16,16]{1,0:T(8,128)} %param.7) | copy-start | bytes 3076
  69.3 23.5 %all-to-all-start.1 = ((f32[32,64,128]{2,1,0:T(8,128)}), f32[32,64,128]{2,1,0:T(8,128)S(1)}, u32[]{:S(2)}, u32[]{:S(2)}) async-start(f32[32,64,128]{2,1,0:T(8,128)} %bitcast.10), calls=%async_computation.1 | async-start | bytes 2097152 | tf_op jit(solution)/shard_map/all_to_all | solution.py:224
  95.3 74.6 %all-to-all-start.2 = ((f32[16,128,128]{2,1,0:T(8,128)}), f32[16,128,128]{2,1,0:T(8,128)S(1)}, u32[]{:S(2)}, u32[]{:S(2)}) async-start(f32[16,128,128]{2,1,0:T(8,128)} %bitcast.15), calls=%async_computation.2 | async-start | bytes 2097152 | tf_op jit(solution)/shard_map/all_to_all | solution.py:226

commit v4 on v2

--- a/solution.py
+++ b/solution.py
@@ -22,10 +22,10 @@
 CENTER = 8.5
 HALF = 6.5
 WIDTH = 6
+YPAD = 8
 NORB, NX, NY, NZ = 16, 1024, 32, 128
 CHUNK = 32
 OWN = 2
-YPAD = 8
 F32 = jnp.float32
 BF16 = jnp.bfloat16
 
@@ -54,7 +54,7 @@
     return dot(ah, bh) + (dot(ah, bl) + dot(al, bh))
 
 
-def filter_kernel(chunk, slabs, before, after, potential, bands, out, field, other, local, zpart, result, turned):
+def filter_kernel(chunk, slabs, before, after, own, beyond, bands, out, field, other, local, zpart, result, turned):
     far, near = 3 * WIDTH, 2 * WIDTH + 2
     rows = slice(YPAD, YPAD + NY)
     zeros = jnp.zeros((YPAD, NZ), F32)
@@ -72,9 +72,9 @@
         field[o, far + CHUNK :, rows, :] = after[o]
         for s in range(4):
             field[o, far + 8 * s : far + 8 * s + 8, rows, :] = slabs[s, o]
-    order = [(0, 1), (1, 1), (0, 0), (1, 0), (2, 0), (3, 0), (2, 1), (3, 1)]
-    for j, (s, h) in enumerate(order):
-        local[8 * j : 8 * j + 8] = (potential[s, h] + (-1.5 * STENCIL[0] - CENTER)) * (1.0 / HALF)
+    order = [beyond[0], beyond[1], own[0], own[1], own[2], own[3], beyond[2], beyond[3]]
+    for j, slab in enumerate(order):
+        local[8 * j : 8 * j + 8] = (slab + (-1.5 * STENCIL[0] - CENTER)) * (1.0 / HALF)
 
     def along_z(source, o, index, band):
         high, low = split(source[o, pl.ds(index, 8), rows, :].reshape(8 * NY, NZ))
@@ -147,16 +147,17 @@
 
     lax.fori_loop(0, 8, turn, 0)
 
-    def pick(q, _):
-        for c in range(4):
-            for b in range(2):
-                out[c, b, q] = turned[pl.ds(b * 8 * NZ + 4 * q + c, 8, stride=NZ), :]
+    def pick(z, _):
+        for x in range(4):
+            for c in range(4):
+                for b in range(2):
+                    out[x, c, b, z] = turned[pl.ds(b * 8 * NZ + 16 * z + 4 * x + c, 8, stride=NZ), :]
         return 0
 
-    lax.fori_loop(0, NZ // 4, pick, 0)
-
-
-def rotate_kernel(ring, weights, out):
+    lax.fori_loop(0, 8, pick, 0)
+
+
+def rotate_kernel(ring, weights, out, gram):
     lane = lax.broadcasted_iota(jnp.int32, (256, 128), 1) // 32
     sums = jnp.zeros((256, 256), F32)
     for t in range(4):
@@ -164,7 +165,7 @@
         for b in range(2):
             value = None
             for c in range(4):
-                piece = ring[c * 2 + b]
+                piece = ring[:, c * 2 + b].reshape(256, 128)
                 if c != t:
                     piece = pltpu.roll(piece, ((c - t) % 4) * 32, 1)
                 value = piece if value is None else jnp.where(lane == c, piece, value)
@@ -172,23 +173,22 @@
         all_orbitals = jnp.concatenate(halves, axis=1)
         turned = dot3(all_orbitals, weights[...], ((1,), (0,)))
         for b in range(2):
-            out[:, b, t] = turned[:, b * 128 : (b + 1) * 128].reshape(32, 8, 128)
+            for x in range(4):
+                out[:, b, x, t] = turned[x * 64 : (x + 1) * 64, b * 128 : (b + 1) * 128].reshape(8, 8, 128)
         sums = sums + dot3(all_orbitals, all_orbitals, ((0,), (0,)))
     row = lax.broadcasted_iota(jnp.int32, (256, 256), 0) % 16
     column = lax.broadcasted_iota(jnp.int32, (256, 256), 1) % 16
     diagonal = jnp.where(row == column, sums, 0.0).reshape(16, 16, 256).sum(axis=1)
     place = lax.broadcasted_iota(jnp.int32, (256, 128), 0) // 16
     ones = (place == lax.broadcasted_iota(jnp.int32, (256, 128), 1)).astype(F32)
-    gram = jnp.dot(diagonal, ones, precision=lax.Precision.HIGHEST, preferred_element_type=F32)
-    tile = gram[0:8] + pltpu.roll(gram[8:16], 16, 1)
-    out[:, :, 4] = jnp.broadcast_to(tile, (32, 2, 8, 128))
+    both = jnp.dot(diagonal, ones, precision=lax.Precision.HIGHEST, preferred_element_type=F32)
+    gram[...] = both[0:8] + pltpu.roll(both[8:16], 16, 1)
 
 
 def lines_kernel(received, out):
-    for b in range(2):
-        for s in range(8):
-            block = received[s * 4 : s * 4 + 4, b, 0:4].reshape(128, 128).T.reshape(8, 16, 128)
-            out[:, b * 16 : b * 16 + 16, s * 128 : (s + 1) * 128] = block
+    for z in range(8):
+        for b in range(2):
+            out[:, b * 16 : b * 16 + 16, z * 128 : (z + 1) * 128] = received[z * 2 + b].T.reshape(8, 16, 128)
 
 
 def call(kernel, out, scratch=()):
@@ -196,9 +196,9 @@
     smem = pl.BlockSpec(memory_space=pltpu.SMEM)
     return lambda *args: pl.pallas_call(
         kernel,
-        out_shape=jax.ShapeDtypeStruct(out, F32),
+        out_shape=[jax.ShapeDtypeStruct(s, F32) for s in out],
         in_specs=[smem if a.dtype == jnp.int32 else vmem for a in args],
-        out_specs=vmem,
+        out_specs=[vmem] * len(out),
         scratch_shapes=[pltpu.VMEM(s, F32) for s in scratch],
         compiler_params=pltpu.CompilerParams(vmem_limit_bytes=48 * 1024 * 1024),
     )(*args)
@@ -214,14 +214,15 @@
     shift = [(d, d + 2 if d % 4 >= 2 else d - 2) for d in range(4 * count)]
     beyond = lax.ppermute(potential, dom, [(i, j) for i, j in shift if 0 <= j < 4 * count])
     slabs = lax.all_to_all(orbitals.reshape(4, OWN, 8, NY, NZ), ("u", "c"), 0, 0, tiled=True)
+    own = lax.all_gather(potential, ("u", "c"))
+    slabs, own, beyond = lax.optimization_barrier((slabs, own, beyond))
     far = 3 * WIDTH
     part = far - 16
     before = lax.ppermute(jnp.concatenate([slabs[1, :, 8 - part :], slabs[2], slabs[3]], axis=1), chunks, up)
     after = lax.ppermute(jnp.concatenate([slabs[0], slabs[1], slabs[2, :, :part]], axis=1), chunks, down)
-    window = lax.all_gather(jnp.stack([potential, beyond]), ("u", "c"))
+    beyond = lax.all_gather(beyond, ("u", "c"))
 
     weights = (coefficients[:, None, :, None] * jnp.eye(16, dtype=F32)[None, :, None, :]).reshape(256, 256)
-    bands = jnp.asarray(np.stack([banded(1.0 / HALF), banded(2.0 / HALF)]))
     scratch = [
         (OWN, CHUNK + 2 * far, NY + 2 * YPAD, NZ),
         (OWN, CHUNK + 2 * (2 * WIDTH + 2), NY + 2 * YPAD, NZ),
@@ -230,15 +231,23 @@
         (OWN, CHUNK, NY, NZ),
         (2 * 8 * NZ, NZ),
     ]
+    bands = jnp.asarray(np.stack([banded(1.0 / HALF), banded(2.0 / HALF)]))
     chunk = lax.axis_index(chunks).reshape(1)
-    message = call(filter_kernel, (4, 2, 32, 8, 128), scratch)(chunk, slabs, before, after, window, bands)
-    ring = lax.all_to_all(message.reshape(8, 256, 128), ("u", "c", "b"), 0, 0, tiled=True)
-    rotated = call(rotate_kernel, (32, 2, 5, 8, 128))(ring, weights)
-    received = lax.all_to_all(rotated.reshape(64, 40, 128), ("z", "x", "b"), 0, 0, tiled=True)
-    received = received.reshape(32, 2, 5, 8, 128)
-    gram = lax.all_gather(received[:, :, 4].sum(axis=(0, 1)), ("u", "c")).sum(axis=0) / (NX * NY * NZ)
+    (message,) = call(filter_kernel, [(4, 4, 2, 8, 8, 128)], scratch)(
+        chunk, slabs, before, after, own, beyond, bands
+    )
+    ring = lax.all_to_all(message.reshape(32, 64, 128), ("x", "u", "c", "b"), 0, 0, tiled=True)
+    rotated, gram = call(rotate_kernel, [(8, 2, 4, 4, 8, 128), (8, 128)])(ring.reshape(4, 8, 64, 128), weights)
+    received = lax.all_to_all(rotated.reshape(16, 128, 128), ("z", "b"), 0, 0, tiled=True)
+    for axes in (("u", "c"), ("x",)):
+        gram = lax.all_gather(gram, axes).sum(axis=0)
+    gram, received = lax.optimization_barrier((gram, received))
+    copies = jnp.broadcast_to(gram[None], (16, 8, 128))
+    gram = lax.all_to_all(copies, ("z", "b"), 0, 0, tiled=True).sum(axis=0)
+    gram = gram / (NX * NY * NZ)
     intersection = jnp.concatenate([gram[:, :NORB], gram[:, NORB : 2 * NORB]], axis=0)
-    return intersection, call(lines_kernel, (8, NY, NX))(received)
+    (lines,) = call(lines_kernel, [(8, NY, NX)])(received)
+    return intersection, lines
 
 
 def solution(mesh):

time: 154 us -> 146 us (0.948); the launches traced: 151 us -> 145 us
  starting transfers between devices: 20 us -> 36.5 us
  between operations: 14.1 us -> 0.75 us
  blocking collectives: 52.2 us -> 39.4 us
  waiting for transfers between devices: 41.9 us -> 45.5 us
    all_to_all x1 -> x0, blocking collectives: 47 us -> none  [local(): lax.all_to_all(rotated.reshape(64, 40, 128), ('z', 'x', 'b'), 0, 0, tiled...]
    all_gather x1 -> x4, blocking collectives: 5.17 us -> 39.4 us  [the longest x2 17.1 us: local(): gram = lax.all_gather(gram, axes).sum(axis=0)]
    all_to_all x1 -> x3, waiting for transfers between devices: 14.2 us -> 34.9 us  [the longest x1 17.4 us: local(): lax.all_to_all(message.reshape(32, 64, 128), ('x', 'u', 'c', 'b'), 0, 0,...]
    all_to_all x1 -> x3, starting transfers between devices: 4.6 us -> 21.2 us  [the longest x1 9.83 us: local(): lax.all_to_all(rotated.reshape(16, 128, 128), ('z', 'b'), 0, 0, tiled=True)]
    ppermute x1, waiting for transfers between devices: 9.77 us -> 3.67 us  [local(): lax.ppermute(jnp.concatenate([slabs[0], slabs[1], slabs[2, :, :part]], ax...]
    all_to_all x1, waiting for transfers between devices: 5.58 us -> 0.01 us  [local(): lax.all_to_all(orbitals.reshape(4, OWN, 8, NY, NZ), ('u', 'c'), 0, 0, til...]
    ppermute x1, waiting for transfers between devices: 5.26 us -> 0.01 us  [local(): lax.ppermute(potential, dom, [(i, j) for i, j in shift if 0 <= j < 4 * co...]
  transfers between devices with their start and end apart: 6 -> 7, of which waited for: 5 -> 5; matrix products, arithmetic and copies ran while one was open for 2% -> 1% of each run, Pallas kernels for 0% -> 1%
where the time goes in v4:
time: 146 us; the launch traced here: 145 us
  waiting for transfers between devices  45.5 us (31%)
  blocking collectives  39.4 us (27%)
  starting transfers between devices  36.5 us (25%)
  Pallas kernels  18.8 us (13%)
  other arithmetic  2.56 us (2%)
  local copies, waits for them, and re-layouts  1.77 us (1%)
    pallas_call x3, Pallas kernels, call(): pl.pallas_call(kernel, out_shape=[jax.ShapeDtypeStruct(s, F32) for s in o...  18.8 us
    all_to_all x1, waiting for transfers between devices, local(): lax.all_to_all(message.reshape(32, 64, 128), ('x', 'u', 'c', 'b'), 0, 0,...  17.4 us
    all_gather x2, blocking collectives, local(): gram = lax.all_gather(gram, axes).sum(axis=0)  17.1 us
    all_gather x1, blocking collectives, local(): own = lax.all_gather(potential, ('u', 'c'))  15.3 us
    all_to_all x1, starting transfers between devices, local(): lax.all_to_all(rotated.reshape(16, 128, 128), ('z', 'b'), 0, 0, tiled=True)  9.83 us
    all_to_all x1, waiting for transfers between devices, local(): lax.all_to_all(rotated.reshape(16, 128, 128), ('z', 'b'), 0, 0, tiled=True)  9.58 us
    all_to_all x1, waiting for transfers between devices, local(): gram = lax.all_to_all(copies, ('z', 'b'), 0, 0, tiled=True).sum(axis=0)  7.94 us
    all_gather x1, blocking collectives, local(): beyond = lax.all_gather(beyond, ('u', 'c'))  7.01 us
  transfers between devices with their start and end apart: 7, of which 5 were waited for; matrix products, arithmetic and copies ran while one was open for 1% of the time, Pallas kernels for 1%

profile of v4, /device:TPU:32, one launch (start us, length us, event | category | flops | bytes accessed | tf_op | source)
XLA Modules:
  0.0 145.2 jit_solution(2156589420204339528)
XLA Ops:
  0.6 3.7 %all-to-all-start = ((f32[4,2,8,32,128]{4,3,2,1,0:T(8,128)}), f32[4,2,8,32,128]{4,3,2,1,0:T(8,128)S(1)}, u32[]{:S(2)}, u32[]{:S(2)}) async-start(f32[4,2,8,32,128]{4,3,2,1,0:T(8,128)} %bitcast.28), calls=%async_computation | async-start | bytes 2097152 | tf_op jit(solution)/shard_map/all_to_all | solution.py:216
  4.3 5.6 %collective-permute-start = (f32[8,32,128]{2,1,0:T(8,128)S(1)}, f32[8,32,128]{2,1,0:T(8,128)S(1)}, u32[]{:S(2)}, u32[]{:S(2)}) collective-permute-start(f32[8,32,128]{2,1,0:T(8,128)S(1)} %copy-done.1), channel_id=1, source_target_pairs={{4,8},{6,10},{8,4},{10,6},{12,16},{14,18},{16,12},{18,14},{20,24},... | collective-permute-start | bytes 393224 | tf_op jit(solution)/shard_map/ppermute | solution.py:215
  9.9 15.3 %all-gather = f32[32,32,128]{2,1,0:T(8,128)S(1)} all-gather(f32[8,32,128]{2,1,0:T(8,128)S(1)} %copy-done.1), channel_id=2, replica_groups=mesh['z'=8,'x'=4,'u'=2,'c'=2,'b'=2] {'u','c'}, dimensions={0}, use_global_device_ids=true | all-gather | bytes 655360 | tf_op jit(solution)/shard_map/all_gather | solution.py:217
  25.4 0.9 pad_maximum_fusion.1
  26.2 4.2 %collective-permute-start.2 = (f32[2,18,32,128]{3,2,1,0:T(8,128)}, f32[2,18,32,128]{3,2,1,0:T(8,128)S(1)}, u32[]{:S(2)}, u32[]{:S(2)}) collective-permute-start(f32[2,18,32,128]{3,2,1,0:T(8,128)} %pad_maximum_fusion.1), channel_id=1, source_target_pairs={{8,0},{16,8},{24,16},{32,24},{40,32},{48,40},{56,48},{64,56},{72,6... | collective-permute-start | bytes 1769480 | tf_op jit(solution)/shard_map/ppermute | solution.py:222
  30.4 0.9 pad_maximum_fusion
  31.3 1.9 %collective-permute-start.1 = (f32[2,18,32,128]{3,2,1,0:T(8,128)}, f32[2,18,32,128]{3,2,1,0:T(8,128)S(1)}, u32[]{:S(2)}, u32[]{:S(2)}) collective-permute-start(f32[2,18,32,128]{3,2,1,0:T(8,128)} %pad_maximum_fusion), channel_id=1, source_target_pairs={{0,8},{8,16},{16,24},{24,32},{32,40},{40,48},{48,56},{56,64},{64,7... | collective-permute-start | bytes 1769480 | tf_op jit(solution)/shard_map/ppermute | solution.py:221
  33.2 7.0 %all-gather.1 = f32[32,32,128]{2,1,0:T(8,128)S(1)} all-gather(f32[8,32,128]{2,1,0:T(8,128)S(1)} %collective-permute-done), channel_id=3, replica_groups=mesh['z'=8,'x'=4,'u'=2,'c'=2,'b'=2] {'u','c'}, dimensions={0}, use_global_device_ids=true | all-gather | bytes 655360 | tf_op jit(solution)/shard_map/all_gather | solution.py:223
  40.2 3.7 %collective-permute-done.2.after = f32[2,18,32,128]{3,2,1,0:T(8,128)S(1)} collective-permute-done((f32[2,18,32,128]{3,2,1,0:T(8,128)}, f32[2,18,32,128]{3,2,1,0:T(8,128)S(1)}, u32[]{:S(2)}, u32[]{:S(2)}) %collective-permute-start.2) | collective-permute-done | bytes 589856 | tf_op jit(solution)/shard_map/ppermute | solution.py:222
  43.9 6.9 %collective-permute-done.1.before = f32[2,18,32,128]{3,2,1,0:T(8,128)S(1)} collective-permute-done((f32[2,18,32,128]{3,2,1,0:T(8,128)}, f32[2,18,32,128]{3,2,1,0:T(8,128)S(1)}, u32[]{:S(2)}, u32[]{:S(2)}) %collective-permute-start.1) | collective-permute-done | bytes 589856 | tf_op jit(solution)/shard_map/ppermute | solution.py:221
  50.8 15.0 %shard_map.59 = f32[4,4,2,8,8,128]{5,4,3,2,1,0:T(8,128)} custom-call(s32[1]{0:T(128)} %bitcast.chunk, f32[4,2,8,32,128]{4,3,2,1,0:T(8,128)S(1)} %all-to-all-done.slabs, f32[2,18,32,128]{3,2,1,0:T(8,128)S(1)} %collective-permute-done.1.before, f32[2,18,32,128]{3,2,1,0:T(8,128)S(1)} %collective-permute-done.2.after, f32[4,8,32,128]{3,2,1,0:T(8,128)S(1)} %bitcast.26, ...), custom_call_target="tpu_custom_call" | custom-call | tf_op jit(solution)/shard_map/pallas_call | solution.py:197
  65.8 5.0 %all-to-all-start.1 = ((f32[32,64,128]{2,1,0:T(8,128)}), f32[32,64,128]{2,1,0:T(8,128)S(1)}, u32[]{:S(2)}, u32[]{:S(2)}) async-start(f32[32,64,128]{2,1,0:T(8,128)} %bitcast.10), calls=%async_computation.1 | async-start | bytes 2097152 | tf_op jit(solution)/shard_map/all_to_all | solution.py:239
  71.0 0.9 mul.24.weights
  71.9 17.4 %all-to-all-done.1 = f32[32,64,128]{2,1,0:T(8,128)S(1)} async-done(((f32[32,64,128]{2,1,0:T(8,128)}), f32[32,64,128]{2,1,0:T(8,128)S(1)}, u32[]{:S(2)}, u32[]{:S(2)}) %all-to-all-start.1) | async-done | bytes 1048608 | tf_op jit(solution)/shard_map/all_to_all | solution.py:239
  89.3 2.5 %shard_map.60 = (f32[8,2,4,4,8,128]{5,4,3,2,1,0:T(8,128)}, f32[8,128]{1,0:T(8,128)S(1)}) custom-call(f32[4,8,64,128]{3,2,1,0:T(8,128)S(1)} %bitcast.25, f32[256,256]{1,0:T(8,128)S(1)} %mul.24.weights), custom_call_target="tpu_custom_call" | custom-call | tf_op jit(solution)/shard_map/pallas_call | solution.py:197
  91.8 9.8 %all-to-all-start.2 = ((f32[16,128,128]{2,1,0:T(8,128)}), f32[16,128,128]{2,1,0:T(8,128)S(1)}, u32[]{:S(2)}, u32[]{:S(2)}) async-start(f32[16,128,128]{2,1,0:T(8,128)} %bitcast.14), calls=%async_computation.2 | async-start | bytes 2097152 | tf_op jit(solution)/shard_map/all_to_all | solution.py:241
  101.6 5.2 %all-gather.2 = f32[32,128]{1,0:T(8,128)S(1)} all-gather(f32[8,128]{1,0:T(8,128)S(1)} %get-tuple-element.12), channel_id=4, replica_groups=mesh['z'=8,'x'=4,'u'=2,'c'=2,'b'=2] {'u','c'}, dimensions={0}, use_global_device_ids=true | all-gather | bytes 20480 | tf_op jit(solution)/shard_map/all_gather | solution.py:243
  106.8 11.9 %all-gather.3 = f32[32,128]{1,0:T(8,128)S(1)} all-gather(f32[8,128]{1,0:T(8,128)S(1)} %bitcast_reduce_fusion.1), channel_id=5, replica_groups=mesh['z'=8,'x'=4,'u'=2,'c'=2,'b'=2] {'x'}, dimensions={0}, use_global_device_ids=true | all-gather | bytes 20480 | tf_op jit(solution)/shard_map/all_gather | solution.py:243
  118.7 9.6 %all-to-all-done.2.received = f32[16,128,128]{2,1,0:T(8,128)S(1)} async-done(((f32[16,128,128]{2,1,0:T(8,128)}), f32[16,128,128]{2,1,0:T(8,128)S(1)}, u32[]{:S(2)}, u32[]{:S(2)}) %all-to-all-start.2) | async-done | bytes 1048608 | tf_op jit(solution)/shard_map/all_to_all | solution.py:241
  128.3 0.6 broadcast_in_dim.2
  128.9 6.3 %all-to-all-start.3 = ((f32[16,8,128]{2,1,0:T(8,128)}), f32[16,8,128]{2,1,0:T(8,128)S(1)}, u32[]{:S(2)}, u32[]{:S(2)}) async-start(f32[16,8,128]{2,1,0:T(8,128)} %broadcast_in_dim.2), calls=%async_computation.3 | async-start | bytes 131072 | tf_op jit(solution)/shard_map/all_to_all | solution.py:246
  135.3 1.3 shard_map.61
  136.6 7.9 %all-to-all-done.3 = f32[16,8,128]{2,1,0:T(8,128)S(1)} async-done(((f32[16,8,128]{2,1,0:T(8,128)}), f32[16,8,128]{2,1,0:T(8,128)S(1)}, u32[]{:S(2)}, u32[]{:S(2)}) %all-to-all-start.3) | async-done | bytes 65568 | tf_op jit(solution)/shard_map/all_to_all | solution.py:246
  144.6 0.6 pad_maximum_fusion.2
  (17 shorter events, 0.5 us)
Async XLA Ops:
  0.6 3.7 %copy-start.1 = (f32[8,32,128]{2,1,0:T(8,128)S(1)}, f32[8,32,128]{2,1,0:T(8,128)}, u32[]{:S(2)}) copy-start(f32[8,32,128]{2,1,0:T(8,128)} %param.5) | copy-start | bytes 393220
  0.6 24.6 %all-to-all-start = ((f32[4,2,8,32,128]{4,3,2,1,0:T(8,128)}), f32[4,2,8,32,128]{4,3,2,1,0:T(8,128)S(1)}, u32[]{:S(2)}, u32[]{:S(2)}) async-start(f32[4,2,8,32,128]{4,3,2,1,0:T(8,128)} %bitcast.28), calls=%async_computation | async-start | bytes 2097152 | tf_op jit(solution)/shard_map/all_to_all | solution.py:216
  4.3 20.9 %collective-permute-start = (f32[8,32,128]{2,1,0:T(8,128)S(1)}, f32[8,32,128]{2,1,0:T(8,128)S(1)}, u32[]{:S(2)}, u32[]{:S(2)}) collective-permute-start(f32[8,32,128]{2,1,0:T(8,128)S(1)} %copy-done.1), channel_id=1, source_target_pairs={{4,8},{6,10},{8,4},{10,6},{12,16},{14,18},{16,12},{18,14},{20,24},... | collective-permute-start | bytes 393224 | tf_op jit(solution)/shard_map/ppermute | solution.py:215
  25.3 25.5 %copy-start = (bf16[2,256,256]{2,1,0:T(8,128)(2,1)S(1)}, bf16[2,256,256]{2,1,0:T(8,128)(2,1)}, u32[]{:S(2)}) copy-start(bf16[2,256,256]{2,1,0:T(8,128)(2,1)} %constant.19.clone.bands) | copy-start | bytes 786436
  26.2 17.7 %collective-permute-start.2 = (f32[2,18,32,128]{3,2,1,0:T(8,128)}, f32[2,18,32,128]{3,2,1,0:T(8,128)S(1)}, u32[]{:S(2)}, u32[]{:S(2)}) collective-permute-start(f32[2,18,32,128]{3,2,1,0:T(8,128)} %pad_maximum_fusion.1), channel_id=1, source_target_pairs={{8,0},{16,8},{24,16},{32,24},{40,32},{48,40},{56,48},{64,56},{72,6... | collective-permute-start | bytes 1769480 | tf_op jit(solution)/shard_map/ppermute | solution.py:222
  31.3 19.5 %collective-permute-start.1 = (f32[2,18,32,128]{3,2,1,0:T(8,128)}, f32[2,18,32,128]{3,2,1,0:T(8,128)S(1)}, u32[]{:S(2)}, u32[]{:S(2)}) collective-permute-start(f32[2,18,32,128]{3,2,1,0:T(8,128)} %pad_maximum_fusion), channel_id=1, source_target_pairs={{0,8},{8,16},{16,24},{24,32},{32,40},{40,48},{48,56},{56,64},{64,7... | collective-permute-start | bytes 1769480 | tf_op jit(solution)/shard_map/ppermute | solution.py:221
  65.8 5.0 %copy-start.2 = (f32[16,16]{1,0:T(8,128)S(1)}, f32[16,16]{1,0:T(8,128)}, u32[]{:S(2)}) copy-start(f32[16,16]{1,0:T(8,128)} %param.6) | copy-start | bytes 3076
  65.8 23.5 %all-to-all-start.1 = ((f32[32,64,128]{2,1,0:T(8,128)}), f32[32,64,128]{2,1,0:T(8,128)S(1)}, u32[]{:S(2)}, u32[]{:S(2)}) async-start(f32[32,64,128]{2,1,0:T(8,128)} %bitcast.10), calls=%async_computation.1 | async-start | bytes 2097152 | tf_op jit(solution)/shard_map/all_to_all | solution.py:239
  91.8 36.5 %all-to-all-start.2 = ((f32[16,128,128]{2,1,0:T(8,128)}), f32[16,128,128]{2,1,0:T(8,128)S(1)}, u32[]{:S(2)}, u32[]{:S(2)}) async-start(f32[16,128,128]{2,1,0:T(8,128)} %bitcast.14), calls=%async_computation.2 | async-start | bytes 2097152 | tf_op jit(solution)/shard_map/all_to_all | solution.py:241
  128.9 15.6 %all-to-all-start.3 = ((f32[16,8,128]{2,1,0:T(8,128)}), f32[16,8,128]{2,1,0:T(8,128)S(1)}, u32[]{:S(2)}, u32[]{:S(2)}) async-start(f32[16,8,128]{2,1,0:T(8,128)} %broadcast_in_dim.2), calls=%async_computation.3 | async-start | bytes 131072 | tf_op jit(solution)/shard_map/all_to_all | solution.py:246

commit v5 on v4

--- a/solution.py
+++ b/solution.py
@@ -147,14 +147,13 @@
 
     lax.fori_loop(0, 8, turn, 0)
 
-    def pick(z, _):
-        for x in range(4):
-            for c in range(4):
-                for b in range(2):
-                    out[x, c, b, z] = turned[pl.ds(b * 8 * NZ + 16 * z + 4 * x + c, 8, stride=NZ), :]
+    def pick(q, _):
+        for c in range(4):
+            for b in range(2):
+                out[c, b, q] = turned[pl.ds(b * 8 * NZ + 4 * q + c, 8, stride=NZ), :]
         return 0
 
-    lax.fori_loop(0, 8, pick, 0)
+    lax.fori_loop(0, NZ // 4, pick, 0)
 
 
 def rotate_kernel(ring, weights, out, gram):
@@ -165,7 +164,7 @@
         for b in range(2):
             value = None
             for c in range(4):
-                piece = ring[:, c * 2 + b].reshape(256, 128)
+                piece = ring[c * 2 + b]
                 if c != t:
                     piece = pltpu.roll(piece, ((c - t) % 4) * 32, 1)
                 value = piece if value is None else jnp.where(lane == c, piece, value)
@@ -173,8 +172,7 @@
         all_orbitals = jnp.concatenate(halves, axis=1)
         turned = dot3(all_orbitals, weights[...], ((1,), (0,)))
         for b in range(2):
-            for x in range(4):
-                out[:, b, x, t] = turned[x * 64 : (x + 1) * 64, b * 128 : (b + 1) * 128].reshape(8, 8, 128)
+            out[:, b, t] = turned[:, b * 128 : (b + 1) * 128].reshape(32, 8, 128)
         sums = sums + dot3(all_orbitals, all_orbitals, ((0,), (0,)))
     row = lax.broadcasted_iota(jnp.int32, (256, 256), 0) % 16
     column = lax.broadcasted_iota(jnp.int32, (256, 256), 1) % 16
@@ -186,9 +184,10 @@
 
 
 def lines_kernel(received, out):
-    for z in range(8):
-        for b in range(2):
-            out[:, b * 16 : b * 16 + 16, z * 128 : (z + 1) * 128] = received[z * 2 + b].T.reshape(8, 16, 128)
+    for b in range(2):
+        for s in range(8):
+            block = received[s * 4 : s * 4 + 4, b].reshape(128, 128).T.reshape(8, 16, 128)
+            out[:, b * 16 : b * 16 + 16, s * 128 : (s + 1) * 128] = block
 
 
 def call(kernel, out, scratch=()):
@@ -214,12 +213,12 @@
     shift = [(d, d + 2 if d % 4 >= 2 else d - 2) for d in range(4 * count)]
     beyond = lax.ppermute(potential, dom, [(i, j) for i, j in shift if 0 <= j < 4 * count])
     slabs = lax.all_to_all(orbitals.reshape(4, OWN, 8, NY, NZ), ("u", "c"), 0, 0, tiled=True)
-    own = lax.all_gather(potential, ("u", "c"))
-    slabs, own, beyond = lax.optimization_barrier((slabs, own, beyond))
+    slabs, beyond = lax.optimization_barrier((slabs, beyond))
     far = 3 * WIDTH
     part = far - 16
     before = lax.ppermute(jnp.concatenate([slabs[1, :, 8 - part :], slabs[2], slabs[3]], axis=1), chunks, up)
     after = lax.ppermute(jnp.concatenate([slabs[0], slabs[1], slabs[2, :, :part]], axis=1), chunks, down)
+    own = lax.all_gather(potential, ("u", "c"))
     beyond = lax.all_gather(beyond, ("u", "c"))
 
     weights = (coefficients[:, None, :, None] * jnp.eye(16, dtype=F32)[None, :, None, :]).reshape(256, 256)
@@ -233,20 +232,18 @@
     ]
     bands = jnp.asarray(np.stack([banded(1.0 / HALF), banded(2.0 / HALF)]))
     chunk = lax.axis_index(chunks).reshape(1)
-    (message,) = call(filter_kernel, [(4, 4, 2, 8, 8, 128)], scratch)(
+    (message,) = call(filter_kernel, [(4, 2, 32, 8, 128)], scratch)(
         chunk, slabs, before, after, own, beyond, bands
     )
-    ring = lax.all_to_all(message.reshape(32, 64, 128), ("x", "u", "c", "b"), 0, 0, tiled=True)
-    rotated, gram = call(rotate_kernel, [(8, 2, 4, 4, 8, 128), (8, 128)])(ring.reshape(4, 8, 64, 128), weights)
-    received = lax.all_to_all(rotated.reshape(16, 128, 128), ("z", "b"), 0, 0, tiled=True)
-    for axes in (("u", "c"), ("x",)):
-        gram = lax.all_gather(gram, axes).sum(axis=0)
-    gram, received = lax.optimization_barrier((gram, received))
-    copies = jnp.broadcast_to(gram[None], (16, 8, 128))
-    gram = lax.all_to_all(copies, ("z", "b"), 0, 0, tiled=True).sum(axis=0)
+    ring = lax.all_to_all(message.reshape(8, 256, 128), ("u", "c", "b"), 0, 0, tiled=True)
+    rotated, gram = call(rotate_kernel, [(32, 2, 4, 8, 128), (8, 128)])(ring, weights)
+    received = lax.all_to_all(rotated.reshape(64, 32, 128), ("z", "x", "b"), 0, 0, tiled=True)
+    gram = lax.all_gather(gram, ("u", "c")).sum(axis=0)
+    for axis, bit in (("x", 1), ("x", 2), ("b", 1), ("z", 1), ("z", 2), ("z", 4)):
+        gram = gram + lax.ppermute(gram, axis, [(i, i ^ bit) for i in range(lax.axis_size(axis))])
     gram = gram / (NX * NY * NZ)
     intersection = jnp.concatenate([gram[:, :NORB], gram[:, NORB : 2 * NORB]], axis=0)
-    (lines,) = call(lines_kernel, [(8, NY, NX)])(received)
+    (lines,) = call(lines_kernel, [(8, NY, NX)])(received.reshape(32, 2, 32, 128))
     return intersection, lines
 
 

time: 146 us -> 134 us (0.918)
  blocking collectives: 39.4 us -> 19 us
  starting transfers between devices: 36.5 us -> 46 us
    all_to_all x3 -> x2, waiting for transfers between devices: 34.9 us -> 14.2 us  [the longest x1 14.2 us: local(): lax.all_to_all(message.reshape(8, 256, 128), ('u', 'c', 'b'), 0, 0, tiled...]
    ppermute x0 -> x6, waiting for transfers between devices: none -> 15.7 us  [local(): lax.ppermute(gram, axis, [(i, i ^ bit) for i in range(lax.axis_size(axis))])]
    ppermute x0 -> x6, starting transfers between devices: none -> 14.4 us  [local(): lax.ppermute(gram, axis, [(i, i ^ bit) for i in range(lax.axis_size(axis))])]
    all_gather x2 -> x1, blocking collectives: 17.1 us -> 5.19 us  [local(): gram = lax.all_gather(gram, ('u', 'c')).sum(axis=0)]
    all_gather x1, blocking collectives: 15.3 us -> 6.51 us  [local(): own = lax.all_gather(potential, ('u', 'c'))]
    all_to_all x1, waiting for transfers between devices: 0.01 us -> 6.36 us  [local(): lax.all_to_all(orbitals.reshape(4, OWN, 8, NY, NZ), ('u', 'c'), 0, 0, til...]
    ppermute x1, waiting for transfers between devices: 0.01 us -> 5.24 us  [local(): lax.ppermute(potential, dom, [(i, j) for i, j in shift if 0 <= j < 4 * co...]
    all_to_all x3 -> x2, starting transfers between devices: 21.2 us -> 16.3 us  [the longest x1 11.7 us: local(): lax.all_to_all(rotated.reshape(64, 32, 128), ('z', 'x', 'b'), 0, 0, tiled...]
  transfers between devices with their start and end apart: 7 -> 12, of which waited for: 5 -> 10; matrix products, arithmetic and copies ran while one was open for 1% -> 2% of each run, Pallas kernels for 1% -> 0%
where the time goes in v5:
time: 134 us; the launch traced here: 132 us
  starting transfers between devices  46 us (34%)
  waiting for transfers between devices  44.5 us (33%)
  blocking collectives  19 us (14%)
  Pallas kernels  19 us (14%)
  other arithmetic  1.73 us (1%)
    pallas_call x3, Pallas kernels, call(): pl.pallas_call(kernel, out_shape=[jax.ShapeDtypeStruct(s, F32) for s in o...  19 us
    ppermute x6, waiting for transfers between devices, local(): lax.ppermute(gram, axis, [(i, i ^ bit) for i in range(lax.axis_size(axis))])  15.7 us
    ppermute x6, starting transfers between devices, local(): lax.ppermute(gram, axis, [(i, i ^ bit) for i in range(lax.axis_size(axis))])  14.4 us
    all_to_all x1, waiting for transfers between devices, local(): lax.all_to_all(message.reshape(8, 256, 128), ('u', 'c', 'b'), 0, 0, tiled...  14.2 us
    all_to_all x1, starting transfers between devices, local(): lax.all_to_all(rotated.reshape(64, 32, 128), ('z', 'x', 'b'), 0, 0, tiled...  11.7 us
    all_gather x1, blocking collectives, local(): beyond = lax.all_gather(beyond, ('u', 'c'))  7.28 us
    all_gather x1, blocking collectives, local(): own = lax.all_gather(potential, ('u', 'c'))  6.51 us
    all_to_all x1, waiting for transfers between devices, local(): lax.all_to_all(orbitals.reshape(4, OWN, 8, NY, NZ), ('u', 'c'), 0, 0, til...  6.36 us
  transfers between devices with their start and end apart: 12, of which 10 were waited for; matrix products, arithmetic and copies ran while one was open for 2% of the time, Pallas kernels for 0%

profile of v5, /device:TPU:32, one launch (start us, length us, event | category | flops | bytes accessed | tf_op | source)
XLA Modules:
  0.0 132.1 jit_solution(9527738073378667722)
XLA Ops:
  0.6 3.7 %all-to-all-start = ((f32[4,2,8,32,128]{4,3,2,1,0:T(8,128)}), f32[4,2,8,32,128]{4,3,2,1,0:T(8,128)S(1)}, u32[]{:S(2)}, u32[]{:S(2)}) async-start(f32[4,2,8,32,128]{4,3,2,1,0:T(8,128)} %bitcast.26), calls=%async_computation | async-start | bytes 2097152 | tf_op jit(solution)/shard_map/all_to_all | solution.py:215
  4.3 5.6 %collective-permute-start = (f32[8,32,128]{2,1,0:T(8,128)S(1)}, f32[8,32,128]{2,1,0:T(8,128)S(1)}, u32[]{:S(2)}, u32[]{:S(2)}) collective-permute-start(f32[8,32,128]{2,1,0:T(8,128)S(1)} %copy-done.1), channel_id=1, source_target_pairs={{4,8},{6,10},{8,4},{10,6},{12,16},{14,18},{16,12},{18,14},{20,24},... | collective-permute-start | bytes 393224 | tf_op jit(solution)/shard_map/ppermute | solution.py:214
  9.9 5.2 %collective-permute-done = f32[8,32,128]{2,1,0:T(8,128)S(1)} collective-permute-done((f32[8,32,128]{2,1,0:T(8,128)S(1)}, f32[8,32,128]{2,1,0:T(8,128)S(1)}, u32[]{:S(2)}, u32[]{:S(2)}) %collective-permute-start) | collective-permute-done | bytes 131104 | tf_op jit(solution)/shard_map/ppermute | solution.py:214
  15.2 6.4 %all-to-all-done.slabs = f32[4,2,8,32,128]{4,3,2,1,0:T(8,128)S(1)} async-done(((f32[4,2,8,32,128]{4,3,2,1,0:T(8,128)}), f32[4,2,8,32,128]{4,3,2,1,0:T(8,128)S(1)}, u32[]{:S(2)}, u32[]{:S(2)}) %all-to-all-start) | async-done | bytes 1048608 | tf_op jit(solution)/shard_map/all_to_all | solution.py:215
  21.7 4.2 %collective-permute-start.2 = (f32[2,18,32,128]{3,2,1,0:T(8,128)S(1)}, f32[2,18,32,128]{3,2,1,0:T(8,128)S(1)}, u32[]{:S(2)}, u32[]{:S(2)}) collective-permute-start(f32[2,18,32,128]{3,2,1,0:T(8,128)S(1)} %pad_maximum_fusion.1), channel_id=1, source_target_pairs={{8,0},{16,8},{24,16},{32,24},{40,32},{48,40},{56,48},{64,56},{72,6... | collective-permute-start | bytes 1769480 | tf_op jit(solution)/shard_map/ppermute | solution.py:220
  28.7 6.5 %all-gather = f32[32,32,128]{2,1,0:T(8,128)S(1)} all-gather(f32[8,32,128]{2,1,0:T(8,128)S(1)} %copy-done.1), channel_id=2, replica_groups=mesh['z'=8,'x'=4,'u'=2,'c'=2,'b'=2] {'u','c'}, dimensions={0}, use_global_device_ids=true | all-gather | bytes 655360 | tf_op jit(solution)/shard_map/all_gather | solution.py:221
  35.2 7.3 %all-gather.1 = f32[32,32,128]{2,1,0:T(8,128)S(1)} all-gather(f32[8,32,128]{2,1,0:T(8,128)S(1)} %collective-permute-done), channel_id=3, replica_groups=mesh['z'=8,'x'=4,'u'=2,'c'=2,'b'=2] {'u','c'}, dimensions={0}, use_global_device_ids=true | all-gather | bytes 655360 | tf_op jit(solution)/shard_map/all_gather | solution.py:222
  42.5 3.1 %collective-permute-done.1.before = f32[2,18,32,128]{3,2,1,0:T(8,128)S(1)} collective-permute-done((f32[2,18,32,128]{3,2,1,0:T(8,128)}, f32[2,18,32,128]{3,2,1,0:T(8,128)S(1)}, u32[]{:S(2)}, u32[]{:S(2)}) %collective-permute-start.1) | collective-permute-done | bytes 589856 | tf_op jit(solution)/shard_map/ppermute | solution.py:219
  45.6 15.2 %shard_map.59 = f32[4,2,32,8,128]{4,3,2,1,0:T(8,128)} custom-call(s32[1]{0:T(128)} %bitcast.chunk, f32[4,2,8,32,128]{4,3,2,1,0:T(8,128)S(1)} %all-to-all-done.slabs, f32[2,18,32,128]{3,2,1,0:T(8,128)S(1)} %collective-permute-done.1.before, f32[2,18,32,128]{3,2,1,0:T(8,128)S(1)} %collective-permute-done.2.after, f32[4,8,32,128]{3,2,1,0:T(8,128)S(1)} %bitcast.24, ...), custom_call_target="tpu_custom_call" | custom-call | tf_op jit(solution)/shard_map/pallas_call | solution.py:196
  60.8 4.6 %all-to-all-start.1 = ((f32[8,256,128]{2,1,0:T(8,128)}), f32[8,256,128]{2,1,0:T(8,128)S(1)}, u32[]{:S(2)}, u32[]{:S(2)}) async-start(f32[8,256,128]{2,1,0:T(8,128)} %bitcast.10), calls=%async_computation.1 | async-start | bytes 2097152 | tf_op jit(solution)/shard_map/all_to_all | solution.py:238
  66.5 14.2 %all-to-all-done.1.ring = f32[8,256,128]{2,1,0:T(8,128)S(1)} async-done(((f32[8,256,128]{2,1,0:T(8,128)}), f32[8,256,128]{2,1,0:T(8,128)S(1)}, u32[]{:S(2)}, u32[]{:S(2)}) %all-to-all-start.1) | async-done | bytes 1048608 | tf_op jit(solution)/shard_map/all_to_all | solution.py:238
  80.7 2.5 %shard_map.60 = (f32[32,2,4,8,128]{4,3,2,1,0:T(8,128)}, f32[8,128]{1,0:T(8,128)S(1)}) custom-call(f32[8,256,128]{2,1,0:T(8,128)S(1)} %all-to-all-done.1.ring, f32[256,256]{1,0:T(8,128)S(1)} %mul.24.weights), custom_call_target="tpu_custom_call" | custom-call | tf_op jit(solution)/shard_map/pallas_call | solution.py:196
  83.2 11.7 %all-to-all-start.2 = ((f32[64,32,128]{2,1,0:T(8,128)}), f32[64,32,128]{2,1,0:T(8,128)S(1)}, u32[]{:S(2)}, u32[]{:S(2)}) async-start(f32[64,32,128]{2,1,0:T(8,128)} %bitcast.12), calls=%async_computation.2 | async-start | bytes 2097152 | tf_op jit(solution)/shard_map/all_to_all | solution.py:240
  94.9 5.2 %all-gather.2 = f32[32,128]{1,0:T(8,128)S(1)} all-gather(f32[8,128]{1,0:T(8,128)S(1)} %get-tuple-element.8), channel_id=4, replica_groups=mesh['z'=8,'x'=4,'u'=2,'c'=2,'b'=2] {'u','c'}, dimensions={0}, use_global_device_ids=true | all-gather | bytes 20480 | tf_op jit(solution)/shard_map/all_gather | solution.py:241
  101.5 2.1 %collective-permute-done.3 = f32[8,128]{1,0:T(8,128)S(1)} collective-permute-done((f32[8,128]{1,0:T(8,128)S(1)}, f32[8,128]{1,0:T(8,128)S(1)}, u32[]{:S(2)}, u32[]{:S(2)}) %collective-permute-start.3) | collective-permute-done | bytes 4128 | tf_op jit(solution)/shard_map/ppermute | solution.py:243
  103.7 3.0 %collective-permute-start.4 = (f32[8,128]{1,0:T(8,128)S(1)}, f32[8,128]{1,0:T(8,128)S(1)}, u32[]{:S(2)}, u32[]{:S(2)}) collective-permute-start(f32[8,128]{1,0:T(8,128)S(1)} %add.22), channel_id=1, source_target_pairs={{0,16},{8,24},{16,0},{24,8},{1,17},{9,25},{17,1},{25,9},{2,18},{10... | collective-permute-start | bytes 12296 | tf_op jit(solution)/shard_map/ppermute | solution.py:243
  106.7 2.5 %collective-permute-done.4 = f32[8,128]{1,0:T(8,128)S(1)} collective-permute-done((f32[8,128]{1,0:T(8,128)S(1)}, f32[8,128]{1,0:T(8,128)S(1)}, u32[]{:S(2)}, u32[]{:S(2)}) %collective-permute-start.4) | collective-permute-done | bytes 4128 | tf_op jit(solution)/shard_map/ppermute | solution.py:243
  109.2 2.6 %collective-permute-start.5 = (f32[8,128]{1,0:T(8,128)S(1)}, f32[8,128]{1,0:T(8,128)S(1)}, u32[]{:S(2)}, u32[]{:S(2)}) collective-permute-start(f32[8,128]{1,0:T(8,128)S(1)} %add.23), channel_id=1, source_target_pairs={{0,1},{1,0},{2,3},{3,2},{4,5},{5,4},{6,7},{7,6},{8,9},{9,8},{10,11... | collective-permute-start | bytes 12296 | tf_op jit(solution)/shard_map/ppermute | solution.py:243
  111.8 2.5 %collective-permute-done.5 = f32[8,128]{1,0:T(8,128)S(1)} collective-permute-done((f32[8,128]{1,0:T(8,128)S(1)}, f32[8,128]{1,0:T(8,128)S(1)}, u32[]{:S(2)}, u32[]{:S(2)}) %collective-permute-start.5) | collective-permute-done | bytes 4128 | tf_op jit(solution)/shard_map/ppermute | solution.py:243
  114.5 3.6 %collective-permute-done.6 = f32[8,128]{1,0:T(8,128)S(1)} collective-permute-done((f32[8,128]{1,0:T(8,128)S(1)}, f32[8,128]{1,0:T(8,128)S(1)}, u32[]{:S(2)}, u32[]{:S(2)}) %collective-permute-start.6) | collective-permute-done | bytes 4128 | tf_op jit(solution)/shard_map/ppermute | solution.py:243
  118.1 2.1 %collective-permute-start.7 = (f32[8,128]{1,0:T(8,128)S(1)}, f32[8,128]{1,0:T(8,128)S(1)}, u32[]{:S(2)}, u32[]{:S(2)}) collective-permute-start(f32[8,128]{1,0:T(8,128)S(1)} %add.25), channel_id=1, source_target_pairs={{0,64},{32,96},{64,0},{96,32},{128,192},{160,224},{192,128},{224,1... | collective-permute-start | bytes 12296 | tf_op jit(solution)/shard_map/ppermute | solution.py:243
  120.2 2.4 %collective-permute-done.7 = f32[8,128]{1,0:T(8,128)S(1)} collective-permute-done((f32[8,128]{1,0:T(8,128)S(1)}, f32[8,128]{1,0:T(8,128)S(1)}, u32[]{:S(2)}, u32[]{:S(2)}) %collective-permute-start.7) | collective-permute-done | bytes 4128 | tf_op jit(solution)/shard_map/ppermute | solution.py:243
  122.6 5.1 %collective-permute-start.8 = (f32[8,128]{1,0:T(8,128)S(1)}, f32[8,128]{1,0:T(8,128)S(1)}, u32[]{:S(2)}, u32[]{:S(2)}) collective-permute-start(f32[8,128]{1,0:T(8,128)S(1)} %add.26), channel_id=1, source_target_pairs={{0,128},{32,160},{64,192},{96,224},{128,0},{160,32},{192,64},{224,... | collective-permute-start | bytes 12296 | tf_op jit(solution)/shard_map/ppermute | solution.py:243
  127.7 2.4 %collective-permute-done.8 = f32[8,128]{1,0:T(8,128)S(1)} collective-permute-done((f32[8,128]{1,0:T(8,128)S(1)}, f32[8,128]{1,0:T(8,128)S(1)}, u32[]{:S(2)}, u32[]{:S(2)}) %collective-permute-start.8) | collective-permute-done | bytes 4128 | tf_op jit(solution)/shard_map/ppermute | solution.py:243
  (28 shorter events, 7.7 us)
Async XLA Ops:
  0.6 3.7 %copy-start.1 = (f32[8,32,128]{2,1,0:T(8,128)S(1)}, f32[8,32,128]{2,1,0:T(8,128)}, u32[]{:S(2)}) copy-start(f32[8,32,128]{2,1,0:T(8,128)} %param.5) | copy-start | bytes 393220
  0.6 20.9 %all-to-all-start = ((f32[4,2,8,32,128]{4,3,2,1,0:T(8,128)}), f32[4,2,8,32,128]{4,3,2,1,0:T(8,128)S(1)}, u32[]{:S(2)}, u32[]{:S(2)}) async-start(f32[4,2,8,32,128]{4,3,2,1,0:T(8,128)} %bitcast.26), calls=%async_computation | async-start | bytes 2097152 | tf_op jit(solution)/shard_map/all_to_all | solution.py:215
  4.3 10.9 %collective-permute-start = (f32[8,32,128]{2,1,0:T(8,128)S(1)}, f32[8,32,128]{2,1,0:T(8,128)S(1)}, u32[]{:S(2)}, u32[]{:S(2)}) collective-permute-start(f32[8,32,128]{2,1,0:T(8,128)S(1)} %copy-done.1), channel_id=1, source_target_pairs={{4,8},{6,10},{8,4},{10,6},{12,16},{14,18},{16,12},{18,14},{20,24},... | collective-permute-start | bytes 393224 | tf_op jit(solution)/shard_map/ppermute | solution.py:214
  21.7 23.9 %copy-start = (bf16[2,256,256]{2,1,0:T(8,128)(2,1)S(1)}, bf16[2,256,256]{2,1,0:T(8,128)(2,1)}, u32[]{:S(2)}) copy-start(bf16[2,256,256]{2,1,0:T(8,128)(2,1)} %constant.19.clone.bands) | copy-start | bytes 786436
  21.7 20.8 %collective-permute-start.2 = (f32[2,18,32,128]{3,2,1,0:T(8,128)S(1)}, f32[2,18,32,128]{3,2,1,0:T(8,128)S(1)}, u32[]{:S(2)}, u32[]{:S(2)}) collective-permute-start(f32[2,18,32,128]{3,2,1,0:T(8,128)S(1)} %pad_maximum_fusion.1), channel_id=1, source_target_pairs={{8,0},{16,8},{24,16},{32,24},{40,32},{48,40},{56,48},{64,56},{72,6... | collective-permute-start | bytes 1769480 | tf_op jit(solution)/shard_map/ppermute | solution.py:220
  26.8 18.8 %collective-permute-start.1 = (f32[2,18,32,128]{3,2,1,0:T(8,128)}, f32[2,18,32,128]{3,2,1,0:T(8,128)S(1)}, u32[]{:S(2)}, u32[]{:S(2)}) collective-permute-start(f32[2,18,32,128]{3,2,1,0:T(8,128)} %pad_maximum_fusion), channel_id=1, source_target_pairs={{0,8},{8,16},{16,24},{24,32},{32,40},{40,48},{48,56},{56,64},{64,7... | collective-permute-start | bytes 1769480 | tf_op jit(solution)/shard_map/ppermute | solution.py:219
  60.8 4.6 %copy-start.2 = (f32[16,16]{1,0:T(8,128)S(1)}, f32[16,16]{1,0:T(8,128)}, u32[]{:S(2)}) copy-start(f32[16,16]{1,0:T(8,128)} %param.6) | copy-start | bytes 3076
  60.8 20.0 %all-to-all-start.1 = ((f32[8,256,128]{2,1,0:T(8,128)}), f32[8,256,128]{2,1,0:T(8,128)S(1)}, u32[]{:S(2)}, u32[]{:S(2)}) async-start(f32[8,256,128]{2,1,0:T(8,128)} %bitcast.10), calls=%async_computation.1 | async-start | bytes 2097152 | tf_op jit(solution)/shard_map/all_to_all | solution.py:238
  83.2 47.6 %all-to-all-start.2 = ((f32[64,32,128]{2,1,0:T(8,128)}), f32[64,32,128]{2,1,0:T(8,128)S(1)}, u32[]{:S(2)}, u32[]{:S(2)}) async-start(f32[64,32,128]{2,1,0:T(8,128)} %bitcast.12), calls=%async_computation.2 | async-start | bytes 2097152 | tf_op jit(solution)/shard_map/all_to_all | solution.py:240
  100.1 3.6 %collective-permute-start.3 = (f32[8,128]{1,0:T(8,128)S(1)}, f32[8,128]{1,0:T(8,128)S(1)}, u32[]{:S(2)}, u32[]{:S(2)}) collective-permute-start(f32[8,128]{1,0:T(8,128)S(1)} %bitcast_reduce_fusion), channel_id=1, source_target_pairs={{0,8},{8,0},{16,24},{24,16},{1,9},{9,1},{17,25},{25,17},{2,10},{10... | collective-permute-start | bytes 12296 | tf_op jit(solution)/shard_map/ppermute | solution.py:243
  103.7 5.5 %collective-permute-start.4 = (f32[8,128]{1,0:T(8,128)S(1)}, f32[8,128]{1,0:T(8,128)S(1)}, u32[]{:S(2)}, u32[]{:S(2)}) collective-permute-start(f32[8,128]{1,0:T(8,128)S(1)} %add.22), channel_id=1, source_target_pairs={{0,16},{8,24},{16,0},{24,8},{1,17},{9,25},{17,1},{25,9},{2,18},{10... | collective-permute-start | bytes 12296 | tf_op jit(solution)/shard_map/ppermute | solution.py:243
  109.2 5.1 %collective-permute-start.5 = (f32[8,128]{1,0:T(8,128)S(1)}, f32[8,128]{1,0:T(8,128)S(1)}, u32[]{:S(2)}, u32[]{:S(2)}) collective-permute-start(f32[8,128]{1,0:T(8,128)S(1)} %add.23), channel_id=1, source_target_pairs={{0,1},{1,0},{2,3},{3,2},{4,5},{5,4},{6,7},{7,6},{8,9},{9,8},{10,11... | collective-permute-start | bytes 12296 | tf_op jit(solution)/shard_map/ppermute | solution.py:243
  114.4 3.7 %collective-permute-start.6 = (f32[8,128]{1,0:T(8,128)S(1)}, f32[8,128]{1,0:T(8,128)S(1)}, u32[]{:S(2)}, u32[]{:S(2)}) collective-permute-start(f32[8,128]{1,0:T(8,128)S(1)} %add.24), channel_id=1, source_target_pairs={{0,32},{32,0},{64,96},{96,64},{128,160},{160,128},{192,224},{224,1... | collective-permute-start | bytes 12296 | tf_op jit(solution)/shard_map/ppermute | solution.py:243
  118.1 4.5 %collective-permute-start.7 = (f32[8,128]{1,0:T(8,128)S(1)}, f32[8,128]{1,0:T(8,128)S(1)}, u32[]{:S(2)}, u32[]{:S(2)}) collective-permute-start(f32[8,128]{1,0:T(8,128)S(1)} %add.25), channel_id=1, source_target_pairs={{0,64},{32,96},{64,0},{96,32},{128,192},{160,224},{192,128},{224,1... | collective-permute-start | bytes 12296 | tf_op jit(solution)/shard_map/ppermute | solution.py:243
  122.6 7.5 %collective-permute-start.8 = (f32[8,128]{1,0:T(8,128)S(1)}, f32[8,128]{1,0:T(8,128)S(1)}, u32[]{:S(2)}, u32[]{:S(2)}) collective-permute-start(f32[8,128]{1,0:T(8,128)S(1)} %add.26), channel_id=1, source_target_pairs={{0,128},{32,160},{64,192},{96,224},{128,0},{160,32},{192,64},{224,... | collective-permute-start | bytes 12296 | tf_op jit(solution)/shard_map/ppermute | solution.py:243

commit v6 on v5

v6 whole, which is shorter than its diff:
```python
import functools

import jax
import jax.numpy as jnp
import ml_dtypes
import numpy as np
from jax import lax
from jax.experimental import pallas as pl
from jax.experimental.pallas import tpu as pltpu
from jax.sharding import Mesh
from jax.sharding import PartitionSpec as P

STENCIL = (
    -5369.0 / 1800.0,
    12.0 / 7.0,
    -15.0 / 56.0,
    10.0 / 189.0,
    -1.0 / 112.0,
    2.0 / 1925.0,
    -1.0 / 16632.0,
)
CENTER = 8.5
HALF = 6.5
WIDTH = 6
EXT = 6
NORB, NX, NY, NZ = 16, 1024, 32, 128
CHUNK = 32
OWN = 2
F32 = jnp.float32
BF16 = jnp.bfloat16


def banded(scale):
    band = np.zeros((NZ, NZ), np.float64)
    for k in range(1, 7):
        band += np.eye(NZ, k=k) * STENCIL[k] + np.eye(NZ, k=-k) * STENCIL[k]
    band = (-0.5 * scale * band).astype(np.float32)
    high = band.astype(ml_dtypes.bfloat16)
    low = (band - high.astype(np.float32)).astype(ml_dtypes.bfloat16)
    zero = np.zeros_like(high)
    return np.block([[high, low], [high, zero]]).astype(ml_dtypes.bfloat16)


def split(x):
    high = x.astype(BF16)
    low = (x - high.astype(F32)).astype(BF16)
    return high, low


def dot3(a, b, dims):
    ah, al = split(a)
    bh, bl = split(b)
    dot = functools.partial(lax.dot_general, dimension_numbers=(dims, ((), ())), preferred_element_type=F32)
    return dot(ah, bh) + (dot(ah, bl) + dot(al, bh))


def filter_kernel(
    chunk, slabs, before, after, own, beyond, bands, out, field, other, local, zy, result, turned
):
    far, near = 3 * WIDTH, 2 * WIDTH + 2
    row = lax.broadcasted_iota(jnp.int32, (8, 8, NZ), 1) % 4

    def store(target, plane, r, value):
        planes = pl.ds(plane, 8)
        target[planes, EXT + r] = value
        if r >= 8 - EXT:
            target[planes, r - (8 - EXT)] = jnp.where(row == 0, 0.0, pltpu.roll(value, 1, 1))
        if r < EXT:
            target[planes, EXT + 8 + r] = jnp.where(row == 3, 0.0, pltpu.roll(value, 7, 1))

    def tiles(pieces):
        return jnp.swapaxes(jnp.concatenate([piece.reshape(4, 8, NZ) for piece in pieces], axis=0), 0, 1)

    def enter(plane, pieces):
        value = tiles(pieces)
        field[plane, EXT : EXT + 8] = value
        field[plane, 0:EXT] = jnp.where(row[:EXT] == 0, 0.0, pltpu.roll(value[8 - EXT :], 1, 1))
        field[plane, EXT + 8 :] = jnp.where(row[:EXT] == 3, 0.0, pltpu.roll(value[:EXT], 7, 1))

    def enter_ends(p, _):
        enter(p, [before[o, p] for o in range(OWN)])
        enter(far + CHUNK + p, [after[o, p] for o in range(OWN)])
        return 0

    lax.fori_loop(0, far, enter_ends, 0)

    def enter_slabs(p, _):
        for s in range(4):
            enter(far + 8 * s + p, [slabs[s, o, p] for o in range(OWN)])
        return 0

    lax.fori_loop(0, 8, enter_slabs, 0)

    def enter_local(p, _):
        for j, (source, s) in enumerate(
            [(beyond, 0), (beyond, 1), (own, 0), (own, 1), (own, 2), (own, 3), (beyond, 2), (beyond, 3)]
        ):
            value = (source[s, p] + (-1.5 * STENCIL[0] - CENTER)) * (1.0 / HALF)
            local[8 * j + p] = tiles([value, value])
        return 0

    lax.fori_loop(0, 8, enter_local, 0)

    def around(window, total):
        for k in range(1, 7):
            beside = window[WIDTH + k : WIDTH + 8 + k] + window[WIDTH - k : WIDTH + 8 - k]
            term = (-0.5 / HALF * STENCIL[k]) * beside
            total = term if total is None else total + term
        return total

    def along_zy(slot, source, index):
        high, low = split(source[pl.ds(index, 8), EXT : EXT + 8].reshape(8 * 64, NZ))
        both = jnp.dot(jnp.concatenate([high, low], axis=1), bands[...], preferred_element_type=F32)
        z = (both[:, :NZ] + both[:, NZ:]).reshape(8, 8, 8, NZ)
        for x in range(8):
            zy[slot, x] = around(source[index + x], z[x])

    def step(source, shift, first, blocks, put):
        def body(i, _):
            start = first + 8 * i
            for r in range(8):
                window = source[pl.ds(start + shift - WIDTH, 8 + 2 * WIDTH), EXT + r]
                total = local[pl.ds(start + 16, 8), r] * window[WIDTH : WIDTH + 8]
                put(start, r, around(window, total + zy[i, :, r]))
            along_zy(i + 1, source, first + 8 * jnp.minimum(i + 1, blocks - 1) + shift)
            return 0

        along_zy(0, source, first + shift)
        lax.fori_loop(0, blocks, body, 0)

    def put_first(start, r, total):
        store(other, start + near, r, total)

    def put_second(start, r, total):
        store(field, start + far, r, (total + total) - field[pl.ds(start + far, 8), EXT + r])

    def put_third(start, r, total):
        result[pl.ds(start, 8), r] = (total + total) - other[pl.ds(start + near, 8), EXT + r]

    def outside(target, shift, count):
        blank = jnp.zeros((count, 8 + 2 * EXT, 8, NZ), F32)

        @pl.when(chunk[0] == 0)
        def _():
            target[shift - count : shift] = blank

        @pl.when(chunk[0] == NX // CHUNK - 1)
        def _():
            target[shift + CHUNK : shift + CHUNK + count] = blank

    step(field, far, -12, 7, put_first)
    outside(other, near, 12)
    step(other, near, -8, 6, put_second)
    outside(field, far, 8)
    step(field, far, 0, 4, put_third)

    def turn(x, _):
        for b in range(2):
            pieces = [result[t * 8 + x, b * 4 + r] for t in range(4) for r in range(4)]
            turned[pl.ds((b * 8 + x) * NZ, NZ), :] = jnp.concatenate(pieces, axis=0).T
        return 0

    lax.fori_loop(0, 8, turn, 0)

    def pick(q, _):
        for c in range(4):
            for b in range(2):
                out[c, b, q] = turned[pl.ds(b * 8 * NZ + 4 * q + c, 8, stride=NZ), :]
        return 0

    lax.fori_loop(0, NZ // 4, pick, 0)


def rotate_kernel(ring, coefficients, out, gram):
    exact = functools.partial(
        lax.dot_general, precision=lax.Precision.HIGHEST, preferred_element_type=F32
    )
    row = lax.broadcasted_iota(jnp.int32, (256, 256), 0)
    column = lax.broadcasted_iota(jnp.int32, (256, 256), 1)
    number = lax.broadcasted_iota(jnp.int32, (256, 16), 0)
    entry = lax.broadcasted_iota(jnp.int32, (256, 16), 1)
    before = (number // 32 * 2 + number // 4 % 2 == entry).astype(F32)
    after = (number // 16 == entry).astype(F32)
    spread = exact(before, exact(coefficients[...], after, (((1,), (1,)), ((), ()))), (((1,), (0,)), ((), ())))
    same = (row // 8 % 4 == column % 4) & (row % 4 == column // 4 % 4)
    weights = jnp.where(same, spread, 0.0)

    lane = lax.broadcasted_iota(jnp.int32, (256, 128), 1) // 32
    sums = jnp.zeros((256, 256), F32)
    for t in range(4):
        halves = []
        for b in range(2):
            value = None
            for c in range(4):
                piece = ring[c * 2 + b]
                if c != t:
                    piece = pltpu.roll(piece, ((c - t) % 4) * 32, 1)
                value = piece if value is None else jnp.where(lane == c, piece, value)
            halves.append(value)
        all_orbitals = jnp.concatenate(halves, axis=1)
        turned = dot3(all_orbitals, weights, ((1,), (0,)))
        for b in range(2):
            out[:, b, t] = turned[:, b * 128 : (b + 1) * 128].reshape(32, 8, 128)
        sums = sums + dot3(all_orbitals, all_orbitals, ((0,), (0,)))
    diagonal = jnp.where((row // 8 % 4 == column // 8 % 4) & (row % 4 == column % 4), sums, 0.0)
    both = exact(before, exact(diagonal, before, (((1,), (0,)), ((), ()))), (((0,), (0,)), ((), ())))
    gram[...] = jnp.concatenate([both[0:8], both[8:16], jnp.zeros((8, 96), F32)], axis=1)


def lines_kernel(received, out):
    low = lax.broadcasted_iota(jnp.int32, (16, 8, 128), 1) < 4
    for s in range(8):
        first, second = (received[s * 4 : s * 4 + 4, b].reshape(128, 128).T.reshape(16, 8, 128) for b in range(2))
        even = jnp.where(low, first, pltpu.roll(second, 4, 1)).reshape(8, 2, 8, 128)
        odd = jnp.where(low, pltpu.roll(first, 4, 1), second).reshape(8, 2, 8, 128)
        for q in range(2):
            out[:, q * 16 : q * 16 + 8, s * 128 : (s + 1) * 128] = even[:, q]
            out[:, q * 16 + 8 : q * 16 + 16, s * 128 : (s + 1) * 128] = odd[:, q]


def call(kernel, out, scratch=()):
    vmem = pl.BlockSpec(memory_space=pltpu.VMEM)
    smem = pl.BlockSpec(memory_space=pltpu.SMEM)
    return lambda *args: pl.pallas_call(
        kernel,
        out_shape=[jax.ShapeDtypeStruct(s, F32) for s in out],
        in_specs=[smem if a.dtype == jnp.int32 else vmem for a in args],
        out_specs=[vmem] * len(out),
        scratch_shapes=[pltpu.VMEM(s, F32) for s in scratch],
        compiler_params=pltpu.CompilerParams(vmem_limit_bytes=48 * 1024 * 1024),
    )(*args)


def four(x, one, one_bit, two, two_bit):
    def swap(axes, bits):
        sizes = [lax.axis_size(a) for a in axes]
        flat = [np.ravel_multi_index([i ^ b for i, b in zip(at, bits)], sizes) for at in np.ndindex(*sizes)]
        return lax.ppermute(x, axes, [(i, int(j)) for i, j in enumerate(flat)])

    if one == two:
        parts = [swap((one,), (bits,)) for bits in (one_bit, two_bit, one_bit ^ two_bit)]
    else:
        parts = [swap((one, two), bits) for bits in ((one_bit, 0), (0, two_bit), (one_bit, two_bit))]
    return (x + parts[0]) + (parts[1] + parts[2])


def local(orbitals, potential, coefficients):
    chunks = ("z", "x")
    dom = ("z", "x", "u", "c")
    count = lax.axis_size(chunks)
    up = [(i, i + 1) for i in range(count - 1)]
    down = [(j, i) for i, j in up]

    shift = [(d, d + 2 if d % 4 >= 2 else d - 2) for d in range(4 * count)]
    beyond = lax.ppermute(potential, dom, [(i, j) for i, j in shift if 0 <= j < 4 * count])
    slabs = lax.all_to_all(orbitals.reshape(4, OWN, 8, NY, NZ), ("u", "c"), 0, 0, tiled=True)
    slabs, beyond = lax.optimization_barrier((slabs, beyond))
    far = 3 * WIDTH
    part = far - 16
    before = lax.ppermute(jnp.concatenate([slabs[1, :, 8 - part :], slabs[2], slabs[3]], axis=1), chunks, up)
    after = lax.ppermute(jnp.concatenate([slabs[0], slabs[1], slabs[2, :, :part]], axis=1), chunks, down)
    own = lax.all_gather(potential, ("u", "c"))
    beyond = lax.all_gather(beyond, ("u", "c"))

    scratch = [
        (CHUNK + 2 * far, 8 + 2 * EXT, 8, NZ),
        (CHUNK + 2 * (2 * WIDTH + 2), 8 + 2 * EXT, 8, NZ),
        (64, 8, 8, NZ),
        (8, 8, 8, 8, NZ),
        (CHUNK, 8, 8, NZ),
        (2 * 8 * NZ, NZ),
    ]
    bands = jnp.asarray(banded(1.0 / HALF))
    chunk = lax.axis_index(chunks).reshape(1)
    (message,) = call(filter_kernel, [(4, 2, 32, 8, 128)], scratch)(
        chunk, slabs, before, after, own, beyond, bands
    )
    ring = lax.all_to_all(message.reshape(8, 256, 128), ("u", "c", "b"), 0, 0, tiled=True)
    rotated, gram = call(rotate_kernel, [(32, 2, 4, 8, 128), (8, 128)])(ring, coefficients)
    received = lax.all_to_all(rotated.reshape(64, 32, 128), ("z", "x", "b"), 0, 0, tiled=True)
    gram = lax.all_gather(gram, ("u", "c")).sum(axis=0)
    for axes in (("x", 1, "x", 2), ("z", 1, "z", 2), ("z", 4, "b", 1)):
        gram = four(gram, *axes)
    gram = gram / (NX * NY * NZ)
    intersection = jnp.concatenate([gram[:, :NORB], gram[:, NORB : 2 * NORB]], axis=0)
    (lines,) = call(lines_kernel, [(8, NY, NX)])(received.reshape(32, 2, 32, 128))
    return intersection, lines


def solution(mesh):
    grid = Mesh(mesh.devices.reshape(8, 4, 2, 2, 2), ("z", "x", "u", "c", "b"))
    dom = ("z", "x", "u", "c")
    return jax.shard_map(
        local,
        mesh=grid,
        in_specs=(P("b", dom, None, None), P(dom, None, None), P()),
        out_specs=(P(), P("b", dom, None)),
        check_vma=False,
    )
```

time: 134 us -> 133 us (level)
  blocking collectives: 19 us -> 38.6 us
  waiting for transfers between devices: 44.5 us -> 28.1 us
  Pallas kernels: 19 us -> 16.6 us
    all_to_all x0 -> x1, blocking collectives: none -> 19.3 us  [local(): lax.all_to_all(message.reshape(8, 256, 128), ('u', 'c', 'b'), 0, 0, tiled...]
    all_to_all x1 -> x0, waiting for transfers between devices: 14.2 us -> none  [local(): lax.all_to_all(message.reshape(8, 256, 128), ('u', 'c', 'b'), 0, 0, tiled...]
    all_to_all x1 -> x0, starting transfers between devices: 4.61 us -> none  [local(): lax.all_to_all(message.reshape(8, 256, 128), ('u', 'c', 'b'), 0, 0, tiled...]
    ppermute x1, waiting for transfers between devices: 3.08 us -> 0.01 us  [local(): lax.ppermute(jnp.concatenate([slabs[1, :, 8 - part:], slabs[2], slabs[3]]...]
    ppermute x6 -> x9, starting transfers between devices: 14.4 us -> 16.9 us  [swap(): return lax.ppermute(x, axes, [(i, int(j)) for i, j in enumerate(flat)])]
    pallas_call x3, Pallas kernels: 19 us -> 16.6 us  [call(): pl.pallas_call(kernel, out_shape=[jax.ShapeDtypeStruct(s, F32) for s in o...]
    ppermute x1, starting transfers between devices: 1.91 us -> 3.4 us  [local(): lax.ppermute(jnp.concatenate([slabs[1, :, 8 - part:], slabs[2], slabs[3]]...]
    all_to_all x1, starting transfers between devices: 11.7 us -> 13 us  [local(): lax.all_to_all(rotated.reshape(64, 32, 128), ('z', 'x', 'b'), 0, 0, tiled...]
  transfers between devices with their start and end apart: 12 -> 14, of which waited for: 10 -> 9; matrix products, arithmetic and copies ran while one was open for 2% -> 1% of each run, Pallas kernels for 0% -> 0%
where the time goes in v6:
time: 133 us; the launch traced here: 132 us
  starting transfers between devices  47.2 us (35%)
  blocking collectives  38.6 us (29%)
  waiting for transfers between devices  28.1 us (21%)
  Pallas kernels  16.6 us (12%)
    all_to_all x1, blocking collectives, local(): lax.all_to_all(message.reshape(8, 256, 128), ('u', 'c', 'b'), 0, 0, tiled...  19.3 us
    ppermute x9, starting transfers between devices, swap(): return lax.ppermute(x, axes, [(i, int(j)) for i, j in enumerate(flat)])  16.9 us
    pallas_call x3, Pallas kernels, call(): pl.pallas_call(kernel, out_shape=[jax.ShapeDtypeStruct(s, F32) for s in o...  16.6 us
    ppermute x9, waiting for transfers between devices, swap(): return lax.ppermute(x, axes, [(i, int(j)) for i, j in enumerate(flat)])  16.4 us
    all_to_all x1, starting transfers between devices, local(): lax.all_to_all(rotated.reshape(64, 32, 128), ('z', 'x', 'b'), 0, 0, tiled...  13 us
    all_gather x1, blocking collectives, local(): beyond = lax.all_gather(beyond, ('u', 'c'))  7.41 us
    all_gather x1, blocking collectives, local(): own = lax.all_gather(potential, ('u', 'c'))  6.64 us
    all_to_all x1, waiting for transfers between devices, local(): lax.all_to_all(orbitals.reshape(4, OWN, 8, NY, NZ), ('u', 'c'), 0, 0, til...  6.36 us
  transfers between devices with their start and end apart: 14, of which 9 were waited for; matrix products, arithmetic and copies ran while one was open for 1% of the time, Pallas kernels for 0%

profile of v6, /device:TPU:32, one launch (start us, length us, event | category | flops | bytes accessed | tf_op | source)
XLA Modules:
  0.0 132.2 jit_solution(18276498008229236661)
XLA Ops:
  0.6 3.7 %all-to-all-start = ((f32[4,2,8,32,128]{4,3,2,1,0:T(8,128)}), f32[4,2,8,32,128]{4,3,2,1,0:T(8,128)S(1)}, u32[]{:S(2)}, u32[]{:S(2)}) async-start(f32[4,2,8,32,128]{4,3,2,1,0:T(8,128)} %bitcast.25), calls=%async_computation | async-start | bytes 2097152 | tf_op jit(solution)/shard_map/all_to_all | solution.py:256
  4.3 5.6 %collective-permute-start = (f32[8,32,128]{2,1,0:T(8,128)S(1)}, f32[8,32,128]{2,1,0:T(8,128)S(1)}, u32[]{:S(2)}, u32[]{:S(2)}) collective-permute-start(f32[8,32,128]{2,1,0:T(8,128)S(1)} %copy-done.2), channel_id=1, source_target_pairs={{4,8},{6,10},{8,4},{10,6},{12,16},{14,18},{16,12},{18,14},{20,24},... | collective-permute-start | bytes 393224 | tf_op jit(solution)/shard_map/ppermute | solution.py:255
  9.9 5.2 %collective-permute-done = f32[8,32,128]{2,1,0:T(8,128)S(1)} collective-permute-done((f32[8,32,128]{2,1,0:T(8,128)S(1)}, f32[8,32,128]{2,1,0:T(8,128)S(1)}, u32[]{:S(2)}, u32[]{:S(2)}) %collective-permute-start) | collective-permute-done | bytes 131104 | tf_op jit(solution)/shard_map/ppermute | solution.py:255
  15.2 6.4 %all-to-all-done.slabs = f32[4,2,8,32,128]{4,3,2,1,0:T(8,128)S(1)} async-done(((f32[4,2,8,32,128]{4,3,2,1,0:T(8,128)}), f32[4,2,8,32,128]{4,3,2,1,0:T(8,128)S(1)}, u32[]{:S(2)}, u32[]{:S(2)}) %all-to-all-start) | async-done | bytes 1048608 | tf_op jit(solution)/shard_map/all_to_all | solution.py:256
  21.7 3.4 %collective-permute-start.1 = (f32[2,18,32,128]{3,2,1,0:T(8,128)S(1)}, f32[2,18,32,128]{3,2,1,0:T(8,128)S(1)}, u32[]{:S(2)}, u32[]{:S(2)}) collective-permute-start(f32[2,18,32,128]{3,2,1,0:T(8,128)S(1)} %pad_maximum_fusion), channel_id=1, source_target_pairs={{0,8},{8,16},{16,24},{24,32},{32,40},{40,48},{48,56},{56,64},{64,7... | collective-permute-start | bytes 1769480 | tf_op jit(solution)/shard_map/ppermute | solution.py:260
  25.2 4.6 %collective-permute-start.2 = (f32[2,18,32,128]{3,2,1,0:T(8,128)S(1)}, f32[2,18,32,128]{3,2,1,0:T(8,128)S(1)}, u32[]{:S(2)}, u32[]{:S(2)}) collective-permute-start(f32[2,18,32,128]{3,2,1,0:T(8,128)S(1)} %pad_maximum_fusion.1), channel_id=1, source_target_pairs={{8,0},{16,8},{24,16},{32,24},{40,32},{48,40},{56,48},{64,56},{72,6... | collective-permute-start | bytes 1769480 | tf_op jit(solution)/shard_map/ppermute | solution.py:261
  29.8 6.6 %all-gather = f32[32,32,128]{2,1,0:T(8,128)S(1)} all-gather(f32[8,32,128]{2,1,0:T(8,128)S(1)} %copy-done.2), channel_id=2, replica_groups=mesh['z'=8,'x'=4,'u'=2,'c'=2,'b'=2] {'u','c'}, dimensions={0}, use_global_device_ids=true | all-gather | bytes 655360 | tf_op jit(solution)/shard_map/all_gather | solution.py:262
  36.4 7.4 %all-gather.1 = f32[32,32,128]{2,1,0:T(8,128)S(1)} all-gather(f32[8,32,128]{2,1,0:T(8,128)S(1)} %copy-done.4), channel_id=3, replica_groups=mesh['z'=8,'x'=4,'u'=2,'c'=2,'b'=2] {'u','c'}, dimensions={0}, use_global_device_ids=true | all-gather | bytes 655360 | tf_op jit(solution)/shard_map/all_gather | solution.py:263
  43.8 12.6 %shard_map.59 = f32[4,2,32,8,128]{4,3,2,1,0:T(8,128)S(1)} custom-call(s32[1]{0:T(128)} %bitcast.chunk, f32[4,2,8,32,128]{4,3,2,1,0:T(8,128)S(1)} %all-to-all-done.slabs, f32[2,18,32,128]{3,2,1,0:T(8,128)S(1)} %collective-permute-done.1.before, f32[2,18,32,128]{3,2,1,0:T(8,128)S(1)} %collective-permute-done.2.after, f32[4,8,32,128]{3,2,1,0:T(8,128)S(1)} %bitcast.23, ...), custom_call_target="tpu_custom_call" | custom-call | tf_op jit(solution)/shard_map/pallas_call | solution.py:224
  56.4 19.3 %all_to_all.15.ring = f32[8,256,128]{2,1,0:T(8,128)S(1)} all-to-all(f32[8,256,128]{2,1,0:T(8,128)S(1)} %bitcast.21), channel_id=1, replica_groups=mesh['z'=8,'x'=4,'u'=2,'c'=2,'b'=2] {'u','c','b'}, dimensions={0} | all-to-all | bytes 2097152 | tf_op jit(solution)/shard_map/all_to_all | solution.py:278
  75.7 2.8 %shard_map.60 = (f32[32,2,4,8,128]{4,3,2,1,0:T(8,128)}, f32[8,128]{1,0:T(8,128)S(1)}) custom-call(f32[8,256,128]{2,1,0:T(8,128)S(1)} %all_to_all.15.ring, f32[16,16]{1,0:T(8,128)S(1)} %copy-done.1), custom_call_target="tpu_custom_call" | custom-call | tf_op jit(solution)/shard_map/pallas_call | solution.py:224
  78.4 13.0 %all-to-all-start.2 = ((f32[64,32,128]{2,1,0:T(8,128)}), f32[64,32,128]{2,1,0:T(8,128)S(1)}, u32[]{:S(2)}, u32[]{:S(2)}) async-start(f32[64,32,128]{2,1,0:T(8,128)} %bitcast.12), calls=%async_computation.2 | async-start | bytes 2097152 | tf_op jit(solution)/shard_map/all_to_all | solution.py:280
  91.5 5.3 %all-gather.2 = f32[32,128]{1,0:T(8,128)S(1)} all-gather(f32[8,128]{1,0:T(8,128)S(1)} %get-tuple-element.8), channel_id=4, replica_groups=mesh['z'=8,'x'=4,'u'=2,'c'=2,'b'=2] {'u','c'}, dimensions={0}, use_global_device_ids=true | all-gather | bytes 20480 | tf_op jit(solution)/shard_map/all_gather | solution.py:281
  96.8 2.8 %collective-permute-start.5 = (f32[8,128]{1,0:T(8,128)S(1)}, f32[8,128]{1,0:T(8,128)S(1)}, u32[]{:S(2)}, u32[]{:S(2)}) collective-permute-start(f32[8,128]{1,0:T(8,128)S(1)} %bitcast_reduce_fusion), channel_id=1, source_target_pairs={{0,24},{8,16},{16,8},{24,0},{1,25},{9,17},{17,9},{25,1},{2,26},{10... | collective-permute-start | bytes 12296 | tf_op jit(solution)/shard_map/ppermute | solution.py:238
  101.6 3.1 %collective-permute-done.4 = f32[8,128]{1,0:T(8,128)S(1)} collective-permute-done((f32[8,128]{1,0:T(8,128)S(1)}, f32[8,128]{1,0:T(8,128)S(1)}, u32[]{:S(2)}, u32[]{:S(2)}) %collective-permute-start.4) | collective-permute-done | bytes 4128 | tf_op jit(solution)/shard_map/ppermute | solution.py:238
  104.7 1.5 %collective-permute-start.8 = (f32[8,128]{1,0:T(8,128)S(1)}, f32[8,128]{1,0:T(8,128)S(1)}, u32[]{:S(2)}, u32[]{:S(2)}) collective-permute-start(f32[8,128]{1,0:T(8,128)S(1)} %add_add_fusion.1), channel_id=1, source_target_pairs={{0,96},{32,64},{64,32},{96,0},{128,224},{160,192},{192,160},{224,1... | collective-permute-start | bytes 12296 | tf_op jit(solution)/shard_map/ppermute | solution.py:238
  106.2 1.3 collective-permute-start.7
  107.5 1.0 collective-permute-start.6
  108.5 5.6 %collective-permute-done.8 = f32[8,128]{1,0:T(8,128)S(1)} collective-permute-done((f32[8,128]{1,0:T(8,128)S(1)}, f32[8,128]{1,0:T(8,128)S(1)}, u32[]{:S(2)}, u32[]{:S(2)}) %collective-permute-start.8) | collective-permute-done | bytes 4128 | tf_op jit(solution)/shard_map/ppermute | solution.py:238
  114.2 7.9 %collective-permute-start.11 = (f32[8,128]{1,0:T(8,128)S(1)}, f32[8,128]{1,0:T(8,128)S(1)}, u32[]{:S(2)}, u32[]{:S(2)}) collective-permute-start(f32[8,128]{1,0:T(8,128)S(1)} %add_add_fusion), channel_id=1, source_target_pairs={{0,129},{1,128},{32,161},{33,160},{64,193},{65,192},{96,225},{97,2... | collective-permute-start | bytes 12296 | tf_op jit(solution)/shard_map/ppermute | solution.py:238
  123.2 1.0 collective-permute-done.11
  124.2 3.0 %collective-permute-done.10 = f32[8,128]{1,0:T(8,128)S(1)} collective-permute-done((f32[8,128]{1,0:T(8,128)S(1)}, f32[8,128]{1,0:T(8,128)S(1)}, u32[]{:S(2)}, u32[]{:S(2)}) %collective-permute-start.10) | collective-permute-done | bytes 4128 | tf_op jit(solution)/shard_map/ppermute | solution.py:238
  127.2 2.9 %collective-permute-done.9 = f32[8,128]{1,0:T(8,128)S(1)} collective-permute-done((f32[8,128]{1,0:T(8,128)S(1)}, f32[8,128]{1,0:T(8,128)S(1)}, u32[]{:S(2)}, u32[]{:S(2)}) %collective-permute-start.9) | collective-permute-done | bytes 4128 | tf_op jit(solution)/shard_map/ppermute | solution.py:238
  130.8 1.3 shard_map.61
  (31 shorter events, 4.2 us)
Async XLA Ops:
  0.6 3.7 %copy-start.2 = (f32[8,32,128]{2,1,0:T(8,128)S(1)}, f32[8,32,128]{2,1,0:T(8,128)}, u32[]{:S(2)}) copy-start(f32[8,32,128]{2,1,0:T(8,128)} %param.5) | copy-start | bytes 393220
  0.6 20.9 %all-to-all-start = ((f32[4,2,8,32,128]{4,3,2,1,0:T(8,128)}), f32[4,2,8,32,128]{4,3,2,1,0:T(8,128)S(1)}, u32[]{:S(2)}, u32[]{:S(2)}) async-start(f32[4,2,8,32,128]{4,3,2,1,0:T(8,128)} %bitcast.25), calls=%async_computation | async-start | bytes 2097152 | tf_op jit(solution)/shard_map/all_to_all | solution.py:256
  4.3 10.9 %collective-permute-start = (f32[8,32,128]{2,1,0:T(8,128)S(1)}, f32[8,32,128]{2,1,0:T(8,128)S(1)}, u32[]{:S(2)}, u32[]{:S(2)}) collective-permute-start(f32[8,32,128]{2,1,0:T(8,128)S(1)} %copy-done.2), channel_id=1, source_target_pairs={{4,8},{6,10},{8,4},{10,6},{12,16},{14,18},{16,12},{18,14},{20,24},... | collective-permute-start | bytes 393224 | tf_op jit(solution)/shard_map/ppermute | solution.py:255
  15.2 6.4 %copy-start.3 = (f32[8,32,128]{2,1,0:T(8,128)}, f32[8,32,128]{2,1,0:T(8,128)S(1)}, u32[]{:S(2)}) copy-start(f32[8,32,128]{2,1,0:T(8,128)S(1)} %collective-permute-done) | copy-start | bytes 393220
  21.7 22.1 %collective-permute-start.1 = (f32[2,18,32,128]{3,2,1,0:T(8,128)S(1)}, f32[2,18,32,128]{3,2,1,0:T(8,128)S(1)}, u32[]{:S(2)}, u32[]{:S(2)}) collective-permute-start(f32[2,18,32,128]{3,2,1,0:T(8,128)S(1)} %pad_maximum_fusion), channel_id=1, source_target_pairs={{0,8},{8,16},{16,24},{24,32},{32,40},{40,48},{48,56},{56,64},{64,7... | collective-permute-start | bytes 1769480 | tf_op jit(solution)/shard_map/ppermute | solution.py:260
  25.2 18.6 %collective-permute-start.2 = (f32[2,18,32,128]{3,2,1,0:T(8,128)S(1)}, f32[2,18,32,128]{3,2,1,0:T(8,128)S(1)}, u32[]{:S(2)}, u32[]{:S(2)}) collective-permute-start(f32[2,18,32,128]{3,2,1,0:T(8,128)S(1)} %pad_maximum_fusion.1), channel_id=1, source_target_pairs={{8,0},{16,8},{24,16},{32,24},{40,32},{48,40},{56,48},{64,56},{72,6... | collective-permute-start | bytes 1769480 | tf_op jit(solution)/shard_map/ppermute | solution.py:261
  29.8 6.7 %copy-start.4 = (f32[8,32,128]{2,1,0:T(8,128)S(1)}, f32[8,32,128]{2,1,0:T(8,128)}, u32[]{:S(2)}) copy-start(f32[8,32,128]{2,1,0:T(8,128)} %copy-done.3) | copy-start | bytes 393220
  36.4 7.4 %copy-start = (bf16[256,256]{1,0:T(8,128)(2,1)S(1)}, bf16[256,256]{1,0:T(8,128)(2,1)}, u32[]{:S(2)}) copy-start(bf16[256,256]{1,0:T(8,128)(2,1)} %constant.19.clone.bands) | copy-start | bytes 393220
  56.4 19.3 %copy-start.1 = (f32[16,16]{1,0:T(8,128)S(1)}, f32[16,16]{1,0:T(8,128)}, u32[]{:S(2)}) copy-start(f32[16,16]{1,0:T(8,128)} %coefficients.1) | copy-start | bytes 3076
  78.4 52.4 %all-to-all-start.2 = ((f32[64,32,128]{2,1,0:T(8,128)}), f32[64,32,128]{2,1,0:T(8,128)S(1)}, u32[]{:S(2)}, u32[]{:S(2)}) async-start(f32[64,32,128]{2,1,0:T(8,128)} %bitcast.12), calls=%async_computation.2 | async-start | bytes 2097152 | tf_op jit(solution)/shard_map/all_to_all | solution.py:280
  96.8 4.9 %collective-permute-start.5 = (f32[8,128]{1,0:T(8,128)S(1)}, f32[8,128]{1,0:T(8,128)S(1)}, u32[]{:S(2)}, u32[]{:S(2)}) collective-permute-start(f32[8,128]{1,0:T(8,128)S(1)} %bitcast_reduce_fusion), channel_id=1, source_target_pairs={{0,24},{8,16},{16,8},{24,0},{1,25},{9,17},{17,9},{25,1},{2,26},{10... | collective-permute-start | bytes 12296 | tf_op jit(solution)/shard_map/ppermute | solution.py:238
  99.5 5.2 %collective-permute-start.4 = (f32[8,128]{1,0:T(8,128)S(1)}, f32[8,128]{1,0:T(8,128)S(1)}, u32[]{:S(2)}, u32[]{:S(2)}) collective-permute-start(f32[8,128]{1,0:T(8,128)S(1)} %bitcast_reduce_fusion), channel_id=1, source_target_pairs={{0,16},{8,24},{16,0},{24,8},{1,17},{9,25},{17,1},{25,9},{2,18},{10... | collective-permute-start | bytes 12296 | tf_op jit(solution)/shard_map/ppermute | solution.py:238
  100.2 4.5 %collective-permute-start.3 = (f32[8,128]{1,0:T(8,128)S(1)}, f32[8,128]{1,0:T(8,128)S(1)}, u32[]{:S(2)}, u32[]{:S(2)}) collective-permute-start(f32[8,128]{1,0:T(8,128)S(1)} %bitcast_reduce_fusion), channel_id=1, source_target_pairs={{0,8},{8,0},{16,24},{24,16},{1,9},{9,1},{17,25},{25,17},{2,10},{10... | collective-permute-start | bytes 12296 | tf_op jit(solution)/shard_map/ppermute | solution.py:238
  104.7 9.4 %collective-permute-start.8 = (f32[8,128]{1,0:T(8,128)S(1)}, f32[8,128]{1,0:T(8,128)S(1)}, u32[]{:S(2)}, u32[]{:S(2)}) collective-permute-start(f32[8,128]{1,0:T(8,128)S(1)} %add_add_fusion.1), channel_id=1, source_target_pairs={{0,96},{32,64},{64,32},{96,0},{128,224},{160,192},{192,160},{224,1... | collective-permute-start | bytes 12296 | tf_op jit(solution)/shard_map/ppermute | solution.py:238
  106.2 8.0 %collective-permute-start.7 = (f32[8,128]{1,0:T(8,128)S(1)}, f32[8,128]{1,0:T(8,128)S(1)}, u32[]{:S(2)}, u32[]{:S(2)}) collective-permute-start(f32[8,128]{1,0:T(8,128)S(1)} %add_add_fusion.1), channel_id=1, source_target_pairs={{0,64},{32,96},{64,0},{96,32},{128,192},{160,224},{192,128},{224,1... | collective-permute-start | bytes 12296 | tf_op jit(solution)/shard_map/ppermute | solution.py:238
  107.5 6.7 %collective-permute-start.6 = (f32[8,128]{1,0:T(8,128)S(1)}, f32[8,128]{1,0:T(8,128)S(1)}, u32[]{:S(2)}, u32[]{:S(2)}) collective-permute-start(f32[8,128]{1,0:T(8,128)S(1)} %add_add_fusion.1), channel_id=1, source_target_pairs={{0,32},{32,0},{64,96},{96,64},{128,160},{160,128},{192,224},{224,1... | collective-permute-start | bytes 12296 | tf_op jit(solution)/shard_map/ppermute | solution.py:238
  114.2 10.0 %collective-permute-start.11 = (f32[8,128]{1,0:T(8,128)S(1)}, f32[8,128]{1,0:T(8,128)S(1)}, u32[]{:S(2)}, u32[]{:S(2)}) collective-permute-start(f32[8,128]{1,0:T(8,128)S(1)} %add_add_fusion), channel_id=1, source_target_pairs={{0,129},{1,128},{32,161},{33,160},{64,193},{65,192},{96,225},{97,2... | collective-permute-start | bytes 12296 | tf_op jit(solution)/shard_map/ppermute | solution.py:238
  122.1 5.1 %collective-permute-start.10 = (f32[8,128]{1,0:T(8,128)S(1)}, f32[8,128]{1,0:T(8,128)S(1)}, u32[]{:S(2)}, u32[]{:S(2)}) collective-permute-start(f32[8,128]{1,0:T(8,128)S(1)} %add_add_fusion), channel_id=1, source_target_pairs={{0,1},{1,0},{32,33},{33,32},{64,65},{65,64},{96,97},{97,96},{128,1... | collective-permute-start | bytes 12296 | tf_op jit(solution)/shard_map/ppermute | solution.py:238
  122.6 7.5 %collective-permute-start.9 = (f32[8,128]{1,0:T(8,128)S(1)}, f32[8,128]{1,0:T(8,128)S(1)}, u32[]{:S(2)}, u32[]{:S(2)}) collective-permute-start(f32[8,128]{1,0:T(8,128)S(1)} %add_add_fusion), channel_id=1, source_target_pairs={{0,128},{1,129},{32,160},{33,161},{64,192},{65,193},{96,224},{97,2... | collective-permute-start | bytes 12296 | tf_op jit(solution)/shard_map/ppermute | solution.py:238

commit v7 on v6

--- a/solution.py
+++ b/solution.py
@@ -68,35 +68,36 @@
         if r < EXT:
             target[planes, EXT + 8 + r] = jnp.where(row == 3, 0.0, pltpu.roll(value, 7, 1))
 
-    def tiles(pieces):
-        return jnp.swapaxes(jnp.concatenate([piece.reshape(4, 8, NZ) for piece in pieces], axis=0), 0, 1)
-
-    def enter(plane, pieces):
-        value = tiles(pieces)
+    def tiles(sources):
+        rows = [jnp.concatenate([source[(*at, pl.ds(r, 4, stride=8), slice(None))] for source, at in sources], axis=0) for r in range(8)]
+        return jnp.stack(rows)
+
+    def enter(plane, sources):
+        value = tiles(sources)
         field[plane, EXT : EXT + 8] = value
         field[plane, 0:EXT] = jnp.where(row[:EXT] == 0, 0.0, pltpu.roll(value[8 - EXT :], 1, 1))
         field[plane, EXT + 8 :] = jnp.where(row[:EXT] == 3, 0.0, pltpu.roll(value[:EXT], 7, 1))
 
     def enter_ends(p, _):
-        enter(p, [before[o, p] for o in range(OWN)])
-        enter(far + CHUNK + p, [after[o, p] for o in range(OWN)])
+        enter(p, [(before, (o, p)) for o in range(OWN)])
+        enter(far + CHUNK + p, [(after, (o, p)) for o in range(OWN)])
         return 0
 
     lax.fori_loop(0, far, enter_ends, 0)
 
     def enter_slabs(p, _):
         for s in range(4):
-            enter(far + 8 * s + p, [slabs[s, o, p] for o in range(OWN)])
+            enter(far + 8 * s + p, [(slabs, (s, o, p)) for o in range(OWN)])
         return 0
 
     lax.fori_loop(0, 8, enter_slabs, 0)
 
     def enter_local(p, _):
         for j, (source, s) in enumerate(
-            [(beyond, 0), (beyond, 1), (own, 0), (own, 1), (own, 2), (own, 3), (beyond, 2), (beyond, 3)]
+            [(beyond, 2), (beyond, 3), (own, 0), (own, 1), (own, 2), (own, 3), (beyond, 0), (beyond, 1)]
         ):
-            value = (source[s, p] + (-1.5 * STENCIL[0] - CENTER)) * (1.0 / HALF)
-            local[8 * j + p] = tiles([value, value])
+            value = tiles([(source, (s, p)), (source, (s, p))])
+            local[8 * j + p] = (value + (-1.5 * STENCIL[0] - CENTER)) * (1.0 / HALF)
         return 0
 
     lax.fori_loop(0, 8, enter_local, 0)
@@ -251,7 +252,7 @@
     up = [(i, i + 1) for i in range(count - 1)]
     down = [(j, i) for i, j in up]
 
-    shift = [(d, d + 2 if d % 4 >= 2 else d - 2) for d in range(4 * count)]
+    shift = [(d, d + 4 if d % 4 >= 2 else d - 4) for d in range(4 * count)]
     beyond = lax.ppermute(potential, dom, [(i, j) for i, j in shift if 0 <= j < 4 * count])
     slabs = lax.all_to_all(orbitals.reshape(4, OWN, 8, NY, NZ), ("u", "c"), 0, 0, tiled=True)
     slabs, beyond = lax.optimization_barrier((slabs, beyond))
@@ -277,10 +278,12 @@
     )
     ring = lax.all_to_all(message.reshape(8, 256, 128), ("u", "c", "b"), 0, 0, tiled=True)
     rotated, gram = call(rotate_kernel, [(32, 2, 4, 8, 128), (8, 128)])(ring, coefficients)
+    gram = four(gram, "z", 4, "b", 1)
+    gram, rotated = lax.optimization_barrier((gram, rotated))
     received = lax.all_to_all(rotated.reshape(64, 32, 128), ("z", "x", "b"), 0, 0, tiled=True)
     gram = lax.all_gather(gram, ("u", "c")).sum(axis=0)
-    for axes in (("x", 1, "x", 2), ("z", 1, "z", 2), ("z", 4, "b", 1)):
-        gram = four(gram, *axes)
+    gram = four(gram, "x", 1, "x", 2)
+    gram = four(gram, "z", 1, "z", 2)
     gram = gram / (NX * NY * NZ)
     intersection = jnp.concatenate([gram[:, :NORB], gram[:, NORB : 2 * NORB]], axis=0)
     (lines,) = call(lines_kernel, [(8, NY, NX)])(received.reshape(32, 2, 32, 128))

time: 133 us -> 132 us (level)
  starting transfers between devices: 47.2 us -> 43 us
  waiting for transfers between devices: 28.1 us -> 31.3 us
    all_to_all x1, waiting for transfers between devices: 0.01 us -> 6.19 us  [local(): lax.all_to_all(rotated.reshape(64, 32, 128), ('z', 'x', 'b'), 0, 0, tiled...]
    all_to_all x1, starting transfers between devices: 13 us -> 9.43 us  [local(): lax.all_to_all(rotated.reshape(64, 32, 128), ('z', 'x', 'b'), 0, 0, tiled...]
    ppermute x1, waiting for transfers between devices: 5.24 us -> 3.53 us  [local(): lax.ppermute(potential, dom, [(i, j) for i, j in shift if 0 <= j < 4 * co...]
    ppermute x9, waiting for transfers between devices: 16.4 us -> 14.9 us  [swap(): return lax.ppermute(x, axes, [(i, int(j)) for i, j in enumerate(flat)])]
    ppermute x1, starting transfers between devices: 5.62 us -> 4.21 us  [local(): lax.ppermute(potential, dom, [(i, j) for i, j in shift if 0 <= j < 4 * co...]
where the time goes in v7:
time: 132 us; the launch traced here: 131 us
  starting transfers between devices  43 us (33%)
  blocking collectives  38.5 us (29%)
  waiting for transfers between devices  31.3 us (24%)
  Pallas kernels  16.8 us (13%)
    all_to_all x1, blocking collectives, local(): lax.all_to_all(message.reshape(8, 256, 128), ('u', 'c', 'b'), 0, 0, tiled...  19.3 us
    ppermute x9, starting transfers between devices, swap(): return lax.ppermute(x, axes, [(i, int(j)) for i, j in enumerate(flat)])  17.8 us
    pallas_call x3, Pallas kernels, call(): pl.pallas_call(kernel, out_shape=[jax.ShapeDtypeStruct(s, F32) for s in o...  16.8 us
    ppermute x9, waiting for transfers between devices, swap(): return lax.ppermute(x, axes, [(i, int(j)) for i, j in enumerate(flat)])  14.9 us
    all_to_all x1, starting transfers between devices, local(): lax.all_to_all(rotated.reshape(64, 32, 128), ('z', 'x', 'b'), 0, 0, tiled...  9.43 us
    all_gather x1, blocking collectives, local(): beyond = lax.all_gather(beyond, ('u', 'c'))  7.41 us
    all_to_all x1, waiting for transfers between devices, local(): lax.all_to_all(orbitals.reshape(4, OWN, 8, NY, NZ), ('u', 'c'), 0, 0, til...  6.67 us
    all_gather x1, blocking collectives, local(): own = lax.all_gather(potential, ('u', 'c'))  6.64 us
  transfers between devices with their start and end apart: 14, of which 9 were waited for; matrix products, arithmetic and copies ran while one was open for 1% of the time, Pallas kernels for 0%

profile of v7, /device:TPU:32, one launch (start us, length us, event | category | flops | bytes accessed | tf_op | source)
XLA Modules:
  0.0 131.4 jit_solution(10004769885213732241)
XLA Ops:
  0.6 3.7 %all-to-all-start = ((f32[4,2,8,32,128]{4,3,2,1,0:T(8,128)}), f32[4,2,8,32,128]{4,3,2,1,0:T(8,128)S(1)}, u32[]{:S(2)}, u32[]{:S(2)}) async-start(f32[4,2,8,32,128]{4,3,2,1,0:T(8,128)} %bitcast.25), calls=%async_computation | async-start | bytes 2097152 | tf_op jit(solution)/shard_map/all_to_all | solution.py:257
  4.3 4.2 %collective-permute-start = (f32[8,32,128]{2,1,0:T(8,128)S(1)}, f32[8,32,128]{2,1,0:T(8,128)S(1)}, u32[]{:S(2)}, u32[]{:S(2)}) collective-permute-start(f32[8,32,128]{2,1,0:T(8,128)S(1)} %copy-done.2), channel_id=1, source_target_pairs={{4,12},{6,14},{8,0},{10,2},{12,20},{14,22},{16,8},{18,10},{20,28},... | collective-permute-start | bytes 393224 | tf_op jit(solution)/shard_map/ppermute | solution.py:256
  8.5 3.5 %collective-permute-done = f32[8,32,128]{2,1,0:T(8,128)S(1)} collective-permute-done((f32[8,32,128]{2,1,0:T(8,128)S(1)}, f32[8,32,128]{2,1,0:T(8,128)S(1)}, u32[]{:S(2)}, u32[]{:S(2)}) %collective-permute-start) | collective-permute-done | bytes 131104 | tf_op jit(solution)/shard_map/ppermute | solution.py:256
  12.1 6.7 %all-to-all-done.slabs = f32[4,2,8,32,128]{4,3,2,1,0:T(8,128)S(1)} async-done(((f32[4,2,8,32,128]{4,3,2,1,0:T(8,128)}), f32[4,2,8,32,128]{4,3,2,1,0:T(8,128)S(1)}, u32[]{:S(2)}, u32[]{:S(2)}) %all-to-all-start) | async-done | bytes 1048608 | tf_op jit(solution)/shard_map/all_to_all | solution.py:257
  18.9 3.4 %collective-permute-start.1 = (f32[2,18,32,128]{3,2,1,0:T(8,128)S(1)}, f32[2,18,32,128]{3,2,1,0:T(8,128)S(1)}, u32[]{:S(2)}, u32[]{:S(2)}) collective-permute-start(f32[2,18,32,128]{3,2,1,0:T(8,128)S(1)} %pad_maximum_fusion), channel_id=1, source_target_pairs={{0,8},{8,16},{16,24},{24,32},{32,40},{40,48},{48,56},{56,64},{64,7... | collective-permute-start | bytes 1769480 | tf_op jit(solution)/shard_map/ppermute | solution.py:261
  22.4 4.6 %collective-permute-start.2 = (f32[2,18,32,128]{3,2,1,0:T(8,128)S(1)}, f32[2,18,32,128]{3,2,1,0:T(8,128)S(1)}, u32[]{:S(2)}, u32[]{:S(2)}) collective-permute-start(f32[2,18,32,128]{3,2,1,0:T(8,128)S(1)} %pad_maximum_fusion.1), channel_id=1, source_target_pairs={{8,0},{16,8},{24,16},{32,24},{40,32},{48,40},{56,48},{64,56},{72,6... | collective-permute-start | bytes 1769480 | tf_op jit(solution)/shard_map/ppermute | solution.py:262
  27.0 6.6 %all-gather = f32[32,32,128]{2,1,0:T(8,128)S(1)} all-gather(f32[8,32,128]{2,1,0:T(8,128)S(1)} %copy-done.2), channel_id=2, replica_groups=mesh['z'=8,'x'=4,'u'=2,'c'=2,'b'=2] {'u','c'}, dimensions={0}, use_global_device_ids=true | all-gather | bytes 655360 | tf_op jit(solution)/shard_map/all_gather | solution.py:263
  33.6 7.4 %all-gather.1 = f32[32,32,128]{2,1,0:T(8,128)S(1)} all-gather(f32[8,32,128]{2,1,0:T(8,128)S(1)} %copy-done.4), channel_id=3, replica_groups=mesh['z'=8,'x'=4,'u'=2,'c'=2,'b'=2] {'u','c'}, dimensions={0}, use_global_device_ids=true | all-gather | bytes 655360 | tf_op jit(solution)/shard_map/all_gather | solution.py:264
  41.0 12.7 %shard_map.59 = f32[4,2,32,8,128]{4,3,2,1,0:T(8,128)S(1)} custom-call(s32[1]{0:T(128)} %bitcast.chunk, f32[4,2,8,32,128]{4,3,2,1,0:T(8,128)S(1)} %all-to-all-done.slabs, f32[2,18,32,128]{3,2,1,0:T(8,128)S(1)} %collective-permute-done.1.before, f32[2,18,32,128]{3,2,1,0:T(8,128)S(1)} %collective-permute-done.2.after, f32[4,8,32,128]{3,2,1,0:T(8,128)S(1)} %bitcast.23, ...), custom_call_target="tpu_custom_call" | custom-call | tf_op jit(solution)/shard_map/pallas_call | solution.py:225
  53.8 19.3 %all_to_all.15.ring = f32[8,256,128]{2,1,0:T(8,128)S(1)} all-to-all(f32[8,256,128]{2,1,0:T(8,128)S(1)} %bitcast.21), channel_id=1, replica_groups=mesh['z'=8,'x'=4,'u'=2,'c'=2,'b'=2] {'u','c','b'}, dimensions={0} | all-to-all | bytes 2097152 | tf_op jit(solution)/shard_map/all_to_all | solution.py:279
  73.0 2.8 %shard_map.60 = (f32[32,2,4,8,128]{4,3,2,1,0:T(8,128)}, f32[8,128]{1,0:T(8,128)S(1)}) custom-call(f32[8,256,128]{2,1,0:T(8,128)S(1)} %all_to_all.15.ring, f32[16,16]{1,0:T(8,128)S(1)} %copy-done.1), custom_call_target="tpu_custom_call" | custom-call | tf_op jit(solution)/shard_map/pallas_call | solution.py:225
  75.8 7.9 %collective-permute-start.5 = (f32[8,128]{1,0:T(8,128)S(1)}, f32[8,128]{1,0:T(8,128)S(1)}, u32[]{:S(2)}, u32[]{:S(2)}) collective-permute-start(f32[8,128]{1,0:T(8,128)S(1)} %get-tuple-element.10), channel_id=1, source_target_pairs={{0,129},{1,128},{32,161},{33,160},{64,193},{65,192},{96,225},{97,2... | collective-permute-start | bytes 12296 | tf_op jit(solution)/shard_map/ppermute | solution.py:239
  83.7 1.4 %collective-permute-start.4 = (f32[8,128]{1,0:T(8,128)S(1)}, f32[8,128]{1,0:T(8,128)S(1)}, u32[]{:S(2)}, u32[]{:S(2)}) collective-permute-start(f32[8,128]{1,0:T(8,128)S(1)} %get-tuple-element.10), channel_id=1, source_target_pairs={{0,1},{1,0},{32,33},{33,32},{64,65},{65,64},{96,97},{97,96},{128,1... | collective-permute-start | bytes 12296 | tf_op jit(solution)/shard_map/ppermute | solution.py:239
  85.7 3.1 %collective-permute-done.4 = f32[8,128]{1,0:T(8,128)S(1)} collective-permute-done((f32[8,128]{1,0:T(8,128)S(1)}, f32[8,128]{1,0:T(8,128)S(1)}, u32[]{:S(2)}, u32[]{:S(2)}) %collective-permute-start.4) | collective-permute-done | bytes 4128 | tf_op jit(solution)/shard_map/ppermute | solution.py:239
  88.8 3.8 %collective-permute-done.3 = f32[8,128]{1,0:T(8,128)S(1)} collective-permute-done((f32[8,128]{1,0:T(8,128)S(1)}, f32[8,128]{1,0:T(8,128)S(1)}, u32[]{:S(2)}, u32[]{:S(2)}) %collective-permute-start.3) | collective-permute-done | bytes 4128 | tf_op jit(solution)/shard_map/ppermute | solution.py:239
  92.6 9.4 %all-to-all-start.2 = ((f32[64,32,128]{2,1,0:T(8,128)}), f32[64,32,128]{2,1,0:T(8,128)S(1)}, u32[]{:S(2)}, u32[]{:S(2)}) async-start(f32[64,32,128]{2,1,0:T(8,128)} %bitcast.12), calls=%async_computation.2 | async-start | bytes 2097152 | tf_op jit(solution)/shard_map/all_to_all | solution.py:283
  102.0 5.2 %all-gather.2 = f32[32,128]{1,0:T(8,128)S(1)} all-gather(f32[8,128]{1,0:T(8,128)S(1)} %add_add_fusion.1), channel_id=4, replica_groups=mesh['z'=8,'x'=4,'u'=2,'c'=2,'b'=2] {'u','c'}, dimensions={0}, use_global_device_ids=true | all-gather | bytes 20480 | tf_op jit(solution)/shard_map/all_gather | solution.py:284
  107.2 2.7 %collective-permute-start.8 = (f32[8,128]{1,0:T(8,128)S(1)}, f32[8,128]{1,0:T(8,128)S(1)}, u32[]{:S(2)}, u32[]{:S(2)}) collective-permute-start(f32[8,128]{1,0:T(8,128)S(1)} %bitcast_reduce_fusion), channel_id=1, source_target_pairs={{0,24},{8,16},{16,8},{24,0},{1,25},{9,17},{17,9},{25,1},{2,26},{10... | collective-permute-start | bytes 12296 | tf_op jit(solution)/shard_map/ppermute | solution.py:239
  112.1 3.0 %collective-permute-done.7 = f32[8,128]{1,0:T(8,128)S(1)} collective-permute-done((f32[8,128]{1,0:T(8,128)S(1)}, f32[8,128]{1,0:T(8,128)S(1)}, u32[]{:S(2)}, u32[]{:S(2)}) %collective-permute-start.7) | collective-permute-done | bytes 4128 | tf_op jit(solution)/shard_map/ppermute | solution.py:239
  115.1 1.5 %collective-permute-start.11 = (f32[8,128]{1,0:T(8,128)S(1)}, f32[8,128]{1,0:T(8,128)S(1)}, u32[]{:S(2)}, u32[]{:S(2)}) collective-permute-start(f32[8,128]{1,0:T(8,128)S(1)} %add_add_fusion), channel_id=1, source_target_pairs={{0,96},{32,64},{64,32},{96,0},{128,224},{160,192},{192,160},{224,1... | collective-permute-start | bytes 12296 | tf_op jit(solution)/shard_map/ppermute | solution.py:239
  116.6 1.7 %collective-permute-start.10 = (f32[8,128]{1,0:T(8,128)S(1)}, f32[8,128]{1,0:T(8,128)S(1)}, u32[]{:S(2)}, u32[]{:S(2)}) collective-permute-start(f32[8,128]{1,0:T(8,128)S(1)} %add_add_fusion), channel_id=1, source_target_pairs={{0,64},{32,96},{64,0},{96,32},{128,192},{160,224},{192,128},{224,1... | collective-permute-start | bytes 12296 | tf_op jit(solution)/shard_map/ppermute | solution.py:239
  119.5 3.7 %collective-permute-done.11 = f32[8,128]{1,0:T(8,128)S(1)} collective-permute-done((f32[8,128]{1,0:T(8,128)S(1)}, f32[8,128]{1,0:T(8,128)S(1)}, u32[]{:S(2)}, u32[]{:S(2)}) %collective-permute-start.11) | collective-permute-done | bytes 4128 | tf_op jit(solution)/shard_map/ppermute | solution.py:239
  123.9 6.2 %all-to-all-done.2 = f32[64,32,128]{2,1,0:T(8,128)S(1)} async-done(((f32[64,32,128]{2,1,0:T(8,128)}), f32[64,32,128]{2,1,0:T(8,128)S(1)}, u32[]{:S(2)}, u32[]{:S(2)}) %all-to-all-start.2) | async-done | bytes 1048608 | tf_op jit(solution)/shard_map/all_to_all | solution.py:283
  130.1 1.3 shard_map.61
  (31 shorter events, 5.0 us)
Async XLA Ops:
  0.6 3.7 %copy-start.2 = (f32[8,32,128]{2,1,0:T(8,128)S(1)}, f32[8,32,128]{2,1,0:T(8,128)}, u32[]{:S(2)}) copy-start(f32[8,32,128]{2,1,0:T(8,128)} %param.5) | copy-start | bytes 393220
  0.6 18.1 %all-to-all-start = ((f32[4,2,8,32,128]{4,3,2,1,0:T(8,128)}), f32[4,2,8,32,128]{4,3,2,1,0:T(8,128)S(1)}, u32[]{:S(2)}, u32[]{:S(2)}) async-start(f32[4,2,8,32,128]{4,3,2,1,0:T(8,128)} %bitcast.25), calls=%async_computation | async-start | bytes 2097152 | tf_op jit(solution)/shard_map/all_to_all | solution.py:257
  4.3 7.7 %collective-permute-start = (f32[8,32,128]{2,1,0:T(8,128)S(1)}, f32[8,32,128]{2,1,0:T(8,128)S(1)}, u32[]{:S(2)}, u32[]{:S(2)}) collective-permute-start(f32[8,32,128]{2,1,0:T(8,128)S(1)} %copy-done.2), channel_id=1, source_target_pairs={{4,12},{6,14},{8,0},{10,2},{12,20},{14,22},{16,8},{18,10},{20,28},... | collective-permute-start | bytes 393224 | tf_op jit(solution)/shard_map/ppermute | solution.py:256
  12.1 6.7 %copy-start.3 = (f32[8,32,128]{2,1,0:T(8,128)}, f32[8,32,128]{2,1,0:T(8,128)S(1)}, u32[]{:S(2)}) copy-start(f32[8,32,128]{2,1,0:T(8,128)S(1)} %collective-permute-done) | copy-start | bytes 393220
  18.9 22.1 %collective-permute-start.1 = (f32[2,18,32,128]{3,2,1,0:T(8,128)S(1)}, f32[2,18,32,128]{3,2,1,0:T(8,128)S(1)}, u32[]{:S(2)}, u32[]{:S(2)}) collective-permute-start(f32[2,18,32,128]{3,2,1,0:T(8,128)S(1)} %pad_maximum_fusion), channel_id=1, source_target_pairs={{0,8},{8,16},{16,24},{24,32},{32,40},{40,48},{48,56},{56,64},{64,7... | collective-permute-start | bytes 1769480 | tf_op jit(solution)/shard_map/ppermute | solution.py:261
  22.4 18.6 %collective-permute-start.2 = (f32[2,18,32,128]{3,2,1,0:T(8,128)S(1)}, f32[2,18,32,128]{3,2,1,0:T(8,128)S(1)}, u32[]{:S(2)}, u32[]{:S(2)}) collective-permute-start(f32[2,18,32,128]{3,2,1,0:T(8,128)S(1)} %pad_maximum_fusion.1), channel_id=1, source_target_pairs={{8,0},{16,8},{24,16},{32,24},{40,32},{48,40},{56,48},{64,56},{72,6... | collective-permute-start | bytes 1769480 | tf_op jit(solution)/shard_map/ppermute | solution.py:262
  26.9 6.7 %copy-start.4 = (f32[8,32,128]{2,1,0:T(8,128)S(1)}, f32[8,32,128]{2,1,0:T(8,128)}, u32[]{:S(2)}) copy-start(f32[8,32,128]{2,1,0:T(8,128)} %copy-done.3) | copy-start | bytes 393220
  33.6 7.4 %copy-start = (bf16[256,256]{1,0:T(8,128)(2,1)S(1)}, bf16[256,256]{1,0:T(8,128)(2,1)}, u32[]{:S(2)}) copy-start(bf16[256,256]{1,0:T(8,128)(2,1)} %constant.19.clone.bands) | copy-start | bytes 393220
  53.8 19.3 %copy-start.1 = (f32[16,16]{1,0:T(8,128)S(1)}, f32[16,16]{1,0:T(8,128)}, u32[]{:S(2)}) copy-start(f32[16,16]{1,0:T(8,128)} %coefficients.1) | copy-start | bytes 3076
  75.8 9.9 %collective-permute-start.5 = (f32[8,128]{1,0:T(8,128)S(1)}, f32[8,128]{1,0:T(8,128)S(1)}, u32[]{:S(2)}, u32[]{:S(2)}) collective-permute-start(f32[8,128]{1,0:T(8,128)S(1)} %get-tuple-element.10), channel_id=1, source_target_pairs={{0,129},{1,128},{32,161},{33,160},{64,193},{65,192},{96,225},{97,2... | collective-permute-start | bytes 12296 | tf_op jit(solution)/shard_map/ppermute | solution.py:239
  83.7 5.1 %collective-permute-start.4 = (f32[8,128]{1,0:T(8,128)S(1)}, f32[8,128]{1,0:T(8,128)S(1)}, u32[]{:S(2)}, u32[]{:S(2)}) collective-permute-start(f32[8,128]{1,0:T(8,128)S(1)} %get-tuple-element.10), channel_id=1, source_target_pairs={{0,1},{1,0},{32,33},{33,32},{64,65},{65,64},{96,97},{97,96},{128,1... | collective-permute-start | bytes 12296 | tf_op jit(solution)/shard_map/ppermute | solution.py:239
  85.1 7.5 %collective-permute-start.3 = (f32[8,128]{1,0:T(8,128)S(1)}, f32[8,128]{1,0:T(8,128)S(1)}, u32[]{:S(2)}, u32[]{:S(2)}) collective-permute-start(f32[8,128]{1,0:T(8,128)S(1)} %get-tuple-element.10), channel_id=1, source_target_pairs={{0,128},{1,129},{32,160},{33,161},{64,192},{65,193},{96,224},{97,2... | collective-permute-start | bytes 12296 | tf_op jit(solution)/shard_map/ppermute | solution.py:239
  92.6 37.5 %all-to-all-start.2 = ((f32[64,32,128]{2,1,0:T(8,128)}), f32[64,32,128]{2,1,0:T(8,128)S(1)}, u32[]{:S(2)}, u32[]{:S(2)}) async-start(f32[64,32,128]{2,1,0:T(8,128)} %bitcast.12), calls=%async_computation.2 | async-start | bytes 2097152 | tf_op jit(solution)/shard_map/all_to_all | solution.py:283
  107.2 4.9 %collective-permute-start.8 = (f32[8,128]{1,0:T(8,128)S(1)}, f32[8,128]{1,0:T(8,128)S(1)}, u32[]{:S(2)}, u32[]{:S(2)}) collective-permute-start(f32[8,128]{1,0:T(8,128)S(1)} %bitcast_reduce_fusion), channel_id=1, source_target_pairs={{0,24},{8,16},{16,8},{24,0},{1,25},{9,17},{17,9},{25,1},{2,26},{10... | collective-permute-start | bytes 12296 | tf_op jit(solution)/shard_map/ppermute | solution.py:239
  109.9 5.1 %collective-permute-start.7 = (f32[8,128]{1,0:T(8,128)S(1)}, f32[8,128]{1,0:T(8,128)S(1)}, u32[]{:S(2)}, u32[]{:S(2)}) collective-permute-start(f32[8,128]{1,0:T(8,128)S(1)} %bitcast_reduce_fusion), channel_id=1, source_target_pairs={{0,16},{8,24},{16,0},{24,8},{1,17},{9,25},{17,1},{25,9},{2,18},{10... | collective-permute-start | bytes 12296 | tf_op jit(solution)/shard_map/ppermute | solution.py:239
  110.8 4.3 %collective-permute-start.6 = (f32[8,128]{1,0:T(8,128)S(1)}, f32[8,128]{1,0:T(8,128)S(1)}, u32[]{:S(2)}, u32[]{:S(2)}) collective-permute-start(f32[8,128]{1,0:T(8,128)S(1)} %bitcast_reduce_fusion), channel_id=1, source_target_pairs={{0,8},{8,0},{16,24},{24,16},{1,9},{9,1},{17,25},{25,17},{2,10},{10... | collective-permute-start | bytes 12296 | tf_op jit(solution)/shard_map/ppermute | solution.py:239
  115.1 8.1 %collective-permute-start.11 = (f32[8,128]{1,0:T(8,128)S(1)}, f32[8,128]{1,0:T(8,128)S(1)}, u32[]{:S(2)}, u32[]{:S(2)}) collective-permute-start(f32[8,128]{1,0:T(8,128)S(1)} %add_add_fusion), channel_id=1, source_target_pairs={{0,96},{32,64},{64,32},{96,0},{128,224},{160,192},{192,160},{224,1... | collective-permute-start | bytes 12296 | tf_op jit(solution)/shard_map/ppermute | solution.py:239
  116.6 6.6 %collective-permute-start.10 = (f32[8,128]{1,0:T(8,128)S(1)}, f32[8,128]{1,0:T(8,128)S(1)}, u32[]{:S(2)}, u32[]{:S(2)}) collective-permute-start(f32[8,128]{1,0:T(8,128)S(1)} %add_add_fusion), channel_id=1, source_target_pairs={{0,64},{32,96},{64,0},{96,32},{128,192},{160,224},{192,128},{224,1... | collective-permute-start | bytes 12296 | tf_op jit(solution)/shard_map/ppermute | solution.py:239
  118.3 4.9 %collective-permute-start.9 = (f32[8,128]{1,0:T(8,128)S(1)}, f32[8,128]{1,0:T(8,128)S(1)}, u32[]{:S(2)}, u32[]{:S(2)}) collective-permute-start(f32[8,128]{1,0:T(8,128)S(1)} %add_add_fusion), channel_id=1, source_target_pairs={{0,32},{32,0},{64,96},{96,64},{128,160},{160,128},{192,224},{224,1... | collective-permute-start | bytes 12296 | tf_op jit(solution)/shard_map/ppermute | solution.py:239

commit v8 on v7

--- a/solution.py
+++ b/solution.py
@@ -55,7 +55,7 @@
 
 
 def filter_kernel(
-    chunk, slabs, before, after, own, beyond, bands, out, field, other, local, zy, result, turned
+    chunk, slabs, before, after, own, beyond, bands, out, field, other, local, z, result, turned
 ):
     far, near = 3 * WIDTH, 2 * WIDTH + 2
     row = lax.broadcasted_iota(jnp.int32, (8, 8, NZ), 1) % 4
@@ -102,31 +102,31 @@
 
     lax.fori_loop(0, 8, enter_local, 0)
 
-    def around(window, total):
-        for k in range(1, 7):
-            beside = window[WIDTH + k : WIDTH + 8 + k] + window[WIDTH - k : WIDTH + 8 - k]
-            term = (-0.5 / HALF * STENCIL[k]) * beside
-            total = term if total is None else total + term
-        return total
-
-    def along_zy(slot, source, index):
-        high, low = split(source[pl.ds(index, 8), EXT : EXT + 8].reshape(8 * 64, NZ))
+    def along_z(source, index):
+        high, low = split(source[pl.ds(index, 4), EXT : EXT + 8].reshape(4 * 64, NZ))
         both = jnp.dot(jnp.concatenate([high, low], axis=1), bands[...], preferred_element_type=F32)
-        z = (both[:, :NZ] + both[:, NZ:]).reshape(8, 8, 8, NZ)
-        for x in range(8):
-            zy[slot, x] = around(source[index + x], z[x])
+        return (both[:, :NZ] + both[:, NZ:]).reshape(4, 8, 8, NZ)
 
     def step(source, shift, first, blocks, put):
         def body(i, _):
             start = first + 8 * i
-            for r in range(8):
-                window = source[pl.ds(start + shift - WIDTH, 8 + 2 * WIDTH), EXT + r]
-                total = local[pl.ds(start + 16, 8), r] * window[WIDTH : WIDTH + 8]
-                put(start, r, around(window, total + zy[i, :, r]))
-            along_zy(i + 1, source, first + 8 * jnp.minimum(i + 1, blocks - 1) + shift)
+            later = first + 8 * jnp.minimum(i + 1, blocks - 1) + shift
+            for half in range(2):
+                ahead = along_z(source, later + 4 * half)
+                for r in range(4 * half, 4 * half + 4):
+                    window = source[pl.ds(start + shift - WIDTH, 8 + 2 * WIDTH), EXT + r]
+                    total = local[pl.ds(start + 16, 8), r] * window[WIDTH : WIDTH + 8] + z[i, :, r]
+                    for k in range(1, 7):
+                        beside = window[WIDTH + k : WIDTH + 8 + k] + window[WIDTH - k : WIDTH + 8 - k]
+                        planes = pl.ds(start + shift, 8)
+                        beside = beside + (source[planes, EXT + r + k] + source[planes, EXT + r - k])
+                        total = total + (-0.5 / HALF * STENCIL[k]) * beside
+                    put(start, r, total)
+                z[i + 1, 4 * half : 4 * half + 4] = ahead
             return 0
 
-        along_zy(0, source, first + shift)
+        for half in range(2):
+            z[0, 4 * half : 4 * half + 4] = along_z(source, first + shift + 4 * half)
         lax.fori_loop(0, blocks, body, 0)
 
     def put_first(start, r, total):
@@ -278,12 +278,12 @@
     )
     ring = lax.all_to_all(message.reshape(8, 256, 128), ("u", "c", "b"), 0, 0, tiled=True)
     rotated, gram = call(rotate_kernel, [(32, 2, 4, 8, 128), (8, 128)])(ring, coefficients)
-    gram = four(gram, "z", 4, "b", 1)
+    gram = lax.all_gather(gram, ("u", "c")).sum(axis=0)
     gram, rotated = lax.optimization_barrier((gram, rotated))
     received = lax.all_to_all(rotated.reshape(64, 32, 128), ("z", "x", "b"), 0, 0, tiled=True)
-    gram = lax.all_gather(gram, ("u", "c")).sum(axis=0)
     gram = four(gram, "x", 1, "x", 2)
-    gram = four(gram, "z", 1, "z", 2)
+    for axis, bit in (("z", 1), ("z", 2), ("b", 1), ("z", 4)):
+        gram = gram + lax.ppermute(gram, axis, [(i, i ^ bit) for i in range(lax.axis_size(axis))])
     gram = gram / (NX * NY * NZ)
     intersection = jnp.concatenate([gram[:, :NORB], gram[:, NORB : 2 * NORB]], axis=0)
     (lines,) = call(lines_kernel, [(8, NY, NX)])(received.reshape(32, 2, 32, 128))

time: 132 us -> 137 us (1.038)
  starting transfers between devices: 43 us -> 46 us
  waiting for transfers between devices: 31.3 us -> 33.3 us
    ppermute x0 -> x4, waiting for transfers between devices: none -> 19.4 us  [local(): lax.ppermute(gram, axis, [(i, i ^ bit) for i in range(lax.axis_size(axis))])]
    ppermute x9 -> x3, starting transfers between devices: 17.8 us -> 4.18 us  [swap(): return lax.ppermute(x, axes, [(i, int(j)) for i, j in enumerate(flat)])]
    ppermute x0 -> x4, starting transfers between devices: none -> 12.9 us  [local(): lax.ppermute(gram, axis, [(i, i ^ bit) for i in range(lax.axis_size(axis))])]
    ppermute x9 -> x3, waiting for transfers between devices: 14.9 us -> 3.72 us  [swap(): return lax.ppermute(x, axes, [(i, int(j)) for i, j in enumerate(flat)])]
    all_to_all x1, waiting for transfers between devices: 6.19 us -> 0.01 us  [local(): lax.all_to_all(rotated.reshape(64, 32, 128), ('z', 'x', 'b'), 0, 0, tiled...]
    all_to_all x1, starting transfers between devices: 9.43 us -> 13.1 us  [local(): lax.all_to_all(rotated.reshape(64, 32, 128), ('z', 'x', 'b'), 0, 0, tiled...]
  transfers between devices with their start and end apart: 14 -> 12, of which waited for: 9 -> 8; matrix products, arithmetic and copies ran while one was open for 1% -> 1% of each run, Pallas kernels for 0% -> 0%
where the time goes in v8:
time: 137 us; the launch traced here: 135 us
  starting transfers between devices  46 us (34%)
  blocking collectives  38.5 us (28%)
  waiting for transfers between devices  33.3 us (24%)
  Pallas kernels  15.8 us (12%)
    ppermute x4, waiting for transfers between devices, local(): lax.ppermute(gram, axis, [(i, i ^ bit) for i in range(lax.axis_size(axis))])  19.4 us
    all_to_all x1, blocking collectives, local(): lax.all_to_all(message.reshape(8, 256, 128), ('u', 'c', 'b'), 0, 0, tiled...  19.3 us
    pallas_call x3, Pallas kernels, call(): pl.pallas_call(kernel, out_shape=[jax.ShapeDtypeStruct(s, F32) for s in o...  15.8 us
    all_to_all x1, starting transfers between devices, local(): lax.all_to_all(rotated.reshape(64, 32, 128), ('z', 'x', 'b'), 0, 0, tiled...  13.1 us
    ppermute x4, starting transfers between devices, local(): lax.ppermute(gram, axis, [(i, i ^ bit) for i in range(lax.axis_size(axis))])  12.9 us
    all_gather x1, blocking collectives, local(): beyond = lax.all_gather(beyond, ('u', 'c'))  7.41 us
    all_to_all x1, waiting for transfers between devices, local(): lax.all_to_all(orbitals.reshape(4, OWN, 8, NY, NZ), ('u', 'c'), 0, 0, til...  6.67 us
    all_gather x1, blocking collectives, local(): own = lax.all_gather(potential, ('u', 'c'))  6.64 us
  transfers between devices with their start and end apart: 12, of which 8 were waited for; matrix products, arithmetic and copies ran while one was open for 1% of the time, Pallas kernels for 0%

profile of v8, /device:TPU:32, one launch (start us, length us, event | category | flops | bytes accessed | tf_op | source)
XLA Modules:
  0.0 135.3 jit_solution(7008514415700493171)
XLA Ops:
  0.6 3.7 %all-to-all-start = ((f32[4,2,8,32,128]{4,3,2,1,0:T(8,128)}), f32[4,2,8,32,128]{4,3,2,1,0:T(8,128)S(1)}, u32[]{:S(2)}, u32[]{:S(2)}) async-start(f32[4,2,8,32,128]{4,3,2,1,0:T(8,128)} %bitcast.25), calls=%async_computation | async-start | bytes 2097152 | tf_op jit(solution)/shard_map/all_to_all | solution.py:257
  4.3 4.2 %collective-permute-start = (f32[8,32,128]{2,1,0:T(8,128)S(1)}, f32[8,32,128]{2,1,0:T(8,128)S(1)}, u32[]{:S(2)}, u32[]{:S(2)}) collective-permute-start(f32[8,32,128]{2,1,0:T(8,128)S(1)} %copy-done.2), channel_id=1, source_target_pairs={{4,12},{6,14},{8,0},{10,2},{12,20},{14,22},{16,8},{18,10},{20,28},... | collective-permute-start | bytes 393224 | tf_op jit(solution)/shard_map/ppermute | solution.py:256
  8.5 3.5 %collective-permute-done = f32[8,32,128]{2,1,0:T(8,128)S(1)} collective-permute-done((f32[8,32,128]{2,1,0:T(8,128)S(1)}, f32[8,32,128]{2,1,0:T(8,128)S(1)}, u32[]{:S(2)}, u32[]{:S(2)}) %collective-permute-start) | collective-permute-done | bytes 131104 | tf_op jit(solution)/shard_map/ppermute | solution.py:256
  12.1 6.7 %all-to-all-done.slabs = f32[4,2,8,32,128]{4,3,2,1,0:T(8,128)S(1)} async-done(((f32[4,2,8,32,128]{4,3,2,1,0:T(8,128)}), f32[4,2,8,32,128]{4,3,2,1,0:T(8,128)S(1)}, u32[]{:S(2)}, u32[]{:S(2)}) %all-to-all-start) | async-done | bytes 1048608 | tf_op jit(solution)/shard_map/all_to_all | solution.py:257
  18.9 3.4 %collective-permute-start.1 = (f32[2,18,32,128]{3,2,1,0:T(8,128)S(1)}, f32[2,18,32,128]{3,2,1,0:T(8,128)S(1)}, u32[]{:S(2)}, u32[]{:S(2)}) collective-permute-start(f32[2,18,32,128]{3,2,1,0:T(8,128)S(1)} %pad_maximum_fusion), channel_id=1, source_target_pairs={{0,8},{8,16},{16,24},{24,32},{32,40},{40,48},{48,56},{56,64},{64,7... | collective-permute-start | bytes 1769480 | tf_op jit(solution)/shard_map/ppermute | solution.py:261
  22.4 4.6 %collective-permute-start.2 = (f32[2,18,32,128]{3,2,1,0:T(8,128)S(1)}, f32[2,18,32,128]{3,2,1,0:T(8,128)S(1)}, u32[]{:S(2)}, u32[]{:S(2)}) collective-permute-start(f32[2,18,32,128]{3,2,1,0:T(8,128)S(1)} %pad_maximum_fusion.1), channel_id=1, source_target_pairs={{8,0},{16,8},{24,16},{32,24},{40,32},{48,40},{56,48},{64,56},{72,6... | collective-permute-start | bytes 1769480 | tf_op jit(solution)/shard_map/ppermute | solution.py:262
  27.0 6.6 %all-gather = f32[32,32,128]{2,1,0:T(8,128)S(1)} all-gather(f32[8,32,128]{2,1,0:T(8,128)S(1)} %copy-done.2), channel_id=2, replica_groups=mesh['z'=8,'x'=4,'u'=2,'c'=2,'b'=2] {'u','c'}, dimensions={0}, use_global_device_ids=true | all-gather | bytes 655360 | tf_op jit(solution)/shard_map/all_gather | solution.py:263
  33.6 7.4 %all-gather.1 = f32[32,32,128]{2,1,0:T(8,128)S(1)} all-gather(f32[8,32,128]{2,1,0:T(8,128)S(1)} %copy-done.4), channel_id=3, replica_groups=mesh['z'=8,'x'=4,'u'=2,'c'=2,'b'=2] {'u','c'}, dimensions={0}, use_global_device_ids=true | all-gather | bytes 655360 | tf_op jit(solution)/shard_map/all_gather | solution.py:264
  41.0 11.7 %shard_map.59 = f32[4,2,32,8,128]{4,3,2,1,0:T(8,128)S(1)} custom-call(s32[1]{0:T(128)} %bitcast.chunk, f32[4,2,8,32,128]{4,3,2,1,0:T(8,128)S(1)} %all-to-all-done.slabs, f32[2,18,32,128]{3,2,1,0:T(8,128)S(1)} %collective-permute-done.1.before, f32[2,18,32,128]{3,2,1,0:T(8,128)S(1)} %collective-permute-done.2.after, f32[4,8,32,128]{3,2,1,0:T(8,128)S(1)} %bitcast.23, ...), custom_call_target="tpu_custom_call" | custom-call | tf_op jit(solution)/shard_map/pallas_call | solution.py:225
  52.8 19.3 %all_to_all.15.ring = f32[8,256,128]{2,1,0:T(8,128)S(1)} all-to-all(f32[8,256,128]{2,1,0:T(8,128)S(1)} %bitcast.21), channel_id=1, replica_groups=mesh['z'=8,'x'=4,'u'=2,'c'=2,'b'=2] {'u','c','b'}, dimensions={0} | all-to-all | bytes 2097152 | tf_op jit(solution)/shard_map/all_to_all | solution.py:279
  72.0 2.8 %shard_map.60 = (f32[32,2,4,8,128]{4,3,2,1,0:T(8,128)}, f32[8,128]{1,0:T(8,128)S(1)}) custom-call(f32[8,256,128]{2,1,0:T(8,128)S(1)} %all_to_all.15.ring, f32[16,16]{1,0:T(8,128)S(1)} %copy-done.1), custom_call_target="tpu_custom_call" | custom-call | tf_op jit(solution)/shard_map/pallas_call | solution.py:225
  74.8 5.2 %all-gather.2 = f32[32,128]{1,0:T(8,128)S(1)} all-gather(f32[8,128]{1,0:T(8,128)S(1)} %get-tuple-element.10), channel_id=4, replica_groups=mesh['z'=8,'x'=4,'u'=2,'c'=2,'b'=2] {'u','c'}, dimensions={0}, use_global_device_ids=true | all-gather | bytes 20480 | tf_op jit(solution)/shard_map/all_gather | solution.py:281
  80.0 13.1 %all-to-all-start.2 = ((f32[64,32,128]{2,1,0:T(8,128)}), f32[64,32,128]{2,1,0:T(8,128)S(1)}, u32[]{:S(2)}, u32[]{:S(2)}) async-start(f32[64,32,128]{2,1,0:T(8,128)} %bitcast.12), calls=%async_computation.2 | async-start | bytes 2097152 | tf_op jit(solution)/shard_map/all_to_all | solution.py:283
  93.1 2.8 %collective-permute-start.5 = (f32[8,128]{1,0:T(8,128)S(1)}, f32[8,128]{1,0:T(8,128)S(1)}, u32[]{:S(2)}, u32[]{:S(2)}) collective-permute-start(f32[8,128]{1,0:T(8,128)S(1)} %bitcast_reduce_fusion), channel_id=1, source_target_pairs={{0,24},{8,16},{16,8},{24,0},{1,25},{9,17},{17,9},{25,1},{2,26},{10... | collective-permute-start | bytes 12296 | tf_op jit(solution)/shard_map/ppermute | solution.py:239
  95.8 0.9 collective-permute-start.4
  98.0 3.0 %collective-permute-done.4 = f32[8,128]{1,0:T(8,128)S(1)} collective-permute-done((f32[8,128]{1,0:T(8,128)S(1)}, f32[8,128]{1,0:T(8,128)S(1)}, u32[]{:S(2)}, u32[]{:S(2)}) %collective-permute-start.4) | collective-permute-done | bytes 4128 | tf_op jit(solution)/shard_map/ppermute | solution.py:239
  101.7 13.9 %collective-permute-done.6 = f32[8,128]{1,0:T(8,128)S(1)} collective-permute-done((f32[8,128]{1,0:T(8,128)S(1)}, f32[8,128]{1,0:T(8,128)S(1)}, u32[]{:S(2)}, u32[]{:S(2)}) %collective-permute-start.6) | collective-permute-done | bytes 4128 | tf_op jit(solution)/shard_map/ppermute | solution.py:286
  115.6 3.3 %collective-permute-start.7 = (f32[8,128]{1,0:T(8,128)S(1)}, f32[8,128]{1,0:T(8,128)S(1)}, u32[]{:S(2)}, u32[]{:S(2)}) collective-permute-start(f32[8,128]{1,0:T(8,128)S(1)} %add.28), channel_id=1, source_target_pairs={{0,64},{32,96},{64,0},{96,32},{128,192},{160,224},{192,128},{224,1... | collective-permute-start | bytes 12296 | tf_op jit(solution)/shard_map/ppermute | solution.py:286
  119.0 1.7 %collective-permute-done.7 = f32[8,128]{1,0:T(8,128)S(1)} collective-permute-done((f32[8,128]{1,0:T(8,128)S(1)}, f32[8,128]{1,0:T(8,128)S(1)}, u32[]{:S(2)}, u32[]{:S(2)}) %collective-permute-start.7) | collective-permute-done | bytes 4128 | tf_op jit(solution)/shard_map/ppermute | solution.py:286
  120.7 3.0 %collective-permute-start.8 = (f32[8,128]{1,0:T(8,128)S(1)}, f32[8,128]{1,0:T(8,128)S(1)}, u32[]{:S(2)}, u32[]{:S(2)}) collective-permute-start(f32[8,128]{1,0:T(8,128)S(1)} %add.29), channel_id=1, source_target_pairs={{0,1},{1,0},{2,3},{3,2},{4,5},{5,4},{6,7},{7,6},{8,9},{9,8},{10,11... | collective-permute-start | bytes 12296 | tf_op jit(solution)/shard_map/ppermute | solution.py:286
  123.7 2.1 %collective-permute-done.8 = f32[8,128]{1,0:T(8,128)S(1)} collective-permute-done((f32[8,128]{1,0:T(8,128)S(1)}, f32[8,128]{1,0:T(8,128)S(1)}, u32[]{:S(2)}, u32[]{:S(2)}) %collective-permute-start.8) | collective-permute-done | bytes 4128 | tf_op jit(solution)/shard_map/ppermute | solution.py:286
  125.8 5.9 %collective-permute-start.9 = (f32[8,128]{1,0:T(8,128)S(1)}, f32[8,128]{1,0:T(8,128)S(1)}, u32[]{:S(2)}, u32[]{:S(2)}) collective-permute-start(f32[8,128]{1,0:T(8,128)S(1)} %add.30), channel_id=1, source_target_pairs={{0,128},{32,160},{64,192},{96,224},{128,0},{160,32},{192,64},{224,... | collective-permute-start | bytes 12296 | tf_op jit(solution)/shard_map/ppermute | solution.py:286
  131.7 1.6 %collective-permute-done.9 = f32[8,128]{1,0:T(8,128)S(1)} collective-permute-done((f32[8,128]{1,0:T(8,128)S(1)}, f32[8,128]{1,0:T(8,128)S(1)}, u32[]{:S(2)}, u32[]{:S(2)}) %collective-permute-start.9) | collective-permute-done | bytes 4128 | tf_op jit(solution)/shard_map/ppermute | solution.py:286
  134.0 1.3 shard_map.61
  (29 shorter events, 3.0 us)
Async XLA Ops:
  0.6 3.7 %copy-start.2 = (f32[8,32,128]{2,1,0:T(8,128)S(1)}, f32[8,32,128]{2,1,0:T(8,128)}, u32[]{:S(2)}) copy-start(f32[8,32,128]{2,1,0:T(8,128)} %param.5) | copy-start | bytes 393220
  0.6 18.1 %all-to-all-start = ((f32[4,2,8,32,128]{4,3,2,1,0:T(8,128)}), f32[4,2,8,32,128]{4,3,2,1,0:T(8,128)S(1)}, u32[]{:S(2)}, u32[]{:S(2)}) async-start(f32[4,2,8,32,128]{4,3,2,1,0:T(8,128)} %bitcast.25), calls=%async_computation | async-start | bytes 2097152 | tf_op jit(solution)/shard_map/all_to_all | solution.py:257
  4.3 7.7 %collective-permute-start = (f32[8,32,128]{2,1,0:T(8,128)S(1)}, f32[8,32,128]{2,1,0:T(8,128)S(1)}, u32[]{:S(2)}, u32[]{:S(2)}) collective-permute-start(f32[8,32,128]{2,1,0:T(8,128)S(1)} %copy-done.2), channel_id=1, source_target_pairs={{4,12},{6,14},{8,0},{10,2},{12,20},{14,22},{16,8},{18,10},{20,28},... | collective-permute-start | bytes 393224 | tf_op jit(solution)/shard_map/ppermute | solution.py:256
  12.1 6.7 %copy-start.3 = (f32[8,32,128]{2,1,0:T(8,128)}, f32[8,32,128]{2,1,0:T(8,128)S(1)}, u32[]{:S(2)}) copy-start(f32[8,32,128]{2,1,0:T(8,128)S(1)} %collective-permute-done) | copy-start | bytes 393220
  18.9 22.1 %collective-permute-start.1 = (f32[2,18,32,128]{3,2,1,0:T(8,128)S(1)}, f32[2,18,32,128]{3,2,1,0:T(8,128)S(1)}, u32[]{:S(2)}, u32[]{:S(2)}) collective-permute-start(f32[2,18,32,128]{3,2,1,0:T(8,128)S(1)} %pad_maximum_fusion), channel_id=1, source_target_pairs={{0,8},{8,16},{16,24},{24,32},{32,40},{40,48},{48,56},{56,64},{64,7... | collective-permute-start | bytes 1769480 | tf_op jit(solution)/shard_map/ppermute | solution.py:261
  22.4 18.6 %collective-permute-start.2 = (f32[2,18,32,128]{3,2,1,0:T(8,128)S(1)}, f32[2,18,32,128]{3,2,1,0:T(8,128)S(1)}, u32[]{:S(2)}, u32[]{:S(2)}) collective-permute-start(f32[2,18,32,128]{3,2,1,0:T(8,128)S(1)} %pad_maximum_fusion.1), channel_id=1, source_target_pairs={{8,0},{16,8},{24,16},{32,24},{40,32},{48,40},{56,48},{64,56},{72,6... | collective-permute-start | bytes 1769480 | tf_op jit(solution)/shard_map/ppermute | solution.py:262
  26.9 6.7 %copy-start.4 = (f32[8,32,128]{2,1,0:T(8,128)S(1)}, f32[8,32,128]{2,1,0:T(8,128)}, u32[]{:S(2)}) copy-start(f32[8,32,128]{2,1,0:T(8,128)} %copy-done.3) | copy-start | bytes 393220
  33.6 7.4 %copy-start = (bf16[256,256]{1,0:T(8,128)(2,1)S(1)}, bf16[256,256]{1,0:T(8,128)(2,1)}, u32[]{:S(2)}) copy-start(bf16[256,256]{1,0:T(8,128)(2,1)} %constant.19.clone.bands) | copy-start | bytes 393220
  52.8 19.3 %copy-start.1 = (f32[16,16]{1,0:T(8,128)S(1)}, f32[16,16]{1,0:T(8,128)}, u32[]{:S(2)}) copy-start(f32[16,16]{1,0:T(8,128)} %coefficients.1) | copy-start | bytes 3076
  80.0 54.0 %all-to-all-start.2 = ((f32[64,32,128]{2,1,0:T(8,128)}), f32[64,32,128]{2,1,0:T(8,128)S(1)}, u32[]{:S(2)}, u32[]{:S(2)}) async-start(f32[64,32,128]{2,1,0:T(8,128)} %bitcast.12), calls=%async_computation.2 | async-start | bytes 2097152 | tf_op jit(solution)/shard_map/all_to_all | solution.py:283
  93.1 4.9 %collective-permute-start.5 = (f32[8,128]{1,0:T(8,128)S(1)}, f32[8,128]{1,0:T(8,128)S(1)}, u32[]{:S(2)}, u32[]{:S(2)}) collective-permute-start(f32[8,128]{1,0:T(8,128)S(1)} %bitcast_reduce_fusion), channel_id=1, source_target_pairs={{0,24},{8,16},{16,8},{24,0},{1,25},{9,17},{17,9},{25,1},{2,26},{10... | collective-permute-start | bytes 12296 | tf_op jit(solution)/shard_map/ppermute | solution.py:239
  95.8 5.1 %collective-permute-start.4 = (f32[8,128]{1,0:T(8,128)S(1)}, f32[8,128]{1,0:T(8,128)S(1)}, u32[]{:S(2)}, u32[]{:S(2)}) collective-permute-start(f32[8,128]{1,0:T(8,128)S(1)} %bitcast_reduce_fusion), channel_id=1, source_target_pairs={{0,16},{8,24},{16,0},{24,8},{1,17},{9,25},{17,1},{25,9},{2,18},{10... | collective-permute-start | bytes 12296 | tf_op jit(solution)/shard_map/ppermute | solution.py:239
  96.7 4.3 %collective-permute-start.3 = (f32[8,128]{1,0:T(8,128)S(1)}, f32[8,128]{1,0:T(8,128)S(1)}, u32[]{:S(2)}, u32[]{:S(2)}) collective-permute-start(f32[8,128]{1,0:T(8,128)S(1)} %bitcast_reduce_fusion), channel_id=1, source_target_pairs={{0,8},{8,0},{16,24},{24,16},{1,9},{9,1},{17,25},{25,17},{2,10},{10... | collective-permute-start | bytes 12296 | tf_op jit(solution)/shard_map/ppermute | solution.py:239
  101.0 14.7 %collective-permute-start.6 = (f32[8,128]{1,0:T(8,128)S(1)}, f32[8,128]{1,0:T(8,128)S(1)}, u32[]{:S(2)}, u32[]{:S(2)}) collective-permute-start(f32[8,128]{1,0:T(8,128)S(1)} %add_add_fusion), channel_id=1, source_target_pairs={{0,32},{32,0},{64,96},{96,64},{128,160},{160,128},{192,224},{224,1... | collective-permute-start | bytes 12296 | tf_op jit(solution)/shard_map/ppermute | solution.py:286
  115.6 5.0 %collective-permute-start.7 = (f32[8,128]{1,0:T(8,128)S(1)}, f32[8,128]{1,0:T(8,128)S(1)}, u32[]{:S(2)}, u32[]{:S(2)}) collective-permute-start(f32[8,128]{1,0:T(8,128)S(1)} %add.28), channel_id=1, source_target_pairs={{0,64},{32,96},{64,0},{96,32},{128,192},{160,224},{192,128},{224,1... | collective-permute-start | bytes 12296 | tf_op jit(solution)/shard_map/ppermute | solution.py:286
  120.7 5.1 %collective-permute-start.8 = (f32[8,128]{1,0:T(8,128)S(1)}, f32[8,128]{1,0:T(8,128)S(1)}, u32[]{:S(2)}, u32[]{:S(2)}) collective-permute-start(f32[8,128]{1,0:T(8,128)S(1)} %add.29), channel_id=1, source_target_pairs={{0,1},{1,0},{2,3},{3,2},{4,5},{5,4},{6,7},{7,6},{8,9},{9,8},{10,11... | collective-permute-start | bytes 12296 | tf_op jit(solution)/shard_map/ppermute | solution.py:286
  125.8 7.5 %collective-permute-start.9 = (f32[8,128]{1,0:T(8,128)S(1)}, f32[8,128]{1,0:T(8,128)S(1)}, u32[]{:S(2)}, u32[]{:S(2)}) collective-permute-start(f32[8,128]{1,0:T(8,128)S(1)} %add.30), channel_id=1, source_target_pairs={{0,128},{32,160},{64,192},{96,224},{128,0},{160,32},{192,64},{224,... | collective-permute-start | bytes 12296 | tf_op jit(solution)/shard_map/ppermute | solution.py:286

commit v9 on v8

--- a/solution.py
+++ b/solution.py
@@ -172,7 +172,7 @@
     lax.fori_loop(0, NZ // 4, pick, 0)
 
 
-def rotate_kernel(ring, coefficients, out, gram):
+def rotate_kernel(ring, coefficients, out):
     exact = functools.partial(
         lax.dot_general, precision=lax.Precision.HIGHEST, preferred_element_type=F32
     )
@@ -201,17 +201,29 @@
         all_orbitals = jnp.concatenate(halves, axis=1)
         turned = dot3(all_orbitals, weights, ((1,), (0,)))
         for b in range(2):
-            out[:, b, t] = turned[:, b * 128 : (b + 1) * 128].reshape(32, 8, 128)
+            rows = turned[:, b * 128 : (b + 1) * 128].reshape(32, 8, 128)
+            out[:, b, 2 * t] = rows[:, 0:4]
+            out[:, b, 2 * t + 1] = rows[:, 4:8]
         sums = sums + dot3(all_orbitals, all_orbitals, ((0,), (0,)))
     diagonal = jnp.where((row // 8 % 4 == column // 8 % 4) & (row % 4 == column % 4), sums, 0.0)
     both = exact(before, exact(diagonal, before, (((1,), (0,)), ((), ()))), (((0,), (0,)), ((), ())))
-    gram[...] = jnp.concatenate([both[0:8], both[8:16], jnp.zeros((8, 96), F32)], axis=1)
+    tile = jnp.concatenate([both[4 * q : 4 * q + 4] for q in range(4)] + [jnp.zeros((4, 64), F32)], axis=1)
+    out[:, :, 8] = jnp.broadcast_to(tile, (32, 2, 4, 128))
 
 
 def lines_kernel(received, out):
     low = lax.broadcasted_iota(jnp.int32, (16, 8, 128), 1) < 4
+
+    def lines(s, b):
+        pieces = [
+            jnp.concatenate([received[s * 4 + c, b, 2 * j], received[s * 4 + c, b, 2 * j + 1]], axis=0)
+            for c in range(4)
+            for j in range(4)
+        ]
+        return jnp.concatenate(pieces, axis=0).T.reshape(16, 8, 128)
+
     for s in range(8):
-        first, second = (received[s * 4 : s * 4 + 4, b].reshape(128, 128).T.reshape(16, 8, 128) for b in range(2))
+        first, second = lines(s, 0), lines(s, 1)
         even = jnp.where(low, first, pltpu.roll(second, 4, 1)).reshape(8, 2, 8, 128)
         odd = jnp.where(low, pltpu.roll(first, 4, 1), second).reshape(8, 2, 8, 128)
         for q in range(2):
@@ -277,16 +289,11 @@
         chunk, slabs, before, after, own, beyond, bands
     )
     ring = lax.all_to_all(message.reshape(8, 256, 128), ("u", "c", "b"), 0, 0, tiled=True)
-    rotated, gram = call(rotate_kernel, [(32, 2, 4, 8, 128), (8, 128)])(ring, coefficients)
-    gram = lax.all_gather(gram, ("u", "c")).sum(axis=0)
-    gram, rotated = lax.optimization_barrier((gram, rotated))
-    received = lax.all_to_all(rotated.reshape(64, 32, 128), ("z", "x", "b"), 0, 0, tiled=True)
-    gram = four(gram, "x", 1, "x", 2)
-    for axis, bit in (("z", 1), ("z", 2), ("b", 1), ("z", 4)):
-        gram = gram + lax.ppermute(gram, axis, [(i, i ^ bit) for i in range(lax.axis_size(axis))])
-    gram = gram / (NX * NY * NZ)
-    intersection = jnp.concatenate([gram[:, :NORB], gram[:, NORB : 2 * NORB]], axis=0)
-    (lines,) = call(lines_kernel, [(8, NY, NX)])(received.reshape(32, 2, 32, 128))
+    (rotated,) = call(rotate_kernel, [(32, 2, 9, 4, 128)])(ring, coefficients)
+    received = lax.all_to_all(rotated.reshape(64, 9, 4, 128), ("z", "x", "b"), 0, 0, tiled=True)
+    gram = four(received[:, 8].sum(axis=0), "u", 1, "c", 1) / (NX * NY * NZ)
+    intersection = jnp.concatenate([gram[:, q * NORB : (q + 1) * NORB] for q in range(4)], axis=0)
+    (lines,) = call(lines_kernel, [(8, NY, NX)])(received.reshape(32, 2, 9, 4, 128))
     return intersection, lines
 
 

time: 137 us -> 126 us (0.920)
  blocking collectives: 38.5 us -> 78.6 us
  starting transfers between devices: 46 us -> 18 us
  waiting for transfers between devices: 33.3 us -> 11 us
    all_to_all x0 -> x1, blocking collectives: none -> 45.1 us  [local(): lax.all_to_all(rotated.reshape(64, 9, 4, 128), ('z', 'x', 'b'), 0, 0, til...]
    ppermute x4 -> x0, waiting for transfers between devices: 19.4 us -> none  [local(): lax.ppermute(gram, axis, [(i, i ^ bit) for i in range(lax.axis_size(axis))])]
    all_to_all x1 -> x0, starting transfers between devices: 13.1 us -> none  [local(): lax.all_to_all(rotated.reshape(64, 32, 128), ('z', 'x', 'b'), 0, 0, tiled...]
    ppermute x4 -> x0, starting transfers between devices: 12.9 us -> none  [local(): lax.ppermute(gram, axis, [(i, i ^ bit) for i in range(lax.axis_size(axis))])]
    all_gather x1 -> x0, blocking collectives: 5.17 us -> none  [local(): gram = lax.all_gather(gram, ('u', 'c')).sum(axis=0)]
    ppermute x3, waiting for transfers between devices: 3.72 us -> 0.79 us  [swap(): return lax.ppermute(x, axes, [(i, int(j)) for i, j in enumerate(flat)])]
    ppermute x3, starting transfers between devices: 4.18 us -> 2.21 us  [swap(): return lax.ppermute(x, axes, [(i, int(j)) for i, j in enumerate(flat)])]
  transfers between devices with their start and end apart: 12 -> 7, of which waited for: 8 -> 3; matrix products, arithmetic and copies ran while one was open for 1% -> 0% of each run, Pallas kernels for 0% -> 1%
where the time goes in v9:
time: 126 us; the launch traced here: 125 us
  blocking collectives  78.6 us (62%)
  starting transfers between devices  18 us (14%)
  Pallas kernels  15.7 us (12%)
  waiting for transfers between devices  11 us (9%)
    all_to_all x1, blocking collectives, local(): lax.all_to_all(rotated.reshape(64, 9, 4, 128), ('z', 'x', 'b'), 0, 0, til...  45.1 us
    all_to_all x1, blocking collectives, local(): lax.all_to_all(message.reshape(8, 256, 128), ('u', 'c', 'b'), 0, 0, tiled...  19.3 us
    pallas_call x3, Pallas kernels, call(): pl.pallas_call(kernel, out_shape=[jax.ShapeDtypeStruct(s, F32) for s in o...  15.7 us
    all_gather x1, blocking collectives, local(): beyond = lax.all_gather(beyond, ('u', 'c'))  7.49 us
    all_gather x1, blocking collectives, local(): own = lax.all_gather(potential, ('u', 'c'))  6.72 us
    all_to_all x1, waiting for transfers between devices, local(): lax.all_to_all(orbitals.reshape(4, OWN, 8, NY, NZ), ('u', 'c'), 0, 0, til...  6.57 us
    ppermute x1, starting transfers between devices, local(): lax.ppermute(jnp.concatenate([slabs[0], slabs[1], slabs[2, :, :part]], ax...  4.55 us
    ppermute x1, starting transfers between devices, local(): lax.ppermute(potential, dom, [(i, j) for i, j in shift if 0 <= j < 4 * co...  4.21 us
  transfers between devices with their start and end apart: 7, of which 3 were waited for; matrix products, arithmetic and copies ran while one was open for 0% of the time, Pallas kernels for 1%

profile of v9, /device:TPU:32, one launch (start us, length us, event | category | flops | bytes accessed | tf_op | source)
XLA Modules:
  0.0 125.1 jit_solution(10078199882499141349)
XLA Ops:
  0.6 0.0 copy-start.2
  0.6 3.7 %all-to-all-start = ((f32[4,2,8,32,128]{4,3,2,1,0:T(8,128)}), f32[4,2,8,32,128]{4,3,2,1,0:T(8,128)S(1)}, u32[]{:S(2)}, u32[]{:S(2)}) async-start(f32[4,2,8,32,128]{4,3,2,1,0:T(8,128)} %bitcast.24), calls=%async_computation | async-start | bytes 2097152 | tf_op jit(solution)/shard_map/all_to_all | solution.py:269
  4.3 4.2 %collective-permute-start = (f32[8,32,128]{2,1,0:T(8,128)S(1)}, f32[8,32,128]{2,1,0:T(8,128)}, u32[]{:S(2)}, u32[]{:S(2)}) collective-permute-start(f32[8,32,128]{2,1,0:T(8,128)S(1)} %copy-done.2), channel_id=1, source_target_pairs={{4,12},{6,14},{8,0},{10,2},{12,20},{14,22},{16,8},{18,10},{20,28},... | collective-permute-start | bytes 393224 | tf_op jit(solution)/shard_map/ppermute | solution.py:268
  8.5 3.6 %collective-permute-done = f32[8,32,128]{2,1,0:T(8,128)} collective-permute-done((f32[8,32,128]{2,1,0:T(8,128)S(1)}, f32[8,32,128]{2,1,0:T(8,128)}, u32[]{:S(2)}, u32[]{:S(2)}) %collective-permute-start) | collective-permute-done | bytes 131104 | tf_op jit(solution)/shard_map/ppermute | solution.py:268
  12.2 6.6 %all-to-all-done.slabs = f32[4,2,8,32,128]{4,3,2,1,0:T(8,128)S(1)} async-done(((f32[4,2,8,32,128]{4,3,2,1,0:T(8,128)}), f32[4,2,8,32,128]{4,3,2,1,0:T(8,128)S(1)}, u32[]{:S(2)}, u32[]{:S(2)}) %all-to-all-start) | async-done | bytes 1048608 | tf_op jit(solution)/shard_map/all_to_all | solution.py:269
  18.7 0.1 slice_bitcast_fusion.1
  18.9 3.4 %collective-permute-start.1 = (f32[2,18,32,128]{3,2,1,0:T(8,128)S(1)}, f32[2,18,32,128]{3,2,1,0:T(8,128)S(1)}, u32[]{:S(2)}, u32[]{:S(2)}) collective-permute-start(f32[2,18,32,128]{3,2,1,0:T(8,128)S(1)} %pad_maximum_fusion), channel_id=1, source_target_pairs={{0,8},{8,16},{16,24},{24,32},{32,40},{40,48},{48,56},{56,64},{64,7... | collective-permute-start | bytes 1769480 | tf_op jit(solution)/shard_map/ppermute | solution.py:273
  22.3 0.0 copy-start
  22.4 4.6 %collective-permute-start.2 = (f32[2,18,32,128]{3,2,1,0:T(8,128)S(1)}, f32[2,18,32,128]{3,2,1,0:T(8,128)S(1)}, u32[]{:S(2)}, u32[]{:S(2)}) collective-permute-start(f32[2,18,32,128]{3,2,1,0:T(8,128)S(1)} %pad_maximum_fusion.1), channel_id=1, source_target_pairs={{8,0},{16,8},{24,16},{32,24},{40,32},{48,40},{56,48},{64,56},{72,6... | collective-permute-start | bytes 1769480 | tf_op jit(solution)/shard_map/ppermute | solution.py:274
  26.9 6.7 %all-gather = f32[32,32,128]{2,1,0:T(8,128)S(1)} all-gather(f32[8,32,128]{2,1,0:T(8,128)} %param.5), channel_id=2, replica_groups=mesh['z'=8,'x'=4,'u'=2,'c'=2,'b'=2] {'u','c'}, dimensions={0}, use_global_device_ids=true | all-gather | bytes 655360 | tf_op jit(solution)/shard_map/all_gather | solution.py:275
  33.7 7.5 %all-gather.1 = f32[32,32,128]{2,1,0:T(8,128)S(1)} all-gather(f32[8,32,128]{2,1,0:T(8,128)} %collective-permute-done), channel_id=3, replica_groups=mesh['z'=8,'x'=4,'u'=2,'c'=2,'b'=2] {'u','c'}, dimensions={0}, use_global_device_ids=true | all-gather | bytes 655360 | tf_op jit(solution)/shard_map/all_gather | solution.py:276
  41.2 11.7 %shard_map.59 = f32[4,2,32,8,128]{4,3,2,1,0:T(8,128)S(1)} custom-call(s32[1]{0:T(128)} %bitcast.chunk, f32[4,2,8,32,128]{4,3,2,1,0:T(8,128)S(1)} %all-to-all-done.slabs, f32[2,18,32,128]{3,2,1,0:T(8,128)S(1)} %collective-permute-done.1.before, f32[2,18,32,128]{3,2,1,0:T(8,128)S(1)} %collective-permute-done.2.after, f32[4,8,32,128]{3,2,1,0:T(8,128)S(1)} %bitcast.22, ...), custom_call_target="tpu_custom_call" | custom-call | tf_op jit(solution)/shard_map/pallas_call | solution.py:237
  52.9 0.0 copy-start.1
  52.9 19.3 %all_to_all.15.ring = f32[8,256,128]{2,1,0:T(8,128)S(1)} all-to-all(f32[8,256,128]{2,1,0:T(8,128)S(1)} %bitcast.21), channel_id=1, replica_groups=mesh['z'=8,'x'=4,'u'=2,'c'=2,'b'=2] {'u','c','b'}, dimensions={0} | all-to-all | bytes 2097152 | tf_op jit(solution)/shard_map/all_to_all | solution.py:291
  72.2 2.7 %shard_map.60 = f32[32,2,9,4,128]{4,3,2,1,0:T(4,128)S(1)} custom-call(f32[8,256,128]{2,1,0:T(8,128)S(1)} %all_to_all.15.ring, f32[16,16]{1,0:T(8,128)S(1)} %copy-done.1), custom_call_target="tpu_custom_call" | custom-call | tf_op jit(solution)/shard_map/pallas_call | solution.py:237
  74.9 45.1 %all_to_all.16 = f32[64,9,4,128]{3,2,1,0:T(4,128)S(1)} all-to-all(f32[64,9,4,128]{3,2,1,0:T(4,128)S(1)} %bitcast.20), channel_id=1, replica_groups=mesh['z'=8,'x'=4,'u'=2,'c'=2,'b'=2] {'z','x','b'}, dimensions={0} | all-to-all | bytes 2359296 | tf_op jit(solution)/shard_map/all_to_all | solution.py:293
  120.0 0.1 slice_reduce_fusion
  120.0 0.1 collective-permute-start.5
  120.1 0.6 collective-permute-start.4
  120.8 1.5 %collective-permute-start.3 = (f32[4,128]{1,0:T(4,128)S(1)}, f32[4,128]{1,0:T(4,128)S(1)}, u32[]{:S(2)}, u32[]{:S(2)}) collective-permute-start(f32[4,128]{1,0:T(4,128)S(1)} %slice_reduce_fusion), channel_id=1, source_target_pairs={{0,4},{2,6},{4,0},{6,2},{1,5},{3,7},{5,1},{7,3},{8,12},{10,14},{12... | collective-permute-start | bytes 6152 | tf_op jit(solution)/shard_map/ppermute | solution.py:251
  122.3 1.3 %shard_map.61 = f32[8,32,1024]{2,1,0:T(8,128)} custom-call(f32[32,2,9,4,128]{4,3,2,1,0:T(4,128)S(1)} %bitcast.19), custom_call_target="tpu_custom_call" | custom-call | tf_op jit(solution)/shard_map/pallas_call | solution.py:237
  123.6 0.8 collective-permute-done.3
  124.4 0.1 fusion
  124.4 0.6 pad_maximum_fusion.2
  (11 shorter events, 0.1 us)
Async XLA Ops:
  0.6 3.7 %copy-start.2 = (f32[8,32,128]{2,1,0:T(8,128)S(1)}, f32[8,32,128]{2,1,0:T(8,128)}, u32[]{:S(2)}) copy-start(f32[8,32,128]{2,1,0:T(8,128)} %param.5) | copy-start | bytes 393220
  0.6 18.1 %all-to-all-start = ((f32[4,2,8,32,128]{4,3,2,1,0:T(8,128)}), f32[4,2,8,32,128]{4,3,2,1,0:T(8,128)S(1)}, u32[]{:S(2)}, u32[]{:S(2)}) async-start(f32[4,2,8,32,128]{4,3,2,1,0:T(8,128)} %bitcast.24), calls=%async_computation | async-start | bytes 2097152 | tf_op jit(solution)/shard_map/all_to_all | solution.py:269
  4.3 7.9 %collective-permute-start = (f32[8,32,128]{2,1,0:T(8,128)S(1)}, f32[8,32,128]{2,1,0:T(8,128)}, u32[]{:S(2)}, u32[]{:S(2)}) collective-permute-start(f32[8,32,128]{2,1,0:T(8,128)S(1)} %copy-done.2), channel_id=1, source_target_pairs={{4,12},{6,14},{8,0},{10,2},{12,20},{14,22},{16,8},{18,10},{20,28},... | collective-permute-start | bytes 393224 | tf_op jit(solution)/shard_map/ppermute | solution.py:268
  18.9 22.3 %collective-permute-start.1 = (f32[2,18,32,128]{3,2,1,0:T(8,128)S(1)}, f32[2,18,32,128]{3,2,1,0:T(8,128)S(1)}, u32[]{:S(2)}, u32[]{:S(2)}) collective-permute-start(f32[2,18,32,128]{3,2,1,0:T(8,128)S(1)} %pad_maximum_fusion), channel_id=1, source_target_pairs={{0,8},{8,16},{16,24},{24,32},{32,40},{40,48},{48,56},{56,64},{64,7... | collective-permute-start | bytes 1769480 | tf_op jit(solution)/shard_map/ppermute | solution.py:273
  22.3 18.9 %copy-start = (bf16[256,256]{1,0:T(8,128)(2,1)S(1)}, bf16[256,256]{1,0:T(8,128)(2,1)}, u32[]{:S(2)}) copy-start(bf16[256,256]{1,0:T(8,128)(2,1)} %constant.19.clone.bands) | copy-start | bytes 393220
  22.4 18.8 %collective-permute-start.2 = (f32[2,18,32,128]{3,2,1,0:T(8,128)S(1)}, f32[2,18,32,128]{3,2,1,0:T(8,128)S(1)}, u32[]{:S(2)}, u32[]{:S(2)}) collective-permute-start(f32[2,18,32,128]{3,2,1,0:T(8,128)S(1)} %pad_maximum_fusion.1), channel_id=1, source_target_pairs={{8,0},{16,8},{24,16},{32,24},{40,32},{48,40},{56,48},{64,56},{72,6... | collective-permute-start | bytes 1769480 | tf_op jit(solution)/shard_map/ppermute | solution.py:274
  52.9 19.3 %copy-start.1 = (f32[16,16]{1,0:T(8,128)S(1)}, f32[16,16]{1,0:T(8,128)}, u32[]{:S(2)}) copy-start(f32[16,16]{1,0:T(8,128)} %coefficients.1) | copy-start | bytes 3076
  120.0 3.5 %collective-permute-start.5 = (f32[4,128]{1,0:T(4,128)S(1)}, f32[4,128]{1,0:T(4,128)S(1)}, u32[]{:S(2)}, u32[]{:S(2)}) collective-permute-start(f32[4,128]{1,0:T(4,128)S(1)} %slice_reduce_fusion), channel_id=1, source_target_pairs={{0,6},{2,4},{4,2},{6,0},{1,7},{3,5},{5,3},{7,1},{8,14},{10,12},{12... | collective-permute-start | bytes 6152 | tf_op jit(solution)/shard_map/ppermute | solution.py:251
  120.1 3.4 %collective-permute-start.4 = (f32[4,128]{1,0:T(4,128)S(1)}, f32[4,128]{1,0:T(4,128)S(1)}, u32[]{:S(2)}, u32[]{:S(2)}) collective-permute-start(f32[4,128]{1,0:T(4,128)S(1)} %slice_reduce_fusion), channel_id=1, source_target_pairs={{0,2},{2,0},{4,6},{6,4},{1,3},{3,1},{5,7},{7,5},{8,10},{10,8},{12,... | collective-permute-start | bytes 6152 | tf_op jit(solution)/shard_map/ppermute | solution.py:251
  120.8 3.6 %collective-permute-start.3 = (f32[4,128]{1,0:T(4,128)S(1)}, f32[4,128]{1,0:T(4,128)S(1)}, u32[]{:S(2)}, u32[]{:S(2)}) collective-permute-start(f32[4,128]{1,0:T(4,128)S(1)} %slice_reduce_fusion), channel_id=1, source_target_pairs={{0,4},{2,6},{4,0},{6,2},{1,5},{3,7},{5,1},{7,3},{8,12},{10,14},{12... | collective-permute-start | bytes 6152 | tf_op jit(solution)/shard_map/ppermute | solution.py:251

commit v10 on v9

--- a/solution.py
+++ b/solution.py
@@ -47,15 +47,8 @@
     return high, low
 
 
-def dot3(a, b, dims):
-    ah, al = split(a)
-    bh, bl = split(b)
-    dot = functools.partial(lax.dot_general, dimension_numbers=(dims, ((), ())), preferred_element_type=F32)
-    return dot(ah, bh) + (dot(ah, bl) + dot(al, bh))
-
-
 def filter_kernel(
-    chunk, slabs, before, after, own, beyond, bands, out, field, other, local, z, result, turned
+    chunk, slabs, ahead, behind, own, beyond, bands, out, field, other, local, z, result, turned
 ):
     far, near = 3 * WIDTH, 2 * WIDTH + 2
     row = lax.broadcasted_iota(jnp.int32, (8, 8, NZ), 1) % 4
@@ -78,9 +71,11 @@
         field[plane, 0:EXT] = jnp.where(row[:EXT] == 0, 0.0, pltpu.roll(value[8 - EXT :], 1, 1))
         field[plane, EXT + 8 :] = jnp.where(row[:EXT] == 3, 0.0, pltpu.roll(value[:EXT], 7, 1))
 
+    odd = chunk[0] % 2
+
     def enter_ends(p, _):
-        enter(p, [(before, (o, p)) for o in range(OWN)])
-        enter(far + CHUNK + p, [(after, (o, p)) for o in range(OWN)])
+        enter(odd * (far + CHUNK) + p, [(ahead, (o, p)) for o in range(OWN)])
+        enter((1 - odd) * (far + CHUNK) + p, [(behind, (o, p)) for o in range(OWN)])
         return 0
 
     lax.fori_loop(0, far, enter_ends, 0)
@@ -172,10 +167,10 @@
     lax.fori_loop(0, NZ // 4, pick, 0)
 
 
-def rotate_kernel(ring, coefficients, out):
-    exact = functools.partial(
-        lax.dot_general, precision=lax.Precision.HIGHEST, preferred_element_type=F32
-    )
+exact = functools.partial(lax.dot_general, precision=lax.Precision.HIGHEST, preferred_element_type=F32)
+
+
+def weights_kernel(coefficients, out):
     row = lax.broadcasted_iota(jnp.int32, (256, 256), 0)
     column = lax.broadcasted_iota(jnp.int32, (256, 256), 1)
     number = lax.broadcasted_iota(jnp.int32, (256, 16), 0)
@@ -184,10 +179,16 @@
     after = (number // 16 == entry).astype(F32)
     spread = exact(before, exact(coefficients[...], after, (((1,), (1,)), ((), ()))), (((1,), (0,)), ((), ())))
     same = (row // 8 % 4 == column % 4) & (row % 4 == column // 4 % 4)
-    weights = jnp.where(same, spread, 0.0)
-
+    out[...] = jnp.where(same, spread, 0.0)
+
+
+def rotate_kernel(ring, weights, out):
     lane = lax.broadcasted_iota(jnp.int32, (256, 128), 1) // 32
-    sums = jnp.zeros((256, 256), F32)
+    weights_high, weights_low = split(weights[...])
+    dot = functools.partial(lax.dot_general, preferred_element_type=F32)
+    right = (((1,), (0,)), ((), ()))
+    rows_out = (((0,), (0,)), ((), ()))
+    straight, cross = jnp.zeros((256, 256), F32), jnp.zeros((256, 256), F32)
     for t in range(4):
         halves = []
         for b in range(2):
@@ -199,14 +200,24 @@
                 value = piece if value is None else jnp.where(lane == c, piece, value)
             halves.append(value)
         all_orbitals = jnp.concatenate(halves, axis=1)
-        turned = dot3(all_orbitals, weights, ((1,), (0,)))
+        high, low = split(all_orbitals)
+        turned = dot(high, weights_high, right) + (dot(high, weights_low, right) + dot(low, weights_high, right))
         for b in range(2):
             rows = turned[:, b * 128 : (b + 1) * 128].reshape(32, 8, 128)
             out[:, b, 2 * t] = rows[:, 0:4]
             out[:, b, 2 * t + 1] = rows[:, 4:8]
-        sums = sums + dot3(all_orbitals, all_orbitals, ((0,), (0,)))
-    diagonal = jnp.where((row // 8 % 4 == column // 8 % 4) & (row % 4 == column % 4), sums, 0.0)
-    both = exact(before, exact(diagonal, before, (((1,), (0,)), ((), ()))), (((0,), (0,)), ((), ())))
+        straight = straight + dot(high, high, rows_out)
+        cross = cross + dot(high, low, rows_out)
+    row = lax.broadcasted_iota(jnp.int32, (256, 256), 0)
+    column = lax.broadcasted_iota(jnp.int32, (256, 256), 1)
+    same = (row // 8 % 4 == column // 8 % 4) & (row % 4 == column % 4)
+    diagonal = jnp.where(same, straight + (cross + cross.T), 0.0).reshape(8, 4, 8, 256).sum(axis=1).reshape(64, 256)
+    number = lax.broadcasted_iota(jnp.int32, (256, 16), 0)
+    entry = lax.broadcasted_iota(jnp.int32, (256, 16), 1)
+    columns = (number // 32 * 2 + number // 4 % 2 == entry).astype(F32)
+    number, entry = number[:64], entry[:64]
+    rows = (number // 8 * 2 + number // 4 % 2 == entry).astype(F32)
+    both = exact(rows, exact(diagonal, columns, (((1,), (0,)), ((), ()))), (((0,), (0,)), ((), ())))
     tile = jnp.concatenate([both[4 * q : 4 * q + 4] for q in range(4)] + [jnp.zeros((4, 64), F32)], axis=1)
     out[:, :, 8] = jnp.broadcast_to(tile, (32, 2, 4, 128))
 
@@ -261,8 +272,6 @@
     chunks = ("z", "x")
     dom = ("z", "x", "u", "c")
     count = lax.axis_size(chunks)
-    up = [(i, i + 1) for i in range(count - 1)]
-    down = [(j, i) for i, j in up]
 
     shift = [(d, d + 4 if d % 4 >= 2 else d - 4) for d in range(4 * count)]
     beyond = lax.ppermute(potential, dom, [(i, j) for i, j in shift if 0 <= j < 4 * count])
@@ -270,8 +279,12 @@
     slabs, beyond = lax.optimization_barrier((slabs, beyond))
     far = 3 * WIDTH
     part = far - 16
-    before = lax.ppermute(jnp.concatenate([slabs[1, :, 8 - part :], slabs[2], slabs[3]], axis=1), chunks, up)
-    after = lax.ppermute(jnp.concatenate([slabs[0], slabs[1], slabs[2, :, :part]], axis=1), chunks, down)
+    chunk = lax.axis_index(chunks)
+    first = jnp.concatenate([slabs[0], slabs[1], slabs[2, :, :part]], axis=1)
+    last = jnp.concatenate([slabs[1, :, 8 - part :], slabs[2], slabs[3]], axis=1)
+    swaps = [[(i, j) for k in range(s, count - 1, 2) for i, j in ((k, k + 1), (k + 1, k))] for s in (1, 0)]
+    ahead = lax.ppermute(jnp.where(chunk % 2 == 1, last, first), chunks, swaps[0])
+    behind = lax.ppermute(jnp.where(chunk % 2 == 1, first, last), chunks, swaps[1])
     own = lax.all_gather(potential, ("u", "c"))
     beyond = lax.all_gather(beyond, ("u", "c"))
 
@@ -284,12 +297,12 @@
         (2 * 8 * NZ, NZ),
     ]
     bands = jnp.asarray(banded(1.0 / HALF))
-    chunk = lax.axis_index(chunks).reshape(1)
+    (weights,) = call(weights_kernel, [(256, 256)])(coefficients)
     (message,) = call(filter_kernel, [(4, 2, 32, 8, 128)], scratch)(
-        chunk, slabs, before, after, own, beyond, bands
+        chunk.reshape(1), slabs, ahead, behind, own, beyond, bands
     )
     ring = lax.all_to_all(message.reshape(8, 256, 128), ("u", "c", "b"), 0, 0, tiled=True)
-    (rotated,) = call(rotate_kernel, [(32, 2, 9, 4, 128)])(ring, coefficients)
+    (rotated,) = call(rotate_kernel, [(32, 2, 9, 4, 128)])(ring, weights)
     received = lax.all_to_all(rotated.reshape(64, 9, 4, 128), ("z", "x", "b"), 0, 0, tiled=True)
     gram = four(received[:, 8].sum(axis=0), "u", 1, "c", 1) / (NX * NY * NZ)
     intersection = jnp.concatenate([gram[:, q * NORB : (q + 1) * NORB] for q in range(4)], axis=0)

time: 126 us -> 124 us (0.984)
  blocking collectives: 78.6 us -> 59 us
  waiting for transfers between devices: 11 us -> 25 us
  starting transfers between devices: 18 us -> 19.8 us
    all_to_all x1 -> x0, blocking collectives: 19.3 us -> none  [local(): lax.all_to_all(message.reshape(8, 256, 128), ('u', 'c', 'b'), 0, 0, tiled...]
    all_to_all x0 -> x1, waiting for transfers between devices: none -> 14.6 us  [local(): lax.all_to_all(message.reshape(8, 256, 128), ('u', 'c', 'b'), 0, 0, tiled...]
    all_to_all x0 -> x1, starting transfers between devices: none -> 4.6 us  [local(): lax.all_to_all(message.reshape(8, 256, 128), ('u', 'c', 'b'), 0, 0, tiled...]
    ppermute x2, starting transfers between devices: 7.95 us -> 5.11 us  [the longest x1 4.34 us: local(): lax.ppermute(jnp.where(chunk % 2 == 1, last, first), chunks, swaps[0])]
    pallas_call x3 -> x4, Pallas kernels: 15.7 us -> 16.8 us  [call(): pl.pallas_call(kernel, out_shape=[jax.ShapeDtypeStruct(s, F32) for s in o...]
  transfers between devices with their start and end apart: 7 -> 8, of which waited for: 3 -> 5; matrix products, arithmetic and copies ran while one was open for 0% -> 0% of each run, Pallas kernels for 1% -> 2%
where the time goes in v10:
time: 124 us; the launch traced here: 122 us
  blocking collectives  59 us (48%)
  waiting for transfers between devices  25 us (20%)
  starting transfers between devices  19.8 us (16%)
  Pallas kernels  16.8 us (14%)
    all_to_all x1, blocking collectives, local(): lax.all_to_all(rotated.reshape(64, 9, 4, 128), ('z', 'x', 'b'), 0, 0, til...  45.2 us
    pallas_call x4, Pallas kernels, call(): pl.pallas_call(kernel, out_shape=[jax.ShapeDtypeStruct(s, F32) for s in o...  16.8 us
    all_to_all x1, waiting for transfers between devices, local(): lax.all_to_all(message.reshape(8, 256, 128), ('u', 'c', 'b'), 0, 0, tiled...  14.6 us
    all_gather x1, blocking collectives, local(): beyond = lax.all_gather(beyond, ('u', 'c'))  7.28 us
    all_to_all x1, waiting for transfers between devices, local(): lax.all_to_all(orbitals.reshape(4, OWN, 8, NY, NZ), ('u', 'c'), 0, 0, til...  6.67 us
    all_gather x1, blocking collectives, local(): own = lax.all_gather(potential, ('u', 'c'))  6.5 us
    all_to_all x1, starting transfers between devices, local(): lax.all_to_all(message.reshape(8, 256, 128), ('u', 'c', 'b'), 0, 0, tiled...  4.6 us
    ppermute x1, starting transfers between devices, local(): lax.ppermute(jnp.where(chunk % 2 == 1, last, first), chunks, swaps[0])  4.34 us
  transfers between devices with their start and end apart: 8, of which 5 were waited for; matrix products, arithmetic and copies ran while one was open for 0% of the time, Pallas kernels for 2%

profile of v10, /device:TPU:32, one launch (start us, length us, event | category | flops | bytes accessed | tf_op | source)
XLA Modules:
  0.0 122.4 jit_solution(10606551042933905224)
XLA Ops:
  0.6 3.7 %all-to-all-start = ((f32[4,2,8,32,128]{4,3,2,1,0:T(8,128)}), f32[4,2,8,32,128]{4,3,2,1,0:T(8,128)S(1)}, u32[]{:S(2)}, u32[]{:S(2)}) async-start(f32[4,2,8,32,128]{4,3,2,1,0:T(8,128)} %bitcast.23), calls=%async_computation | async-start | bytes 2097152 | tf_op jit(solution)/shard_map/all_to_all | solution.py:278
  4.3 4.2 %collective-permute-start = (f32[8,32,128]{2,1,0:T(8,128)S(1)}, f32[8,32,128]{2,1,0:T(8,128)S(1)}, u32[]{:S(2)}, u32[]{:S(2)}) collective-permute-start(f32[8,32,128]{2,1,0:T(8,128)S(1)} %copy-done.2), channel_id=1, source_target_pairs={{4,12},{6,14},{8,0},{10,2},{12,20},{14,22},{16,8},{18,10},{20,28},... | collective-permute-start | bytes 393224 | tf_op jit(solution)/shard_map/ppermute | solution.py:277
  8.6 3.5 %collective-permute-done = f32[8,32,128]{2,1,0:T(8,128)S(1)} collective-permute-done((f32[8,32,128]{2,1,0:T(8,128)S(1)}, f32[8,32,128]{2,1,0:T(8,128)S(1)}, u32[]{:S(2)}, u32[]{:S(2)}) %collective-permute-start) | collective-permute-done | bytes 131104 | tf_op jit(solution)/shard_map/ppermute | solution.py:277
  12.1 6.7 %all-to-all-done.slabs = f32[4,2,8,32,128]{4,3,2,1,0:T(8,128)S(1)} async-done(((f32[4,2,8,32,128]{4,3,2,1,0:T(8,128)}), f32[4,2,8,32,128]{4,3,2,1,0:T(8,128)S(1)}, u32[]{:S(2)}, u32[]{:S(2)}) %all-to-all-start) | async-done | bytes 1048608 | tf_op jit(solution)/shard_map/all_to_all | solution.py:278
  18.7 0.1 slice_bitcast_fusion.3
  18.9 0.1 fusion
  19.0 4.3 %collective-permute-start.1 = (f32[2,18,32,128]{3,2,1,0:T(8,128)S(1)}, f32[2,18,32,128]{3,2,1,0:T(8,128)S(1)}, u32[]{:S(2)}, u32[]{:S(2)}) collective-permute-start(f32[2,18,32,128]{3,2,1,0:T(8,128)S(1)} %get-tuple-element.7), channel_id=1, source_target_pairs={{8,16},{16,8},{24,32},{32,24},{40,48},{48,40},{56,64},{64,56},{72,... | collective-permute-start | bytes 1769480 | tf_op jit(solution)/shard_map/ppermute | solution.py:286
  23.4 0.8 collective-permute-start.2
  24.1 6.5 %all-gather = f32[32,32,128]{2,1,0:T(8,128)S(1)} all-gather(f32[8,32,128]{2,1,0:T(8,128)S(1)} %copy-done.2), channel_id=2, replica_groups=mesh['z'=8,'x'=4,'u'=2,'c'=2,'b'=2] {'u','c'}, dimensions={0}, use_global_device_ids=true | all-gather | bytes 655360 | tf_op jit(solution)/shard_map/all_gather | solution.py:288
  30.6 7.3 %all-gather.1 = f32[32,32,128]{2,1,0:T(8,128)S(1)} all-gather(f32[8,32,128]{2,1,0:T(8,128)S(1)} %collective-permute-done), channel_id=3, replica_groups=mesh['z'=8,'x'=4,'u'=2,'c'=2,'b'=2] {'u','c'}, dimensions={0}, use_global_device_ids=true | all-gather | bytes 655360 | tf_op jit(solution)/shard_map/all_gather | solution.py:289
  37.9 0.1 collective-permute-done.1.ahead
  38.0 12.8 %shard_map.59 = f32[4,2,32,8,128]{4,3,2,1,0:T(8,128)} custom-call(s32[1]{0:T(128)} %bitcast.chunk, f32[4,2,8,32,128]{4,3,2,1,0:T(8,128)S(1)} %all-to-all-done.slabs, f32[2,18,32,128]{3,2,1,0:T(8,128)S(1)} %collective-permute-done.1.ahead, f32[2,18,32,128]{3,2,1,0:T(8,128)S(1)} %collective-permute-done.2.behind, f32[4,8,32,128]{3,2,1,0:T(8,128)S(1)} %bitcast.21, ...), custom_call_target="tpu_custom_call" | custom-call | tf_op jit(solution)/shard_map/pallas_call | solution.py:248
  50.8 4.6 %all-to-all-start.1 = ((f32[8,256,128]{2,1,0:T(8,128)}), f32[8,256,128]{2,1,0:T(8,128)S(1)}, u32[]{:S(2)}, u32[]{:S(2)}) async-start(f32[8,256,128]{2,1,0:T(8,128)} %bitcast.10), calls=%async_computation.1 | async-start | bytes 2097152 | tf_op jit(solution)/shard_map/all_to_all | solution.py:304
  55.5 0.8 shard_map.60.weights
  56.2 14.6 %all-to-all-done.1.ring = f32[8,256,128]{2,1,0:T(8,128)S(1)} async-done(((f32[8,256,128]{2,1,0:T(8,128)}), f32[8,256,128]{2,1,0:T(8,128)S(1)}, u32[]{:S(2)}, u32[]{:S(2)}) %all-to-all-start.1) | async-done | bytes 1048608 | tf_op jit(solution)/shard_map/all_to_all | solution.py:304
  70.8 2.0 %shard_map.61 = f32[32,2,9,4,128]{4,3,2,1,0:T(4,128)S(1)} custom-call(f32[8,256,128]{2,1,0:T(8,128)S(1)} %all-to-all-done.1.ring, f32[256,256]{1,0:T(8,128)S(1)} %shard_map.60.weights), custom_call_target="tpu_custom_call" | custom-call | tf_op jit(solution)/shard_map/pallas_call | solution.py:248
  72.8 45.2 %all_to_all.15 = f32[64,9,4,128]{3,2,1,0:T(4,128)S(1)} all-to-all(f32[64,9,4,128]{3,2,1,0:T(4,128)S(1)} %bitcast.20), channel_id=1, replica_groups=mesh['z'=8,'x'=4,'u'=2,'c'=2,'b'=2] {'z','x','b'}, dimensions={0} | all-to-all | bytes 2359296 | tf_op jit(solution)/shard_map/all_to_all | solution.py:306
  118.0 0.1 slice_reduce_fusion
  118.1 0.3 collective-permute-start.3
  118.4 1.9 %collective-permute-start.5 = (f32[4,128]{1,0:T(4,128)S(1)}, f32[4,128]{1,0:T(4,128)S(1)}, u32[]{:S(2)}, u32[]{:S(2)}) collective-permute-start(f32[4,128]{1,0:T(4,128)S(1)} %slice_reduce_fusion), channel_id=1, source_target_pairs={{0,6},{2,4},{4,2},{6,0},{1,7},{3,5},{5,3},{7,1},{8,14},{10,12},{12... | collective-permute-start | bytes 6152 | tf_op jit(solution)/shard_map/ppermute | solution.py:262
  120.3 1.3 %shard_map.62 = f32[8,32,1024]{2,1,0:T(8,128)} custom-call(f32[32,2,9,4,128]{4,3,2,1,0:T(4,128)S(1)} %bitcast.19), custom_call_target="tpu_custom_call" | custom-call | tf_op jit(solution)/shard_map/pallas_call | solution.py:248
  121.6 0.1 collective-permute-done.3
  121.7 0.1 fusion.2
  121.8 0.6 pad_maximum_fusion.2
  (12 shorter events, 0.1 us)
Async XLA Ops:
  0.6 3.7 %copy-start.2 = (f32[8,32,128]{2,1,0:T(8,128)S(1)}, f32[8,32,128]{2,1,0:T(8,128)}, u32[]{:S(2)}) copy-start(f32[8,32,128]{2,1,0:T(8,128)} %param.5) | copy-start | bytes 393220
  0.6 18.1 %all-to-all-start = ((f32[4,2,8,32,128]{4,3,2,1,0:T(8,128)}), f32[4,2,8,32,128]{4,3,2,1,0:T(8,128)S(1)}, u32[]{:S(2)}, u32[]{:S(2)}) async-start(f32[4,2,8,32,128]{4,3,2,1,0:T(8,128)} %bitcast.23), calls=%async_computation | async-start | bytes 2097152 | tf_op jit(solution)/shard_map/all_to_all | solution.py:278
  4.3 7.7 %collective-permute-start = (f32[8,32,128]{2,1,0:T(8,128)S(1)}, f32[8,32,128]{2,1,0:T(8,128)S(1)}, u32[]{:S(2)}, u32[]{:S(2)}) collective-permute-start(f32[8,32,128]{2,1,0:T(8,128)S(1)} %copy-done.2), channel_id=1, source_target_pairs={{4,12},{6,14},{8,0},{10,2},{12,20},{14,22},{16,8},{18,10},{20,28},... | collective-permute-start | bytes 393224 | tf_op jit(solution)/shard_map/ppermute | solution.py:277
  19.0 19.0 %copy-start = (bf16[256,256]{1,0:T(8,128)(2,1)S(1)}, bf16[256,256]{1,0:T(8,128)(2,1)}, u32[]{:S(2)}) copy-start(bf16[256,256]{1,0:T(8,128)(2,1)} %constant.35.clone.bands) | copy-start | bytes 393220
  19.0 19.0 %collective-permute-start.1 = (f32[2,18,32,128]{3,2,1,0:T(8,128)S(1)}, f32[2,18,32,128]{3,2,1,0:T(8,128)S(1)}, u32[]{:S(2)}, u32[]{:S(2)}) collective-permute-start(f32[2,18,32,128]{3,2,1,0:T(8,128)S(1)} %get-tuple-element.7), channel_id=1, source_target_pairs={{8,16},{16,8},{24,32},{32,24},{40,48},{48,40},{56,64},{64,56},{72,... | collective-permute-start | bytes 1769480 | tf_op jit(solution)/shard_map/ppermute | solution.py:286
  23.4 14.7 %collective-permute-start.2 = (f32[2,18,32,128]{3,2,1,0:T(8,128)S(1)}, f32[2,18,32,128]{3,2,1,0:T(8,128)S(1)}, u32[]{:S(2)}, u32[]{:S(2)}) collective-permute-start(f32[2,18,32,128]{3,2,1,0:T(8,128)S(1)} %get-tuple-element.6), channel_id=1, source_target_pairs={{0,8},{8,0},{16,24},{24,16},{32,40},{40,32},{48,56},{56,48},{64,72... | collective-permute-start | bytes 1769480 | tf_op jit(solution)/shard_map/ppermute | solution.py:287
  50.8 4.6 %copy-start.1 = (f32[16,16]{1,0:T(8,128)S(1)}, f32[16,16]{1,0:T(8,128)}, u32[]{:S(2)}) copy-start(f32[16,16]{1,0:T(8,128)} %coefficients.1) | copy-start | bytes 3076
  50.8 19.9 %all-to-all-start.1 = ((f32[8,256,128]{2,1,0:T(8,128)}), f32[8,256,128]{2,1,0:T(8,128)S(1)}, u32[]{:S(2)}, u32[]{:S(2)}) async-start(f32[8,256,128]{2,1,0:T(8,128)} %bitcast.10), calls=%async_computation.1 | async-start | bytes 2097152 | tf_op jit(solution)/shard_map/all_to_all | solution.py:304
  118.1 3.7 %collective-permute-start.3 = (f32[4,128]{1,0:T(4,128)S(1)}, f32[4,128]{1,0:T(4,128)S(1)}, u32[]{:S(2)}, u32[]{:S(2)}) collective-permute-start(f32[4,128]{1,0:T(4,128)S(1)} %slice_reduce_fusion), channel_id=1, source_target_pairs={{0,4},{2,6},{4,0},{6,2},{1,5},{3,7},{5,1},{7,3},{8,12},{10,14},{12... | collective-permute-start | bytes 6152 | tf_op jit(solution)/shard_map/ppermute | solution.py:262
  118.4 3.3 %collective-permute-start.4 = (f32[4,128]{1,0:T(4,128)S(1)}, f32[4,128]{1,0:T(4,128)S(1)}, u32[]{:S(2)}, u32[]{:S(2)}) collective-permute-start(f32[4,128]{1,0:T(4,128)S(1)} %slice_reduce_fusion), channel_id=1, source_target_pairs={{0,2},{2,0},{4,6},{6,4},{1,3},{3,1},{5,7},{7,5},{8,10},{10,8},{12,... | collective-permute-start | bytes 6152 | tf_op jit(solution)/shard_map/ppermute | solution.py:262
  118.4 3.3 %collective-permute-start.5 = (f32[4,128]{1,0:T(4,128)S(1)}, f32[4,128]{1,0:T(4,128)S(1)}, u32[]{:S(2)}, u32[]{:S(2)}) collective-permute-start(f32[4,128]{1,0:T(4,128)S(1)} %slice_reduce_fusion), channel_id=1, source_target_pairs={{0,6},{2,4},{4,2},{6,0},{1,7},{3,5},{5,3},{7,1},{8,14},{10,12},{12... | collective-permute-start | bytes 6152 | tf_op jit(solution)/shard_map/ppermute | solution.py:262

commit v11 on v10

--- a/solution.py
+++ b/solution.py
@@ -203,9 +203,10 @@
         high, low = split(all_orbitals)
         turned = dot(high, weights_high, right) + (dot(high, weights_low, right) + dot(low, weights_high, right))
         for b in range(2):
-            rows = turned[:, b * 128 : (b + 1) * 128].reshape(32, 8, 128)
-            out[:, b, 2 * t] = rows[:, 0:4]
-            out[:, b, 2 * t + 1] = rows[:, 4:8]
+            rows = turned[:, b * 128 : (b + 1) * 128].reshape(8, 4, 8, 128)
+            for x in range(4):
+                out[x, b, :, 2 * t] = rows[:, x, 0:4]
+                out[x, b, :, 2 * t + 1] = rows[:, x, 4:8]
         straight = straight + dot(high, high, rows_out)
         cross = cross + dot(high, low, rows_out)
     row = lax.broadcasted_iota(jnp.int32, (256, 256), 0)
@@ -219,7 +220,7 @@
     rows = (number // 8 * 2 + number // 4 % 2 == entry).astype(F32)
     both = exact(rows, exact(diagonal, columns, (((1,), (0,)), ((), ()))), (((0,), (0,)), ((), ())))
     tile = jnp.concatenate([both[4 * q : 4 * q + 4] for q in range(4)] + [jnp.zeros((4, 64), F32)], axis=1)
-    out[:, :, 8] = jnp.broadcast_to(tile, (32, 2, 4, 128))
+    out[:, :, :, 8] = jnp.broadcast_to(tile, (4, 2, 8, 4, 128))
 
 
 def lines_kernel(received, out):
@@ -227,7 +228,7 @@
 
     def lines(s, b):
         pieces = [
-            jnp.concatenate([received[s * 4 + c, b, 2 * j], received[s * 4 + c, b, 2 * j + 1]], axis=0)
+            jnp.concatenate([received[c, b, s, 2 * j], received[c, b, s, 2 * j + 1]], axis=0)
             for c in range(4)
             for j in range(4)
         ]
@@ -276,7 +277,8 @@
     shift = [(d, d + 4 if d % 4 >= 2 else d - 4) for d in range(4 * count)]
     beyond = lax.ppermute(potential, dom, [(i, j) for i, j in shift if 0 <= j < 4 * count])
     slabs = lax.all_to_all(orbitals.reshape(4, OWN, 8, NY, NZ), ("u", "c"), 0, 0, tiled=True)
-    slabs, beyond = lax.optimization_barrier((slabs, beyond))
+    (weights,) = call(weights_kernel, [(256, 256)])(coefficients)
+    slabs, beyond, weights = lax.optimization_barrier((slabs, beyond, weights))
     far = 3 * WIDTH
     part = far - 16
     chunk = lax.axis_index(chunks)
@@ -297,16 +299,19 @@
         (2 * 8 * NZ, NZ),
     ]
     bands = jnp.asarray(banded(1.0 / HALF))
-    (weights,) = call(weights_kernel, [(256, 256)])(coefficients)
     (message,) = call(filter_kernel, [(4, 2, 32, 8, 128)], scratch)(
         chunk.reshape(1), slabs, ahead, behind, own, beyond, bands
     )
     ring = lax.all_to_all(message.reshape(8, 256, 128), ("u", "c", "b"), 0, 0, tiled=True)
-    (rotated,) = call(rotate_kernel, [(32, 2, 9, 4, 128)])(ring, weights)
-    received = lax.all_to_all(rotated.reshape(64, 9, 4, 128), ("z", "x", "b"), 0, 0, tiled=True)
+    (rotated,) = call(rotate_kernel, [(4, 2, 8, 9, 4, 128)])(ring, weights)
+    everyone = np.arange(256).reshape(8, 4, 4, 2)
+    groups = everyone.transpose(2, 1, 3, 0).reshape(4, 64).tolist()
+    received = lax.all_to_all(
+        rotated.reshape(64, 9, 4, 128), ("z", "x", "u", "c", "b"), 0, 0, axis_index_groups=groups, tiled=True
+    )
     gram = four(received[:, 8].sum(axis=0), "u", 1, "c", 1) / (NX * NY * NZ)
     intersection = jnp.concatenate([gram[:, q * NORB : (q + 1) * NORB] for q in range(4)], axis=0)
-    (lines,) = call(lines_kernel, [(8, NY, NX)])(received.reshape(32, 2, 9, 4, 128))
+    (lines,) = call(lines_kernel, [(8, NY, NX)])(received.reshape(4, 2, 8, 9, 4, 128))
     return intersection, lines
 
 

time: 124 us -> 123 us (level)
  blocking collectives: 59 us -> 78.8 us
  waiting for transfers between devices: 25 us -> 9.69 us
  starting transfers between devices: 19.8 us -> 15.2 us
    all_to_all x1 -> x2, blocking collectives: 45.2 us -> 65 us  [the longest x1 45.7 us: local(): lax.all_to_all(rotated.reshape(64, 9, 4, 128), ('z', 'x', 'u', 'c', 'b'),...]
    all_to_all x1 -> x0, waiting for transfers between devices: 14.6 us -> none  [local(): lax.all_to_all(message.reshape(8, 256, 128), ('u', 'c', 'b'), 0, 0, tiled...]
    all_to_all x1 -> x0, starting transfers between devices: 4.6 us -> none  [local(): lax.all_to_all(message.reshape(8, 256, 128), ('u', 'c', 'b'), 0, 0, tiled...]
  transfers between devices with their start and end apart: 8 -> 7, of which waited for: 5 -> 4; matrix products, arithmetic and copies ran while one was open for 0% -> 0% of each run, Pallas kernels for 2% -> 2%
where the time goes in v11:
time: 123 us; the launch traced here: 121 us
  blocking collectives  78.8 us (64%)
  Pallas kernels  15.8 us (13%)
  starting transfers between devices  15.2 us (12%)
  waiting for transfers between devices  9.69 us (8%)
    all_to_all x1, blocking collectives, local(): lax.all_to_all(rotated.reshape(64, 9, 4, 128), ('z', 'x', 'u', 'c', 'b'),...  45.7 us
    all_to_all x1, blocking collectives, local(): lax.all_to_all(message.reshape(8, 256, 128), ('u', 'c', 'b'), 0, 0, tiled...  19.3 us
    pallas_call x4, Pallas kernels, call(): pl.pallas_call(kernel, out_shape=[jax.ShapeDtypeStruct(s, F32) for s in o...  15.8 us
    all_gather x1, blocking collectives, local(): beyond = lax.all_gather(beyond, ('u', 'c'))  7.28 us
    all_to_all x1, waiting for transfers between devices, local(): lax.all_to_all(orbitals.reshape(4, OWN, 8, NY, NZ), ('u', 'c'), 0, 0, til...  6.67 us
    all_gather x1, blocking collectives, local(): own = lax.all_gather(potential, ('u', 'c'))  6.5 us
    ppermute x1, starting transfers between devices, local(): lax.ppermute(jnp.where(chunk % 2 == 1, last, first), chunks, swaps[0])  4.34 us
    ppermute x1, starting transfers between devices, local(): lax.ppermute(potential, dom, [(i, j) for i, j in shift if 0 <= j < 4 * co...  4.21 us
  transfers between devices with their start and end apart: 7, of which 4 were waited for; matrix products, arithmetic and copies ran while one was open for 0% of the time, Pallas kernels for 2%

profile of v11, /device:TPU:32, one launch (start us, length us, event | category | flops | bytes accessed | tf_op | source)
XLA Modules:
  0.0 121.2 jit_solution(4569194037619781130)
XLA Ops:
  0.6 3.7 %all-to-all-start = ((f32[4,2,8,32,128]{4,3,2,1,0:T(8,128)}), f32[4,2,8,32,128]{4,3,2,1,0:T(8,128)S(1)}, u32[]{:S(2)}, u32[]{:S(2)}) async-start(f32[4,2,8,32,128]{4,3,2,1,0:T(8,128)} %bitcast.24), calls=%async_computation | async-start | bytes 2097152 | tf_op jit(solution)/shard_map/all_to_all | solution.py:279
  4.3 4.2 %collective-permute-start = (f32[8,32,128]{2,1,0:T(8,128)S(1)}, f32[8,32,128]{2,1,0:T(8,128)S(1)}, u32[]{:S(2)}, u32[]{:S(2)}) collective-permute-start(f32[8,32,128]{2,1,0:T(8,128)S(1)} %copy-done.2), channel_id=1, source_target_pairs={{4,12},{6,14},{8,0},{10,2},{12,20},{14,22},{16,8},{18,10},{20,28},... | collective-permute-start | bytes 393224 | tf_op jit(solution)/shard_map/ppermute | solution.py:278
  8.6 0.8 shard_map.59.weights
  9.3 2.7 %collective-permute-done = f32[8,32,128]{2,1,0:T(8,128)S(1)} collective-permute-done((f32[8,32,128]{2,1,0:T(8,128)S(1)}, f32[8,32,128]{2,1,0:T(8,128)S(1)}, u32[]{:S(2)}, u32[]{:S(2)}) %collective-permute-start) | collective-permute-done | bytes 131104 | tf_op jit(solution)/shard_map/ppermute | solution.py:278
  12.1 6.7 %all-to-all-done.slabs = f32[4,2,8,32,128]{4,3,2,1,0:T(8,128)S(1)} async-done(((f32[4,2,8,32,128]{4,3,2,1,0:T(8,128)}), f32[4,2,8,32,128]{4,3,2,1,0:T(8,128)S(1)}, u32[]{:S(2)}, u32[]{:S(2)}) %all-to-all-start) | async-done | bytes 1048608 | tf_op jit(solution)/shard_map/all_to_all | solution.py:279
  18.7 0.1 slice_bitcast_fusion.3
  18.9 0.1 fusion
  19.0 4.3 %collective-permute-start.1 = (f32[2,18,32,128]{3,2,1,0:T(8,128)S(1)}, f32[2,18,32,128]{3,2,1,0:T(8,128)S(1)}, u32[]{:S(2)}, u32[]{:S(2)}) collective-permute-start(f32[2,18,32,128]{3,2,1,0:T(8,128)S(1)} %get-tuple-element.9), channel_id=1, source_target_pairs={{8,16},{16,8},{24,32},{32,24},{40,48},{48,40},{56,64},{64,56},{72,... | collective-permute-start | bytes 1769480 | tf_op jit(solution)/shard_map/ppermute | solution.py:288
  23.3 0.8 collective-permute-start.2
  24.1 6.5 %all-gather = f32[32,32,128]{2,1,0:T(8,128)S(1)} all-gather(f32[8,32,128]{2,1,0:T(8,128)S(1)} %copy-done.2), channel_id=2, replica_groups=mesh['z'=8,'x'=4,'u'=2,'c'=2,'b'=2] {'u','c'}, dimensions={0}, use_global_device_ids=true | all-gather | bytes 655360 | tf_op jit(solution)/shard_map/all_gather | solution.py:290
  30.6 7.3 %all-gather.1 = f32[32,32,128]{2,1,0:T(8,128)S(1)} all-gather(f32[8,32,128]{2,1,0:T(8,128)S(1)} %collective-permute-done), channel_id=3, replica_groups=mesh['z'=8,'x'=4,'u'=2,'c'=2,'b'=2] {'u','c'}, dimensions={0}, use_global_device_ids=true | all-gather | bytes 655360 | tf_op jit(solution)/shard_map/all_gather | solution.py:291
  37.9 0.1 collective-permute-done.1.ahead
  38.0 0.0 collective-permute-done.2.behind
  38.0 11.8 %shard_map.60 = f32[4,2,32,8,128]{4,3,2,1,0:T(8,128)S(1)} custom-call(s32[1]{0:T(128)} %bitcast.chunk, f32[4,2,8,32,128]{4,3,2,1,0:T(8,128)S(1)} %all-to-all-done.slabs, f32[2,18,32,128]{3,2,1,0:T(8,128)S(1)} %collective-permute-done.1.ahead, f32[2,18,32,128]{3,2,1,0:T(8,128)S(1)} %collective-permute-done.2.behind, f32[4,8,32,128]{3,2,1,0:T(8,128)S(1)} %bitcast.22, ...), custom_call_target="tpu_custom_call" | custom-call | tf_op jit(solution)/shard_map/pallas_call | solution.py:249
  49.8 19.3 %all_to_all.15.ring = f32[8,256,128]{2,1,0:T(8,128)S(1)} all-to-all(f32[8,256,128]{2,1,0:T(8,128)S(1)} %bitcast.21), channel_id=1, replica_groups=mesh['z'=8,'x'=4,'u'=2,'c'=2,'b'=2] {'u','c','b'}, dimensions={0} | all-to-all | bytes 2097152 | tf_op jit(solution)/shard_map/all_to_all | solution.py:305
  69.1 1.9 %shard_map.61 = f32[4,2,8,9,4,128]{5,4,3,2,1,0:T(4,128)S(1)} custom-call(f32[8,256,128]{2,1,0:T(8,128)S(1)} %all_to_all.15.ring, f32[256,256]{1,0:T(8,128)S(1)} %shard_map.59.weights), custom_call_target="tpu_custom_call" | custom-call | tf_op jit(solution)/shard_map/pallas_call | solution.py:249
  71.0 45.7 %all_to_all.16 = f32[64,9,4,128]{3,2,1,0:T(4,128)S(1)} all-to-all(f32[64,9,4,128]{3,2,1,0:T(4,128)S(1)} %bitcast.20), channel_id=1, replica_groups={{0,32,64,96,128,160,192,224,1,33,65,97,129,161,193,225,8,40,72,104,136,..., dimensions={0} | all-to-all | bytes 2359296 | tf_op jit(solution)/shard_map/all_to_all | solution.py:309
  116.7 0.1 slice_reduce_fusion
  116.8 0.6 collective-permute-start.3
  117.4 1.6 %collective-permute-start.5 = (f32[4,128]{1,0:T(4,128)S(1)}, f32[4,128]{1,0:T(4,128)S(1)}, u32[]{:S(2)}, u32[]{:S(2)}) collective-permute-start(f32[4,128]{1,0:T(4,128)S(1)} %slice_reduce_fusion), channel_id=1, source_target_pairs={{0,6},{2,4},{4,2},{6,0},{1,7},{3,5},{5,3},{7,1},{8,14},{10,12},{12... | collective-permute-start | bytes 6152 | tf_op jit(solution)/shard_map/ppermute | solution.py:263
  119.0 1.3 %shard_map.62 = f32[8,32,1024]{2,1,0:T(8,128)} custom-call(f32[4,2,8,9,4,128]{5,4,3,2,1,0:T(4,128)S(1)} %bitcast.19), custom_call_target="tpu_custom_call" | custom-call | tf_op jit(solution)/shard_map/pallas_call | solution.py:249
  120.3 0.1 collective-permute-done.3
  120.5 0.1 fusion.2
  120.6 0.6 pad_maximum_fusion.2
  (11 shorter events, 0.0 us)
Async XLA Ops:
  0.6 3.7 %copy-start.2 = (f32[8,32,128]{2,1,0:T(8,128)S(1)}, f32[8,32,128]{2,1,0:T(8,128)}, u32[]{:S(2)}) copy-start(f32[8,32,128]{2,1,0:T(8,128)} %param.5) | copy-start | bytes 393220
  0.6 7.9 %copy-start.1 = (f32[16,16]{1,0:T(8,128)S(1)}, f32[16,16]{1,0:T(8,128)}, u32[]{:S(2)}) copy-start(f32[16,16]{1,0:T(8,128)} %coefficients.1) | copy-start | bytes 3076
  0.6 18.1 %all-to-all-start = ((f32[4,2,8,32,128]{4,3,2,1,0:T(8,128)}), f32[4,2,8,32,128]{4,3,2,1,0:T(8,128)S(1)}, u32[]{:S(2)}, u32[]{:S(2)}) async-start(f32[4,2,8,32,128]{4,3,2,1,0:T(8,128)} %bitcast.24), calls=%async_computation | async-start | bytes 2097152 | tf_op jit(solution)/shard_map/all_to_all | solution.py:279
  4.3 7.7 %collective-permute-start = (f32[8,32,128]{2,1,0:T(8,128)S(1)}, f32[8,32,128]{2,1,0:T(8,128)S(1)}, u32[]{:S(2)}, u32[]{:S(2)}) collective-permute-start(f32[8,32,128]{2,1,0:T(8,128)S(1)} %copy-done.2), channel_id=1, source_target_pairs={{4,12},{6,14},{8,0},{10,2},{12,20},{14,22},{16,8},{18,10},{20,28},... | collective-permute-start | bytes 393224 | tf_op jit(solution)/shard_map/ppermute | solution.py:278
  19.0 19.0 %copy-start = (bf16[256,256]{1,0:T(8,128)(2,1)S(1)}, bf16[256,256]{1,0:T(8,128)(2,1)}, u32[]{:S(2)}) copy-start(bf16[256,256]{1,0:T(8,128)(2,1)} %constant.35.clone.bands) | copy-start | bytes 393220
  19.0 19.0 %collective-permute-start.1 = (f32[2,18,32,128]{3,2,1,0:T(8,128)S(1)}, f32[2,18,32,128]{3,2,1,0:T(8,128)S(1)}, u32[]{:S(2)}, u32[]{:S(2)}) collective-permute-start(f32[2,18,32,128]{3,2,1,0:T(8,128)S(1)} %get-tuple-element.9), channel_id=1, source_target_pairs={{8,16},{16,8},{24,32},{32,24},{40,48},{48,40},{56,64},{64,56},{72,... | collective-permute-start | bytes 1769480 | tf_op jit(solution)/shard_map/ppermute | solution.py:288
  23.3 14.7 %collective-permute-start.2 = (f32[2,18,32,128]{3,2,1,0:T(8,128)S(1)}, f32[2,18,32,128]{3,2,1,0:T(8,128)S(1)}, u32[]{:S(2)}, u32[]{:S(2)}) collective-permute-start(f32[2,18,32,128]{3,2,1,0:T(8,128)S(1)} %get-tuple-element.8), channel_id=1, source_target_pairs={{0,8},{8,0},{16,24},{24,16},{32,40},{40,32},{48,56},{56,48},{64,72... | collective-permute-start | bytes 1769480 | tf_op jit(solution)/shard_map/ppermute | solution.py:289
  116.8 3.7 %collective-permute-start.3 = (f32[4,128]{1,0:T(4,128)S(1)}, f32[4,128]{1,0:T(4,128)S(1)}, u32[]{:S(2)}, u32[]{:S(2)}) collective-permute-start(f32[4,128]{1,0:T(4,128)S(1)} %slice_reduce_fusion), channel_id=1, source_target_pairs={{0,4},{2,6},{4,0},{6,2},{1,5},{3,7},{5,1},{7,3},{8,12},{10,14},{12... | collective-permute-start | bytes 6152 | tf_op jit(solution)/shard_map/ppermute | solution.py:263
  117.4 3.0 %collective-permute-start.4 = (f32[4,128]{1,0:T(4,128)S(1)}, f32[4,128]{1,0:T(4,128)S(1)}, u32[]{:S(2)}, u32[]{:S(2)}) collective-permute-start(f32[4,128]{1,0:T(4,128)S(1)} %slice_reduce_fusion), channel_id=1, source_target_pairs={{0,2},{2,0},{4,6},{6,4},{1,3},{3,1},{5,7},{7,5},{8,10},{10,8},{12,... | collective-permute-start | bytes 6152 | tf_op jit(solution)/shard_map/ppermute | solution.py:263
  117.4 3.0 %collective-permute-start.5 = (f32[4,128]{1,0:T(4,128)S(1)}, f32[4,128]{1,0:T(4,128)S(1)}, u32[]{:S(2)}, u32[]{:S(2)}) collective-permute-start(f32[4,128]{1,0:T(4,128)S(1)} %slice_reduce_fusion), channel_id=1, source_target_pairs={{0,6},{2,4},{4,2},{6,0},{1,7},{3,5},{5,3},{7,1},{8,14},{10,12},{12... | collective-permute-start | bytes 6152 | tf_op jit(solution)/shard_map/ppermute | solution.py:263

commit v12 on v11

--- a/solution.py
+++ b/solution.py
@@ -47,8 +47,41 @@
     return high, low
 
 
+def edges_kernel(place, piece_0, piece_1, piece_2, piece_3, ahead, behind):
+    def copy(first, last):
+        for m, piece in enumerate((piece_0, piece_1, piece_2, piece_3)):
+            slab = place[1] ^ m
+
+            @pl.when(slab == 0)
+            def _():
+                first[:, 0:8] = piece[...]
+
+            @pl.when(slab == 1)
+            def _():
+                first[:, 8:16] = piece[...]
+                last[:, 0:2] = piece[:, 6:8]
+
+            @pl.when(slab == 2)
+            def _():
+                first[:, 16:18] = piece[:, 0:2]
+                last[:, 2:10] = piece[...]
+
+            @pl.when(slab == 3)
+            def _():
+                last[:, 10:18] = piece[...]
+
+    @pl.when(place[0] % 2 == 1)
+    def _():
+        copy(behind, ahead)
+
+    @pl.when(place[0] % 2 == 0)
+    def _():
+        copy(ahead, behind)
+
+
 def filter_kernel(
-    chunk, slabs, ahead, behind, own, beyond, bands, out, field, other, local, z, result, turned
+    place, piece_0, piece_1, piece_2, piece_3, ahead, behind, own, beyond, bands,
+    out, field, other, local, z, result, turned,
 ):
     far, near = 3 * WIDTH, 2 * WIDTH + 2
     row = lax.broadcasted_iota(jnp.int32, (8, 8, NZ), 1) % 4
@@ -71,7 +104,7 @@
         field[plane, 0:EXT] = jnp.where(row[:EXT] == 0, 0.0, pltpu.roll(value[8 - EXT :], 1, 1))
         field[plane, EXT + 8 :] = jnp.where(row[:EXT] == 3, 0.0, pltpu.roll(value[:EXT], 7, 1))
 
-    odd = chunk[0] % 2
+    odd = place[0] % 2
 
     def enter_ends(p, _):
         enter(odd * (far + CHUNK) + p, [(ahead, (o, p)) for o in range(OWN)])
@@ -81,8 +114,8 @@
     lax.fori_loop(0, far, enter_ends, 0)
 
     def enter_slabs(p, _):
-        for s in range(4):
-            enter(far + 8 * s + p, [(slabs, (s, o, p)) for o in range(OWN)])
+        for m, piece in enumerate((piece_0, piece_1, piece_2, piece_3)):
+            enter(far + 8 * (place[1] ^ m) + p, [(piece, (o, p)) for o in range(OWN)])
         return 0
 
     lax.fori_loop(0, 8, enter_slabs, 0)
@@ -136,11 +169,11 @@
     def outside(target, shift, count):
         blank = jnp.zeros((count, 8 + 2 * EXT, 8, NZ), F32)
 
-        @pl.when(chunk[0] == 0)
+        @pl.when(place[0] == 0)
         def _():
             target[shift - count : shift] = blank
 
-        @pl.when(chunk[0] == NX // CHUNK - 1)
+        @pl.when(place[0] == NX // CHUNK - 1)
         def _():
             target[shift + CHUNK : shift + CHUNK + count] = blank
 
@@ -276,17 +309,20 @@
 
     shift = [(d, d + 4 if d % 4 >= 2 else d - 4) for d in range(4 * count)]
     beyond = lax.ppermute(potential, dom, [(i, j) for i, j in shift if 0 <= j < 4 * count])
-    slabs = lax.all_to_all(orbitals.reshape(4, OWN, 8, NY, NZ), ("u", "c"), 0, 0, tiled=True)
+    group = lax.axis_index(("u", "c"))
+    pieces = {0: lax.dynamic_slice_in_dim(orbitals, OWN * group, OWN, 0)}
+    for m in (2, 3, 1):
+        piece = lax.dynamic_slice_in_dim(orbitals, OWN * (group ^ m), OWN, 0)
+        pieces[m] = lax.ppermute(piece, ("u", "c"), [(i, i ^ m) for i in range(4)])
     (weights,) = call(weights_kernel, [(256, 256)])(coefficients)
-    slabs, beyond, weights = lax.optimization_barrier((slabs, beyond, weights))
+    pieces, beyond, weights = lax.optimization_barrier(([pieces[m] for m in range(4)], beyond, weights))
     far = 3 * WIDTH
-    part = far - 16
     chunk = lax.axis_index(chunks)
-    first = jnp.concatenate([slabs[0], slabs[1], slabs[2, :, :part]], axis=1)
-    last = jnp.concatenate([slabs[1, :, 8 - part :], slabs[2], slabs[3]], axis=1)
+    place = jnp.stack([chunk, group])
+    ahead, behind = call(edges_kernel, [(OWN, far, NY, NZ)] * 2)(place, *pieces)
     swaps = [[(i, j) for k in range(s, count - 1, 2) for i, j in ((k, k + 1), (k + 1, k))] for s in (1, 0)]
-    ahead = lax.ppermute(jnp.where(chunk % 2 == 1, last, first), chunks, swaps[0])
-    behind = lax.ppermute(jnp.where(chunk % 2 == 1, first, last), chunks, swaps[1])
+    ahead = lax.ppermute(ahead, chunks, swaps[0])
+    behind = lax.ppermute(behind, chunks, swaps[1])
     own = lax.all_gather(potential, ("u", "c"))
     beyond = lax.all_gather(beyond, ("u", "c"))
 
@@ -300,7 +336,7 @@
     ]
     bands = jnp.asarray(banded(1.0 / HALF))
     (message,) = call(filter_kernel, [(4, 2, 32, 8, 128)], scratch)(
-        chunk.reshape(1), slabs, ahead, behind, own, beyond, bands
+        place, *pieces, ahead, behind, own, beyond, bands
     )
     ring = lax.all_to_all(message.reshape(8, 256, 128), ("u", "c", "b"), 0, 0, tiled=True)
     (rotated,) = call(rotate_kernel, [(4, 2, 8, 9, 4, 128)])(ring, weights)

time: 123 us -> 121 us (0.984); the launches traced: 121 us -> 121 us
  waiting for transfers between devices: 9.69 us -> 7.8 us
  starting transfers between devices: 15.2 us -> 13.6 us
  Pallas kernels: 15.8 us -> 17.1 us
    all_to_all x1 -> x0, waiting for transfers between devices: 6.67 us -> none  [local(): lax.all_to_all(orbitals.reshape(4, OWN, 8, NY, NZ), ('u', 'c'), 0, 0, til...]
    ppermute x2 -> x5, waiting for transfers between devices: 0.14 us -> 5.03 us  [the longest x3 5.03 us: local(): pieces[m] = lax.ppermute(piece, ('u', 'c'), [(i, i ^ m) for i in range(4)])]
    all_to_all x1 -> x0, starting transfers between devices: 3.66 us -> none  [local(): lax.all_to_all(orbitals.reshape(4, OWN, 8, NY, NZ), ('u', 'c'), 0, 0, til...]
    ppermute x2 -> x5, starting transfers between devices: 5.11 us -> 7.21 us  [the longest x1 4.21 us: local(): ahead = lax.ppermute(ahead, chunks, swaps[0])]
    pallas_call x4 -> x5, Pallas kernels: 15.8 us -> 17.1 us  [call(): pl.pallas_call(kernel, out_shape=[jax.ShapeDtypeStruct(s, F32) for s in o...]
    dynamic_slice x0 -> x1, local copies, waits for them, and re-layouts: none -> 1.29 us  [local(): piece = lax.dynamic_slice_in_dim(orbitals, OWN * (group ^ m), OWN, 0)]
  transfers between devices with their start and end apart: 7 -> 9, of which waited for: 4 -> 3; matrix products, arithmetic and copies ran while one was open for 0% -> 0% of each run, Pallas kernels for 2% -> 2%
where the time goes in v12:
time: 121 us
  blocking collectives  79.3 us (66%)
  Pallas kernels  17.1 us (14%)
  starting transfers between devices  13.6 us (11%)
  waiting for transfers between devices  7.8 us (6%)
  local copies, waits for them, and re-layouts  1.38 us (1%)
    all_to_all x1, blocking collectives, local(): lax.all_to_all(rotated.reshape(64, 9, 4, 128), ('z', 'x', 'u', 'c', 'b'),...  45.7 us
    all_to_all x1, blocking collectives, local(): lax.all_to_all(message.reshape(8, 256, 128), ('u', 'c', 'b'), 0, 0, tiled...  19.1 us
    pallas_call x5, Pallas kernels, call(): pl.pallas_call(kernel, out_shape=[jax.ShapeDtypeStruct(s, F32) for s in o...  17.1 us
    all_gather x1, blocking collectives, local(): beyond = lax.all_gather(beyond, ('u', 'c'))  7.28 us
    all_gather x1, blocking collectives, local(): own = lax.all_gather(potential, ('u', 'c'))  7.24 us
    ppermute x3, waiting for transfers between devices, local(): pieces[m] = lax.ppermute(piece, ('u', 'c'), [(i, i ^ m) for i in range(4)])  5.03 us
    ppermute x1, starting transfers between devices, local(): ahead = lax.ppermute(ahead, chunks, swaps[0])  4.21 us
    ppermute x1, starting transfers between devices, local(): lax.ppermute(potential, dom, [(i, j) for i, j in shift if 0 <= j < 4 * co...  4.2 us
  transfers between devices with their start and end apart: 9, of which 3 were waited for; matrix products, arithmetic and copies ran while one was open for 0% of the time, Pallas kernels for 2%

profile of v12, /device:TPU:32, one launch (start us, length us, event | category | flops | bytes accessed | tf_op | source)
XLA Modules:
  0.0 120.8 jit_solution(9843705432337965567)
XLA Ops:
  0.7 1.3 %constant_dynamic-slice_fusion = (f32[2,8,32,128]{3,2,1,0:T(8,128)S(1)}, f32[2,8,32,128]{3,2,1,0:T(8,128)S(1)}, f32[2,8,32,128]{3,2,1,0:T(8,128)S(1)}, f32[2,8,32,128]{3,2,1,0:T(8,128)S(1)}) fusion(f32[8,8,32,128]{3,2,1,0:T(8,128)} %param.4, s32[]{:T(128)S(6)} %select_n.15, s32[]{:T(128)S(6)} %select_n.13, s32[]{:T(128)S(6)} %select_n.12, s32[]{:T(128)S(6)} %select_n.14), kind=kLoop, calls=%fused_computation.3 | loop fusion | bytes 2097168 | tf_op jit(solution)/shard_map/dynamic_slice | solution.py:315
  2.0 1.1 collective-permute-start.2
  3.1 0.7 collective-permute-start
  3.8 0.4 collective-permute-start.1
  4.2 4.2 %collective-permute-start.3 = (f32[8,32,128]{2,1,0:T(8,128)S(1)}, f32[8,32,128]{2,1,0:T(8,128)S(1)}, u32[]{:S(2)}, u32[]{:S(2)}) collective-permute-start(f32[8,32,128]{2,1,0:T(8,128)S(1)} %copy-done.2), channel_id=1, source_target_pairs={{4,12},{6,14},{8,0},{10,2},{12,20},{14,22},{16,8},{18,10},{20,28},... | collective-permute-start | bytes 393224 | tf_op jit(solution)/shard_map/ppermute | solution.py:311
  8.4 0.8 shard_map.59.weights
  9.2 0.1 pad_add_fusion.place
  9.3 2.0 %collective-permute-done.3 = f32[8,32,128]{2,1,0:T(8,128)S(1)} collective-permute-done((f32[8,32,128]{2,1,0:T(8,128)S(1)}, f32[8,32,128]{2,1,0:T(8,128)S(1)}, u32[]{:S(2)}, u32[]{:S(2)}) %collective-permute-start.3) | collective-permute-done | bytes 131104 | tf_op jit(solution)/shard_map/ppermute | solution.py:311
  11.3 5.0 %collective-permute-done.1.piece_2 = f32[2,8,32,128]{3,2,1,0:T(8,128)S(1)} collective-permute-done((f32[2,8,32,128]{3,2,1,0:T(8,128)S(1)}, f32[2,8,32,128]{3,2,1,0:T(8,128)S(1)}, u32[]{:S(2)}, u32[]{:S(2)}) %collective-permute-start.1) | collective-permute-done | bytes 262176 | tf_op jit(solution)/shard_map/ppermute | solution.py:316
  16.3 0.7 shard_map.60
  17.0 4.2 %collective-permute-start.4 = (f32[2,18,32,128]{3,2,1,0:T(8,128)S(1)}, f32[2,18,32,128]{3,2,1,0:T(8,128)S(1)}, u32[]{:S(2)}, u32[]{:S(2)}) collective-permute-start(f32[2,18,32,128]{3,2,1,0:T(8,128)S(1)} %get-tuple-element.14), channel_id=1, source_target_pairs={{8,16},{16,8},{24,32},{32,24},{40,48},{48,40},{56,64},{64,56},{72,... | collective-permute-start | bytes 1769480 | tf_op jit(solution)/shard_map/ppermute | solution.py:324
  21.2 0.8 collective-permute-start.5
  22.0 7.2 %all-gather = f32[32,32,128]{2,1,0:T(8,128)S(1)} all-gather(f32[8,32,128]{2,1,0:T(8,128)S(1)} %copy-done.2), channel_id=2, replica_groups=mesh['z'=8,'x'=4,'u'=2,'c'=2,'b'=2] {'u','c'}, dimensions={0}, use_global_device_ids=true | all-gather | bytes 655360 | tf_op jit(solution)/shard_map/all_gather | solution.py:326
  29.2 7.3 %all-gather.1 = f32[32,32,128]{2,1,0:T(8,128)S(1)} all-gather(f32[8,32,128]{2,1,0:T(8,128)S(1)} %collective-permute-done.3), channel_id=3, replica_groups=mesh['z'=8,'x'=4,'u'=2,'c'=2,'b'=2] {'u','c'}, dimensions={0}, use_global_device_ids=true | all-gather | bytes 655360 | tf_op jit(solution)/shard_map/all_gather | solution.py:327
  36.5 12.4 %shard_map.61 = f32[4,2,32,8,128]{4,3,2,1,0:T(8,128)S(1)} custom-call(s32[2]{0:T(128)S(1)} %pad_add_fusion.place, f32[2,8,32,128]{3,2,1,0:T(8,128)S(1)} %get-tuple-element.10.piece_0, f32[2,8,32,128]{3,2,1,0:T(8,128)S(1)} %collective-permute-done.piece_1, f32[2,8,32,128]{3,2,1,0:T(8,128)S(1)} %collective-permute-done.1.piece_2, ...), custom_call_target="tpu_custom_call" | custom-call | tf_op jit(solution)/shard_map/pallas_call | solution.py:282
  48.9 19.1 %all_to_all.10.ring = f32[8,256,128]{2,1,0:T(8,128)S(1)} all-to-all(f32[8,256,128]{2,1,0:T(8,128)S(1)} %bitcast.9), channel_id=1, replica_groups=mesh['z'=8,'x'=4,'u'=2,'c'=2,'b'=2] {'u','c','b'}, dimensions={0} | all-to-all | bytes 2097152 | tf_op jit(solution)/shard_map/all_to_all | solution.py:341
  68.0 1.9 %shard_map.62 = f32[4,2,8,9,4,128]{5,4,3,2,1,0:T(4,128)S(1)} custom-call(f32[8,256,128]{2,1,0:T(8,128)S(1)} %all_to_all.10.ring, f32[256,256]{1,0:T(8,128)S(1)} %shard_map.59.weights), custom_call_target="tpu_custom_call" | custom-call | tf_op jit(solution)/shard_map/pallas_call | solution.py:282
  69.9 45.7 %all_to_all.11 = f32[64,9,4,128]{3,2,1,0:T(4,128)S(1)} all-to-all(f32[64,9,4,128]{3,2,1,0:T(4,128)S(1)} %bitcast.8), channel_id=1, replica_groups={{0,32,64,96,128,160,192,224,1,33,65,97,129,161,193,225,8,40,72,104,136,..., dimensions={0} | all-to-all | bytes 2359296 | tf_op jit(solution)/shard_map/all_to_all | solution.py:345
  115.7 0.1 collective-permute-start.8
  115.8 0.6 collective-permute-start.7
  116.5 1.5 %collective-permute-start.6 = (f32[4,128]{1,0:T(4,128)S(1)}, f32[4,128]{1,0:T(4,128)S(1)}, u32[]{:S(2)}, u32[]{:S(2)}) collective-permute-start(f32[4,128]{1,0:T(4,128)S(1)} %slice_reduce_fusion), channel_id=1, source_target_pairs={{0,4},{2,6},{4,0},{6,2},{1,5},{3,7},{5,1},{7,3},{8,12},{10,14},{12... | collective-permute-start | bytes 6152 | tf_op jit(solution)/shard_map/ppermute | solution.py:296
  118.0 1.3 %shard_map.63 = f32[8,32,1024]{2,1,0:T(8,128)} custom-call(f32[4,2,8,9,4,128]{5,4,3,2,1,0:T(4,128)S(1)} %bitcast.7), custom_call_target="tpu_custom_call" | custom-call | tf_op jit(solution)/shard_map/pallas_call | solution.py:282
  119.3 0.8 collective-permute-done.6
  120.2 0.6 pad_maximum_fusion
  (15 shorter events, 0.2 us)
Async XLA Ops:
  0.6 3.6 %copy-start.2 = (f32[8,32,128]{2,1,0:T(8,128)S(1)}, f32[8,32,128]{2,1,0:T(8,128)}, u32[]{:S(2)}) copy-start(f32[8,32,128]{2,1,0:T(8,128)} %param.5) | copy-start | bytes 393220
  0.6 7.8 %copy-start.1 = (f32[16,16]{1,0:T(8,128)S(1)}, f32[16,16]{1,0:T(8,128)}, u32[]{:S(2)}) copy-start(f32[16,16]{1,0:T(8,128)} %coefficients.1) | copy-start | bytes 3076
  2.0 9.3 %collective-permute-start.2 = (f32[2,8,32,128]{3,2,1,0:T(8,128)S(1)}, f32[2,8,32,128]{3,2,1,0:T(8,128)S(1)}, u32[]{:S(2)}, u32[]{:S(2)}) collective-permute-start(f32[2,8,32,128]{3,2,1,0:T(8,128)S(1)} %get-tuple-element.18), channel_id=1, source_target_pairs={{0,6},{2,4},{4,2},{6,0},{1,7},{3,5},{5,3},{7,1},{8,14},{10,12},{12... | collective-permute-start | bytes 786440 | tf_op jit(solution)/shard_map/ppermute | solution.py:316
  3.1 8.2 %collective-permute-start = (f32[2,8,32,128]{3,2,1,0:T(8,128)S(1)}, f32[2,8,32,128]{3,2,1,0:T(8,128)S(1)}, u32[]{:S(2)}, u32[]{:S(2)}) collective-permute-start(f32[2,8,32,128]{3,2,1,0:T(8,128)S(1)} %get-tuple-element.19), channel_id=1, source_target_pairs={{0,2},{2,0},{4,6},{6,4},{1,3},{3,1},{5,7},{7,5},{8,10},{10,8},{12,... | collective-permute-start | bytes 786440 | tf_op jit(solution)/shard_map/ppermute | solution.py:316
  3.8 12.5 %collective-permute-start.1 = (f32[2,8,32,128]{3,2,1,0:T(8,128)S(1)}, f32[2,8,32,128]{3,2,1,0:T(8,128)S(1)}, u32[]{:S(2)}, u32[]{:S(2)}) collective-permute-start(f32[2,8,32,128]{3,2,1,0:T(8,128)S(1)} %get-tuple-element.21), channel_id=1, source_target_pairs={{0,4},{2,6},{4,0},{6,2},{1,5},{3,7},{5,1},{7,3},{8,12},{10,14},{12... | collective-permute-start | bytes 786440 | tf_op jit(solution)/shard_map/ppermute | solution.py:316
  4.2 7.0 %collective-permute-start.3 = (f32[8,32,128]{2,1,0:T(8,128)S(1)}, f32[8,32,128]{2,1,0:T(8,128)S(1)}, u32[]{:S(2)}, u32[]{:S(2)}) collective-permute-start(f32[8,32,128]{2,1,0:T(8,128)S(1)} %copy-done.2), channel_id=1, source_target_pairs={{4,12},{6,14},{8,0},{10,2},{12,20},{14,22},{16,8},{18,10},{20,28},... | collective-permute-start | bytes 393224 | tf_op jit(solution)/shard_map/ppermute | solution.py:311
  16.3 20.2 %copy-start = (bf16[256,256]{1,0:T(8,128)(2,1)S(1)}, bf16[256,256]{1,0:T(8,128)(2,1)}, u32[]{:S(2)}) copy-start(bf16[256,256]{1,0:T(8,128)(2,1)} %constant.36.clone.bands) | copy-start | bytes 393220
  17.0 19.5 %collective-permute-start.4 = (f32[2,18,32,128]{3,2,1,0:T(8,128)S(1)}, f32[2,18,32,128]{3,2,1,0:T(8,128)S(1)}, u32[]{:S(2)}, u32[]{:S(2)}) collective-permute-start(f32[2,18,32,128]{3,2,1,0:T(8,128)S(1)} %get-tuple-element.14), channel_id=1, source_target_pairs={{8,16},{16,8},{24,32},{32,24},{40,48},{48,40},{56,64},{64,56},{72,... | collective-permute-start | bytes 1769480 | tf_op jit(solution)/shard_map/ppermute | solution.py:324
  21.2 15.3 %collective-permute-start.5 = (f32[2,18,32,128]{3,2,1,0:T(8,128)S(1)}, f32[2,18,32,128]{3,2,1,0:T(8,128)S(1)}, u32[]{:S(2)}, u32[]{:S(2)}) collective-permute-start(f32[2,18,32,128]{3,2,1,0:T(8,128)S(1)} %get-tuple-element.15), channel_id=1, source_target_pairs={{0,8},{8,0},{16,24},{24,16},{32,40},{40,32},{48,56},{56,48},{64,72... | collective-permute-start | bytes 1769480 | tf_op jit(solution)/shard_map/ppermute | solution.py:325
  115.7 3.5 %collective-permute-start.8 = (f32[4,128]{1,0:T(4,128)S(1)}, f32[4,128]{1,0:T(4,128)S(1)}, u32[]{:S(2)}, u32[]{:S(2)}) collective-permute-start(f32[4,128]{1,0:T(4,128)S(1)} %slice_reduce_fusion), channel_id=1, source_target_pairs={{0,6},{2,4},{4,2},{6,0},{1,7},{3,5},{5,3},{7,1},{8,14},{10,12},{12... | collective-permute-start | bytes 6152 | tf_op jit(solution)/shard_map/ppermute | solution.py:296
  115.8 3.4 %collective-permute-start.7 = (f32[4,128]{1,0:T(4,128)S(1)}, f32[4,128]{1,0:T(4,128)S(1)}, u32[]{:S(2)}, u32[]{:S(2)}) collective-permute-start(f32[4,128]{1,0:T(4,128)S(1)} %slice_reduce_fusion), channel_id=1, source_target_pairs={{0,2},{2,0},{4,6},{6,4},{1,3},{3,1},{5,7},{7,5},{8,10},{10,8},{12,... | collective-permute-start | bytes 6152 | tf_op jit(solution)/shard_map/ppermute | solution.py:296
  116.5 3.6 %collective-permute-start.6 = (f32[4,128]{1,0:T(4,128)S(1)}, f32[4,128]{1,0:T(4,128)S(1)}, u32[]{:S(2)}, u32[]{:S(2)}) collective-permute-start(f32[4,128]{1,0:T(4,128)S(1)} %slice_reduce_fusion), channel_id=1, source_target_pairs={{0,4},{2,6},{4,0},{6,2},{1,5},{3,7},{5,1},{7,3},{8,12},{10,14},{12... | collective-permute-start | bytes 6152 | tf_op jit(solution)/shard_map/ppermute | solution.py:296

commit v13 on v12

--- a/solution.py
+++ b/solution.py
@@ -98,34 +98,37 @@
         rows = [jnp.concatenate([source[(*at, pl.ds(r, 4, stride=8), slice(None))] for source, at in sources], axis=0) for r in range(8)]
         return jnp.stack(rows)
 
-    def enter(plane, sources):
-        value = tiles(sources)
-        field[plane, EXT : EXT + 8] = value
-        field[plane, 0:EXT] = jnp.where(row[:EXT] == 0, 0.0, pltpu.roll(value[8 - EXT :], 1, 1))
-        field[plane, EXT + 8 :] = jnp.where(row[:EXT] == 3, 0.0, pltpu.roll(value[:EXT], 7, 1))
+    def enter(*entries):
+        values = [tiles(sources) for _, sources in entries]
+        for (plane, _), value in zip(entries, values):
+            field[plane, EXT : EXT + 8] = value
+            field[plane, 0:EXT] = jnp.where(row[:EXT] == 0, 0.0, pltpu.roll(value[8 - EXT :], 1, 1))
+            field[plane, EXT + 8 :] = jnp.where(row[:EXT] == 3, 0.0, pltpu.roll(value[:EXT], 7, 1))
 
     odd = place[0] % 2
 
     def enter_ends(p, _):
-        enter(odd * (far + CHUNK) + p, [(ahead, (o, p)) for o in range(OWN)])
-        enter((1 - odd) * (far + CHUNK) + p, [(behind, (o, p)) for o in range(OWN)])
+        enter(
+            (odd * (far + CHUNK) + p, [(ahead, (o, p)) for o in range(OWN)]),
+            ((1 - odd) * (far + CHUNK) + p, [(behind, (o, p)) for o in range(OWN)]),
+        )
         return 0
 
     lax.fori_loop(0, far, enter_ends, 0)
 
     def enter_slabs(p, _):
-        for m, piece in enumerate((piece_0, piece_1, piece_2, piece_3)):
-            enter(far + 8 * (place[1] ^ m) + p, [(piece, (o, p)) for o in range(OWN)])
+        for pair in (((0, piece_0), (1, piece_1)), ((2, piece_2), (3, piece_3))):
+            enter(*[(far + 8 * (place[1] ^ m) + p, [(piece, (o, p)) for o in range(OWN)]) for m, piece in pair])
         return 0
 
     lax.fori_loop(0, 8, enter_slabs, 0)
 
     def enter_local(p, _):
-        for j, (source, s) in enumerate(
-            [(beyond, 2), (beyond, 3), (own, 0), (own, 1), (own, 2), (own, 3), (beyond, 0), (beyond, 1)]
-        ):
-            value = tiles([(source, (s, p)), (source, (s, p))])
-            local[8 * j + p] = (value + (-1.5 * STENCIL[0] - CENTER)) * (1.0 / HALF)
+        order = [(beyond, 2), (beyond, 3), (own, 0), (own, 1), (own, 2), (own, 3), (beyond, 0), (beyond, 1)]
+        for j in (0, 4):
+            values = [tiles([(source, (s, p)), (source, (s, p))]) for source, s in order[j : j + 4]]
+            for i, value in enumerate(values):
+                local[8 * (j + i) + p] = (value + (-1.5 * STENCIL[0] - CENTER)) * (1.0 / HALF)
         return 0
 
     lax.fori_loop(0, 8, enter_local, 0)
@@ -135,36 +138,50 @@
         both = jnp.dot(jnp.concatenate([high, low], axis=1), bands[...], preferred_element_type=F32)
         return (both[:, :NZ] + both[:, NZ:]).reshape(4, 8, 8, NZ)
 
-    def step(source, shift, first, blocks, put):
+    def step(source, shift, first, blocks, finish, put):
+        def row_of(i, start, r):
+            window = source[pl.ds(start + shift - WIDTH, 8 + 2 * WIDTH), EXT + r]
+            total = local[pl.ds(start + 16, 8), r] * window[WIDTH : WIDTH + 8] + z[i, :, r]
+            for k in range(1, 7):
+                beside = window[WIDTH + k : WIDTH + 8 + k] + window[WIDTH - k : WIDTH + 8 - k]
+                planes = pl.ds(start + shift, 8)
+                beside = beside + (source[planes, EXT + r + k] + source[planes, EXT + r - k])
+                total = total + (-0.5 / HALF * STENCIL[k]) * beside
+            return finish(start, r, total)
+
         def body(i, _):
             start = first + 8 * i
             later = first + 8 * jnp.minimum(i + 1, blocks - 1) + shift
+            last = None
             for half in range(2):
-                ahead = along_z(source, later + 4 * half)
+                next_z = along_z(source, later + 4 * half)
                 for r in range(4 * half, 4 * half + 4):
-                    window = source[pl.ds(start + shift - WIDTH, 8 + 2 * WIDTH), EXT + r]
-                    total = local[pl.ds(start + 16, 8), r] * window[WIDTH : WIDTH + 8] + z[i, :, r]
-                    for k in range(1, 7):
-                        beside = window[WIDTH + k : WIDTH + 8 + k] + window[WIDTH - k : WIDTH + 8 - k]
-                        planes = pl.ds(start + shift, 8)
-                        beside = beside + (source[planes, EXT + r + k] + source[planes, EXT + r - k])
-                        total = total + (-0.5 / HALF * STENCIL[k]) * beside
-                    put(start, r, total)
-                z[i + 1, 4 * half : 4 * half + 4] = ahead
+                    value = row_of(i, start, r)
+                    if last is not None:
+                        put(start, r - 1, last)
+                    last = value
+                z[i + 1, 4 * half : 4 * half + 4] = next_z
+            put(start, 7, last)
             return 0
 
         for half in range(2):
             z[0, 4 * half : 4 * half + 4] = along_z(source, first + shift + 4 * half)
         lax.fori_loop(0, blocks, body, 0)
 
-    def put_first(start, r, total):
-        store(other, start + near, r, total)
-
-    def put_second(start, r, total):
-        store(field, start + far, r, (total + total) - field[pl.ds(start + far, 8), EXT + r])
-
-    def put_third(start, r, total):
-        result[pl.ds(start, 8), r] = (total + total) - other[pl.ds(start + near, 8), EXT + r]
+    def put_first(start, r, value):
+        store(other, start + near, r, value)
+
+    def finish_second(start, r, total):
+        return (total + total) - field[pl.ds(start + far, 8), EXT + r]
+
+    def put_second(start, r, value):
+        store(field, start + far, r, value)
+
+    def finish_third(start, r, total):
+        return (total + total) - other[pl.ds(start + near, 8), EXT + r]
+
+    def put_third(start, r, value):
+        result[pl.ds(start, 8), r] = value
 
     def outside(target, shift, count):
         blank = jnp.zeros((count, 8 + 2 * EXT, 8, NZ), F32)
@@ -177,27 +194,30 @@
         def _():
             target[shift + CHUNK : shift + CHUNK + count] = blank
 
-    step(field, far, -12, 7, put_first)
+    step(field, far, -12, 7, lambda start, r, total: total, put_first)
     outside(other, near, 12)
-    step(other, near, -8, 6, put_second)
+    step(other, near, -8, 6, finish_second, put_second)
     outside(field, far, 8)
-    step(field, far, 0, 4, put_third)
+    step(field, far, 0, 4, finish_third, put_third)
 
     def turn(x, _):
+        blocks = [
+            jnp.concatenate([result[t * 8 + x, b * 4 + r] for t in range(4) for r in range(4)], axis=0) for b in range(2)
+        ]
         for b in range(2):
-            pieces = [result[t * 8 + x, b * 4 + r] for t in range(4) for r in range(4)]
-            turned[pl.ds((b * 8 + x) * NZ, NZ), :] = jnp.concatenate(pieces, axis=0).T
+            turned[pl.ds((b * 8 + x) * NZ, NZ), :] = blocks[b].T
         return 0
 
     lax.fori_loop(0, 8, turn, 0)
 
-    def pick(q, _):
-        for c in range(4):
-            for b in range(2):
-                out[c, b, q] = turned[pl.ds(b * 8 * NZ + 4 * q + c, 8, stride=NZ), :]
-        return 0
-
-    lax.fori_loop(0, NZ // 4, pick, 0)
+    def pick(i, _):
+        places = [(c, b, 4 * i + q) for q in range(4) for c in range(4) for b in range(2)]
+        values = [turned[pl.ds(b * 8 * NZ + 4 * q + c, 8, stride=NZ), :] for c, b, q in places]
+        for (c, b, q), value in zip(places, values):
+            out[c, b, q] = value
+        return 0
+
+    lax.fori_loop(0, NZ // 16, pick, 0)
 
 
 exact = functools.partial(lax.dot_general, precision=lax.Precision.HIGHEST, preferred_element_type=F32)
@@ -310,10 +330,15 @@
     shift = [(d, d + 4 if d % 4 >= 2 else d - 4) for d in range(4 * count)]
     beyond = lax.ppermute(potential, dom, [(i, j) for i, j in shift if 0 <= j < 4 * count])
     group = lax.axis_index(("u", "c"))
-    pieces = {0: lax.dynamic_slice_in_dim(orbitals, OWN * group, OWN, 0)}
+    pieces = {}
     for m in (2, 3, 1):
+        if m == 3:
+            orbitals, piece = lax.optimization_barrier((orbitals, piece))
+            pieces[2] = lax.ppermute(piece, ("u", "c"), [(i, i ^ 2) for i in range(4)])
         piece = lax.dynamic_slice_in_dim(orbitals, OWN * (group ^ m), OWN, 0)
-        pieces[m] = lax.ppermute(piece, ("u", "c"), [(i, i ^ m) for i in range(4)])
+        if m != 2:
+            pieces[m] = lax.ppermute(piece, ("u", "c"), [(i, i ^ m) for i in range(4)])
+    pieces[0] = lax.dynamic_slice_in_dim(orbitals, OWN * group, OWN, 0)
     (weights,) = call(weights_kernel, [(256, 256)])(coefficients)
     pieces, beyond, weights = lax.optimization_barrier(([pieces[m] for m in range(4)], beyond, weights))
     far = 3 * WIDTH

time: 121 us -> 120 us (level)
  waiting for transfers between devices: 7.8 us -> 5.71 us
    ppermute x3 -> x2, waiting for transfers between devices: 5.03 us -> 2.03 us  [local(): pieces[m] = lax.ppermute(piece, ('u', 'c'), [(i, i ^ m) for i in range(4)])]
    ppermute x0 -> x1, starting transfers between devices: none -> 1.66 us  [local(): pieces[2] = lax.ppermute(piece, ('u', 'c'), [(i, i ^ 2) for i in range(4)])]
    ppermute x3 -> x2, starting transfers between devices: 2.23 us -> 0.64 us  [local(): pieces[m] = lax.ppermute(piece, ('u', 'c'), [(i, i ^ m) for i in range(4)])]
  transfers between devices with their start and end apart: 9 -> 9, of which waited for: 3 -> 4; matrix products, arithmetic and copies ran while one was open for 0% -> 1% of each run, Pallas kernels for 2% -> 2%
where the time goes in v13:
time: 120 us; the launch traced here: 119 us
  blocking collectives  79.4 us (66%)
  Pallas kernels  16.7 us (14%)
  starting transfers between devices  13.7 us (11%)
  waiting for transfers between devices  5.71 us (5%)
  local copies, waits for them, and re-layouts  2.26 us (2%)
    all_to_all x1, blocking collectives, local(): lax.all_to_all(rotated.reshape(64, 9, 4, 128), ('z', 'x', 'u', 'c', 'b'),...  45.7 us
    all_to_all x1, blocking collectives, local(): lax.all_to_all(message.reshape(8, 256, 128), ('u', 'c', 'b'), 0, 0, tiled...  19.3 us
    pallas_call x5, Pallas kernels, call(): pl.pallas_call(kernel, out_shape=[jax.ShapeDtypeStruct(s, F32) for s in o...  16.7 us
    all_gather x1, blocking collectives, local(): beyond = lax.all_gather(beyond, ('u', 'c'))  7.28 us
    all_gather x1, blocking collectives, local(): own = lax.all_gather(potential, ('u', 'c'))  7.09 us
    ppermute x1, starting transfers between devices, local(): ahead = lax.ppermute(ahead, chunks, swaps[0])  4.31 us
    ppermute x1, starting transfers between devices, local(): lax.ppermute(potential, dom, [(i, j) for i, j in shift if 0 <= j < 4 * co...  4.2 us
  transfers between devices with their start and end apart: 9, of which 4 were waited for; matrix products, arithmetic and copies ran while one was open for 1% of the time, Pallas kernels for 2%

profile of v13, /device:TPU:32, one launch (start us, length us, event | category | flops | bytes accessed | tf_op | source)
XLA Modules:
  0.0 119.3 jit_solution(1786223220311562836)
XLA Ops:
  0.7 1.0 constant_dynamic-slice_fusion.3
  1.7 1.7 %collective-permute-start.1 = (f32[2,8,32,128]{3,2,1,0:T(8,128)S(1)}, f32[2,8,32,128]{3,2,1,0:T(8,128)S(1)}, u32[]{:S(2)}, u32[]{:S(2)}) collective-permute-start(f32[2,8,32,128]{3,2,1,0:T(8,128)S(1)} %constant_dynamic-slice_fusion.3), channel_id=1, source_target_pairs={{0,4},{2,6},{4,0},{6,2},{1,5},{3,7},{5,1},{7,3},{8,12},{10,14},{12... | collective-permute-start | bytes 786440 | tf_op jit(solution)/shard_map/ppermute | solution.py:337
  3.3 1.2 constant_dynamic-slice_fusion
  4.5 0.1 collective-permute-start.2
  4.6 0.6 collective-permute-start
  5.2 4.2 %collective-permute-start.3 = (f32[8,32,128]{2,1,0:T(8,128)S(1)}, f32[8,32,128]{2,1,0:T(8,128)S(1)}, u32[]{:S(2)}, u32[]{:S(2)}) collective-permute-start(f32[8,32,128]{2,1,0:T(8,128)S(1)} %copy-done.2), channel_id=1, source_target_pairs={{4,12},{6,14},{8,0},{10,2},{12,20},{14,22},{16,8},{18,10},{20,28},... | collective-permute-start | bytes 393224 | tf_op jit(solution)/shard_map/ppermute | solution.py:331
  9.4 0.8 shard_map.59.weights
  10.2 2.3 %collective-permute-done.3 = f32[8,32,128]{2,1,0:T(8,128)S(1)} collective-permute-done((f32[8,32,128]{2,1,0:T(8,128)S(1)}, f32[8,32,128]{2,1,0:T(8,128)S(1)}, u32[]{:S(2)}, u32[]{:S(2)}) %collective-permute-start.3) | collective-permute-done | bytes 131104 | tf_op jit(solution)/shard_map/ppermute | solution.py:331
  12.5 2.0 %collective-permute-done.2.piece_3 = f32[2,8,32,128]{3,2,1,0:T(8,128)S(1)} collective-permute-done((f32[2,8,32,128]{3,2,1,0:T(8,128)S(1)}, f32[2,8,32,128]{3,2,1,0:T(8,128)S(1)}, u32[]{:S(2)}, u32[]{:S(2)}) %collective-permute-start.2) | collective-permute-done | bytes 262176 | tf_op jit(solution)/shard_map/ppermute | solution.py:340
  14.5 0.7 shard_map.60
  15.3 4.3 %collective-permute-start.4 = (f32[2,18,32,128]{3,2,1,0:T(8,128)S(1)}, f32[2,18,32,128]{3,2,1,0:T(8,128)S(1)}, u32[]{:S(2)}, u32[]{:S(2)}) collective-permute-start(f32[2,18,32,128]{3,2,1,0:T(8,128)S(1)} %get-tuple-element.18), channel_id=1, source_target_pairs={{8,16},{16,8},{24,32},{32,24},{40,48},{48,40},{56,64},{64,56},{72,... | collective-permute-start | bytes 1769480 | tf_op jit(solution)/shard_map/ppermute | solution.py:349
  19.6 0.7 collective-permute-start.5
  20.2 7.1 %all-gather = f32[32,32,128]{2,1,0:T(8,128)S(1)} all-gather(f32[8,32,128]{2,1,0:T(8,128)S(1)} %copy-done.2), channel_id=2, replica_groups=mesh['z'=8,'x'=4,'u'=2,'c'=2,'b'=2] {'u','c'}, dimensions={0}, use_global_device_ids=true | all-gather | bytes 655360 | tf_op jit(solution)/shard_map/all_gather | solution.py:351
  27.3 7.3 %all-gather.1 = f32[32,32,128]{2,1,0:T(8,128)S(1)} all-gather(f32[8,32,128]{2,1,0:T(8,128)S(1)} %collective-permute-done.3), channel_id=3, replica_groups=mesh['z'=8,'x'=4,'u'=2,'c'=2,'b'=2] {'u','c'}, dimensions={0}, use_global_device_ids=true | all-gather | bytes 655360 | tf_op jit(solution)/shard_map/all_gather | solution.py:352
  34.6 0.6 collective-permute-done.4.ahead
  35.2 12.0 %shard_map.61 = f32[4,2,32,8,128]{4,3,2,1,0:T(8,128)S(1)} custom-call(s32[2]{0:T(128)S(1)} %pad_add_fusion.place, f32[2,8,32,128]{3,2,1,0:T(8,128)S(1)} %get-tuple-element.14.piece_0, f32[2,8,32,128]{3,2,1,0:T(8,128)S(1)} %collective-permute-done.piece_1, f32[2,8,32,128]{3,2,1,0:T(8,128)S(1)} %collective-permute-done.1.piece_2, ...), custom_call_target="tpu_custom_call" | custom-call | tf_op jit(solution)/shard_map/pallas_call | solution.py:302
  47.2 19.3 %all_to_all.10.ring = f32[8,256,128]{2,1,0:T(8,128)S(1)} all-to-all(f32[8,256,128]{2,1,0:T(8,128)S(1)} %bitcast.9), channel_id=1, replica_groups=mesh['z'=8,'x'=4,'u'=2,'c'=2,'b'=2] {'u','c','b'}, dimensions={0} | all-to-all | bytes 2097152 | tf_op jit(solution)/shard_map/all_to_all | solution.py:366
  66.5 1.9 %shard_map.62 = f32[4,2,8,9,4,128]{5,4,3,2,1,0:T(4,128)S(1)} custom-call(f32[8,256,128]{2,1,0:T(8,128)S(1)} %all_to_all.10.ring, f32[256,256]{1,0:T(8,128)S(1)} %shard_map.59.weights), custom_call_target="tpu_custom_call" | custom-call | tf_op jit(solution)/shard_map/pallas_call | solution.py:302
  68.4 45.7 %all_to_all.11 = f32[64,9,4,128]{3,2,1,0:T(4,128)S(1)} all-to-all(f32[64,9,4,128]{3,2,1,0:T(4,128)S(1)} %bitcast.8), channel_id=1, replica_groups={{0,32,64,96,128,160,192,224,1,33,65,97,129,161,193,225,8,40,72,104,136,..., dimensions={0} | all-to-all | bytes 2359296 | tf_op jit(solution)/shard_map/all_to_all | solution.py:370
  114.3 0.6 collective-permute-start.7
  115.0 1.5 %collective-permute-start.6 = (f32[4,128]{1,0:T(4,128)S(1)}, f32[4,128]{1,0:T(4,128)S(1)}, u32[]{:S(2)}, u32[]{:S(2)}) collective-permute-start(f32[4,128]{1,0:T(4,128)S(1)} %slice_reduce_fusion), channel_id=1, source_target_pairs={{0,4},{2,6},{4,0},{6,2},{1,5},{3,7},{5,1},{7,3},{8,12},{10,14},{12... | collective-permute-start | bytes 6152 | tf_op jit(solution)/shard_map/ppermute | solution.py:316
  116.5 1.3 %shard_map.63 = f32[8,32,1024]{2,1,0:T(8,128)} custom-call(f32[4,2,8,9,4,128]{5,4,3,2,1,0:T(4,128)S(1)} %bitcast.7), custom_call_target="tpu_custom_call" | custom-call | tf_op jit(solution)/shard_map/pallas_call | solution.py:302
  117.8 0.8 collective-permute-done.6
  118.6 0.6 pad_maximum_fusion
  (16 shorter events, 0.4 us)
Async XLA Ops:
  0.6 4.5 %copy-start.2 = (f32[8,32,128]{2,1,0:T(8,128)S(1)}, f32[8,32,128]{2,1,0:T(8,128)}, u32[]{:S(2)}) copy-start(f32[8,32,128]{2,1,0:T(8,128)} %param.5) | copy-start | bytes 393220
  0.6 8.7 %copy-start.1 = (f32[16,16]{1,0:T(8,128)S(1)}, f32[16,16]{1,0:T(8,128)}, u32[]{:S(2)}) copy-start(f32[16,16]{1,0:T(8,128)} %coefficients.1) | copy-start | bytes 3076
  1.7 10.8 %collective-permute-start.1 = (f32[2,8,32,128]{3,2,1,0:T(8,128)S(1)}, f32[2,8,32,128]{3,2,1,0:T(8,128)S(1)}, u32[]{:S(2)}, u32[]{:S(2)}) collective-permute-start(f32[2,8,32,128]{3,2,1,0:T(8,128)S(1)} %constant_dynamic-slice_fusion.3), channel_id=1, source_target_pairs={{0,4},{2,6},{4,0},{6,2},{1,5},{3,7},{5,1},{7,3},{8,12},{10,14},{12... | collective-permute-start | bytes 786440 | tf_op jit(solution)/shard_map/ppermute | solution.py:337
  4.5 10.0 %collective-permute-start.2 = (f32[2,8,32,128]{3,2,1,0:T(8,128)S(1)}, f32[2,8,32,128]{3,2,1,0:T(8,128)S(1)}, u32[]{:S(2)}, u32[]{:S(2)}) collective-permute-start(f32[2,8,32,128]{3,2,1,0:T(8,128)S(1)} %get-tuple-element.22), channel_id=1, source_target_pairs={{0,6},{2,4},{4,2},{6,0},{1,7},{3,5},{5,3},{7,1},{8,14},{10,12},{12... | collective-permute-start | bytes 786440 | tf_op jit(solution)/shard_map/ppermute | solution.py:340
  4.6 9.9 %collective-permute-start = (f32[2,8,32,128]{3,2,1,0:T(8,128)S(1)}, f32[2,8,32,128]{3,2,1,0:T(8,128)S(1)}, u32[]{:S(2)}, u32[]{:S(2)}) collective-permute-start(f32[2,8,32,128]{3,2,1,0:T(8,128)S(1)} %get-tuple-element.23), channel_id=1, source_target_pairs={{0,2},{2,0},{4,6},{6,4},{1,3},{3,1},{5,7},{7,5},{8,10},{10,8},{12,... | collective-permute-start | bytes 786440 | tf_op jit(solution)/shard_map/ppermute | solution.py:340
  5.2 7.3 %collective-permute-start.3 = (f32[8,32,128]{2,1,0:T(8,128)S(1)}, f32[8,32,128]{2,1,0:T(8,128)S(1)}, u32[]{:S(2)}, u32[]{:S(2)}) collective-permute-start(f32[8,32,128]{2,1,0:T(8,128)S(1)} %copy-done.2), channel_id=1, source_target_pairs={{4,12},{6,14},{8,0},{10,2},{12,20},{14,22},{16,8},{18,10},{20,28},... | collective-permute-start | bytes 393224 | tf_op jit(solution)/shard_map/ppermute | solution.py:331
  14.5 20.7 %copy-start = (bf16[256,256]{1,0:T(8,128)(2,1)S(1)}, bf16[256,256]{1,0:T(8,128)(2,1)}, u32[]{:S(2)}) copy-start(bf16[256,256]{1,0:T(8,128)(2,1)} %constant.36.clone.bands) | copy-start | bytes 393220
  15.3 20.0 %collective-permute-start.4 = (f32[2,18,32,128]{3,2,1,0:T(8,128)S(1)}, f32[2,18,32,128]{3,2,1,0:T(8,128)S(1)}, u32[]{:S(2)}, u32[]{:S(2)}) collective-permute-start(f32[2,18,32,128]{3,2,1,0:T(8,128)S(1)} %get-tuple-element.18), channel_id=1, source_target_pairs={{8,16},{16,8},{24,32},{32,24},{40,48},{48,40},{56,64},{64,56},{72,... | collective-permute-start | bytes 1769480 | tf_op jit(solution)/shard_map/ppermute | solution.py:349
  19.6 15.7 %collective-permute-start.5 = (f32[2,18,32,128]{3,2,1,0:T(8,128)S(1)}, f32[2,18,32,128]{3,2,1,0:T(8,128)S(1)}, u32[]{:S(2)}, u32[]{:S(2)}) collective-permute-start(f32[2,18,32,128]{3,2,1,0:T(8,128)S(1)} %get-tuple-element.19), channel_id=1, source_target_pairs={{0,8},{8,0},{16,24},{24,16},{32,40},{40,32},{48,56},{56,48},{64,72... | collective-permute-start | bytes 1769480 | tf_op jit(solution)/shard_map/ppermute | solution.py:350
  114.2 3.5 %collective-permute-start.8 = (f32[4,128]{1,0:T(4,128)S(1)}, f32[4,128]{1,0:T(4,128)S(1)}, u32[]{:S(2)}, u32[]{:S(2)}) collective-permute-start(f32[4,128]{1,0:T(4,128)S(1)} %slice_reduce_fusion), channel_id=1, source_target_pairs={{0,6},{2,4},{4,2},{6,0},{1,7},{3,5},{5,3},{7,1},{8,14},{10,12},{12... | collective-permute-start | bytes 6152 | tf_op jit(solution)/shard_map/ppermute | solution.py:316
  114.3 3.4 %collective-permute-start.7 = (f32[4,128]{1,0:T(4,128)S(1)}, f32[4,128]{1,0:T(4,128)S(1)}, u32[]{:S(2)}, u32[]{:S(2)}) collective-permute-start(f32[4,128]{1,0:T(4,128)S(1)} %slice_reduce_fusion), channel_id=1, source_target_pairs={{0,2},{2,0},{4,6},{6,4},{1,3},{3,1},{5,7},{7,5},{8,10},{10,8},{12,... | collective-permute-start | bytes 6152 | tf_op jit(solution)/shard_map/ppermute | solution.py:316
  115.0 3.6 %collective-permute-start.6 = (f32[4,128]{1,0:T(4,128)S(1)}, f32[4,128]{1,0:T(4,128)S(1)}, u32[]{:S(2)}, u32[]{:S(2)}) collective-permute-start(f32[4,128]{1,0:T(4,128)S(1)} %slice_reduce_fusion), channel_id=1, source_target_pairs={{0,4},{2,6},{4,0},{6,2},{1,5},{3,7},{5,1},{7,3},{8,12},{10,14},{12... | collective-permute-start | bytes 6152 | tf_op jit(solution)/shard_map/ppermute | solution.py:316

commit v14 on v13

--- a/solution.py
+++ b/solution.py
@@ -80,7 +80,8 @@
 
 
 def filter_kernel(
-    place, piece_0, piece_1, piece_2, piece_3, ahead, behind, own, beyond, bands,
+    place, piece_0, piece_1, piece_2, piece_3, ahead, behind,
+    own_0, own_1, own_2, own_3, beyond_0, beyond_1, beyond_2, beyond_3, bands,
     out, field, other, local, z, result, turned,
 ):
     far, near = 3 * WIDTH, 2 * WIDTH + 2
@@ -124,11 +125,11 @@
     lax.fori_loop(0, 8, enter_slabs, 0)
 
     def enter_local(p, _):
-        order = [(beyond, 2), (beyond, 3), (own, 0), (own, 1), (own, 2), (own, 3), (beyond, 0), (beyond, 1)]
-        for j in (0, 4):
-            values = [tiles([(source, (s, p)), (source, (s, p))]) for source, s in order[j : j + 4]]
-            for i, value in enumerate(values):
-                local[8 * (j + i) + p] = (value + (-1.5 * STENCIL[0] - CENTER)) * (1.0 / HALF)
+        for first, sources in ((2, (own_0, own_1, own_2, own_3)), (6, (beyond_0, beyond_1, beyond_2, beyond_3))):
+            values = [tiles([(source, (p,)), (source, (p,))]) for source in sources]
+            for m, value in enumerate(values):
+                start = 8 * ((first + (place[1] ^ m)) % 8)
+                local[start + p] = (value + (-1.5 * STENCIL[0] - CENTER)) * (1.0 / HALF)
         return 0
 
     lax.fori_loop(0, 8, enter_local, 0)
@@ -340,17 +341,22 @@
             pieces[m] = lax.ppermute(piece, ("u", "c"), [(i, i ^ m) for i in range(4)])
     pieces[0] = lax.dynamic_slice_in_dim(orbitals, OWN * group, OWN, 0)
     (weights,) = call(weights_kernel, [(256, 256)])(coefficients)
-    pieces, beyond, weights = lax.optimization_barrier(([pieces[m] for m in range(4)], beyond, weights))
+    pieces, beyond, potential, weights = lax.optimization_barrier(
+        ([pieces[m] for m in range(4)], beyond, potential, weights)
+    )
     far = 3 * WIDTH
     chunk = lax.axis_index(chunks)
     place = jnp.stack([chunk, group])
     ahead, behind = call(edges_kernel, [(OWN, far, NY, NZ)] * 2)(place, *pieces)
+    ahead, behind, beyond, potential = lax.optimization_barrier((ahead, behind, beyond, potential))
     swaps = [[(i, j) for k in range(s, count - 1, 2) for i, j in ((k, k + 1), (k + 1, k))] for s in (1, 0)]
     ahead = lax.ppermute(ahead, chunks, swaps[0])
     behind = lax.ppermute(behind, chunks, swaps[1])
-    own = lax.all_gather(potential, ("u", "c"))
-    beyond = lax.all_gather(beyond, ("u", "c"))
-
+
+    def of_group(x):
+        return [x] + [lax.ppermute(x, ("u", "c"), [(i, i ^ m) for i in range(4)]) for m in (1, 2, 3)]
+
+    own, beyond = of_group(potential), of_group(beyond)
     scratch = [
         (CHUNK + 2 * far, 8 + 2 * EXT, 8, NZ),
         (CHUNK + 2 * (2 * WIDTH + 2), 8 + 2 * EXT, 8, NZ),
@@ -361,7 +367,7 @@
     ]
     bands = jnp.asarray(banded(1.0 / HALF))
     (message,) = call(filter_kernel, [(4, 2, 32, 8, 128)], scratch)(
-        place, *pieces, ahead, behind, own, beyond, bands
+        place, *pieces, ahead, behind, *own, *beyond, bands
     )
     ring = lax.all_to_all(message.reshape(8, 256, 128), ("u", "c", "b"), 0, 0, tiled=True)
     (rotated,) = call(rotate_kernel, [(4, 2, 8, 9, 4, 128)])(ring, weights)

time: 120 us -> 120 us (level)
  blocking collectives: 79.4 us -> 65 us
  waiting for transfers between devices: 5.71 us -> 14.6 us
  starting transfers between devices: 13.7 us -> 19.1 us
    all_gather x2 -> x0, blocking collectives: 14.4 us -> none  [the longest x1 7.28 us: local(): beyond = lax.all_gather(beyond, ('u', 'c'))]
    ppermute x0 -> x6, waiting for transfers between devices: none -> 8.81 us  [of_group(): lax.ppermute(x, ('u', 'c'), [(i, i ^ m) for i in range(4)])]
    ppermute x0 -> x6, starting transfers between devices: none -> 5.44 us  [of_group(): lax.ppermute(x, ('u', 'c'), [(i, i ^ m) for i in range(4)])]
  transfers between devices with their start and end apart: 9 -> 15, of which waited for: 4 -> 8; matrix products, arithmetic and copies ran while one was open for 1% -> 1% of each run, Pallas kernels for 2% -> 2%
where the time goes in v14:
time: 120 us; the launch traced here: 119 us
  blocking collectives  65 us (54%)
  starting transfers between devices  19.1 us (16%)
  Pallas kernels  16.7 us (14%)
  waiting for transfers between devices  14.6 us (12%)
  local copies, waits for them, and re-layouts  2.29 us (2%)
    all_to_all x1, blocking collectives, local(): lax.all_to_all(rotated.reshape(64, 9, 4, 128), ('z', 'x', 'u', 'c', 'b'),...  45.7 us
    all_to_all x1, blocking collectives, local(): lax.all_to_all(message.reshape(8, 256, 128), ('u', 'c', 'b'), 0, 0, tiled...  19.3 us
    pallas_call x5, Pallas kernels, call(): pl.pallas_call(kernel, out_shape=[jax.ShapeDtypeStruct(s, F32) for s in o...  16.7 us
    ppermute x6, waiting for transfers between devices, of_group(): lax.ppermute(x, ('u', 'c'), [(i, i ^ m) for i in range(4)])  8.81 us
    ppermute x6, starting transfers between devices, of_group(): lax.ppermute(x, ('u', 'c'), [(i, i ^ m) for i in range(4)])  5.44 us
    ppermute x1, starting transfers between devices, local(): ahead = lax.ppermute(ahead, chunks, swaps[0])  4.33 us
    ppermute x1, starting transfers between devices, local(): lax.ppermute(potential, dom, [(i, j) for i, j in shift if 0 <= j < 4 * co...  4.2 us
  transfers between devices with their start and end apart: 15, of which 8 were waited for; matrix products, arithmetic and copies ran while one was open for 1% of the time, Pallas kernels for 2%

profile of v14, /device:TPU:32, one launch (start us, length us, event | category | flops | bytes accessed | tf_op | source)
XLA Modules:
  0.0 119.3 jit_solution(7999323619057031445)
XLA Ops:
  0.7 1.0 constant_dynamic-slice_fusion.3
  1.7 1.7 %collective-permute-start.1 = (f32[2,8,32,128]{3,2,1,0:T(8,128)S(1)}, f32[2,8,32,128]{3,2,1,0:T(8,128)S(1)}, u32[]{:S(2)}, u32[]{:S(2)}) collective-permute-start(f32[2,8,32,128]{3,2,1,0:T(8,128)S(1)} %constant_dynamic-slice_fusion.3), channel_id=1, source_target_pairs={{0,4},{2,6},{4,0},{6,2},{1,5},{3,7},{5,1},{7,3},{8,12},{10,14},{12... | collective-permute-start | bytes 786440 | tf_op jit(solution)/shard_map/ppermute | solution.py:338
  3.3 1.2 %constant_dynamic-slice_fusion = (f32[2,8,32,128]{3,2,1,0:T(8,128)S(1)}, f32[2,8,32,128]{3,2,1,0:T(8,128)S(1)}, f32[2,8,32,128]{3,2,1,0:T(8,128)S(1)}) fusion(f32[8,8,32,128]{3,2,1,0:T(8,128)} %param.4, s32[]{:T(128)S(6)} %select_n.15, s32[]{:T(128)S(6)} %select_n.14, s32[]{:T(128)S(6)} %select_n.13), kind=kLoop, calls=%fused_computation.3 | loop fusion | bytes 1572876 | tf_op jit(solution)/shard_map/dynamic_slice | solution.py:339
  5.2 4.2 %collective-permute-start.3 = (f32[8,32,128]{2,1,0:T(8,128)S(1)}, f32[8,32,128]{2,1,0:T(8,128)S(1)}, u32[]{:S(2)}, u32[]{:S(2)}) collective-permute-start(f32[8,32,128]{2,1,0:T(8,128)S(1)} %copy-done), channel_id=1, source_target_pairs={{4,12},{6,14},{8,0},{10,2},{12,20},{14,22},{16,8},{18,10},{20,28},... | collective-permute-start | bytes 393224 | tf_op jit(solution)/shard_map/ppermute | solution.py:332
  9.4 0.8 shard_map.59.weights
  10.3 2.3 %collective-permute-done.3.beyond_0 = f32[8,32,128]{2,1,0:T(8,128)S(1)} collective-permute-done((f32[8,32,128]{2,1,0:T(8,128)S(1)}, f32[8,32,128]{2,1,0:T(8,128)S(1)}, u32[]{:S(2)}, u32[]{:S(2)}) %collective-permute-start.3) | collective-permute-done | bytes 131104 | tf_op jit(solution)/shard_map/ppermute | solution.py:332
  12.5 2.0 %collective-permute-done.2.piece_3 = f32[2,8,32,128]{3,2,1,0:T(8,128)S(1)} collective-permute-done((f32[2,8,32,128]{3,2,1,0:T(8,128)S(1)}, f32[2,8,32,128]{3,2,1,0:T(8,128)S(1)}, u32[]{:S(2)}, u32[]{:S(2)}) %collective-permute-start.2) | collective-permute-done | bytes 262176 | tf_op jit(solution)/shard_map/ppermute | solution.py:341
  14.5 0.7 shard_map.60
  15.2 4.3 %collective-permute-start.4 = (f32[2,18,32,128]{3,2,1,0:T(8,128)S(1)}, f32[2,18,32,128]{3,2,1,0:T(8,128)S(1)}, u32[]{:S(2)}, u32[]{:S(2)}) collective-permute-start(f32[2,18,32,128]{3,2,1,0:T(8,128)S(1)} %get-tuple-element.27), channel_id=1, source_target_pairs={{8,16},{16,8},{24,32},{32,24},{40,48},{48,40},{56,64},{64,56},{72,... | collective-permute-start | bytes 1769480 | tf_op jit(solution)/shard_map/ppermute | solution.py:353
  20.2 1.4 %collective-permute-start.8 = (f32[8,32,128]{2,1,0:T(8,128)S(1)}, f32[8,32,128]{2,1,0:T(8,128)S(1)}, u32[]{:S(2)}, u32[]{:S(2)}) collective-permute-start(f32[8,32,128]{2,1,0:T(8,128)S(1)} %copy-done), channel_id=1, source_target_pairs={{0,6},{2,4},{4,2},{6,0},{1,7},{3,5},{5,3},{7,1},{8,14},{10,12},{12... | collective-permute-start | bytes 393224 | tf_op jit(solution)/shard_map/ppermute | solution.py:357
  22.1 3.6 %collective-permute-done.8.own_3 = f32[8,32,128]{2,1,0:T(8,128)S(1)} collective-permute-done((f32[8,32,128]{2,1,0:T(8,128)S(1)}, f32[8,32,128]{2,1,0:T(8,128)S(1)}, u32[]{:S(2)}, u32[]{:S(2)}) %collective-permute-start.8) | collective-permute-done | bytes 131104 | tf_op jit(solution)/shard_map/ppermute | solution.py:357
  25.7 1.9 %collective-permute-start.11 = (f32[8,32,128]{2,1,0:T(8,128)S(1)}, f32[8,32,128]{2,1,0:T(8,128)S(1)}, u32[]{:S(2)}, u32[]{:S(2)}) collective-permute-start(f32[8,32,128]{2,1,0:T(8,128)S(1)} %collective-permute-done.3.beyond_0), channel_id=1, source_target_pairs={{0,6},{2,4},{4,2},{6,0},{1,7},{3,5},{5,3},{7,1},{8,14},{10,12},{12... | collective-permute-start | bytes 393224 | tf_op jit(solution)/shard_map/ppermute | solution.py:357
  27.6 1.2 %collective-permute-done.7.own_2 = f32[8,32,128]{2,1,0:T(8,128)S(1)} collective-permute-done((f32[8,32,128]{2,1,0:T(8,128)S(1)}, f32[8,32,128]{2,1,0:T(8,128)S(1)}, u32[]{:S(2)}, u32[]{:S(2)}) %collective-permute-start.7) | collective-permute-done | bytes 131104 | tf_op jit(solution)/shard_map/ppermute | solution.py:357
  28.8 1.6 %collective-permute-start.10 = (f32[8,32,128]{2,1,0:T(8,128)S(1)}, f32[8,32,128]{2,1,0:T(8,128)S(1)}, u32[]{:S(2)}, u32[]{:S(2)}) collective-permute-start(f32[8,32,128]{2,1,0:T(8,128)S(1)} %collective-permute-done.3.beyond_0), channel_id=1, source_target_pairs={{0,4},{2,6},{4,0},{6,2},{1,5},{3,7},{5,1},{7,3},{8,12},{10,14},{12... | collective-permute-start | bytes 393224 | tf_op jit(solution)/shard_map/ppermute | solution.py:357
  30.5 0.6 collective-permute-done.11.beyond_3
  31.1 3.4 %collective-permute-done.10.beyond_2 = f32[8,32,128]{2,1,0:T(8,128)S(1)} collective-permute-done((f32[8,32,128]{2,1,0:T(8,128)S(1)}, f32[8,32,128]{2,1,0:T(8,128)S(1)}, u32[]{:S(2)}, u32[]{:S(2)}) %collective-permute-start.10) | collective-permute-done | bytes 131104 | tf_op jit(solution)/shard_map/ppermute | solution.py:357
  34.5 0.7 collective-permute-done.4.ahead
  35.2 12.0 %shard_map.61 = f32[4,2,32,8,128]{4,3,2,1,0:T(8,128)S(1)} custom-call(s32[2]{0:T(128)S(1)} %pad_add_fusion.place, f32[2,8,32,128]{3,2,1,0:T(8,128)S(1)} %get-tuple-element.19.piece_0, f32[2,8,32,128]{3,2,1,0:T(8,128)S(1)} %collective-permute-done.piece_1, f32[2,8,32,128]{3,2,1,0:T(8,128)S(1)} %collective-permute-done.1.piece_2, ...), custom_call_target="tpu_custom_call" | custom-call | tf_op jit(solution)/shard_map/pallas_call | solution.py:303
  47.3 19.3 %all_to_all.10.ring = f32[8,256,128]{2,1,0:T(8,128)S(1)} all-to-all(f32[8,256,128]{2,1,0:T(8,128)S(1)} %bitcast.7), channel_id=1, replica_groups=mesh['z'=8,'x'=4,'u'=2,'c'=2,'b'=2] {'u','c','b'}, dimensions={0} | all-to-all | bytes 2097152 | tf_op jit(solution)/shard_map/all_to_all | solution.py:372
  66.5 1.9 %shard_map.62 = f32[4,2,8,9,4,128]{5,4,3,2,1,0:T(4,128)S(1)} custom-call(f32[8,256,128]{2,1,0:T(8,128)S(1)} %all_to_all.10.ring, f32[256,256]{1,0:T(8,128)S(1)} %shard_map.59.weights), custom_call_target="tpu_custom_call" | custom-call | tf_op jit(solution)/shard_map/pallas_call | solution.py:303
  68.5 45.7 %all_to_all.11 = f32[64,9,4,128]{3,2,1,0:T(4,128)S(1)} all-to-all(f32[64,9,4,128]{3,2,1,0:T(4,128)S(1)} %bitcast.6), channel_id=1, replica_groups={{0,32,64,96,128,160,192,224,1,33,65,97,129,161,193,225,8,40,72,104,136,..., dimensions={0} | all-to-all | bytes 2359296 | tf_op jit(solution)/shard_map/all_to_all | solution.py:376
  115.0 1.5 %collective-permute-start.12 = (f32[4,128]{1,0:T(4,128)S(1)}, f32[4,128]{1,0:T(4,128)S(1)}, u32[]{:S(2)}, u32[]{:S(2)}) collective-permute-start(f32[4,128]{1,0:T(4,128)S(1)} %slice_reduce_fusion), channel_id=1, source_target_pairs={{0,4},{2,6},{4,0},{6,2},{1,5},{3,7},{5,1},{7,3},{8,12},{10,14},{12... | collective-permute-start | bytes 6152 | tf_op jit(solution)/shard_map/ppermute | solution.py:317
  116.5 1.3 %shard_map.63 = f32[8,32,1024]{2,1,0:T(8,128)} custom-call(f32[4,2,8,9,4,128]{5,4,3,2,1,0:T(4,128)S(1)} %bitcast.5), custom_call_target="tpu_custom_call" | custom-call | tf_op jit(solution)/shard_map/pallas_call | solution.py:303
  117.8 0.8 collective-permute-done.12
  (26 shorter events, 3.4 us)
Async XLA Ops:
  0.6 4.6 %copy-start = (f32[8,32,128]{2,1,0:T(8,128)S(1)}, f32[8,32,128]{2,1,0:T(8,128)}, u32[]{:S(2)}) copy-start(f32[8,32,128]{2,1,0:T(8,128)} %own_0) | copy-start | bytes 393220
  0.6 8.8 %copy-start.2 = (f32[16,16]{1,0:T(8,128)S(1)}, f32[16,16]{1,0:T(8,128)}, u32[]{:S(2)}) copy-start(f32[16,16]{1,0:T(8,128)} %coefficients.1) | copy-start | bytes 3076
  1.7 10.9 %collective-permute-start.1 = (f32[2,8,32,128]{3,2,1,0:T(8,128)S(1)}, f32[2,8,32,128]{3,2,1,0:T(8,128)S(1)}, u32[]{:S(2)}, u32[]{:S(2)}) collective-permute-start(f32[2,8,32,128]{3,2,1,0:T(8,128)S(1)} %constant_dynamic-slice_fusion.3), channel_id=1, source_target_pairs={{0,4},{2,6},{4,0},{6,2},{1,5},{3,7},{5,1},{7,3},{8,12},{10,14},{12... | collective-permute-start | bytes 786440 | tf_op jit(solution)/shard_map/ppermute | solution.py:338
  3.3 31.9 %copy-start.1 = (bf16[256,256]{1,0:T(8,128)(2,1)S(1)}, bf16[256,256]{1,0:T(8,128)(2,1)}, u32[]{:S(2)}) copy-start(bf16[256,256]{1,0:T(8,128)(2,1)} %constant.36.clone.bands) | copy-start | bytes 393220
  4.5 10.0 %collective-permute-start.2 = (f32[2,8,32,128]{3,2,1,0:T(8,128)S(1)}, f32[2,8,32,128]{3,2,1,0:T(8,128)S(1)}, u32[]{:S(2)}, u32[]{:S(2)}) collective-permute-start(f32[2,8,32,128]{3,2,1,0:T(8,128)S(1)} %get-tuple-element.32), channel_id=1, source_target_pairs={{0,6},{2,4},{4,2},{6,0},{1,7},{3,5},{5,3},{7,1},{8,14},{10,12},{12... | collective-permute-start | bytes 786440 | tf_op jit(solution)/shard_map/ppermute | solution.py:341
  4.6 9.9 %collective-permute-start = (f32[2,8,32,128]{3,2,1,0:T(8,128)S(1)}, f32[2,8,32,128]{3,2,1,0:T(8,128)S(1)}, u32[]{:S(2)}, u32[]{:S(2)}) collective-permute-start(f32[2,8,32,128]{3,2,1,0:T(8,128)S(1)} %get-tuple-element.33), channel_id=1, source_target_pairs={{0,2},{2,0},{4,6},{6,4},{1,3},{3,1},{5,7},{7,5},{8,10},{10,8},{12,... | collective-permute-start | bytes 786440 | tf_op jit(solution)/shard_map/ppermute | solution.py:341
  5.2 7.3 %collective-permute-start.3 = (f32[8,32,128]{2,1,0:T(8,128)S(1)}, f32[8,32,128]{2,1,0:T(8,128)S(1)}, u32[]{:S(2)}, u32[]{:S(2)}) collective-permute-start(f32[8,32,128]{2,1,0:T(8,128)S(1)} %copy-done), channel_id=1, source_target_pairs={{4,12},{6,14},{8,0},{10,2},{12,20},{14,22},{16,8},{18,10},{20,28},... | collective-permute-start | bytes 393224 | tf_op jit(solution)/shard_map/ppermute | solution.py:332
  15.2 20.0 %collective-permute-start.4 = (f32[2,18,32,128]{3,2,1,0:T(8,128)S(1)}, f32[2,18,32,128]{3,2,1,0:T(8,128)S(1)}, u32[]{:S(2)}, u32[]{:S(2)}) collective-permute-start(f32[2,18,32,128]{3,2,1,0:T(8,128)S(1)} %get-tuple-element.27), channel_id=1, source_target_pairs={{8,16},{16,8},{24,32},{32,24},{40,48},{48,40},{56,64},{64,56},{72,... | collective-permute-start | bytes 1769480 | tf_op jit(solution)/shard_map/ppermute | solution.py:353
  19.6 15.6 %collective-permute-start.5 = (f32[2,18,32,128]{3,2,1,0:T(8,128)S(1)}, f32[2,18,32,128]{3,2,1,0:T(8,128)S(1)}, u32[]{:S(2)}, u32[]{:S(2)}) collective-permute-start(f32[2,18,32,128]{3,2,1,0:T(8,128)S(1)} %get-tuple-element.28), channel_id=1, source_target_pairs={{0,8},{8,0},{16,24},{24,16},{32,40},{40,32},{48,56},{56,48},{64,72... | collective-permute-start | bytes 1769480 | tf_op jit(solution)/shard_map/ppermute | solution.py:354
  20.2 5.5 %collective-permute-start.8 = (f32[8,32,128]{2,1,0:T(8,128)S(1)}, f32[8,32,128]{2,1,0:T(8,128)S(1)}, u32[]{:S(2)}, u32[]{:S(2)}) collective-permute-start(f32[8,32,128]{2,1,0:T(8,128)S(1)} %copy-done), channel_id=1, source_target_pairs={{0,6},{2,4},{4,2},{6,0},{1,7},{3,5},{5,3},{7,1},{8,14},{10,12},{12... | collective-permute-start | bytes 393224 | tf_op jit(solution)/shard_map/ppermute | solution.py:357
  21.6 7.2 %collective-permute-start.7 = (f32[8,32,128]{2,1,0:T(8,128)S(1)}, f32[8,32,128]{2,1,0:T(8,128)S(1)}, u32[]{:S(2)}, u32[]{:S(2)}) collective-permute-start(f32[8,32,128]{2,1,0:T(8,128)S(1)} %copy-done), channel_id=1, source_target_pairs={{0,4},{2,6},{4,0},{6,2},{1,5},{3,7},{5,1},{7,3},{8,12},{10,14},{12... | collective-permute-start | bytes 393224 | tf_op jit(solution)/shard_map/ppermute | solution.py:357
  22.0 8.4 %collective-permute-start.6 = (f32[8,32,128]{2,1,0:T(8,128)S(1)}, f32[8,32,128]{2,1,0:T(8,128)S(1)}, u32[]{:S(2)}, u32[]{:S(2)}) collective-permute-start(f32[8,32,128]{2,1,0:T(8,128)S(1)} %copy-done), channel_id=1, source_target_pairs={{0,2},{2,0},{4,6},{6,4},{1,3},{3,1},{5,7},{7,5},{8,10},{10,8},{12,... | collective-permute-start | bytes 393224 | tf_op jit(solution)/shard_map/ppermute | solution.py:357
  25.7 5.4 %collective-permute-start.11 = (f32[8,32,128]{2,1,0:T(8,128)S(1)}, f32[8,32,128]{2,1,0:T(8,128)S(1)}, u32[]{:S(2)}, u32[]{:S(2)}) collective-permute-start(f32[8,32,128]{2,1,0:T(8,128)S(1)} %collective-permute-done.3.beyond_0), channel_id=1, source_target_pairs={{0,6},{2,4},{4,2},{6,0},{1,7},{3,5},{5,3},{7,1},{8,14},{10,12},{12... | collective-permute-start | bytes 393224 | tf_op jit(solution)/shard_map/ppermute | solution.py:357
  28.8 5.7 %collective-permute-start.10 = (f32[8,32,128]{2,1,0:T(8,128)S(1)}, f32[8,32,128]{2,1,0:T(8,128)S(1)}, u32[]{:S(2)}, u32[]{:S(2)}) collective-permute-start(f32[8,32,128]{2,1,0:T(8,128)S(1)} %collective-permute-done.3.beyond_0), channel_id=1, source_target_pairs={{0,4},{2,6},{4,0},{6,2},{1,5},{3,7},{5,1},{7,3},{8,12},{10,14},{12... | collective-permute-start | bytes 393224 | tf_op jit(solution)/shard_map/ppermute | solution.py:357
  30.5 4.0 %collective-permute-start.9 = (f32[8,32,128]{2,1,0:T(8,128)S(1)}, f32[8,32,128]{2,1,0:T(8,128)S(1)}, u32[]{:S(2)}, u32[]{:S(2)}) collective-permute-start(f32[8,32,128]{2,1,0:T(8,128)S(1)} %collective-permute-done.3.beyond_0), channel_id=1, source_target_pairs={{0,2},{2,0},{4,6},{6,4},{1,3},{3,1},{5,7},{7,5},{8,10},{10,8},{12,... | collective-permute-start | bytes 393224 | tf_op jit(solution)/shard_map/ppermute | solution.py:357
  114.3 3.5 %collective-permute-start.14 = (f32[4,128]{1,0:T(4,128)S(1)}, f32[4,128]{1,0:T(4,128)S(1)}, u32[]{:S(2)}, u32[]{:S(2)}) collective-permute-start(f32[4,128]{1,0:T(4,128)S(1)} %slice_reduce_fusion), channel_id=1, source_target_pairs={{0,6},{2,4},{4,2},{6,0},{1,7},{3,5},{5,3},{7,1},{8,14},{10,12},{12... | collective-permute-start | bytes 6152 | tf_op jit(solution)/shard_map/ppermute | solution.py:317
  114.4 3.4 %collective-permute-start.13 = (f32[4,128]{1,0:T(4,128)S(1)}, f32[4,128]{1,0:T(4,128)S(1)}, u32[]{:S(2)}, u32[]{:S(2)}) collective-permute-start(f32[4,128]{1,0:T(4,128)S(1)} %slice_reduce_fusion), channel_id=1, source_target_pairs={{0,2},{2,0},{4,6},{6,4},{1,3},{3,1},{5,7},{7,5},{8,10},{10,8},{12,... | collective-permute-start | bytes 6152 | tf_op jit(solution)/shard_map/ppermute | solution.py:317
  115.0 3.6 %collective-permute-start.12 = (f32[4,128]{1,0:T(4,128)S(1)}, f32[4,128]{1,0:T(4,128)S(1)}, u32[]{:S(2)}, u32[]{:S(2)}) collective-permute-start(f32[4,128]{1,0:T(4,128)S(1)} %slice_reduce_fusion), channel_id=1, source_target_pairs={{0,4},{2,6},{4,0},{6,2},{1,5},{3,7},{5,1},{7,3},{8,12},{10,14},{12... | collective-permute-start | bytes 6152 | tf_op jit(solution)/shard_map/ppermute | solution.py:317

commit v15 on v14

--- a/solution.py
+++ b/solution.py
@@ -115,14 +115,14 @@
         )
         return 0
 
-    lax.fori_loop(0, far, enter_ends, 0)
+    lax.fori_loop(0, far, enter_ends, 0, unroll=3)
 
     def enter_slabs(p, _):
         for pair in (((0, piece_0), (1, piece_1)), ((2, piece_2), (3, piece_3))):
             enter(*[(far + 8 * (place[1] ^ m) + p, [(piece, (o, p)) for o in range(OWN)]) for m, piece in pair])
         return 0
 
-    lax.fori_loop(0, 8, enter_slabs, 0)
+    lax.fori_loop(0, 8, enter_slabs, 0, unroll=2)
 
     def enter_local(p, _):
         for first, sources in ((2, (own_0, own_1, own_2, own_3)), (6, (beyond_0, beyond_1, beyond_2, beyond_3))):
@@ -132,7 +132,7 @@
                 local[start + p] = (value + (-1.5 * STENCIL[0] - CENTER)) * (1.0 / HALF)
         return 0
 
-    lax.fori_loop(0, 8, enter_local, 0)
+    lax.fori_loop(0, 8, enter_local, 0, unroll=2)
 
     def along_z(source, index):
         high, low = split(source[pl.ds(index, 4), EXT : EXT + 8].reshape(4 * 64, NZ))
@@ -209,7 +209,7 @@
             turned[pl.ds((b * 8 + x) * NZ, NZ), :] = blocks[b].T
         return 0
 
-    lax.fori_loop(0, 8, turn, 0)
+    lax.fori_loop(0, 8, turn, 0, unroll=2)
 
     def pick(i, _):
         places = [(c, b, 4 * i + q) for q in range(4) for c in range(4) for b in range(2)]
@@ -218,7 +218,7 @@
             out[c, b, q] = value
         return 0
 
-    lax.fori_loop(0, NZ // 16, pick, 0)
+    lax.fori_loop(0, NZ // 16, pick, 0, unroll=2)
 
 
 exact = functools.partial(lax.dot_general, precision=lax.Precision.HIGHEST, preferred_element_type=F32)

time: 120 us -> 119 us (level)
  no operation moved by 1% of the time
where the time goes in v15:
time: 119 us
  blocking collectives  65 us (55%)
  starting transfers between devices  19.1 us (16%)
  Pallas kernels  16.3 us (14%)
  waiting for transfers between devices  14.6 us (12%)
  local copies, waits for them, and re-layouts  2.29 us (2%)
    all_to_all x1, blocking collectives, local(): lax.all_to_all(rotated.reshape(64, 9, 4, 128), ('z', 'x', 'u', 'c', 'b'),...  45.7 us
    all_to_all x1, blocking collectives, local(): lax.all_to_all(message.reshape(8, 256, 128), ('u', 'c', 'b'), 0, 0, tiled...  19.3 us
    pallas_call x5, Pallas kernels, call(): pl.pallas_call(kernel, out_shape=[jax.ShapeDtypeStruct(s, F32) for s in o...  16.3 us
    ppermute x6, waiting for transfers between devices, of_group(): lax.ppermute(x, ('u', 'c'), [(i, i ^ m) for i in range(4)])  8.81 us
    ppermute x6, starting transfers between devices, of_group(): lax.ppermute(x, ('u', 'c'), [(i, i ^ m) for i in range(4)])  5.44 us
    ppermute x1, starting transfers between devices, local(): ahead = lax.ppermute(ahead, chunks, swaps[0])  4.33 us
    ppermute x1, starting transfers between devices, local(): lax.ppermute(potential, dom, [(i, j) for i, j in shift if 0 <= j < 4 * co...  4.2 us
  transfers between devices with their start and end apart: 15, of which 8 were waited for; matrix products, arithmetic and copies ran while one was open for 1% of the time, Pallas kernels for 2%

profile of v15, /device:TPU:32, one launch (start us, length us, event | category | flops | bytes accessed | tf_op | source)
XLA Modules:
  0.0 118.9 jit_solution(9781594642101881954)
XLA Ops:
  0.7 1.0 constant_dynamic-slice_fusion.3
  1.7 1.7 %collective-permute-start.1 = (f32[2,8,32,128]{3,2,1,0:T(8,128)S(1)}, f32[2,8,32,128]{3,2,1,0:T(8,128)S(1)}, u32[]{:S(2)}, u32[]{:S(2)}) collective-permute-start(f32[2,8,32,128]{3,2,1,0:T(8,128)S(1)} %constant_dynamic-slice_fusion.3), channel_id=1, source_target_pairs={{0,4},{2,6},{4,0},{6,2},{1,5},{3,7},{5,1},{7,3},{8,12},{10,14},{12... | collective-permute-start | bytes 786440 | tf_op jit(solution)/shard_map/ppermute | solution.py:338
  3.3 1.2 %constant_dynamic-slice_fusion = (f32[2,8,32,128]{3,2,1,0:T(8,128)S(1)}, f32[2,8,32,128]{3,2,1,0:T(8,128)S(1)}, f32[2,8,32,128]{3,2,1,0:T(8,128)S(1)}) fusion(f32[8,8,32,128]{3,2,1,0:T(8,128)} %param.4, s32[]{:T(128)S(6)} %select_n.15, s32[]{:T(128)S(6)} %select_n.14, s32[]{:T(128)S(6)} %select_n.13), kind=kLoop, calls=%fused_computation.3 | loop fusion | bytes 1572876 | tf_op jit(solution)/shard_map/dynamic_slice | solution.py:339
  5.2 4.2 %collective-permute-start.3 = (f32[8,32,128]{2,1,0:T(8,128)S(1)}, f32[8,32,128]{2,1,0:T(8,128)S(1)}, u32[]{:S(2)}, u32[]{:S(2)}) collective-permute-start(f32[8,32,128]{2,1,0:T(8,128)S(1)} %copy-done), channel_id=1, source_target_pairs={{4,12},{6,14},{8,0},{10,2},{12,20},{14,22},{16,8},{18,10},{20,28},... | collective-permute-start | bytes 393224 | tf_op jit(solution)/shard_map/ppermute | solution.py:332
  9.4 0.8 shard_map.59.weights
  10.3 2.3 %collective-permute-done.3.beyond_0 = f32[8,32,128]{2,1,0:T(8,128)S(1)} collective-permute-done((f32[8,32,128]{2,1,0:T(8,128)S(1)}, f32[8,32,128]{2,1,0:T(8,128)S(1)}, u32[]{:S(2)}, u32[]{:S(2)}) %collective-permute-start.3) | collective-permute-done | bytes 131104 | tf_op jit(solution)/shard_map/ppermute | solution.py:332
  12.5 2.0 %collective-permute-done.2.piece_3 = f32[2,8,32,128]{3,2,1,0:T(8,128)S(1)} collective-permute-done((f32[2,8,32,128]{3,2,1,0:T(8,128)S(1)}, f32[2,8,32,128]{3,2,1,0:T(8,128)S(1)}, u32[]{:S(2)}, u32[]{:S(2)}) %collective-permute-start.2) | collective-permute-done | bytes 262176 | tf_op jit(solution)/shard_map/ppermute | solution.py:341
  14.5 0.7 shard_map.60
  15.2 4.3 %collective-permute-start.4 = (f32[2,18,32,128]{3,2,1,0:T(8,128)S(1)}, f32[2,18,32,128]{3,2,1,0:T(8,128)S(1)}, u32[]{:S(2)}, u32[]{:S(2)}) collective-permute-start(f32[2,18,32,128]{3,2,1,0:T(8,128)S(1)} %get-tuple-element.27), channel_id=1, source_target_pairs={{8,16},{16,8},{24,32},{32,24},{40,48},{48,40},{56,64},{64,56},{72,... | collective-permute-start | bytes 1769480 | tf_op jit(solution)/shard_map/ppermute | solution.py:353
  20.2 1.4 %collective-permute-start.8 = (f32[8,32,128]{2,1,0:T(8,128)S(1)}, f32[8,32,128]{2,1,0:T(8,128)S(1)}, u32[]{:S(2)}, u32[]{:S(2)}) collective-permute-start(f32[8,32,128]{2,1,0:T(8,128)S(1)} %copy-done), channel_id=1, source_target_pairs={{0,6},{2,4},{4,2},{6,0},{1,7},{3,5},{5,3},{7,1},{8,14},{10,12},{12... | collective-permute-start | bytes 393224 | tf_op jit(solution)/shard_map/ppermute | solution.py:357
  22.1 3.6 %collective-permute-done.8.own_3 = f32[8,32,128]{2,1,0:T(8,128)S(1)} collective-permute-done((f32[8,32,128]{2,1,0:T(8,128)S(1)}, f32[8,32,128]{2,1,0:T(8,128)S(1)}, u32[]{:S(2)}, u32[]{:S(2)}) %collective-permute-start.8) | collective-permute-done | bytes 131104 | tf_op jit(solution)/shard_map/ppermute | solution.py:357
  25.7 1.9 %collective-permute-start.11 = (f32[8,32,128]{2,1,0:T(8,128)S(1)}, f32[8,32,128]{2,1,0:T(8,128)S(1)}, u32[]{:S(2)}, u32[]{:S(2)}) collective-permute-start(f32[8,32,128]{2,1,0:T(8,128)S(1)} %collective-permute-done.3.beyond_0), channel_id=1, source_target_pairs={{0,6},{2,4},{4,2},{6,0},{1,7},{3,5},{5,3},{7,1},{8,14},{10,12},{12... | collective-permute-start | bytes 393224 | tf_op jit(solution)/shard_map/ppermute | solution.py:357
  27.6 1.2 %collective-permute-done.7.own_2 = f32[8,32,128]{2,1,0:T(8,128)S(1)} collective-permute-done((f32[8,32,128]{2,1,0:T(8,128)S(1)}, f32[8,32,128]{2,1,0:T(8,128)S(1)}, u32[]{:S(2)}, u32[]{:S(2)}) %collective-permute-start.7) | collective-permute-done | bytes 131104 | tf_op jit(solution)/shard_map/ppermute | solution.py:357
  28.8 1.6 %collective-permute-start.10 = (f32[8,32,128]{2,1,0:T(8,128)S(1)}, f32[8,32,128]{2,1,0:T(8,128)S(1)}, u32[]{:S(2)}, u32[]{:S(2)}) collective-permute-start(f32[8,32,128]{2,1,0:T(8,128)S(1)} %collective-permute-done.3.beyond_0), channel_id=1, source_target_pairs={{0,4},{2,6},{4,0},{6,2},{1,5},{3,7},{5,1},{7,3},{8,12},{10,14},{12... | collective-permute-start | bytes 393224 | tf_op jit(solution)/shard_map/ppermute | solution.py:357
  30.5 0.6 collective-permute-done.11.beyond_3
  31.1 3.4 %collective-permute-done.10.beyond_2 = f32[8,32,128]{2,1,0:T(8,128)S(1)} collective-permute-done((f32[8,32,128]{2,1,0:T(8,128)S(1)}, f32[8,32,128]{2,1,0:T(8,128)S(1)}, u32[]{:S(2)}, u32[]{:S(2)}) %collective-permute-start.10) | collective-permute-done | bytes 131104 | tf_op jit(solution)/shard_map/ppermute | solution.py:357
  34.5 0.7 collective-permute-done.4.ahead
  35.2 11.6 %shard_map.61 = f32[4,2,32,8,128]{4,3,2,1,0:T(8,128)S(1)} custom-call(s32[2]{0:T(128)S(1)} %pad_add_fusion.place, f32[2,8,32,128]{3,2,1,0:T(8,128)S(1)} %get-tuple-element.19.piece_0, f32[2,8,32,128]{3,2,1,0:T(8,128)S(1)} %collective-permute-done.piece_1, f32[2,8,32,128]{3,2,1,0:T(8,128)S(1)} %collective-permute-done.1.piece_2, ...), custom_call_target="tpu_custom_call" | custom-call | tf_op jit(solution)/shard_map/pallas_call | solution.py:303
  46.9 19.3 %all_to_all.10.ring = f32[8,256,128]{2,1,0:T(8,128)S(1)} all-to-all(f32[8,256,128]{2,1,0:T(8,128)S(1)} %bitcast.7), channel_id=1, replica_groups=mesh['z'=8,'x'=4,'u'=2,'c'=2,'b'=2] {'u','c','b'}, dimensions={0} | all-to-all | bytes 2097152 | tf_op jit(solution)/shard_map/all_to_all | solution.py:372
  66.1 1.9 %shard_map.62 = f32[4,2,8,9,4,128]{5,4,3,2,1,0:T(4,128)S(1)} custom-call(f32[8,256,128]{2,1,0:T(8,128)S(1)} %all_to_all.10.ring, f32[256,256]{1,0:T(8,128)S(1)} %shard_map.59.weights), custom_call_target="tpu_custom_call" | custom-call | tf_op jit(solution)/shard_map/pallas_call | solution.py:303
  68.0 45.7 %all_to_all.11 = f32[64,9,4,128]{3,2,1,0:T(4,128)S(1)} all-to-all(f32[64,9,4,128]{3,2,1,0:T(4,128)S(1)} %bitcast.6), channel_id=1, replica_groups={{0,32,64,96,128,160,192,224,1,33,65,97,129,161,193,225,8,40,72,104,136,..., dimensions={0} | all-to-all | bytes 2359296 | tf_op jit(solution)/shard_map/all_to_all | solution.py:376
  114.6 1.5 %collective-permute-start.12 = (f32[4,128]{1,0:T(4,128)S(1)}, f32[4,128]{1,0:T(4,128)S(1)}, u32[]{:S(2)}, u32[]{:S(2)}) collective-permute-start(f32[4,128]{1,0:T(4,128)S(1)} %slice_reduce_fusion), channel_id=1, source_target_pairs={{0,4},{2,6},{4,0},{6,2},{1,5},{3,7},{5,1},{7,3},{8,12},{10,14},{12... | collective-permute-start | bytes 6152 | tf_op jit(solution)/shard_map/ppermute | solution.py:317
  116.1 1.3 %shard_map.63 = f32[8,32,1024]{2,1,0:T(8,128)} custom-call(f32[4,2,8,9,4,128]{5,4,3,2,1,0:T(4,128)S(1)} %bitcast.5), custom_call_target="tpu_custom_call" | custom-call | tf_op jit(solution)/shard_map/pallas_call | solution.py:303
  117.4 0.8 collective-permute-done.12
  (26 shorter events, 3.4 us)
Async XLA Ops:
  0.6 4.6 %copy-start = (f32[8,32,128]{2,1,0:T(8,128)S(1)}, f32[8,32,128]{2,1,0:T(8,128)}, u32[]{:S(2)}) copy-start(f32[8,32,128]{2,1,0:T(8,128)} %own_0) | copy-start | bytes 393220
  0.6 8.8 %copy-start.2 = (f32[16,16]{1,0:T(8,128)S(1)}, f32[16,16]{1,0:T(8,128)}, u32[]{:S(2)}) copy-start(f32[16,16]{1,0:T(8,128)} %coefficients.1) | copy-start | bytes 3076
  1.7 10.9 %collective-permute-start.1 = (f32[2,8,32,128]{3,2,1,0:T(8,128)S(1)}, f32[2,8,32,128]{3,2,1,0:T(8,128)S(1)}, u32[]{:S(2)}, u32[]{:S(2)}) collective-permute-start(f32[2,8,32,128]{3,2,1,0:T(8,128)S(1)} %constant_dynamic-slice_fusion.3), channel_id=1, source_target_pairs={{0,4},{2,6},{4,0},{6,2},{1,5},{3,7},{5,1},{7,3},{8,12},{10,14},{12... | collective-permute-start | bytes 786440 | tf_op jit(solution)/shard_map/ppermute | solution.py:338
  3.3 31.9 %copy-start.1 = (bf16[256,256]{1,0:T(8,128)(2,1)S(1)}, bf16[256,256]{1,0:T(8,128)(2,1)}, u32[]{:S(2)}) copy-start(bf16[256,256]{1,0:T(8,128)(2,1)} %constant.36.clone.bands) | copy-start | bytes 393220
  4.5 10.0 %collective-permute-start.2 = (f32[2,8,32,128]{3,2,1,0:T(8,128)S(1)}, f32[2,8,32,128]{3,2,1,0:T(8,128)S(1)}, u32[]{:S(2)}, u32[]{:S(2)}) collective-permute-start(f32[2,8,32,128]{3,2,1,0:T(8,128)S(1)} %get-tuple-element.32), channel_id=1, source_target_pairs={{0,6},{2,4},{4,2},{6,0},{1,7},{3,5},{5,3},{7,1},{8,14},{10,12},{12... | collective-permute-start | bytes 786440 | tf_op jit(solution)/shard_map/ppermute | solution.py:341
  4.6 9.9 %collective-permute-start = (f32[2,8,32,128]{3,2,1,0:T(8,128)S(1)}, f32[2,8,32,128]{3,2,1,0:T(8,128)S(1)}, u32[]{:S(2)}, u32[]{:S(2)}) collective-permute-start(f32[2,8,32,128]{3,2,1,0:T(8,128)S(1)} %get-tuple-element.33), channel_id=1, source_target_pairs={{0,2},{2,0},{4,6},{6,4},{1,3},{3,1},{5,7},{7,5},{8,10},{10,8},{12,... | collective-permute-start | bytes 786440 | tf_op jit(solution)/shard_map/ppermute | solution.py:341
  5.2 7.3 %collective-permute-start.3 = (f32[8,32,128]{2,1,0:T(8,128)S(1)}, f32[8,32,128]{2,1,0:T(8,128)S(1)}, u32[]{:S(2)}, u32[]{:S(2)}) collective-permute-start(f32[8,32,128]{2,1,0:T(8,128)S(1)} %copy-done), channel_id=1, source_target_pairs={{4,12},{6,14},{8,0},{10,2},{12,20},{14,22},{16,8},{18,10},{20,28},... | collective-permute-start | bytes 393224 | tf_op jit(solution)/shard_map/ppermute | solution.py:332
  15.2 20.0 %collective-permute-start.4 = (f32[2,18,32,128]{3,2,1,0:T(8,128)S(1)}, f32[2,18,32,128]{3,2,1,0:T(8,128)S(1)}, u32[]{:S(2)}, u32[]{:S(2)}) collective-permute-start(f32[2,18,32,128]{3,2,1,0:T(8,128)S(1)} %get-tuple-element.27), channel_id=1, source_target_pairs={{8,16},{16,8},{24,32},{32,24},{40,48},{48,40},{56,64},{64,56},{72,... | collective-permute-start | bytes 1769480 | tf_op jit(solution)/shard_map/ppermute | solution.py:353
  19.6 15.6 %collective-permute-start.5 = (f32[2,18,32,128]{3,2,1,0:T(8,128)S(1)}, f32[2,18,32,128]{3,2,1,0:T(8,128)S(1)}, u32[]{:S(2)}, u32[]{:S(2)}) collective-permute-start(f32[2,18,32,128]{3,2,1,0:T(8,128)S(1)} %get-tuple-element.28), channel_id=1, source_target_pairs={{0,8},{8,0},{16,24},{24,16},{32,40},{40,32},{48,56},{56,48},{64,72... | collective-permute-start | bytes 1769480 | tf_op jit(solution)/shard_map/ppermute | solution.py:354
  20.2 5.5 %collective-permute-start.8 = (f32[8,32,128]{2,1,0:T(8,128)S(1)}, f32[8,32,128]{2,1,0:T(8,128)S(1)}, u32[]{:S(2)}, u32[]{:S(2)}) collective-permute-start(f32[8,32,128]{2,1,0:T(8,128)S(1)} %copy-done), channel_id=1, source_target_pairs={{0,6},{2,4},{4,2},{6,0},{1,7},{3,5},{5,3},{7,1},{8,14},{10,12},{12... | collective-permute-start | bytes 393224 | tf_op jit(solution)/shard_map/ppermute | solution.py:357
  21.6 7.2 %collective-permute-start.7 = (f32[8,32,128]{2,1,0:T(8,128)S(1)}, f32[8,32,128]{2,1,0:T(8,128)S(1)}, u32[]{:S(2)}, u32[]{:S(2)}) collective-permute-start(f32[8,32,128]{2,1,0:T(8,128)S(1)} %copy-done), channel_id=1, source_target_pairs={{0,4},{2,6},{4,0},{6,2},{1,5},{3,7},{5,1},{7,3},{8,12},{10,14},{12... | collective-permute-start | bytes 393224 | tf_op jit(solution)/shard_map/ppermute | solution.py:357
  22.0 8.4 %collective-permute-start.6 = (f32[8,32,128]{2,1,0:T(8,128)S(1)}, f32[8,32,128]{2,1,0:T(8,128)S(1)}, u32[]{:S(2)}, u32[]{:S(2)}) collective-permute-start(f32[8,32,128]{2,1,0:T(8,128)S(1)} %copy-done), channel_id=1, source_target_pairs={{0,2},{2,0},{4,6},{6,4},{1,3},{3,1},{5,7},{7,5},{8,10},{10,8},{12,... | collective-permute-start | bytes 393224 | tf_op jit(solution)/shard_map/ppermute | solution.py:357
  25.7 5.4 %collective-permute-start.11 = (f32[8,32,128]{2,1,0:T(8,128)S(1)}, f32[8,32,128]{2,1,0:T(8,128)S(1)}, u32[]{:S(2)}, u32[]{:S(2)}) collective-permute-start(f32[8,32,128]{2,1,0:T(8,128)S(1)} %collective-permute-done.3.beyond_0), channel_id=1, source_target_pairs={{0,6},{2,4},{4,2},{6,0},{1,7},{3,5},{5,3},{7,1},{8,14},{10,12},{12... | collective-permute-start | bytes 393224 | tf_op jit(solution)/shard_map/ppermute | solution.py:357
  28.8 5.7 %collective-permute-start.10 = (f32[8,32,128]{2,1,0:T(8,128)S(1)}, f32[8,32,128]{2,1,0:T(8,128)S(1)}, u32[]{:S(2)}, u32[]{:S(2)}) collective-permute-start(f32[8,32,128]{2,1,0:T(8,128)S(1)} %collective-permute-done.3.beyond_0), channel_id=1, source_target_pairs={{0,4},{2,6},{4,0},{6,2},{1,5},{3,7},{5,1},{7,3},{8,12},{10,14},{12... | collective-permute-start | bytes 393224 | tf_op jit(solution)/shard_map/ppermute | solution.py:357
  30.5 4.0 %collective-permute-start.9 = (f32[8,32,128]{2,1,0:T(8,128)S(1)}, f32[8,32,128]{2,1,0:T(8,128)S(1)}, u32[]{:S(2)}, u32[]{:S(2)}) collective-permute-start(f32[8,32,128]{2,1,0:T(8,128)S(1)} %collective-permute-done.3.beyond_0), channel_id=1, source_target_pairs={{0,2},{2,0},{4,6},{6,4},{1,3},{3,1},{5,7},{7,5},{8,10},{10,8},{12,... | collective-permute-start | bytes 393224 | tf_op jit(solution)/shard_map/ppermute | solution.py:357
  113.8 3.5 %collective-permute-start.14 = (f32[4,128]{1,0:T(4,128)S(1)}, f32[4,128]{1,0:T(4,128)S(1)}, u32[]{:S(2)}, u32[]{:S(2)}) collective-permute-start(f32[4,128]{1,0:T(4,128)S(1)} %slice_reduce_fusion), channel_id=1, source_target_pairs={{0,6},{2,4},{4,2},{6,0},{1,7},{3,5},{5,3},{7,1},{8,14},{10,12},{12... | collective-permute-start | bytes 6152 | tf_op jit(solution)/shard_map/ppermute | solution.py:317
  113.9 3.4 %collective-permute-start.13 = (f32[4,128]{1,0:T(4,128)S(1)}, f32[4,128]{1,0:T(4,128)S(1)}, u32[]{:S(2)}, u32[]{:S(2)}) collective-permute-start(f32[4,128]{1,0:T(4,128)S(1)} %slice_reduce_fusion), channel_id=1, source_target_pairs={{0,2},{2,0},{4,6},{6,4},{1,3},{3,1},{5,7},{7,5},{8,10},{10,8},{12,... | collective-permute-start | bytes 6152 | tf_op jit(solution)/shard_map/ppermute | solution.py:317
  114.6 3.6 %collective-permute-start.12 = (f32[4,128]{1,0:T(4,128)S(1)}, f32[4,128]{1,0:T(4,128)S(1)}, u32[]{:S(2)}, u32[]{:S(2)}) collective-permute-start(f32[4,128]{1,0:T(4,128)S(1)} %slice_reduce_fusion), channel_id=1, source_target_pairs={{0,4},{2,6},{4,0},{6,2},{1,5},{3,7},{5,1},{7,3},{8,12},{10,14},{12... | collective-permute-start | bytes 6152 | tf_op jit(solution)/shard_map/ppermute | solution.py:317

commit v16 on v15

--- a/solution.py
+++ b/solution.py
@@ -259,8 +259,8 @@
         for b in range(2):
             rows = turned[:, b * 128 : (b + 1) * 128].reshape(8, 4, 8, 128)
             for x in range(4):
-                out[x, b, :, 2 * t] = rows[:, x, 0:4]
-                out[x, b, :, 2 * t + 1] = rows[:, x, 4:8]
+                for q in range(4):
+                    out[x, b, :, 4 * t + q] = rows[:, x, 2 * q : 2 * q + 2]
         straight = straight + dot(high, high, rows_out)
         cross = cross + dot(high, low, rows_out)
     row = lax.broadcasted_iota(jnp.int32, (256, 256), 0)
@@ -273,8 +273,8 @@
     number, entry = number[:64], entry[:64]
     rows = (number // 8 * 2 + number // 4 % 2 == entry).astype(F32)
     both = exact(rows, exact(diagonal, columns, (((1,), (0,)), ((), ()))), (((0,), (0,)), ((), ())))
-    tile = jnp.concatenate([both[4 * q : 4 * q + 4] for q in range(4)] + [jnp.zeros((4, 64), F32)], axis=1)
-    out[:, :, :, 8] = jnp.broadcast_to(tile, (4, 2, 8, 4, 128))
+    tile = jnp.concatenate([both[2 * q : 2 * q + 2] for q in range(8)], axis=1)
+    out[:, :, :, 16] = jnp.broadcast_to(tile, (4, 2, 8, 2, 128))
 
 
 def lines_kernel(received, out):
@@ -282,7 +282,7 @@
 
     def lines(s, b):
         pieces = [
-            jnp.concatenate([received[c, b, s, 2 * j], received[c, b, s, 2 * j + 1]], axis=0)
+            jnp.concatenate([received[c, b, s, 4 * j + q] for q in range(4)], axis=0)
             for c in range(4)
             for j in range(4)
         ]
@@ -370,15 +370,15 @@
         place, *pieces, ahead, behind, *own, *beyond, bands
     )
     ring = lax.all_to_all(message.reshape(8, 256, 128), ("u", "c", "b"), 0, 0, tiled=True)
-    (rotated,) = call(rotate_kernel, [(4, 2, 8, 9, 4, 128)])(ring, weights)
+    (rotated,) = call(rotate_kernel, [(4, 2, 8, 17, 2, 128)])(ring, weights)
     everyone = np.arange(256).reshape(8, 4, 4, 2)
     groups = everyone.transpose(2, 1, 3, 0).reshape(4, 64).tolist()
     received = lax.all_to_all(
-        rotated.reshape(64, 9, 4, 128), ("z", "x", "u", "c", "b"), 0, 0, axis_index_groups=groups, tiled=True
+        rotated.reshape(64, 17, 2, 128), ("z", "x", "u", "c", "b"), 0, 0, axis_index_groups=groups, tiled=True
     )
-    gram = four(received[:, 8].sum(axis=0), "u", 1, "c", 1) / (NX * NY * NZ)
-    intersection = jnp.concatenate([gram[:, q * NORB : (q + 1) * NORB] for q in range(4)], axis=0)
-    (lines,) = call(lines_kernel, [(8, NY, NX)])(received.reshape(4, 2, 8, 9, 4, 128))
+    gram = four(received[:, 16].sum(axis=0), "u", 1, "c", 1) / (NX * NY * NZ)
+    intersection = jnp.concatenate([gram[:, q * NORB : (q + 1) * NORB] for q in range(8)], axis=0)
+    (lines,) = call(lines_kernel, [(8, NY, NX)])(received.reshape(4, 2, 8, 17, 2, 128))
     return intersection, lines
 
 

time: 119 us -> 118 us (level)
  blocking collectives: 65 us -> 63.6 us
  local copies, waits for them, and re-layouts: 2.29 us -> 3.52 us
    all_to_all x1, blocking collectives: 45.7 us -> 44.4 us  [local(): lax.all_to_all(rotated.reshape(64, 17, 2, 128), ('z', 'x', 'u', 'c', 'b')...]
    concatenate x0 -> x1, local copies, waits for them, and re-layouts: none -> 1.22 us  [local(): jnp.concatenate([gram[:, q * NORB:(q + 1) * NORB] for q in range(8)], axi...]
where the time goes in v16:
time: 118 us
  blocking collectives  63.6 us (54%)
  starting transfers between devices  19.1 us (16%)
  Pallas kernels  16.4 us (14%)
  waiting for transfers between devices  14.6 us (12%)
  local copies, waits for them, and re-layouts  3.52 us (3%)
    all_to_all x1, blocking collectives, local(): lax.all_to_all(rotated.reshape(64, 17, 2, 128), ('z', 'x', 'u', 'c', 'b')...  44.4 us
    all_to_all x1, blocking collectives, local(): lax.all_to_all(message.reshape(8, 256, 128), ('u', 'c', 'b'), 0, 0, tiled...  19.3 us
    pallas_call x5, Pallas kernels, call(): pl.pallas_call(kernel, out_shape=[jax.ShapeDtypeStruct(s, F32) for s in o...  16.4 us
    ppermute x6, waiting for transfers between devices, of_group(): lax.ppermute(x, ('u', 'c'), [(i, i ^ m) for i in range(4)])  8.81 us
    ppermute x6, starting transfers between devices, of_group(): lax.ppermute(x, ('u', 'c'), [(i, i ^ m) for i in range(4)])  5.44 us
    ppermute x1, starting transfers between devices, local(): ahead = lax.ppermute(ahead, chunks, swaps[0])  4.33 us
    ppermute x1, starting transfers between devices, local(): lax.ppermute(potential, dom, [(i, j) for i, j in shift if 0 <= j < 4 * co...  4.2 us
  transfers between devices with their start and end apart: 15, of which 8 were waited for; matrix products, arithmetic and copies ran while one was open for 1% of the time, Pallas kernels for 2%

profile of v16, /device:TPU:32, one launch (start us, length us, event | category | flops | bytes accessed | tf_op | source)
XLA Modules:
  0.0 118.1 jit_solution(14770958007719089822)
XLA Ops:
  0.7 1.0 constant_dynamic-slice_fusion.3
  1.7 1.7 %collective-permute-start.1 = (f32[2,8,32,128]{3,2,1,0:T(8,128)S(1)}, f32[2,8,32,128]{3,2,1,0:T(8,128)S(1)}, u32[]{:S(2)}, u32[]{:S(2)}) collective-permute-start(f32[2,8,32,128]{3,2,1,0:T(8,128)S(1)} %constant_dynamic-slice_fusion.3), channel_id=1, source_target_pairs={{0,4},{2,6},{4,0},{6,2},{1,5},{3,7},{5,1},{7,3},{8,12},{10,14},{12... | collective-permute-start | bytes 786440 | tf_op jit(solution)/shard_map/ppermute | solution.py:338
  3.3 1.2 %constant_dynamic-slice_fusion = (f32[2,8,32,128]{3,2,1,0:T(8,128)S(1)}, f32[2,8,32,128]{3,2,1,0:T(8,128)S(1)}, f32[2,8,32,128]{3,2,1,0:T(8,128)S(1)}) fusion(f32[8,8,32,128]{3,2,1,0:T(8,128)} %param.4, s32[]{:T(128)S(6)} %select_n.15, s32[]{:T(128)S(6)} %select_n.14, s32[]{:T(128)S(6)} %select_n.13), kind=kLoop, calls=%fused_computation.2 | loop fusion | bytes 1572876 | tf_op jit(solution)/shard_map/dynamic_slice | solution.py:339
  5.2 4.2 %collective-permute-start.3 = (f32[8,32,128]{2,1,0:T(8,128)S(1)}, f32[8,32,128]{2,1,0:T(8,128)S(1)}, u32[]{:S(2)}, u32[]{:S(2)}) collective-permute-start(f32[8,32,128]{2,1,0:T(8,128)S(1)} %copy-done), channel_id=1, source_target_pairs={{4,12},{6,14},{8,0},{10,2},{12,20},{14,22},{16,8},{18,10},{20,28},... | collective-permute-start | bytes 393224 | tf_op jit(solution)/shard_map/ppermute | solution.py:332
  9.4 0.8 shard_map.59.weights
  10.3 2.3 %collective-permute-done.3.beyond_0 = f32[8,32,128]{2,1,0:T(8,128)S(1)} collective-permute-done((f32[8,32,128]{2,1,0:T(8,128)S(1)}, f32[8,32,128]{2,1,0:T(8,128)S(1)}, u32[]{:S(2)}, u32[]{:S(2)}) %collective-permute-start.3) | collective-permute-done | bytes 131104 | tf_op jit(solution)/shard_map/ppermute | solution.py:332
  12.5 2.0 %collective-permute-done.2.piece_3 = f32[2,8,32,128]{3,2,1,0:T(8,128)S(1)} collective-permute-done((f32[2,8,32,128]{3,2,1,0:T(8,128)S(1)}, f32[2,8,32,128]{3,2,1,0:T(8,128)S(1)}, u32[]{:S(2)}, u32[]{:S(2)}) %collective-permute-start.2) | collective-permute-done | bytes 262176 | tf_op jit(solution)/shard_map/ppermute | solution.py:341
  14.5 0.7 shard_map.60
  15.2 4.3 %collective-permute-start.4 = (f32[2,18,32,128]{3,2,1,0:T(8,128)S(1)}, f32[2,18,32,128]{3,2,1,0:T(8,128)S(1)}, u32[]{:S(2)}, u32[]{:S(2)}) collective-permute-start(f32[2,18,32,128]{3,2,1,0:T(8,128)S(1)} %get-tuple-element.27), channel_id=1, source_target_pairs={{8,16},{16,8},{24,32},{32,24},{40,48},{48,40},{56,64},{64,56},{72,... | collective-permute-start | bytes 1769480 | tf_op jit(solution)/shard_map/ppermute | solution.py:353
  20.2 1.4 %collective-permute-start.8 = (f32[8,32,128]{2,1,0:T(8,128)S(1)}, f32[8,32,128]{2,1,0:T(8,128)S(1)}, u32[]{:S(2)}, u32[]{:S(2)}) collective-permute-start(f32[8,32,128]{2,1,0:T(8,128)S(1)} %copy-done), channel_id=1, source_target_pairs={{0,6},{2,4},{4,2},{6,0},{1,7},{3,5},{5,3},{7,1},{8,14},{10,12},{12... | collective-permute-start | bytes 393224 | tf_op jit(solution)/shard_map/ppermute | solution.py:357
  22.1 3.6 %collective-permute-done.8.own_3 = f32[8,32,128]{2,1,0:T(8,128)S(1)} collective-permute-done((f32[8,32,128]{2,1,0:T(8,128)S(1)}, f32[8,32,128]{2,1,0:T(8,128)S(1)}, u32[]{:S(2)}, u32[]{:S(2)}) %collective-permute-start.8) | collective-permute-done | bytes 131104 | tf_op jit(solution)/shard_map/ppermute | solution.py:357
  25.7 1.9 %collective-permute-start.11 = (f32[8,32,128]{2,1,0:T(8,128)S(1)}, f32[8,32,128]{2,1,0:T(8,128)S(1)}, u32[]{:S(2)}, u32[]{:S(2)}) collective-permute-start(f32[8,32,128]{2,1,0:T(8,128)S(1)} %collective-permute-done.3.beyond_0), channel_id=1, source_target_pairs={{0,6},{2,4},{4,2},{6,0},{1,7},{3,5},{5,3},{7,1},{8,14},{10,12},{12... | collective-permute-start | bytes 393224 | tf_op jit(solution)/shard_map/ppermute | solution.py:357
  27.6 1.2 %collective-permute-done.7.own_2 = f32[8,32,128]{2,1,0:T(8,128)S(1)} collective-permute-done((f32[8,32,128]{2,1,0:T(8,128)S(1)}, f32[8,32,128]{2,1,0:T(8,128)S(1)}, u32[]{:S(2)}, u32[]{:S(2)}) %collective-permute-start.7) | collective-permute-done | bytes 131104 | tf_op jit(solution)/shard_map/ppermute | solution.py:357
  28.8 1.6 %collective-permute-start.10 = (f32[8,32,128]{2,1,0:T(8,128)S(1)}, f32[8,32,128]{2,1,0:T(8,128)S(1)}, u32[]{:S(2)}, u32[]{:S(2)}) collective-permute-start(f32[8,32,128]{2,1,0:T(8,128)S(1)} %collective-permute-done.3.beyond_0), channel_id=1, source_target_pairs={{0,4},{2,6},{4,0},{6,2},{1,5},{3,7},{5,1},{7,3},{8,12},{10,14},{12... | collective-permute-start | bytes 393224 | tf_op jit(solution)/shard_map/ppermute | solution.py:357
  31.1 3.4 %collective-permute-done.10.beyond_2 = f32[8,32,128]{2,1,0:T(8,128)S(1)} collective-permute-done((f32[8,32,128]{2,1,0:T(8,128)S(1)}, f32[8,32,128]{2,1,0:T(8,128)S(1)}, u32[]{:S(2)}, u32[]{:S(2)}) %collective-permute-start.10) | collective-permute-done | bytes 131104 | tf_op jit(solution)/shard_map/ppermute | solution.py:357
  34.5 0.7 collective-permute-done.4.ahead
  35.2 11.6 %shard_map.61 = f32[4,2,32,8,128]{4,3,2,1,0:T(8,128)S(1)} custom-call(s32[2]{0:T(128)S(1)} %pad_add_fusion.place, f32[2,8,32,128]{3,2,1,0:T(8,128)S(1)} %get-tuple-element.19.piece_0, f32[2,8,32,128]{3,2,1,0:T(8,128)S(1)} %collective-permute-done.piece_1, f32[2,8,32,128]{3,2,1,0:T(8,128)S(1)} %collective-permute-done.1.piece_2, ...), custom_call_target="tpu_custom_call" | custom-call | tf_op jit(solution)/shard_map/pallas_call | solution.py:303
  46.9 19.3 %all_to_all.10.ring = f32[8,256,128]{2,1,0:T(8,128)S(1)} all-to-all(f32[8,256,128]{2,1,0:T(8,128)S(1)} %bitcast.7), channel_id=1, replica_groups=mesh['z'=8,'x'=4,'u'=2,'c'=2,'b'=2] {'u','c','b'}, dimensions={0} | all-to-all | bytes 2097152 | tf_op jit(solution)/shard_map/all_to_all | solution.py:372
  66.1 2.0 %shard_map.62 = f32[4,2,8,17,2,128]{5,4,3,2,1,0:T(2,128)S(1)} custom-call(f32[8,256,128]{2,1,0:T(8,128)S(1)} %all_to_all.10.ring, f32[256,256]{1,0:T(8,128)S(1)} %shard_map.59.weights), custom_call_target="tpu_custom_call" | custom-call | tf_op jit(solution)/shard_map/pallas_call | solution.py:303
  68.1 44.4 %all_to_all.11 = f32[64,17,2,128]{3,2,1,0:T(2,128)S(1)} all-to-all(f32[64,17,2,128]{3,2,1,0:T(2,128)S(1)} %bitcast.6), channel_id=1, replica_groups={{0,32,64,96,128,160,192,224,1,33,65,97,129,161,193,225,8,40,72,104,136,..., dimensions={0} | all-to-all | bytes 2228224 | tf_op jit(solution)/shard_map/all_to_all | solution.py:376
  113.3 1.5 %collective-permute-start.12 = (f32[2,128]{1,0:T(2,128)S(1)}, f32[2,128]{1,0:T(2,128)S(1)}, u32[]{:S(2)}, u32[]{:S(2)}) collective-permute-start(f32[2,128]{1,0:T(2,128)S(1)} %slice_reduce_fusion), channel_id=1, source_target_pairs={{0,4},{2,6},{4,0},{6,2},{1,5},{3,7},{5,1},{7,3},{8,12},{10,14},{12... | collective-permute-start | bytes 3080 | tf_op jit(solution)/shard_map/ppermute | solution.py:317
  114.7 1.3 %shard_map.63 = f32[8,32,1024]{2,1,0:T(8,128)} custom-call(f32[4,2,8,17,2,128]{5,4,3,2,1,0:T(2,128)S(1)} %bitcast.5), custom_call_target="tpu_custom_call" | custom-call | tf_op jit(solution)/shard_map/pallas_call | solution.py:303
  116.1 0.7 collective-permute-done.12
  116.9 1.2 %concatenate.3 = f32[16,16]{1,0:T(8,128)} concatenate(f32[2,16]{1,0:T(2,128)S(1)} %get-tuple-element.42, f32[2,16]{1,0:T(2,128)S(1)} %get-tuple-element.41, f32[2,16]{1,0:T(2,128)S(1)} %get-tuple-element.40, f32[2,16]{1,0:T(2,128)S(1)} %get-tuple-element.39, f32[2,16]{1,0:T(2,128)S(1)} %get-tuple-element.38, f32[2,16]{1,0:T(2,128)S(1)} %get-tuple-element.37, ...), dimensions={0} | concatenate | bytes 2048 | tf_op jit(solution)/shard_map/concatenate | solution.py:380
  (26 shorter events, 3.4 us)
Async XLA Ops:
  0.6 4.6 %copy-start = (f32[8,32,128]{2,1,0:T(8,128)S(1)}, f32[8,32,128]{2,1,0:T(8,128)}, u32[]{:S(2)}) copy-start(f32[8,32,128]{2,1,0:T(8,128)} %own_0) | copy-start | bytes 393220
  0.6 8.8 %copy-start.2 = (f32[16,16]{1,0:T(8,128)S(1)}, f32[16,16]{1,0:T(8,128)}, u32[]{:S(2)}) copy-start(f32[16,16]{1,0:T(8,128)} %coefficients.1) | copy-start | bytes 3076
  1.7 10.9 %collective-permute-start.1 = (f32[2,8,32,128]{3,2,1,0:T(8,128)S(1)}, f32[2,8,32,128]{3,2,1,0:T(8,128)S(1)}, u32[]{:S(2)}, u32[]{:S(2)}) collective-permute-start(f32[2,8,32,128]{3,2,1,0:T(8,128)S(1)} %constant_dynamic-slice_fusion.3), channel_id=1, source_target_pairs={{0,4},{2,6},{4,0},{6,2},{1,5},{3,7},{5,1},{7,3},{8,12},{10,14},{12... | collective-permute-start | bytes 786440 | tf_op jit(solution)/shard_map/ppermute | solution.py:338
  3.3 31.9 %copy-start.1 = (bf16[256,256]{1,0:T(8,128)(2,1)S(1)}, bf16[256,256]{1,0:T(8,128)(2,1)}, u32[]{:S(2)}) copy-start(bf16[256,256]{1,0:T(8,128)(2,1)} %constant.36.clone.bands) | copy-start | bytes 393220
  4.5 10.0 %collective-permute-start.2 = (f32[2,8,32,128]{3,2,1,0:T(8,128)S(1)}, f32[2,8,32,128]{3,2,1,0:T(8,128)S(1)}, u32[]{:S(2)}, u32[]{:S(2)}) collective-permute-start(f32[2,8,32,128]{3,2,1,0:T(8,128)S(1)} %get-tuple-element.32), channel_id=1, source_target_pairs={{0,6},{2,4},{4,2},{6,0},{1,7},{3,5},{5,3},{7,1},{8,14},{10,12},{12... | collective-permute-start | bytes 786440 | tf_op jit(solution)/shard_map/ppermute | solution.py:341
  4.6 9.9 %collective-permute-start = (f32[2,8,32,128]{3,2,1,0:T(8,128)S(1)}, f32[2,8,32,128]{3,2,1,0:T(8,128)S(1)}, u32[]{:S(2)}, u32[]{:S(2)}) collective-permute-start(f32[2,8,32,128]{3,2,1,0:T(8,128)S(1)} %get-tuple-element.33), channel_id=1, source_target_pairs={{0,2},{2,0},{4,6},{6,4},{1,3},{3,1},{5,7},{7,5},{8,10},{10,8},{12,... | collective-permute-start | bytes 786440 | tf_op jit(solution)/shard_map/ppermute | solution.py:341
  5.2 7.3 %collective-permute-start.3 = (f32[8,32,128]{2,1,0:T(8,128)S(1)}, f32[8,32,128]{2,1,0:T(8,128)S(1)}, u32[]{:S(2)}, u32[]{:S(2)}) collective-permute-start(f32[8,32,128]{2,1,0:T(8,128)S(1)} %copy-done), channel_id=1, source_target_pairs={{4,12},{6,14},{8,0},{10,2},{12,20},{14,22},{16,8},{18,10},{20,28},... | collective-permute-start | bytes 393224 | tf_op jit(solution)/shard_map/ppermute | solution.py:332
  15.2 20.0 %collective-permute-start.4 = (f32[2,18,32,128]{3,2,1,0:T(8,128)S(1)}, f32[2,18,32,128]{3,2,1,0:T(8,128)S(1)}, u32[]{:S(2)}, u32[]{:S(2)}) collective-permute-start(f32[2,18,32,128]{3,2,1,0:T(8,128)S(1)} %get-tuple-element.27), channel_id=1, source_target_pairs={{8,16},{16,8},{24,32},{32,24},{40,48},{48,40},{56,64},{64,56},{72,... | collective-permute-start | bytes 1769480 | tf_op jit(solution)/shard_map/ppermute | solution.py:353
  19.6 15.6 %collective-permute-start.5 = (f32[2,18,32,128]{3,2,1,0:T(8,128)S(1)}, f32[2,18,32,128]{3,2,1,0:T(8,128)S(1)}, u32[]{:S(2)}, u32[]{:S(2)}) collective-permute-start(f32[2,18,32,128]{3,2,1,0:T(8,128)S(1)} %get-tuple-element.28), channel_id=1, source_target_pairs={{0,8},{8,0},{16,24},{24,16},{32,40},{40,32},{48,56},{56,48},{64,72... | collective-permute-start | bytes 1769480 | tf_op jit(solution)/shard_map/ppermute | solution.py:354
  20.2 5.5 %collective-permute-start.8 = (f32[8,32,128]{2,1,0:T(8,128)S(1)}, f32[8,32,128]{2,1,0:T(8,128)S(1)}, u32[]{:S(2)}, u32[]{:S(2)}) collective-permute-start(f32[8,32,128]{2,1,0:T(8,128)S(1)} %copy-done), channel_id=1, source_target_pairs={{0,6},{2,4},{4,2},{6,0},{1,7},{3,5},{5,3},{7,1},{8,14},{10,12},{12... | collective-permute-start | bytes 393224 | tf_op jit(solution)/shard_map/ppermute | solution.py:357
  21.6 7.2 %collective-permute-start.7 = (f32[8,32,128]{2,1,0:T(8,128)S(1)}, f32[8,32,128]{2,1,0:T(8,128)S(1)}, u32[]{:S(2)}, u32[]{:S(2)}) collective-permute-start(f32[8,32,128]{2,1,0:T(8,128)S(1)} %copy-done), channel_id=1, source_target_pairs={{0,4},{2,6},{4,0},{6,2},{1,5},{3,7},{5,1},{7,3},{8,12},{10,14},{12... | collective-permute-start | bytes 393224 | tf_op jit(solution)/shard_map/ppermute | solution.py:357
  22.0 8.4 %collective-permute-start.6 = (f32[8,32,128]{2,1,0:T(8,128)S(1)}, f32[8,32,128]{2,1,0:T(8,128)S(1)}, u32[]{:S(2)}, u32[]{:S(2)}) collective-permute-start(f32[8,32,128]{2,1,0:T(8,128)S(1)} %copy-done), channel_id=1, source_target_pairs={{0,2},{2,0},{4,6},{6,4},{1,3},{3,1},{5,7},{7,5},{8,10},{10,8},{12,... | collective-permute-start | bytes 393224 | tf_op jit(solution)/shard_map/ppermute | solution.py:357
  25.7 5.4 %collective-permute-start.11 = (f32[8,32,128]{2,1,0:T(8,128)S(1)}, f32[8,32,128]{2,1,0:T(8,128)S(1)}, u32[]{:S(2)}, u32[]{:S(2)}) collective-permute-start(f32[8,32,128]{2,1,0:T(8,128)S(1)} %collective-permute-done.3.beyond_0), channel_id=1, source_target_pairs={{0,6},{2,4},{4,2},{6,0},{1,7},{3,5},{5,3},{7,1},{8,14},{10,12},{12... | collective-permute-start | bytes 393224 | tf_op jit(solution)/shard_map/ppermute | solution.py:357
  28.8 5.7 %collective-permute-start.10 = (f32[8,32,128]{2,1,0:T(8,128)S(1)}, f32[8,32,128]{2,1,0:T(8,128)S(1)}, u32[]{:S(2)}, u32[]{:S(2)}) collective-permute-start(f32[8,32,128]{2,1,0:T(8,128)S(1)} %collective-permute-done.3.beyond_0), channel_id=1, source_target_pairs={{0,4},{2,6},{4,0},{6,2},{1,5},{3,7},{5,1},{7,3},{8,12},{10,14},{12... | collective-permute-start | bytes 393224 | tf_op jit(solution)/shard_map/ppermute | solution.py:357
  30.5 4.0 %collective-permute-start.9 = (f32[8,32,128]{2,1,0:T(8,128)S(1)}, f32[8,32,128]{2,1,0:T(8,128)S(1)}, u32[]{:S(2)}, u32[]{:S(2)}) collective-permute-start(f32[8,32,128]{2,1,0:T(8,128)S(1)} %collective-permute-done.3.beyond_0), channel_id=1, source_target_pairs={{0,2},{2,0},{4,6},{6,4},{1,3},{3,1},{5,7},{7,5},{8,10},{10,8},{12,... | collective-permute-start | bytes 393224 | tf_op jit(solution)/shard_map/ppermute | solution.py:357
  112.5 3.6 %collective-permute-start.14 = (f32[2,128]{1,0:T(2,128)S(1)}, f32[2,128]{1,0:T(2,128)S(1)}, u32[]{:S(2)}, u32[]{:S(2)}) collective-permute-start(f32[2,128]{1,0:T(2,128)S(1)} %slice_reduce_fusion), channel_id=1, source_target_pairs={{0,6},{2,4},{4,2},{6,0},{1,7},{3,5},{5,3},{7,1},{8,14},{10,12},{12... | collective-permute-start | bytes 3080 | tf_op jit(solution)/shard_map/ppermute | solution.py:317
  112.6 3.5 %collective-permute-start.13 = (f32[2,128]{1,0:T(2,128)S(1)}, f32[2,128]{1,0:T(2,128)S(1)}, u32[]{:S(2)}, u32[]{:S(2)}) collective-permute-start(f32[2,128]{1,0:T(2,128)S(1)} %slice_reduce_fusion), channel_id=1, source_target_pairs={{0,2},{2,0},{4,6},{6,4},{1,3},{3,1},{5,7},{7,5},{8,10},{10,8},{12,... | collective-permute-start | bytes 3080 | tf_op jit(solution)/shard_map/ppermute | solution.py:317
  113.3 3.6 %collective-permute-start.12 = (f32[2,128]{1,0:T(2,128)S(1)}, f32[2,128]{1,0:T(2,128)S(1)}, u32[]{:S(2)}, u32[]{:S(2)}) collective-permute-start(f32[2,128]{1,0:T(2,128)S(1)} %slice_reduce_fusion), channel_id=1, source_target_pairs={{0,4},{2,6},{4,0},{6,2},{1,5},{3,7},{5,1},{7,3},{8,12},{10,14},{12... | collective-permute-start | bytes 3080 | tf_op jit(solution)/shard_map/ppermute | solution.py:317
